TPU v7x, 32 devices: a whole 2x2x4 slice. The times are simulated.
32 devices in a mesh: rep: 2 (over y), shard: 4 (over x, core), ctx: 4 (over z).
Axes of the slice: x: 2, y: 2, z: 4, core: 2. Of those that a mesh axis runs over, the one named last changes fastest.
Arguments:
- tokens: bfloat16 [8, 768, 1024], P(('rep', 'shard'), 'ctx'), may hold values from -6 to 6
- lengths: int32 [8, 8], P(('rep', 'shard')), may hold values from 1 to 623, as said below
- norm_one: bfloat16 [2, 1024], P(None, ('shard', 'ctx')), may hold values from 0.5 to 1.5
- w_query: bfloat16 [2, 1024, 2048], P(None, ('shard', 'ctx')), may hold values from -0.1875 to 0.1875
- w_key: bfloat16 [2, 1024, 1024], P(None, ('shard', 'ctx')), may hold values from -0.1875 to 0.1875
- w_value: bfloat16 [2, 1024, 1024], P(None, ('shard', 'ctx')), may hold values from -0.1875 to 0.1875
- query_gain: bfloat16 [2, 128], P(None, ('shard', 'ctx')), may hold values from 0.5 to 1.5
- key_gain: bfloat16 [2, 128], P(None, ('shard', 'ctx')), may hold values from 0.5 to 1.5
- w_output: bfloat16 [2, 2048, 1024], P(None, ('shard', 'ctx')), may hold values from -0.75 to 0.75
- norm_two: bfloat16 [2, 1024], P(None, ('shard', 'ctx')), may hold values from 0.5 to 1.5
- w_gate: bfloat16 [2, 1024, 3072], P(None, ('shard', 'ctx')), may hold values from -0.1875 to 0.1875
- w_up: bfloat16 [2, 1024, 3072], P(None, ('shard', 'ctx')), may hold values from -0.1875 to 0.1875
- w_down: bfloat16 [2, 3072, 1024], P(None, ('shard', 'ctx')), may hold values from -0.109375 to 0.109375
- cotangent: bfloat16 [8, 768, 1024], P(('rep', 'shard'), 'ctx'), may hold values from -6 to 6
Outputs:
- output: bfloat16 [8, 768, 1024], P(('rep', 'shard'), 'ctx')
- grad_tokens: bfloat16 [8, 768, 1024], P(('rep', 'shard'), 'ctx')
- grad_norm_one: float32 [2, 1024], P(None, ('shard', 'ctx'))
- grad_w_query: float32 [2, 1024, 2048], P(None, ('shard', 'ctx'))
- grad_w_key: float32 [2, 1024, 1024], P(None, ('shard', 'ctx'))
- grad_w_value: float32 [2, 1024, 1024], P(None, ('shard', 'ctx'))
- grad_query_gain: float32 [2, 128], P(None, ('shard', 'ctx'))
- grad_key_gain: float32 [2, 128], P(None, ('shard', 'ctx'))
- grad_w_output: float32 [2, 2048, 1024], P(None, ('shard', 'ctx'))
- grad_norm_two: float32 [2, 1024], P(None, ('shard', 'ctx'))
- grad_w_gate: float32 [2, 1024, 3072], P(None, ('shard', 'ctx'))
- grad_w_up: float32 [2, 1024, 3072], P(None, ('shard', 'ctx'))
- grad_w_down: float32 [2, 3072, 1024], P(None, ('shard', 'ctx'))
Inputs may be any that keep to these rules, and one draw needn't show every extreme that they name: `lengths`: each sequence holds 8 documents one after another from its first token, then padding of one token or more. The second document starts before token 48 and ends within the last 192 tokens.
All inputs are finite; a program needn't handle non-finite values.
Results may differ from a plain program's by a relative error of at most 0.033.
Values may be sent and summed in bfloat16 or wider, within the bound.
A program may use at most 320 MiB of HBM per device.

v0:
```python
import math

import jax
import jax.numpy as jnp
from jax import lax
from jax.sharding import PartitionSpec as P

QUERY_HEADS = 16
KEYVALUE_HEADS = 8
HEAD_SIZE = 128
LAYERS = 2
QD = 2048
KEY_FEATURES = 1024


NORM_EPS = 1e-06
ROPE_BASE = 1000000.0
VERY_NEGATIVE = -1e30


def segment_of(doc_ends, token_index):
    return jnp.sum((token_index[:, None] >= doc_ends[None, :]).astype(jnp.int32), axis=1)


def doc_layout(doc_ends, token_index):
    token_segment = segment_of(doc_ends, token_index)
    starts = jnp.concatenate([jnp.zeros((1,), jnp.int32), doc_ends])
    labels = jnp.arange(starts.shape[0], dtype=jnp.int32)
    doc_begin = jnp.sum(
        jnp.where(token_segment[:, None] == labels[None, :], starts[None, :], 0), axis=1
    )
    return (token_segment, token_index - doc_begin)


def rotary(positions, head_width):
    middle = head_width // 2
    inv_rates = jnp.exp(
        jnp.arange(middle, dtype=jnp.float32) * jnp.float32(-2.0 * math.log(ROPE_BASE) / head_width)
    )
    angles = positions.astype(jnp.float32)[:, None] * inv_rates[None, :]
    cosine = jnp.cos(angles)
    sine = jnp.sin(angles)
    return (jnp.concatenate([cosine, cosine], axis=1), jnp.concatenate([sine, sine], axis=1))


def rms_scale(values, gain_vec):
    return (
        values * lax.rsqrt(jnp.mean(values * values, axis=-1, keepdims=True) + NORM_EPS) * gain_vec
    )


def rotate(values, cosine, sine):
    middle = values.shape[-1] // 2
    turned = jnp.concatenate([-values[..., middle:], values[..., :middle]], axis=-1)
    return values * cosine[:, None, :] + turned * sine[:, None, :]


def swiglu(gate_pre, upward):
    return jax.nn.silu(gate_pre) * upward


def visible(token_segment, token_index, doc_ends, portion_rows):
    key_index = jnp.arange(portion_rows, dtype=jnp.int32)
    key_segment = segment_of(doc_ends, key_index)
    allowed = (token_segment[:, None] == key_segment[None, :]) & (
        token_index[:, None] >= key_index[None, :]
    )
    return allowed[:, None, None, :]


def layer_ahead(hidden, weights, tables):
    (
        gain_first,
        query_weight,
        key_matrix,
        value_matrix,
        gain_query,
        gain_key,
        output_weight,
        gain_second,
        gate_weight,
        up_weight,
        down_weight,
    ) = weights
    cosine, sine, token_segment, token_index, doc_ends, sequence_rows = tables
    token_rows = hidden.shape[0]
    query_group_size = QUERY_HEADS // KEYVALUE_HEADS
    score_scale = 1.0 / math.sqrt(HEAD_SIZE)
    normalized_rows = rms_scale(hidden, gain_first.astype(jnp.float32)).astype(jnp.bfloat16)
    query_proj = jnp.dot(normalized_rows, query_weight, preferred_element_type=jnp.float32).reshape(
        token_rows, QUERY_HEADS, HEAD_SIZE
    )
    key_projection = jnp.dot(
        normalized_rows, key_matrix, preferred_element_type=jnp.float32
    ).reshape(token_rows, KEYVALUE_HEADS, HEAD_SIZE)
    rows_of_values = jnp.dot(
        normalized_rows, value_matrix, preferred_element_type=jnp.float32
    ).astype(jnp.bfloat16)
    query_rows = (
        rotate(rms_scale(query_proj, gain_query.astype(jnp.float32)), cosine, sine)
        .astype(jnp.bfloat16)
        .reshape(token_rows, KEYVALUE_HEADS, query_group_size, HEAD_SIZE)
    )
    key_rows = (
        rotate(rms_scale(key_projection, gain_key.astype(jnp.float32)), cosine, sine)
        .astype(jnp.bfloat16)
        .reshape(token_rows, KEY_FEATURES)
    )
    running_maximum = jnp.full(
        (token_rows, KEYVALUE_HEADS, query_group_size), VERY_NEGATIVE, jnp.float32
    )
    key_portion = lax.all_gather(key_rows, "ctx", axis=0, tiled=True)
    value_portion = lax.all_gather(rows_of_values, "ctx", axis=0, tiled=True)
    portion_rows = key_portion.shape[0]
    allowed = visible(token_segment, token_index, doc_ends, portion_rows)
    scores = (
        jnp.einsum(
            "thgd,nhd->thgn",
            query_rows,
            key_portion.reshape(portion_rows, KEYVALUE_HEADS, HEAD_SIZE),
            preferred_element_type=jnp.float32,
        )
        * score_scale
    )
    masked = jnp.where(allowed, scores, VERY_NEGATIVE)
    new_max = jnp.maximum(running_maximum, jnp.max(masked, axis=-1))
    unnormed = jnp.where(allowed, jnp.exp(masked - new_max[..., None]), 0.0)
    running_sum = jnp.sum(unnormed, axis=-1)
    running_out = jnp.einsum(
        "thgn,nhd->thgd",
        unnormed.astype(jnp.bfloat16),
        value_portion.reshape(portion_rows, KEYVALUE_HEADS, HEAD_SIZE),
        preferred_element_type=jnp.float32,
    )
    running_maximum, running_sum, running_out = (new_max, running_sum, running_out)
    attended_rows = running_out / running_sum[..., None]
    log_sum = running_maximum + jnp.log(running_sum)
    attended_low = attended_rows.reshape(token_rows, QD).astype(jnp.bfloat16)
    hidden_mid = hidden + jnp.dot(attended_low, output_weight, preferred_element_type=jnp.float32)
    normed_two = rms_scale(hidden_mid, gain_second.astype(jnp.float32)).astype(jnp.bfloat16)
    gate_pre = jnp.dot(normed_two, gate_weight, preferred_element_type=jnp.float32)
    upward = jnp.dot(normed_two, up_weight, preferred_element_type=jnp.float32)
    activated = swiglu(gate_pre, upward).astype(jnp.bfloat16)
    hidden_out = hidden_mid + jnp.dot(activated, down_weight, preferred_element_type=jnp.float32)
    saved = (
        hidden,
        normalized_rows,
        query_proj,
        key_projection,
        rows_of_values,
        query_rows,
        key_rows,
        attended_rows,
        attended_low,
        log_sum,
        hidden_mid,
        normed_two,
        gate_pre,
        upward,
        activated,
    )
    return (hidden_out, saved)


def layer_back(upstream, weights, saved, tables):
    (
        gain_first,
        query_weight,
        key_matrix,
        value_matrix,
        gain_query,
        gain_key,
        output_weight,
        gain_second,
        gate_weight,
        up_weight,
        down_weight,
    ) = weights
    (
        hidden,
        normalized_rows,
        query_proj,
        key_projection,
        rows_of_values,
        query_rows,
        key_rows,
        attended_rows,
        attended_low,
        log_sum,
        hidden_mid,
        normed_two,
        gate_pre,
        upward,
        activated,
    ) = saved
    cosine, sine, token_segment, token_index, doc_ends, sequence_rows = tables
    token_rows = upstream.shape[0]
    query_group_size = QUERY_HEADS // KEYVALUE_HEADS
    score_scale = 1.0 / math.sqrt(HEAD_SIZE)
    branch_low = upstream.astype(jnp.bfloat16)
    grad_down = jnp.einsum("tf,td->fd", activated, branch_low, preferred_element_type=jnp.float32)
    grad_act = jnp.einsum("td,fd->tf", branch_low, down_weight, preferred_element_type=jnp.float32)
    ignored, swiglu_back = jax.vjp(swiglu, gate_pre, upward)
    grad_gate_pre, grad_upward = swiglu_back(grad_act)
    gate_low = grad_gate_pre.astype(jnp.bfloat16)
    up_low = grad_upward.astype(jnp.bfloat16)
    grad_gate = jnp.einsum("td,tf->df", normed_two, gate_low, preferred_element_type=jnp.float32)
    grad_up = jnp.einsum("td,tf->df", normed_two, up_low, preferred_element_type=jnp.float32)
    grad_normed_two = jnp.einsum(
        "tf,df->td", gate_low, gate_weight, preferred_element_type=jnp.float32
    ) + jnp.einsum("tf,df->td", up_low, up_weight, preferred_element_type=jnp.float32)
    ignored, second_back = jax.vjp(rms_scale, hidden_mid, gain_second.astype(jnp.float32))
    grad_mid, grad_gain_second = second_back(grad_normed_two)
    upstream_mid = upstream + grad_mid
    attn_low = upstream_mid.astype(jnp.bfloat16)
    grad_output = jnp.einsum(
        "tq,td->qd", attended_low, attn_low, preferred_element_type=jnp.float32
    )
    grad_attended = (
        jnp.einsum("td,qd->tq", attn_low, output_weight, preferred_element_type=jnp.float32)
        .astype(jnp.bfloat16)
        .reshape(token_rows, KEYVALUE_HEADS, query_group_size, HEAD_SIZE)
    )
    row_delta = jnp.sum(grad_attended.astype(jnp.float32) * attended_rows, axis=-1)
    key_portion = lax.all_gather(key_rows, "ctx", axis=0, tiled=True)
    value_portion = lax.all_gather(rows_of_values, "ctx", axis=0, tiled=True)
    portion_rows = key_portion.shape[0]
    heads_of_keys = key_portion.reshape(portion_rows, KEYVALUE_HEADS, HEAD_SIZE)
    heads_of_values = value_portion.reshape(portion_rows, KEYVALUE_HEADS, HEAD_SIZE)
    allowed = visible(token_segment, token_index, doc_ends, portion_rows)
    scores = (
        jnp.einsum("thgd,nhd->thgn", query_rows, heads_of_keys, preferred_element_type=jnp.float32)
        * score_scale
    )
    probability = jnp.where(allowed, jnp.exp(scores - log_sum[..., None]), 0.0)
    grad_prob = jnp.einsum(
        "thgd,nhd->thgn", grad_attended, heads_of_values, preferred_element_type=jnp.float32
    )
    grad_scores = (probability * (grad_prob - row_delta[..., None])).astype(jnp.bfloat16)
    grad_queries = (
        jnp.einsum("thgn,nhd->thgd", grad_scores, heads_of_keys, preferred_element_type=jnp.float32)
        * score_scale
    )
    grad_key_piece = (
        jnp.einsum("thgn,thgd->nhd", grad_scores, query_rows, preferred_element_type=jnp.float32)
        * score_scale
    )
    grad_value_piece = jnp.einsum(
        "thgn,thgd->nhd",
        probability.astype(jnp.bfloat16),
        grad_attended,
        preferred_element_type=jnp.float32,
    )
    update = jnp.concatenate(
        [
            grad_key_piece.reshape(portion_rows, KEY_FEATURES),
            grad_value_piece.reshape(portion_rows, KEY_FEATURES),
        ],
        axis=1,
    )
    grad_keyval = update
    grad_queries, grad_keyval = (grad_queries, grad_keyval)
    local_key_value = lax.psum_scatter(
        grad_keyval.astype(jnp.bfloat16), "ctx", scatter_dimension=0, tiled=True
    ).astype(jnp.float32)

    def prepare(projected, gain_vec):
        return rotate(rms_scale(projected, gain_vec), cosine, sine)

    ignored, query_back = jax.vjp(prepare, query_proj, gain_query.astype(jnp.float32))
    grad_query_proj, grad_gain_query = query_back(
        grad_queries.reshape(token_rows, QUERY_HEADS, HEAD_SIZE)
    )
    ignored, key_reverse_pass = jax.vjp(prepare, key_projection, gain_key.astype(jnp.float32))
    key_projection_gradient, key_gain_gradient = key_reverse_pass(
        local_key_value[:, :KEY_FEATURES].reshape(token_rows, KEYVALUE_HEADS, HEAD_SIZE)
    )
    query_low = grad_query_proj.reshape(token_rows, QD).astype(jnp.bfloat16)
    key_low = key_projection_gradient.reshape(token_rows, KEY_FEATURES).astype(jnp.bfloat16)
    value_low = local_key_value[:, KEY_FEATURES:].astype(jnp.bfloat16)
    grad_query = jnp.einsum(
        "td,tq->dq", normalized_rows, query_low, preferred_element_type=jnp.float32
    )
    grad_key = jnp.einsum("td,tk->dk", normalized_rows, key_low, preferred_element_type=jnp.float32)
    grad_value = jnp.einsum(
        "td,tk->dk", normalized_rows, value_low, preferred_element_type=jnp.float32
    )
    grad_normed = jnp.einsum(
        "tq,dq->td", query_low, query_weight, preferred_element_type=jnp.float32
    )
    grad_normed = grad_normed + jnp.einsum(
        "tk,dk->td", key_low, key_matrix, preferred_element_type=jnp.float32
    )
    grad_normed = grad_normed + jnp.einsum(
        "tk,dk->td", value_low, value_matrix, preferred_element_type=jnp.float32
    )
    ignored, first_back = jax.vjp(rms_scale, hidden, gain_first.astype(jnp.float32))
    grad_hidden, grad_gain_first = first_back(grad_normed)
    terms = (
        grad_gain_first,
        grad_query,
        grad_key,
        grad_value,
        grad_gain_query,
        key_gain_gradient,
        grad_output,
        grad_gain_second,
        grad_gate,
        grad_up,
        grad_down,
    )
    return (upstream_mid + grad_hidden, terms)


def local(
    tokens,
    lengths,
    norm_one,
    w_query,
    w_key,
    w_value,
    query_gain,
    key_gain,
    w_output,
    norm_two,
    w_gate,
    w_up,
    w_down,
    cotangent,
):
    token_rows = tokens.shape[1]
    ctx_count = lax.axis_size("ctx")
    token_index = lax.axis_index("ctx") * token_rows + jnp.arange(token_rows, dtype=jnp.int32)
    doc_lengths = lengths[0]
    doc_ends = jnp.cumsum(doc_lengths)
    token_segment, positions = doc_layout(doc_ends, token_index)
    cosine, sine = rotary(positions, HEAD_SIZE)
    tables = (cosine, sine, token_segment, token_index, doc_ends, token_rows * ctx_count)
    hidden = tokens[0].astype(jnp.float32)
    stored = []
    held_weights = []
    for which_layer in range(LAYERS):
        weights = (
            lax.all_gather(norm_one[which_layer], ("shard", "ctx"), axis=0, tiled=True),
            lax.all_gather(w_query[which_layer], ("shard", "ctx"), axis=0, tiled=True),
            lax.all_gather(w_key[which_layer], ("shard", "ctx"), axis=0, tiled=True),
            lax.all_gather(w_value[which_layer], ("shard", "ctx"), axis=0, tiled=True),
            lax.all_gather(query_gain[which_layer], ("shard", "ctx"), axis=0, tiled=True),
            lax.all_gather(key_gain[which_layer], ("shard", "ctx"), axis=0, tiled=True),
            lax.all_gather(w_output[which_layer], ("shard", "ctx"), axis=0, tiled=True),
            lax.all_gather(norm_two[which_layer], ("shard", "ctx"), axis=0, tiled=True),
            lax.all_gather(w_gate[which_layer], ("shard", "ctx"), axis=0, tiled=True),
            lax.all_gather(w_up[which_layer], ("shard", "ctx"), axis=0, tiled=True),
            lax.all_gather(w_down[which_layer], ("shard", "ctx"), axis=0, tiled=True),
        )
        held_weights.append(weights)
        hidden, saved = layer_ahead(hidden, weights, tables)
        stored.append(saved)
    output = hidden.astype(jnp.bfloat16)[None]
    live_mask = (token_segment < doc_lengths.shape[0]).astype(jnp.float32)
    upstream = cotangent[0].astype(jnp.float32) * live_mask[:, None]
    layer_grads = [None] * LAYERS
    for which_layer in reversed(range(LAYERS)):
        weights = (
            lax.all_gather(norm_one[which_layer], ("shard", "ctx"), axis=0, tiled=True),
            lax.all_gather(w_query[which_layer], ("shard", "ctx"), axis=0, tiled=True),
            lax.all_gather(w_key[which_layer], ("shard", "ctx"), axis=0, tiled=True),
            lax.all_gather(w_value[which_layer], ("shard", "ctx"), axis=0, tiled=True),
            lax.all_gather(query_gain[which_layer], ("shard", "ctx"), axis=0, tiled=True),
            lax.all_gather(key_gain[which_layer], ("shard", "ctx"), axis=0, tiled=True),
            lax.all_gather(w_output[which_layer], ("shard", "ctx"), axis=0, tiled=True),
            lax.all_gather(norm_two[which_layer], ("shard", "ctx"), axis=0, tiled=True),
            lax.all_gather(w_gate[which_layer], ("shard", "ctx"), axis=0, tiled=True),
            lax.all_gather(w_up[which_layer], ("shard", "ctx"), axis=0, tiled=True),
            lax.all_gather(w_down[which_layer], ("shard", "ctx"), axis=0, tiled=True),
        )
        upstream, terms = layer_back(upstream, weights, stored[which_layer], tables)
        owned = (
            lax.psum_scatter(terms[0], ("shard", "ctx"), scatter_dimension=0, tiled=True),
            lax.psum_scatter(terms[1], ("shard", "ctx"), scatter_dimension=0, tiled=True),
            lax.psum_scatter(terms[2], ("shard", "ctx"), scatter_dimension=0, tiled=True),
            lax.psum_scatter(terms[3], ("shard", "ctx"), scatter_dimension=0, tiled=True),
            lax.psum_scatter(terms[4], ("shard", "ctx"), scatter_dimension=0, tiled=True),
            lax.psum_scatter(terms[5], ("shard", "ctx"), scatter_dimension=0, tiled=True),
            lax.psum_scatter(terms[6], ("shard", "ctx"), scatter_dimension=0, tiled=True),
            lax.psum_scatter(terms[7], ("shard", "ctx"), scatter_dimension=0, tiled=True),
            lax.psum_scatter(terms[8], ("shard", "ctx"), scatter_dimension=0, tiled=True),
            lax.psum_scatter(terms[9], ("shard", "ctx"), scatter_dimension=0, tiled=True),
            lax.psum_scatter(terms[10], ("shard", "ctx"), scatter_dimension=0, tiled=True),
        )
        layer_grads[which_layer] = (
            lax.psum(owned[0].astype(jnp.bfloat16), "rep").astype(jnp.float32),
            lax.psum(owned[1].astype(jnp.bfloat16), "rep").astype(jnp.float32),
            lax.psum(owned[2].astype(jnp.bfloat16), "rep").astype(jnp.float32),
            lax.psum(owned[3].astype(jnp.bfloat16), "rep").astype(jnp.float32),
            lax.psum(owned[4].astype(jnp.bfloat16), "rep").astype(jnp.float32),
            lax.psum(owned[5].astype(jnp.bfloat16), "rep").astype(jnp.float32),
            lax.psum(owned[6].astype(jnp.bfloat16), "rep").astype(jnp.float32),
            lax.psum(owned[7].astype(jnp.bfloat16), "rep").astype(jnp.float32),
            lax.psum(owned[8].astype(jnp.bfloat16), "rep").astype(jnp.float32),
            lax.psum(owned[9].astype(jnp.bfloat16), "rep").astype(jnp.float32),
            lax.psum(owned[10].astype(jnp.bfloat16), "rep").astype(jnp.float32),
        )
    grad_tokens = upstream.astype(jnp.bfloat16)[None]
    stacked = tuple(
        (
            jnp.stack([layer_grads[which_layer][member] for which_layer in range(LAYERS)])
            for member in range(11)
        )
    )
    return (output, grad_tokens) + stacked


def solution(mesh):
    return jax.shard_map(
        local,
        mesh=mesh,
        in_specs=(
            P(("rep", "shard"), "ctx", None),
            P(("rep", "shard"), None),
            P(None, ("shard", "ctx")),
            P(None, ("shard", "ctx"), None),
            P(None, ("shard", "ctx"), None),
            P(None, ("shard", "ctx"), None),
            P(None, ("shard", "ctx")),
            P(None, ("shard", "ctx")),
            P(None, ("shard", "ctx"), None),
            P(None, ("shard", "ctx")),
            P(None, ("shard", "ctx"), None),
            P(None, ("shard", "ctx"), None),
            P(None, ("shard", "ctx"), None),
            P(("rep", "shard"), "ctx", None),
        ),
        out_specs=(
            P(("rep", "shard"), "ctx", None),
            P(("rep", "shard"), "ctx", None),
            P(None, ("shard", "ctx")),
            P(None, ("shard", "ctx"), None),
            P(None, ("shard", "ctx"), None),
            P(None, ("shard", "ctx"), None),
            P(None, ("shard", "ctx")),
            P(None, ("shard", "ctx")),
            P(None, ("shard", "ctx"), None),
            P(None, ("shard", "ctx")),
            P(None, ("shard", "ctx"), None),
            P(None, ("shard", "ctx"), None),
            P(None, ("shard", "ctx"), None),
        ),
        check_vma=False,
    )
```

profile of v0, /device:TPU:0, one launch (start us, length us, event | category | flops | bytes accessed | tf_op | source)
XLA Modules:
  0.0 2832.2 jit_solution(8218429256849705454)
XLA Ops:
  18.1 63.9 %all-reduce.25 = (bf16[1024]{0:T(1024)(128)(2,1)S(1)}, bf16[128]{0:T(256)(128)(2,1)S(1)}, bf16[128]{0:T(256)(128)(2,1)S(1)}, bf16[1024]{0:T(1024)(128)(2,1)S(1)}...) all-reduce(bf16[1024]{0:T(1024)(128)(2,1)S(1)} %dynamic-update-slic, ...), channel_id=2, replica_groups=mesh['rep'=2,'shard'=4,'ctx'=4] {'shard','ctx'}, use_global_device_ids=true, to_apply=%add.8 | all-reduce | flops 4608 | bytes 18432
  88.1 9.9 all-gather.51.cloned.1.call-done
  116.0 20.2 all-gather.41.cloned.1.call-done
  139.1 35.0 %all-gather.43.cloned.1.call-done = bf16[768,1024]{1,0:T(8,128)(2,1)} async-done(((bf16[192,1024]{1,0:T(8,128)(2,1)}), bf16[768,1024]{1,0:T(8,128)(2,1)}) %all-gather.43.cloned.1.call-update) | async-done | bytes 1572880 | tf_op jit(solution)/shard_map/all_gather | solution.py:112
  175.8 50.5 %all-gather.53.cloned.1.call-done = bf16[1,1024,2048]{2,1,0:T(8,128)(2,1)} async-done(((bf16[1,64,2048]{2,1,0:T(8,128)(2,1)}), bf16[1,1024,2048]{2,1,0:T(8,128)(2,1)}) %all-gather.53.cloned.1.call-update) | async-done | bytes 4194320 | tf_op jit(solution)/shard_map/all_gather | solution.py:345
  226.4 6.4 copy.227
  250.2 27.5 all-gather.55.cloned.1.call-done
  281.2 59.8 %all-gather.57.cloned.1.call-done = bf16[1,1024,3072]{2,1,0:T(8,128)(2,1)} async-done(((bf16[1,64,3072]{2,1,0:T(8,128)(2,1)}), bf16[1,1024,3072]{2,1,0:T(8,128)(2,1)}) %all-gather.57.cloned.1.call-update) | async-done | bytes 6291472 | tf_op jit(solution)/shard_map/all_gather | solution.py:352
  346.5 57.8 %all-gather.59.cloned.1.call-done = bf16[1,1024,3072]{2,1,0:T(8,128)(2,1)} async-done(((bf16[1,64,3072]{2,1,0:T(8,128)(2,1)}), bf16[1,1024,3072]{2,1,0:T(8,128)(2,1)}) %all-gather.59.cloned.1.call-update) | async-done | bytes 6291472 | tf_op jit(solution)/shard_map/all_gather | solution.py:353
  404.3 6.6 multiply_convert_fusion.3
  410.9 56.8 %all-gather.61.cloned.1.call-done = bf16[1,3072,1024]{2,1,0:T(8,128)(2,1)} async-done(((bf16[1,192,1024]{2,1,0:T(8,128)(2,1)}), bf16[1,3072,1024]{2,1,0:T(8,128)(2,1)}) %all-gather.61.cloned.1.call-update) | async-done | bytes 6291472 | tf_op jit(solution)/shard_map/all_gather | solution.py:354
  473.0 36.7 %all-gather.63.cloned.1.call-done = bf16[1,1024,1024]{2,1,0:T(8,128)(2,1)} async-done(((bf16[1,64,1024]{2,1,0:T(8,128)(2,1)}), bf16[1,1024,1024]{2,1,0:T(8,128)(2,1)}) %all-gather.63.cloned.1.call-update) | async-done | bytes 2097168 | tf_op jit(solution)/shard_map/all_gather | solution.py:347
  512.7 39.3 %all-gather.65.cloned.1.call-done = bf16[1,1024,1024]{2,1,0:T(8,128)(2,1)} async-done(((bf16[1,64,1024]{2,1,0:T(8,128)(2,1)}), bf16[1,1024,1024]{2,1,0:T(8,128)(2,1)}) %all-gather.65.cloned.1.call-update) | async-done | bytes 2097168 | tf_op jit(solution)/shard_map/all_gather | solution.py:346
  559.5 44.0 %all-gather.67.cloned.1.call-done = bf16[1,1024,2048]{2,1,0:T(8,128)(2,1)} async-done(((bf16[1,64,2048]{2,1,0:T(8,128)(2,1)}), bf16[1,1024,2048]{2,1,0:T(8,128)(2,1)}) %all-gather.67.cloned.1.call-update) | async-done | bytes 4194320 | tf_op jit(solution)/shard_map/all_gather | solution.py:345
  613.0 53.7 %all-gather.75.cloned.1.call-done = bf16[1,3072,1024]{2,1,0:T(8,128)(2,1)} async-done(((bf16[1,192,1024]{2,1,0:T(8,128)(2,1)}), bf16[1,3072,1024]{2,1,0:T(8,128)(2,1)}) %all-gather.75.cloned.1.call-update) | async-done | bytes 6291472 | tf_op jit(solution)/shard_map/all_gather | solution.py:354
  666.7 6.6 fusion.16
  673.4 31.1 %all-gather.45.cloned.1.call-done = bf16[768,1024]{1,0:T(8,128)(2,1)} async-done(((bf16[192,1024]{1,0:T(8,128)(2,1)}), bf16[768,1024]{1,0:T(8,128)(2,1)}) %all-gather.45.cloned.1.call-update) | async-done | bytes 1572880 | tf_op jit(solution)/shard_map/all_gather | solution.py:113
  707.5 35.0 %all-gather.47.cloned.1.call-done = bf16[768,1024]{1,0:T(8,128)(2,1)} async-done(((bf16[192,1024]{1,0:T(8,128)(2,1)}), bf16[768,1024]{1,0:T(8,128)(2,1)}) %all-gather.47.cloned.1.call-update) | async-done | bytes 1572880 | tf_op jit(solution)/shard_map/all_gather | solution.py:112
  756.5 37.6 %all-gather.69.cloned.1.call-done = bf16[1,2048,1024]{2,1,0:T(8,128)(2,1)} async-done(((bf16[1,128,1024]{2,1,0:T(8,128)(2,1)}), bf16[1,2048,1024]{2,1,0:T(8,128)(2,1)}) %all-gather.69.cloned.1.call-update) | async-done | bytes 4194320 | tf_op jit(solution)/shard_map/all_gather | solution.py:350
  799.4 57.2 %all-gather.73.cloned.1.call-done = bf16[1,1024,3072]{2,1,0:T(8,128)(2,1)} async-done(((bf16[1,64,3072]{2,1,0:T(8,128)(2,1)}), bf16[1,1024,3072]{2,1,0:T(8,128)(2,1)}) %all-gather.73.cloned.1.call-update) | async-done | bytes 6291472 | tf_op jit(solution)/shard_map/all_gather | solution.py:353
  862.4 57.5 %all-gather.71.cloned.1.call-done = bf16[1,1024,3072]{2,1,0:T(8,128)(2,1)} async-done(((bf16[1,64,3072]{2,1,0:T(8,128)(2,1)}), bf16[1,1024,3072]{2,1,0:T(8,128)(2,1)}) %all-gather.71.cloned.1.call-update) | async-done | bytes 6291472 | tf_op jit(solution)/shard_map/all_gather | solution.py:352
  919.9 8.0 fusion.82
  944.1 6.6 bitcast_convert_fusion.1
  980.3 46.5 %reduce-scatter.17.cloned.1.call-done = bf16[192,2048]{1,0:T(8,128)(2,1)} async-done(((bf16[768,2048]{1,0:T(8,128)(2,1)}), bf16[192,2048]{1,0:T(8,128)(2,1)}) %reduce-scatter.17.cloned.1.call-update) | async-done | bytes 786448 | tf_op jit(solution)/shard_map/reduce_scatter | solution.py:263
  1041.1 5.9 fusion.32
  1058.1 6.6 bitcast_convert_fusion
  1101.3 41.0 %reduce-scatter.19.cloned.1.call-done = bf16[192,2048]{1,0:T(8,128)(2,1)} async-done(((bf16[768,2048]{1,0:T(8,128)(2,1)}), bf16[192,2048]{1,0:T(8,128)(2,1)}) %reduce-scatter.19.cloned.1.call-update) | async-done | bytes 786448 | tf_op jit(solution)/shard_map/reduce_scatter | solution.py:263
  1173.8 7.8 fusion.257
  1182.6 7.7 fusion.309
  1190.5 7.7 fusion.311
  1199.4 7.7 fusion.251
  1208.1 7.7 fusion.308
  1215.9 7.7 fusion.310
  1225.3 69.3 %reduce-scatter.27.cloned.1.call-done = f32[64,1024]{1,0:T(8,128)} async-done(((f32[1024,1024]{1,0:T(8,128)}), f32[64,1024]{1,0:T(8,128)}) %reduce-scatter.27.cloned.1.call-update) | async-done | bytes 262160 | tf_op jit(solution)/shard_map/reduce_scatter | solution.py:381
  1296.2 106.2 %reduce-scatter.35.cloned.1.call-done = f32[128,1024]{1,0:T(8,128)} async-done(((f32[2048,1024]{1,0:T(8,128)}), f32[128,1024]{1,0:T(8,128)}) %reduce-scatter.35.cloned.1.call-update) | async-done | bytes 524304 | tf_op jit(solution)/shard_map/reduce_scatter | solution.py:385
  1404.2 106.6 %reduce-scatter.23.cloned.1.call-done = f32[64,2048]{1,0:T(8,128)} async-done(((f32[1024,2048]{1,0:T(8,128)}), f32[64,2048]{1,0:T(8,128)}) %reduce-scatter.23.cloned.1.call-update) | async-done | bytes 524304 | tf_op jit(solution)/shard_map/reduce_scatter | solution.py:380
  1512.6 74.5 %reduce-scatter.29.cloned.1.call-done = f32[64,1024]{1,0:T(8,128)} async-done(((f32[1024,1024]{1,0:T(8,128)}), f32[64,1024]{1,0:T(8,128)}) %reduce-scatter.29.cloned.1.call-update) | async-done | bytes 262160 | tf_op jit(solution)/shard_map/reduce_scatter | solution.py:382
  1588.8 74.1 %reduce-scatter.25.cloned.1.call-done = f32[64,1024]{1,0:T(8,128)} async-done(((f32[1024,1024]{1,0:T(8,128)}), f32[64,1024]{1,0:T(8,128)}) %reduce-scatter.25.cloned.1.call-update) | async-done | bytes 262160 | tf_op jit(solution)/shard_map/reduce_scatter | solution.py:381
  1664.4 106.1 %reduce-scatter.33.cloned.1.call-done = f32[128,1024]{1,0:T(8,128)} async-done(((f32[2048,1024]{1,0:T(8,128)}), f32[128,1024]{1,0:T(8,128)}) %reduce-scatter.33.cloned.1.call-update) | async-done | bytes 524304 | tf_op jit(solution)/shard_map/reduce_scatter | solution.py:385
  1772.3 106.6 %reduce-scatter.21.cloned.1.call-done = f32[64,2048]{1,0:T(8,128)} async-done(((f32[1024,2048]{1,0:T(8,128)}), f32[64,2048]{1,0:T(8,128)}) %reduce-scatter.21.cloned.1.call-update) | async-done | bytes 524304 | tf_op jit(solution)/shard_map/reduce_scatter | solution.py:380
  1880.7 136.8 %reduce-scatter.47.cloned.1.call-done = f32[192,1024]{1,0:T(8,128)} async-done(((f32[3072,1024]{1,0:T(8,128)}), f32[192,1024]{1,0:T(8,128)}) %reduce-scatter.47.cloned.1.call-update) | async-done | bytes 786448 | tf_op jit(solution)/shard_map/reduce_scatter | solution.py:389
  2019.4 135.9 %reduce-scatter.39.cloned.1.call-done = f32[64,3072]{1,0:T(8,128)} async-done(((f32[1024,3072]{1,0:T(8,128)}), f32[64,3072]{1,0:T(8,128)}) %reduce-scatter.39.cloned.1.call-update) | async-done | bytes 786448 | tf_op jit(solution)/shard_map/reduce_scatter | solution.py:387
  2157.2 136.1 %reduce-scatter.43.cloned.1.call-done = f32[64,3072]{1,0:T(8,128)} async-done(((f32[1024,3072]{1,0:T(8,128)}), f32[64,3072]{1,0:T(8,128)}) %reduce-scatter.43.cloned.1.call-update) | async-done | bytes 786448 | tf_op jit(solution)/shard_map/reduce_scatter | solution.py:388
  2295.2 136.0 %reduce-scatter.45.cloned.1.call-done = f32[192,1024]{1,0:T(8,128)} async-done(((f32[3072,1024]{1,0:T(8,128)}), f32[192,1024]{1,0:T(8,128)}) %reduce-scatter.45.cloned.1.call-update) | async-done | bytes 786448 | tf_op jit(solution)/shard_map/reduce_scatter | solution.py:389
  2433.2 135.9 %reduce-scatter.37.cloned.1.call-done = f32[64,3072]{1,0:T(8,128)} async-done(((f32[1024,3072]{1,0:T(8,128)}), f32[64,3072]{1,0:T(8,128)}) %reduce-scatter.37.cloned.1.call-update) | async-done | bytes 786448 | tf_op jit(solution)/shard_map/reduce_scatter | solution.py:387
  2571.0 136.1 %reduce-scatter.41.cloned.1.call-done = f32[64,3072]{1,0:T(8,128)} async-done(((f32[1024,3072]{1,0:T(8,128)}), f32[64,3072]{1,0:T(8,128)}) %reduce-scatter.41.cloned.1.call-update) | async-done | bytes 786448 | tf_op jit(solution)/shard_map/reduce_scatter | solution.py:388
  2721.1 60.1 %all-reduce.24 = (bf16[1024]{0:T(1024)(128)(2,1)S(1)}, bf16[1024]{0:T(1024)(128)(2,1)S(1)}, bf16[128]{0:T(256)(128)(2,1)S(1)}, bf16[128]{0:T(256)(128)(2,1)S(1)}...) all-reduce(f32[1024]{0:T(1024)S(1)} %get-tuple-element.25, ...), channel_id=27, replica_groups=mesh['rep'=2,'shard'=4,'ctx'=4] {'shard','ctx'}, use_global_device_ids=true, to_apply=%region_32.33.clone | all-reduce | flops 4608 | bytes 27648
  2790.1 25.8 all-reduce.30.cloned.1.call-done
  (592 shorter events, 313.2 us)
Async XLA Ops:
  7.2 76.9 %all-gather.49.cloned.1.call-start = ((), (), s32[]{:S(2)}) async-start(), calls=%async_computation.36 | async-start | bytes 2228224 | tf_op jit(solution)/shard_map/all_gather | solution.py:347
  8.9 89.1 %all-gather.51.cloned.1.call-start = ((), (), s32[]{:S(2)}) async-start(), calls=%async_computation.37 | async-start | bytes 2228224 | tf_op jit(solution)/shard_map/all_gather | solution.py:346
  10.7 125.4 %all-gather.41.cloned.1.call-start = ((), (), s32[]{:S(2)}) async-start(), calls=%async_computation.16 | async-start | bytes 1966080 | tf_op jit(solution)/shard_map/all_gather | solution.py:113
  82.0 150.8 %copy-start.85 = (f32[1024]{0:T(1024)}, f32[1024]{0:T(1024)S(1)}, u32[]{:S(2)}) copy-start(f32[1024]{0:T(1024)S(1)} %convert_element_type.406) | copy-start | bytes 12292
  84.0 148.7 %copy-start.109 = (f32[192]{0:T(256)}, f32[192]{0:T(256)S(1)}, u32[]{:S(2)}) copy-start(f32[192]{0:T(256)S(1)} %fusion.266) | copy-start | bytes 2308
  87.2 86.9 %all-gather.43.cloned.1.call-start = ((), (), s32[]{:S(2)}) async-start(), calls=%async_computation.17 | async-start | bytes 1966080 | tf_op jit(solution)/shard_map/all_gather | solution.py:112
  88.1 467.3 %copy-start.43 = (f32[192,128]{1,0:T(8,128)}, f32[192,128]{1,0:T(8,128)S(1)}, u32[]{:S(2)}) copy-start(f32[192,128]{1,0:T(8,128)S(1)} %get-tuple-element.140) | copy-start | bytes 294916
  88.1 938.7 %copy-start.41 = (f32[192,128]{1,0:T(8,128)}, f32[192,128]{1,0:T(8,128)S(1)}, u32[]{:S(2)}) copy-start(f32[192,128]{1,0:T(8,128)S(1)} %get-tuple-element.141) | copy-start | bytes 294916
  106.8 119.5 %all-gather.53.cloned.1.call-start = ((), (), s32[]{:S(2)}) async-start(), calls=%async_computation.38 | async-start | bytes 4456448 | tf_op jit(solution)/shard_map/all_gather | solution.py:345
  107.7 169.9 %all-gather.55.cloned.1.call-start = ((), (), s32[]{:S(2)}) async-start(), calls=%async_computation.39 | async-start | bytes 4456448 | tf_op jit(solution)/shard_map/all_gather | solution.py:350
  109.7 231.3 %all-gather.57.cloned.1.call-start = ((), (), s32[]{:S(2)}) async-start(), calls=%async_computation.40 | async-start | bytes 6684672 | tf_op jit(solution)/shard_map/all_gather | solution.py:352
  110.7 293.6 %all-gather.59.cloned.1.call-start = ((), (), s32[]{:S(2)}) async-start(), calls=%async_computation.41 | async-start | bytes 6684672 | tf_op jit(solution)/shard_map/all_gather | solution.py:353
  111.7 356.0 %all-gather.61.cloned.1.call-start = ((), (), s32[]{:S(2)}) async-start(), calls=%async_computation.42 | async-start | bytes 6684672 | tf_op jit(solution)/shard_map/all_gather | solution.py:354
  112.7 397.0 %all-gather.63.cloned.1.call-start = ((), (), s32[]{:S(2)}) async-start(), calls=%async_computation.43 | async-start | bytes 2228224 | tf_op jit(solution)/shard_map/all_gather | solution.py:347
  113.3 438.8 %all-gather.65.cloned.1.call-start = ((), (), s32[]{:S(2)}) async-start(), calls=%async_computation.44 | async-start | bytes 2228224 | tf_op jit(solution)/shard_map/all_gather | solution.py:346
  114.0 489.4 %all-gather.67.cloned.1.call-start = ((), (), s32[]{:S(2)}) async-start(), calls=%async_computation.45 | async-start | bytes 4456448 | tf_op jit(solution)/shard_map/all_gather | solution.py:345
  114.6 552.1 %all-gather.75.cloned.1.call-start = ((), (), s32[]{:S(2)}) async-start(), calls=%async_computation.49 | async-start | bytes 6684672 | tf_op jit(solution)/shard_map/all_gather | solution.py:354
  115.3 589.1 %all-gather.45.cloned.1.call-start = ((), (), s32[]{:S(2)}) async-start(), calls=%async_computation.18 | async-start | bytes 1966080 | tf_op jit(solution)/shard_map/all_gather | solution.py:113
  115.6 165.4 %copy-start.103 = (f32[1024]{0:T(1024)}, f32[1024]{0:T(1024)S(1)}, u32[]{:S(2)}) copy-start(f32[1024]{0:T(1024)S(1)} %convert_element_type.409) | copy-start | bytes 12292
  115.6 356.4 %copy-start.107 = (f32[1024]{0:T(1024)}, f32[1024]{0:T(1024)S(1)}, u32[]{:S(2)}) copy-start(f32[1024]{0:T(1024)S(1)} %convert_element_type.410) | copy-start | bytes 12292
  116.0 128.0 %copy-start.53 = (pred[192,768]{1,0:T(8,128)(4,1)}, pred[192,768]{1,0:T(8,128)(4,1)S(1)}, u32[]{:S(2)}) copy-start(pred[192,768]{1,0:T(8,128)(4,1)S(1)} %fusion.221) | copy-start | bytes 442372
  281.0 186.7 %copy-start.18 = (f32[192,1024]{1,0:T(8,128)}, f32[192,1024]{1,0:T(8,128)S(1)}, u32[]{:S(2)}) copy-start(f32[192,1024]{1,0:T(8,128)S(1)} %get-tuple-element.125) | copy-start | bytes 2359300
  281.2 123.1 %copy-start.38 = (bf16[192,1024]{1,0:T(8,128)(2,1)}, bf16[192,1024]{1,0:T(8,128)(2,1)S(1)}, u32[]{:S(2)}) copy-start(bf16[192,1024]{1,0:T(8,128)(2,1)S(1)} %multiply_convert_fusion.6) | copy-start | bytes 1179652
  473.0 130.5 %copy-start.11 = (bf16[192,1024]{1,0:T(8,128)(2,1)}, bf16[192,1024]{1,0:T(8,128)(2,1)S(1)}, u32[]{:S(2)}) copy-start(bf16[192,1024]{1,0:T(8,128)(2,1)S(1)} %multiply_convert_fusion.5) | copy-start | bytes 1179652
  512.6 229.8 %all-gather.47.cloned.1.call-start = ((), (), s32[]{:S(2)}) async-start(), calls=%async_computation.19 | async-start | bytes 1966080 | tf_op jit(solution)/shard_map/all_gather | solution.py:112
  557.2 236.9 %all-gather.69.cloned.1.call-start = ((), (), s32[]{:S(2)}) async-start(), calls=%async_computation.46 | async-start | bytes 4456448 | tf_op jit(solution)/shard_map/all_gather | solution.py:350
  557.8 298.9 %all-gather.73.cloned.1.call-start = ((), (), s32[]{:S(2)}) async-start(), calls=%async_computation.48 | async-start | bytes 6684672 | tf_op jit(solution)/shard_map/all_gather | solution.py:353
  558.4 361.5 %all-gather.71.cloned.1.call-start = ((), (), s32[]{:S(2)}) async-start(), calls=%async_computation.47 | async-start | bytes 6684672 | tf_op jit(solution)/shard_map/all_gather | solution.py:352
  558.9 467.9 %reduce-scatter.17.cloned.1.call-start = ((), (), s32[]{:S(2)}) async-start(), calls=%async_computation.20 | async-start | bytes 3932160 | tf_op jit(solution)/shard_map/reduce_scatter | solution.py:263
  559.5 375.1 %copy-start.113 = (f32[192]{0:T(256)}, f32[192]{0:T(256)S(1)}, u32[]{:S(2)}) copy-start(f32[192]{0:T(256)S(1)} %compare_convert_fusion) | copy-start | bytes 2308
  613.0 131.3 %copy-start.28 = (bf16[192,8,2,128]{3,0,2,1:T(8,128)(2,1)}, bf16[192,8,2,128]{3,0,2,1:T(8,128)(2,1)S(1)}, u32[]{:S(2)}) copy-start(bf16[192,8,2,128]{3,0,2,1:T(8,128)(2,1)S(1)} %fusion.112) | copy-start | bytes 2359300
  797.9 136.7 %copy-start.22 = (f32[192,1024]{1,0:T(8,128)}, f32[192,1024]{1,0:T(8,128)S(1)}, u32[]{:S(2)}) copy-start(f32[192,1024]{1,0:T(8,128)S(1)} %get-tuple-element.135) | copy-start | bytes 2359300
  967.8 174.4 %reduce-scatter.19.cloned.1.call-start = ((), (), s32[]{:S(2)}) async-start(), calls=%async_computation.21 | async-start | bytes 3932160 | tf_op jit(solution)/shard_map/reduce_scatter | solution.py:263
  1081.8 141.9 %reduce-scatter.31.cloned.1.call-start = ((), (), s32[]{:S(2)}) async-start(), calls=%async_computation.27 | async-start | bytes 4456448 | tf_op jit(solution)/shard_map/reduce_scatter | solution.py:382
  1085.7 208.9 %reduce-scatter.27.cloned.1.call-start = ((), (), s32[]{:S(2)}) async-start(), calls=%async_computation.25 | async-start | bytes 4456448 | tf_op jit(solution)/shard_map/reduce_scatter | solution.py:381
  1089.6 312.9 %reduce-scatter.35.cloned.1.call-start = ((), (), s32[]{:S(2)}) async-start(), calls=%async_computation.29 | async-start | bytes 8912896 | tf_op jit(solution)/shard_map/reduce_scatter | solution.py:385
  1095.4 415.5 %reduce-scatter.23.cloned.1.call-start = ((), (), s32[]{:S(2)}) async-start(), calls=%async_computation.23 | async-start | bytes 8912896 | tf_op jit(solution)/shard_map/reduce_scatter | solution.py:380
  1101.2 485.9 %reduce-scatter.29.cloned.1.call-start = ((), (), s32[]{:S(2)}) async-start(), calls=%async_computation.26 | async-start | bytes 4456448 | tf_op jit(solution)/shard_map/reduce_scatter | solution.py:382
  1146.1 516.8 %reduce-scatter.25.cloned.1.call-start = ((), (), s32[]{:S(2)}) async-start(), calls=%async_computation.24 | async-start | bytes 4456448 | tf_op jit(solution)/shard_map/reduce_scatter | solution.py:381
  1152.5 618.0 %reduce-scatter.33.cloned.1.call-start = ((), (), s32[]{:S(2)}) async-start(), calls=%async_computation.28 | async-start | bytes 8912896 | tf_op jit(solution)/shard_map/reduce_scatter | solution.py:385
  1158.3 720.6 %reduce-scatter.21.cloned.1.call-start = ((), (), s32[]{:S(2)}) async-start(), calls=%async_computation.22 | async-start | bytes 8912896 | tf_op jit(solution)/shard_map/reduce_scatter | solution.py:380
  1172.8 844.7 %reduce-scatter.47.cloned.1.call-start = ((), (), s32[]{:S(2)}) async-start(), calls=%async_computation.35 | async-start | bytes 13369344 | tf_op jit(solution)/shard_map/reduce_scatter | solution.py:389
  1181.6 973.7 %reduce-scatter.39.cloned.1.call-start = ((), (), s32[]{:S(2)}) async-start(), calls=%async_computation.31 | async-start | bytes 13369344 | tf_op jit(solution)/shard_map/reduce_scatter | solution.py:387
  1190.3 1103.0 %reduce-scatter.43.cloned.1.call-start = ((), (), s32[]{:S(2)}) async-start(), calls=%async_computation.33 | async-start | bytes 13369344 | tf_op jit(solution)/shard_map/reduce_scatter | solution.py:388
  1198.3 1233.0 %reduce-scatter.45.cloned.1.call-start = ((), (), s32[]{:S(2)}) async-start(), calls=%async_computation.34 | async-start | bytes 13369344 | tf_op jit(solution)/shard_map/reduce_scatter | solution.py:389
  1207.1 1361.9 %reduce-scatter.37.cloned.1.call-start = ((), (), s32[]{:S(2)}) async-start(), calls=%async_computation.30 | async-start | bytes 13369344 | tf_op jit(solution)/shard_map/reduce_scatter | solution.py:387
  1215.8 1491.2 %reduce-scatter.41.cloned.1.call-start = ((), (), s32[]{:S(2)}) async-start(), calls=%async_computation.32 | async-start | bytes 13369344 | tf_op jit(solution)/shard_map/reduce_scatter | solution.py:388
  1223.6 1592.2 %all-reduce.30.cloned.1.call-start = ((), (), s32[]{:S(2)}) async-start(), calls=%async_computation.50 | async-start | bytes 7864320 | tf_op jit(solution)/shard_map/psum | solution.py:393
  (138 other events, 1324.1 us)
Sparse Core Ops, SparseCore 0:
  10.8 44.1 all-gather.48
  57.8 40.1 all-gather.50
  100.2 35.9 all-gather.40
  138.1 35.9 all-gather.42
  176.7 49.5 all-gather.52
  228.4 49.2 all-gather.54
  280.5 60.3 all-gather.56
  343.8 60.4 all-gather.58
  407.2 60.4 all-gather.60
  469.7 39.9 all-gather.62
  511.9 40.0 all-gather.64
  554.1 49.3 all-gather.66
  606.3 60.3 all-gather.74
  668.7 35.6 all-gather.44
  706.4 35.9 all-gather.46
  744.5 49.5 all-gather.68
  796.3 60.3 all-gather.72
  859.4 60.4 all-gather.70
  967.9 58.8 reduce-scatter.16
  1081.9 60.2 reduce-scatter.18
  1146.1 72.6 reduce-scatter.30
  1223.1 71.4 reduce-scatter.26
  1298.7 103.7 reduce-scatter.34
  1406.4 104.3 reduce-scatter.22
  1514.7 72.4 reduce-scatter.28
  1591.3 71.4 reduce-scatter.24
  1666.7 103.7 reduce-scatter.32
  1774.6 104.3 reduce-scatter.20
  1883.0 134.4 reduce-scatter.46
  2021.4 133.8 reduce-scatter.38
  2159.4 133.8 reduce-scatter.42
  2297.4 133.8 reduce-scatter.44
  2435.2 133.8 reduce-scatter.36
  2573.1 133.8 reduce-scatter.40
  2711.4 104.3 all-reduce.29
where the time goes:
time: 2840 us; the launch traced here: 2830 us
  waiting for transfers between devices  2290 us (81%)
  matrix products  222 us (8%)
  blocking collectives  129 us (5%)
  local copies, waits for them, and re-layouts  87.8 us (3%)
  other arithmetic  84.7 us (3%)
    reduce_scatter x2, waiting for transfers between devices, local(): lax.psum_scatter(terms[10], ('shard', 'ctx'), scatter_dimension=0, tiled=...  273 us
    reduce_scatter x2, waiting for transfers between devices, local(): lax.psum_scatter(terms[9], ('shard', 'ctx'), scatter_dimension=0, tiled=T...  272 us
    reduce_scatter x2, waiting for transfers between devices, local(): lax.psum_scatter(terms[8], ('shard', 'ctx'), scatter_dimension=0, tiled=T...  272 us
    reduce_scatter x2, waiting for transfers between devices, local(): lax.psum_scatter(terms[1], ('shard', 'ctx'), scatter_dimension=0, tiled=T...  213 us
    reduce_scatter x2, waiting for transfers between devices, local(): lax.psum_scatter(terms[6], ('shard', 'ctx'), scatter_dimension=0, tiled=T...  212 us
    reduce_scatter x2, waiting for transfers between devices, local(): lax.psum_scatter(terms[2], ('shard', 'ctx'), scatter_dimension=0, tiled=T...  143 us
    unnamed x2, blocking collectives  124 us
    all_gather x2, waiting for transfers between devices, local(): lax.all_gather(w_gate[which_layer], ('shard', 'ctx'), axis=0, tiled=True)  117 us
  transfers between devices with their start and end apart: 35, of which 33 were waited for; matrix products, arithmetic and copies ran while one was open for 9% of the time, Pallas kernels for 0%

commit v1 on v0

--- a/solution.py
+++ b/solution.py
@@ -1,8 +1,11 @@
+import functools
 import math
 
 import jax
 import jax.numpy as jnp
 from jax import lax
+from jax.experimental import pallas as pl
+from jax.experimental.pallas import tpu as pltpu
 from jax.sharding import PartitionSpec as P
 
 QUERY_HEADS = 16
@@ -16,6 +19,234 @@
 NORM_EPS = 1e-06
 ROPE_BASE = 1000000.0
 VERY_NEGATIVE = -1e30
+
+MESH = pl.DeviceIdType.MESH
+
+
+def gather_kernel(shapes, nx, nz, *refs):
+    count = len(shapes)
+    shards, wholes = refs[:count], refs[count : 2 * count]
+    own_sem, z_sem, x_sem, y_sem, core_sem, out_sem = refs[2 * count :]
+    y = lax.axis_index("rep")
+    shard = lax.axis_index("shard")
+    z = lax.axis_index("ctx")
+    core, x = lax.rem(shard, 2), lax.div(shard, 2)
+    to_core = (y, x * 2 + 1 - core, z)
+    to_y = (1 - y, shard, z)
+
+    def to_x(step):
+        return (y, shard + 2 * step, z)
+
+    def to_z(step):
+        return (y, shard, z + step)
+
+    def rows_of(k, xs, zs, start, size, of_core=core):
+        rows = shapes[k][0]
+        first = ((xs * 2 + of_core) * nz + zs) * rows + start
+        return wholes[k].at[pl.ds(pl.multiple_of(first, 16), size)]
+
+    def inplane(k):
+        rows, _, near = shapes[k]
+        return y * (rows - near), near
+
+    def send(src, dst, send_sem, recv_sem, device):
+        pltpu.make_async_remote_copy(
+            src_ref=src,
+            dst_ref=dst,
+            send_sem=send_sem,
+            recv_sem=recv_sem,
+            device_id=device,
+            device_id_type=MESH,
+        ).start()
+
+    def arrived(ref, sem):
+        pltpu.make_async_copy(ref, ref, sem).wait()
+
+    def pass_z(k, src, zs, step, kind):
+        start, size = inplane(k)
+        send(src, rows_of(k, x, zs, start, size), out_sem.at[k, kind], z_sem.at[k, zs], to_z(step))
+
+    def pass_x(k, src, xs, zs, step, kind):
+        start, size = inplane(k)
+        send(src, rows_of(k, xs, zs, start, size), out_sem.at[k, kind], x_sem.at[k, xs * nz + zs], to_x(step))
+
+    def pass_y(k, xs, zs):
+        rows, _, near = shapes[k]
+        if rows > near:
+            part = rows_of(k, xs, zs, y * near, rows - near)
+            send(part, part, out_sem.at[k, 4], y_sem.at[k, xs * nz + zs], to_y)
+
+    def pass_core(k, xs, zs, start, size):
+        part = rows_of(k, xs, zs, start, size)
+        send(part, part, out_sem.at[k, 5], core_sem.at[k], to_core)
+
+    def stage_own(k):
+        rows, _, near = shapes[k]
+        start, size = inplane(k)
+        part = shards[k].at[pl.ds(pl.multiple_of(start, 16), size)]
+
+        @pl.when(z < nz - 1)
+        def _():
+            pass_z(k, part, z, 1, 0)
+
+        @pl.when(z > 0)
+        def _():
+            pass_z(k, part, z, -1, 1)
+
+        @pl.when(x < nx - 1)
+        def _():
+            pass_x(k, part, x, z, 1, 2)
+
+        @pl.when(x > 0)
+        def _():
+            pass_x(k, part, x, z, -1, 3)
+
+        send(shards[k], rows_of(k, x, z, 0, rows), out_sem.at[k, 5], core_sem.at[k], to_core)
+        pltpu.make_async_copy(shards[k], rows_of(k, x, z, 0, rows), own_sem.at[k]).start()
+
+    def stage_z(k, d):
+        start, size = inplane(k)
+        for step, kind in ((1, 0), (-1, 1)):
+            zs = z - step * d
+
+            @pl.when((zs >= 0) & (zs < nz))
+            def _():
+                part = rows_of(k, x, zs, start, size)
+                arrived(part, z_sem.at[k, zs])
+
+                @pl.when((z + step >= 0) & (z + step < nz))
+                def _():
+                    pass_z(k, part, zs, step, kind)
+
+                @pl.when(x < nx - 1)
+                def _():
+                    pass_x(k, part, x, zs, 1, 2)
+
+                @pl.when(x > 0)
+                def _():
+                    pass_x(k, part, x, zs, -1, 3)
+
+                pass_y(k, x, zs)
+                pass_core(k, x, zs, start, size)
+
+    def stage_x(k, d):
+        start, size = inplane(k)
+        for step, kind in ((1, 2), (-1, 3)):
+            xs = x - step * d
+
+            @pl.when((xs >= 0) & (xs < nx))
+            def _():
+                def body(zs, carry):
+                    part = rows_of(k, xs, zs, start, size)
+                    arrived(part, x_sem.at[k, xs * nz + zs])
+                    if nx > 2:
+
+                        @pl.when((x + step >= 0) & (x + step < nx))
+                        def _():
+                            pass_x(k, part, xs, zs, step, kind)
+
+                    pass_y(k, xs, zs)
+                    pass_core(k, xs, zs, start, size)
+                    return carry
+
+                lax.fori_loop(0, nz, body, 0)
+
+    def stage_y(k):
+        rows, _, near = shapes[k]
+        if rows > near:
+
+            def body(i, carry):
+                xs, zs = lax.div(i, nz), lax.rem(i, nz)
+
+                @pl.when((xs != x) | (zs != z))
+                def _():
+                    start = (1 - y) * near
+                    arrived(rows_of(k, xs, zs, start, rows - near), y_sem.at[k, i])
+                    pass_core(k, xs, zs, start, rows - near)
+
+                return carry
+
+            lax.fori_loop(0, nx * nz, body, 0)
+
+    def first_rows(k, size):
+        return wholes[k].at[pl.ds(0, size)]
+
+    def stage_end(k):
+        rows, _, near = shapes[k]
+        arrived(first_rows(k, nx * nz * rows), core_sem.at[k])
+        arrived(first_rows(k, rows), own_sem.at[k])
+        for zz in range(nz):
+
+            @pl.when(z == zz)
+            def _():
+                if zz < nz - 1:
+                    arrived(first_rows(k, (zz + 1) * near), out_sem.at[k, 0])
+                if zz > 0:
+                    arrived(first_rows(k, (nz - zz) * near), out_sem.at[k, 1])
+
+        for xx in range(nx):
+
+            @pl.when(x == xx)
+            def _():
+                if xx < nx - 1:
+                    arrived(first_rows(k, (xx + 1) * nz * near), out_sem.at[k, 2])
+                if xx > 0:
+                    arrived(first_rows(k, (nx - xx) * nz * near), out_sem.at[k, 3])
+
+        if rows > near:
+            arrived(first_rows(k, (nx * nz - 1) * (rows - near)), out_sem.at[k, 4])
+            arrived(
+                first_rows(k, nx * nz * rows), out_sem.at[k, 5]
+            )
+        else:
+            arrived(first_rows(k, nx * nz * rows), out_sem.at[k, 5])
+
+    barrier = pltpu.get_barrier_semaphore()
+    pl.semaphore_signal(barrier, inc=1, device_id=to_core, device_id_type=MESH)
+    pl.semaphore_signal(barrier, inc=1, device_id=to_y, device_id_type=MESH)
+    for here, there in ((z > 0, to_z(-1)), (z < nz - 1, to_z(1)), (x > 0, to_x(-1)), (x < nx - 1, to_x(1))):
+
+        @pl.when(here)
+        def _():
+            pl.semaphore_signal(barrier, inc=1, device_id=there, device_id_type=MESH)
+
+    greeted = 2 + (z > 0).astype(jnp.int32) + (z < nz - 1).astype(jnp.int32)
+    greeted = greeted + (x > 0).astype(jnp.int32) + (x < nx - 1).astype(jnp.int32)
+    pl.semaphore_wait(barrier, greeted)
+
+    stages = [stage_own]
+    stages += [functools.partial(stage_z, d=d) for d in range(1, nz)]
+    stages += [functools.partial(stage_x, d=d) for d in range(1, nx)]
+    stages += [stage_y]
+    for tick in range(count + len(stages) - 1):
+        for depth, stage in enumerate(stages):
+            k = tick - depth
+            if 0 <= k < count:
+                stage(k)
+    for k in range(count):
+        stage_end(k)
+
+
+def gather_weights(shards, nears, nx, nz, collective_id):
+    count = len(shards)
+    shapes = tuple((a.shape[0], a.shape[1], near) for a, near in zip(shards, nears))
+    return pl.pallas_call(
+        functools.partial(gather_kernel, shapes, nx, nz),
+        out_shape=[
+            jax.ShapeDtypeStruct((a.shape[0] * 2 * nx * nz, a.shape[1]), a.dtype) for a in shards
+        ],
+        in_specs=[pl.BlockSpec(memory_space=pl.ANY)] * count,
+        out_specs=[pl.BlockSpec(memory_space=pl.ANY)] * count,
+        scratch_shapes=[
+            pltpu.SemaphoreType.DMA((count,)),
+            pltpu.SemaphoreType.DMA((count, nz)),
+            pltpu.SemaphoreType.DMA((count, nx * nz)),
+            pltpu.SemaphoreType.DMA((count, nx * nz)),
+            pltpu.SemaphoreType.DMA((count,)),
+            pltpu.SemaphoreType.DMA((count, 6)),
+        ],
+        compiler_params=pltpu.CompilerParams(collective_id=collective_id, has_side_effects=True),
+    )(*shards)
 
 
 def segment_of(doc_ends, token_index):
@@ -312,6 +543,36 @@
     return (upstream_mid + grad_hidden, terms)
 
 
+def near_rows(rows, share):
+    return min(rows, -(-int(rows * share) // 16) * 16)
+
+
+def gather_all(parts):
+    nx, nz = lax.axis_size("shard") // 2, lax.axis_size("ctx")
+    gains = (parts[0], parts[4], parts[5], parts[7])
+    flat = jnp.concatenate([g.reshape(-1) for g in gains])
+    small = jnp.zeros((16 * 128,), flat.dtype).at[: flat.shape[0]].set(flat).reshape(16, 128)
+    big = (1, 2, 3, 6, 8, 9, 10)
+    shares = (0.75, 0.75, 0.75, 0.6, 0.5, 0.75, 0.55)
+    shards, nears = [small], [16]
+    for which_layer in range(LAYERS):
+        for member, share in zip(big, shares):
+            shards.append(parts[member][which_layer])
+            nears.append(near_rows(parts[member].shape[1], share))
+    wholes = gather_weights(shards, nears, nx, nz, 0)
+    every = wholes[0].reshape(2 * nx * nz, 16 * 128)[:, : flat.shape[0]]
+    out, used = [[None] * 11 for _ in range(LAYERS)], 0
+    for member, g in zip((0, 4, 5, 7), gains):
+        here = every[:, used : used + g.size].reshape(-1, LAYERS, g.shape[1])
+        used += g.size
+        for which_layer in range(LAYERS):
+            out[which_layer][member] = here[:, which_layer].reshape(-1)
+    for which_layer in range(LAYERS):
+        for i, member in enumerate(big):
+            out[which_layer][member] = wholes[1 + which_layer * 7 + i]
+    return out
+
+
 def local(
     tokens,
     lengths,
@@ -332,27 +593,17 @@
     ctx_count = lax.axis_size("ctx")
     token_index = lax.axis_index("ctx") * token_rows + jnp.arange(token_rows, dtype=jnp.int32)
     doc_lengths = lengths[0]
-    doc_ends = jnp.cumsum(doc_lengths)
+    upto = jnp.arange(doc_lengths.shape[0])
+    doc_ends = jnp.sum(jnp.where(upto[:, None] >= upto[None, :], doc_lengths[None, :], 0), axis=1)
     token_segment, positions = doc_layout(doc_ends, token_index)
     cosine, sine = rotary(positions, HEAD_SIZE)
     tables = (cosine, sine, token_segment, token_index, doc_ends, token_rows * ctx_count)
     hidden = tokens[0].astype(jnp.float32)
     stored = []
     held_weights = []
+    gathered = gather_all((norm_one, w_query, w_key, w_value, query_gain, key_gain, w_output, norm_two, w_gate, w_up, w_down))
     for which_layer in range(LAYERS):
-        weights = (
-            lax.all_gather(norm_one[which_layer], ("shard", "ctx"), axis=0, tiled=True),
-            lax.all_gather(w_query[which_layer], ("shard", "ctx"), axis=0, tiled=True),
-            lax.all_gather(w_key[which_layer], ("shard", "ctx"), axis=0, tiled=True),
-            lax.all_gather(w_value[which_layer], ("shard", "ctx"), axis=0, tiled=True),
-            lax.all_gather(query_gain[which_layer], ("shard", "ctx"), axis=0, tiled=True),
-            lax.all_gather(key_gain[which_layer], ("shard", "ctx"), axis=0, tiled=True),
-            lax.all_gather(w_output[which_layer], ("shard", "ctx"), axis=0, tiled=True),
-            lax.all_gather(norm_two[which_layer], ("shard", "ctx"), axis=0, tiled=True),
-            lax.all_gather(w_gate[which_layer], ("shard", "ctx"), axis=0, tiled=True),
-            lax.all_gather(w_up[which_layer], ("shard", "ctx"), axis=0, tiled=True),
-            lax.all_gather(w_down[which_layer], ("shard", "ctx"), axis=0, tiled=True),
-        )
+        weights = gathered[which_layer]
         held_weights.append(weights)
         hidden, saved = layer_ahead(hidden, weights, tables)
         stored.append(saved)
@@ -361,32 +612,20 @@
     upstream = cotangent[0].astype(jnp.float32) * live_mask[:, None]
     layer_grads = [None] * LAYERS
     for which_layer in reversed(range(LAYERS)):
-        weights = (
-            lax.all_gather(norm_one[which_layer], ("shard", "ctx"), axis=0, tiled=True),
-            lax.all_gather(w_query[which_layer], ("shard", "ctx"), axis=0, tiled=True),
-            lax.all_gather(w_key[which_layer], ("shard", "ctx"), axis=0, tiled=True),
-            lax.all_gather(w_value[which_layer], ("shard", "ctx"), axis=0, tiled=True),
-            lax.all_gather(query_gain[which_layer], ("shard", "ctx"), axis=0, tiled=True),
-            lax.all_gather(key_gain[which_layer], ("shard", "ctx"), axis=0, tiled=True),
-            lax.all_gather(w_output[which_layer], ("shard", "ctx"), axis=0, tiled=True),
-            lax.all_gather(norm_two[which_layer], ("shard", "ctx"), axis=0, tiled=True),
-            lax.all_gather(w_gate[which_layer], ("shard", "ctx"), axis=0, tiled=True),
-            lax.all_gather(w_up[which_layer], ("shard", "ctx"), axis=0, tiled=True),
-            lax.all_gather(w_down[which_layer], ("shard", "ctx"), axis=0, tiled=True),
-        )
+        weights = gathered[which_layer]
         upstream, terms = layer_back(upstream, weights, stored[which_layer], tables)
         owned = (
-            lax.psum_scatter(terms[0], ("shard", "ctx"), scatter_dimension=0, tiled=True),
-            lax.psum_scatter(terms[1], ("shard", "ctx"), scatter_dimension=0, tiled=True),
-            lax.psum_scatter(terms[2], ("shard", "ctx"), scatter_dimension=0, tiled=True),
-            lax.psum_scatter(terms[3], ("shard", "ctx"), scatter_dimension=0, tiled=True),
-            lax.psum_scatter(terms[4], ("shard", "ctx"), scatter_dimension=0, tiled=True),
-            lax.psum_scatter(terms[5], ("shard", "ctx"), scatter_dimension=0, tiled=True),
-            lax.psum_scatter(terms[6], ("shard", "ctx"), scatter_dimension=0, tiled=True),
-            lax.psum_scatter(terms[7], ("shard", "ctx"), scatter_dimension=0, tiled=True),
-            lax.psum_scatter(terms[8], ("shard", "ctx"), scatter_dimension=0, tiled=True),
-            lax.psum_scatter(terms[9], ("shard", "ctx"), scatter_dimension=0, tiled=True),
-            lax.psum_scatter(terms[10], ("shard", "ctx"), scatter_dimension=0, tiled=True),
+            lax.psum_scatter(terms[0].astype(jnp.bfloat16), ("shard", "ctx"), scatter_dimension=0, tiled=True),
+            lax.psum_scatter(terms[1].astype(jnp.bfloat16), ("shard", "ctx"), scatter_dimension=0, tiled=True),
+            lax.psum_scatter(terms[2].astype(jnp.bfloat16), ("shard", "ctx"), scatter_dimension=0, tiled=True),
+            lax.psum_scatter(terms[3].astype(jnp.bfloat16), ("shard", "ctx"), scatter_dimension=0, tiled=True),
+            lax.psum_scatter(terms[4].astype(jnp.bfloat16), ("shard", "ctx"), scatter_dimension=0, tiled=True),
+            lax.psum_scatter(terms[5].astype(jnp.bfloat16), ("shard", "ctx"), scatter_dimension=0, tiled=True),
+            lax.psum_scatter(terms[6].astype(jnp.bfloat16), ("shard", "ctx"), scatter_dimension=0, tiled=True),
+            lax.psum_scatter(terms[7].astype(jnp.bfloat16), ("shard", "ctx"), scatter_dimension=0, tiled=True),
+            lax.psum_scatter(terms[8].astype(jnp.bfloat16), ("shard", "ctx"), scatter_dimension=0, tiled=True),
+            lax.psum_scatter(terms[9].astype(jnp.bfloat16), ("shard", "ctx"), scatter_dimension=0, tiled=True),
+            lax.psum_scatter(terms[10].astype(jnp.bfloat16), ("shard", "ctx"), scatter_dimension=0, tiled=True),
         )
         layer_grads[which_layer] = (
             lax.psum(owned[0].astype(jnp.bfloat16), "rep").astype(jnp.float32),

time: 2840 us -> 1930 us (0.68)
  waiting for transfers between devices: 2290 us -> 1270 us
  Pallas kernels: 0 us -> 249 us
  blocking collectives: 129 us -> 64.4 us
  matrix products: 222 us -> 171 us
    all_gather x14 -> x0, waiting for transfers between devices: 588 us -> none  [the longest x2 117 us: local(): lax.all_gather(w_gate[which_layer], ('shard', 'ctx'), axis=0, tiled=True)]
    reduce_scatter x14, waiting for transfers between devices: 1460 us -> 1070 us  [the longest x2 177 us: local(): lax.psum_scatter(terms[8].astype(jnp.bfloat16), ('shard', 'ctx'), scatter...]
    pallas_call x0 -> x1, Pallas kernels: none -> 249 us  [gather_weights(): pl.pallas_call(functools.partial(gather_kernel, shapes, nx, nz), out_shap...]
    unnamed x2 -> x1, blocking collectives: 124 us -> 59.4 us
    reduce_scatter x2, waiting for transfers between devices: 87.5 us -> 58.9 us  [layer_back(): lax.psum_scatter(grad_keyval.astype(jnp.bfloat16), 'ctx', scatter_dimensi...]
  transfers between devices with their start and end apart: 35 -> 21, of which waited for: 33 -> 21; matrix products, arithmetic and copies ran while one was open for 9% -> 7% of each run, Pallas kernels for 0% -> 0%
where the time goes in v1:
time: 1930 us; the launch traced here: 1920 us
  waiting for transfers between devices  1270 us (66%)
  Pallas kernels  249 us (13%)
  matrix products  171 us (9%)
  local copies, waits for them, and re-layouts  85.3 us (4%)
  blocking collectives  64.4 us (3%)
  other arithmetic  59.1 us (3%)
    pallas_call x1, Pallas kernels, gather_weights(): pl.pallas_call(functools.partial(gather_kernel, shapes, nx, nz), out_shap...  249 us
    reduce_scatter x2, waiting for transfers between devices, local(): lax.psum_scatter(terms[8].astype(jnp.bfloat16), ('shard', 'ctx'), scatter...  177 us
    reduce_scatter x2, waiting for transfers between devices, local(): lax.psum_scatter(terms[9].astype(jnp.bfloat16), ('shard', 'ctx'), scatter...  177 us
    reduce_scatter x2, waiting for transfers between devices, local(): lax.psum_scatter(terms[10].astype(jnp.bfloat16), ('shard', 'ctx'), scatte...  177 us
    reduce_scatter x2, waiting for transfers between devices, local(): lax.psum_scatter(terms[1].astype(jnp.bfloat16), ('shard', 'ctx'), scatter...  151 us
    reduce_scatter x2, waiting for transfers between devices, local(): lax.psum_scatter(terms[3].astype(jnp.bfloat16), ('shard', 'ctx'), scatter...  129 us
    reduce_scatter x2, waiting for transfers between devices, local(): lax.psum_scatter(terms[2].astype(jnp.bfloat16), ('shard', 'ctx'), scatter...  129 us
    reduce_scatter x2, waiting for transfers between devices, local(): lax.psum_scatter(terms[6].astype(jnp.bfloat16), ('shard', 'ctx'), scatter...  128 us
  transfers between devices with their start and end apart: 21, of which 21 were waited for; matrix products, arithmetic and copies ran while one was open for 7% of the time, Pallas kernels for 0%

profile of v1, /device:TPU:0, one launch (start us, length us, event | category | flops | bytes accessed | tf_op | source)
XLA Modules:
  0.0 1917.5 jit_solution(7226240876208421368)
XLA Ops:
  19.0 249.2 %shard_map.237 = (bf16[256,128]{1,0:T(8,128)(2,1)}, bf16[1024,2048]{1,0:T(8,128)(2,1)}, bf16[1024,1024]{1,0:T(8,128)(2,1)}, bf16[1024,1024]{1,0:T(8,128)(2,1)}, ...) custom-call(bf16[16,128]{1,0:T(8,128)(2,1)} %fusion.173.refs_0_, ...), custom_call_target="tpu_custom_call" | custom-call | tf_op jit(solution)/shard_map/pallas_call | solution.py:233
  283.3 6.4 copy.315
  289.8 3.9 multiply_reduce_fusion.6
  296.5 21.9 %all-gather.5.cloned.1.call-done = bf16[768,1024]{1,0:T(8,128)(2,1)} async-done(((bf16[192,1024]{1,0:T(8,128)(2,1)}), bf16[768,1024]{1,0:T(8,128)(2,1)}) %all-gather.5.cloned.1.call-update) | async-done | bytes 1572880 | tf_op jit(solution)/shard_map/all_gather | solution.py:344
  321.5 35.1 %all-gather.7.cloned.1.call-done = bf16[768,1024]{1,0:T(8,128)(2,1)} async-done(((bf16[192,1024]{1,0:T(8,128)(2,1)}), bf16[768,1024]{1,0:T(8,128)(2,1)}) %all-gather.7.cloned.1.call-update) | async-done | bytes 1572880 | tf_op jit(solution)/shard_map/all_gather | solution.py:343
  364.0 4.3 fusion.200
  373.6 4.4 fusion.202
  399.7 21.8 %all-gather.9.cloned.1.call-done = bf16[768,1024]{1,0:T(8,128)(2,1)} async-done(((bf16[192,1024]{1,0:T(8,128)(2,1)}), bf16[768,1024]{1,0:T(8,128)(2,1)}) %all-gather.9.cloned.1.call-update) | async-done | bytes 1572880 | tf_op jit(solution)/shard_map/all_gather | solution.py:344
  424.5 35.0 %all-gather.11.cloned.1.call-done = bf16[768,1024]{1,0:T(8,128)(2,1)} async-done(((bf16[192,1024]{1,0:T(8,128)(2,1)}), bf16[768,1024]{1,0:T(8,128)(2,1)}) %all-gather.11.cloned.1.call-update) | async-done | bytes 1572880 | tf_op jit(solution)/shard_map/all_gather | solution.py:343
  467.2 4.0 fusion.201
  476.2 3.7 multiply_reduce_fusion.16
  480.0 4.5 fusion.206
  486.0 7.0 multiply_convert_fusion.1
  501.7 3.6 reshape.558
  507.8 6.6 bitcast_convert_fusion.1
  514.5 3.7 fusion.3
  527.6 3.9 pad_maximum_fusion
  532.9 4.2 convolution_multiply_fusion.1
  543.6 47.2 %reduce-scatter.17.cloned.1.call-done = bf16[192,2048]{1,0:T(8,128)(2,1)} async-done(((bf16[768,2048]{1,0:T(8,128)(2,1)}), bf16[192,2048]{1,0:T(8,128)(2,1)}) %reduce-scatter.17.cloned.1.call-update) | async-done | bytes 786448 | tf_op jit(solution)/shard_map/reduce_scatter | solution.py:494
  598.1 6.4 multiply_convert_fusion
  618.0 6.6 bitcast_convert_fusion
  624.7 3.7 fusion.1
  654.2 4.5 convolution_convert_fusion
  660.1 4.5 convolution_convert_fusion.2
  665.9 4.4 convolution_convert_fusion.4
  676.1 3.7 convolution_multiply_fusion
  688.1 11.7 reduce-scatter.19.cloned.1.call-done
  708.3 4.4 convolution_convert_fusion.1
  714.3 4.4 convolution_convert_fusion.3
  720.0 4.4 convolution_convert_fusion.5
  724.8 51.7 %reduce-scatter.35.cloned.1.call-done = bf16[128,1024]{1,0:T(8,128)(2,1)} async-done(((bf16[2048,1024]{1,0:T(8,128)(2,1)}), bf16[128,1024]{1,0:T(8,128)(2,1)}) %reduce-scatter.35.cloned.1.call-update) | async-done | bytes 262160 | tf_op jit(solution)/shard_map/reduce_scatter | solution.py:624
  776.5 75.8 %reduce-scatter.23.cloned.1.call-done = bf16[64,2048]{1,0:T(8,128)(2,1)} async-done(((bf16[1024,2048]{1,0:T(8,128)(2,1)}), bf16[64,2048]{1,0:T(8,128)(2,1)}) %reduce-scatter.23.cloned.1.call-update) | async-done | bytes 262160 | tf_op jit(solution)/shard_map/reduce_scatter | solution.py:619
  852.3 64.3 %reduce-scatter.31.cloned.1.call-done = bf16[64,1024]{1,0:T(8,128)(2,1)} async-done(((bf16[1024,1024]{1,0:T(8,128)(2,1)}), bf16[64,1024]{1,0:T(8,128)(2,1)}) %reduce-scatter.31.cloned.1.call-update) | async-done | bytes 131088 | tf_op jit(solution)/shard_map/reduce_scatter | solution.py:621
  916.7 64.6 %reduce-scatter.27.cloned.1.call-done = bf16[64,1024]{1,0:T(8,128)(2,1)} async-done(((bf16[1024,1024]{1,0:T(8,128)(2,1)}), bf16[64,1024]{1,0:T(8,128)(2,1)}) %reduce-scatter.27.cloned.1.call-update) | async-done | bytes 131088 | tf_op jit(solution)/shard_map/reduce_scatter | solution.py:620
  981.3 88.2 %reduce-scatter.47.cloned.1.call-done = bf16[192,1024]{1,0:T(8,128)(2,1)} async-done(((bf16[3072,1024]{1,0:T(8,128)(2,1)}), bf16[192,1024]{1,0:T(8,128)(2,1)}) %reduce-scatter.47.cloned.1.call-update) | async-done | bytes 393232 | tf_op jit(solution)/shard_map/reduce_scatter | solution.py:628
  1069.5 88.8 %reduce-scatter.43.cloned.1.call-done = bf16[64,3072]{1,0:T(8,128)(2,1)} async-done(((bf16[1024,3072]{1,0:T(8,128)(2,1)}), bf16[64,3072]{1,0:T(8,128)(2,1)}) %reduce-scatter.43.cloned.1.call-update) | async-done | bytes 393232 | tf_op jit(solution)/shard_map/reduce_scatter | solution.py:627
  1158.3 88.5 %reduce-scatter.39.cloned.1.call-done = bf16[64,3072]{1,0:T(8,128)(2,1)} async-done(((bf16[1024,3072]{1,0:T(8,128)(2,1)}), bf16[64,3072]{1,0:T(8,128)(2,1)}) %reduce-scatter.39.cloned.1.call-update) | async-done | bytes 393232 | tf_op jit(solution)/shard_map/reduce_scatter | solution.py:626
  1246.8 76.2 %reduce-scatter.33.cloned.1.call-done = bf16[128,1024]{1,0:T(8,128)(2,1)} async-done(((bf16[2048,1024]{1,0:T(8,128)(2,1)}), bf16[128,1024]{1,0:T(8,128)(2,1)}) %reduce-scatter.33.cloned.1.call-update) | async-done | bytes 262160 | tf_op jit(solution)/shard_map/reduce_scatter | solution.py:624
  1323.1 75.3 %reduce-scatter.21.cloned.1.call-done = bf16[64,2048]{1,0:T(8,128)(2,1)} async-done(((bf16[1024,2048]{1,0:T(8,128)(2,1)}), bf16[64,2048]{1,0:T(8,128)(2,1)}) %reduce-scatter.21.cloned.1.call-update) | async-done | bytes 262160 | tf_op jit(solution)/shard_map/reduce_scatter | solution.py:619
  1398.4 64.6 %reduce-scatter.29.cloned.1.call-done = bf16[64,1024]{1,0:T(8,128)(2,1)} async-done(((bf16[1024,1024]{1,0:T(8,128)(2,1)}), bf16[64,1024]{1,0:T(8,128)(2,1)}) %reduce-scatter.29.cloned.1.call-update) | async-done | bytes 131088 | tf_op jit(solution)/shard_map/reduce_scatter | solution.py:621
  1463.0 64.2 %reduce-scatter.25.cloned.1.call-done = bf16[64,1024]{1,0:T(8,128)(2,1)} async-done(((bf16[1024,1024]{1,0:T(8,128)(2,1)}), bf16[64,1024]{1,0:T(8,128)(2,1)}) %reduce-scatter.25.cloned.1.call-update) | async-done | bytes 131088 | tf_op jit(solution)/shard_map/reduce_scatter | solution.py:620
  1527.2 88.5 %reduce-scatter.45.cloned.1.call-done = bf16[192,1024]{1,0:T(8,128)(2,1)} async-done(((bf16[3072,1024]{1,0:T(8,128)(2,1)}), bf16[192,1024]{1,0:T(8,128)(2,1)}) %reduce-scatter.45.cloned.1.call-update) | async-done | bytes 393232 | tf_op jit(solution)/shard_map/reduce_scatter | solution.py:628
  1615.7 88.5 %reduce-scatter.41.cloned.1.call-done = bf16[64,3072]{1,0:T(8,128)(2,1)} async-done(((bf16[1024,3072]{1,0:T(8,128)(2,1)}), bf16[64,3072]{1,0:T(8,128)(2,1)}) %reduce-scatter.41.cloned.1.call-update) | async-done | bytes 393232 | tf_op jit(solution)/shard_map/reduce_scatter | solution.py:627
  1704.2 88.9 %reduce-scatter.37.cloned.1.call-done = bf16[64,3072]{1,0:T(8,128)(2,1)} async-done(((bf16[1024,3072]{1,0:T(8,128)(2,1)}), bf16[64,3072]{1,0:T(8,128)(2,1)}) %reduce-scatter.37.cloned.1.call-update) | async-done | bytes 393232 | tf_op jit(solution)/shard_map/reduce_scatter | solution.py:626
  1795.6 5.1 fusion.74
  1806.0 59.4 %all-reduce.17 = (bf16[1024]{0:T(1024)(128)(2,1)S(1)}, bf16[1024]{0:T(1024)(128)(2,1)S(1)}, bf16[128]{0:T(256)(128)(2,1)S(1)}, bf16[128]{0:T(256)(128)(2,1)S(1)}...) all-reduce(bf16[1024]{0:T(1024)(128)(2,1)S(1)} %get-tuple-element.6, ...), channel_id=5, replica_groups=mesh['rep'=2,'shard'=4,'ctx'=4] {'shard','ctx'}, use_global_device_ids=true, to_apply=%region_32.33.clone | all-reduce | flops 4608 | bytes 18432
  1866.0 5.0 all-reduce.18
  1874.3 26.5 %all-reduce.22.cloned.1.call-done = (bf16[1,64,2048]{2,1,0:T(8,128)(2,1)}, bf16[1,64,2048]{2,1,0:T(8,128)(2,1)}, bf16[1,64,1024]{2,1,0:T(8,128)(2,1)}, bf16[1,64...) async-done(((bf16[1,64,2048]{2,1,0:T(8,128)(2,1)}, ...) | async-done | bytes 3932176 | tf_op jit(solution)/shard_map/psum | solution.py:632
  (591 shorter events, 205.7 us)
Async XLA Ops:
  7.2 9.1 copy-start.104
  7.2 9.1 copy-start.105
  7.2 311.3 %all-gather.5.cloned.1.call-start = ((), (), s32[]{:S(2)}) async-start(), calls=%async_computation.16 | async-start | bytes 1966080 | tf_op jit(solution)/shard_map/all_gather | solution.py:344
  11.5 278.3 %copy-start.116 = (f32[192]{0:T(256)}, f32[192]{0:T(256)S(1)}, u32[]{:S(2)}) copy-start(f32[192]{0:T(256)S(1)} %fusion.174) | copy-start | bytes 2308
  18.3 251.2 %copy-start.6 = (bf16[1,192,1024]{2,1,0:T(8,128)(2,1)S(1)}, bf16[1,192,1024]{2,1,0:T(8,128)(2,1)}, u32[]{:S(2)}) copy-start(bf16[1,192,1024]{2,1,0:T(8,128)(2,1)} %param.16) | copy-start | bytes 1179652
  269.5 20.3 %copy-start.96 = (f32[1024]{0:T(1024)}, f32[1024]{0:T(1024)S(1)}, u32[]{:S(2)}) copy-start(f32[1024]{0:T(1024)S(1)} %reshape.571) | copy-start | bytes 12292
  272.5 84.1 %all-gather.7.cloned.1.call-start = ((), (), s32[]{:S(2)}) async-start(), calls=%async_computation.17 | async-start | bytes 1966080 | tf_op jit(solution)/shard_map/all_gather | solution.py:343
  275.8 18.5 copy-start.127
  276.5 19.1 copy-start.45
  281.3 140.2 %all-gather.9.cloned.1.call-start = ((), (), s32[]{:S(2)}) async-start(), calls=%async_computation.18 | async-start | bytes 1966080 | tf_op jit(solution)/shard_map/all_gather | solution.py:344
  282.5 13.1 copy-start.140
  282.5 100.5 %copy-start.120 = (f32[1024]{0:T(1024)}, f32[1024]{0:T(1024)S(1)}, u32[]{:S(2)}) copy-start(f32[1024]{0:T(1024)S(1)} %reshape.575) | copy-start | bytes 12292
  283.3 90.2 %copy-start.118 = (f32[1024]{0:T(1024)}, f32[1024]{0:T(1024)S(1)}, u32[]{:S(2)}) copy-start(f32[1024]{0:T(1024)S(1)} %reshape.574) | copy-start | bytes 12292
  294.6 68.9 %copy-start.57 = (pred[192,768]{1,0:T(8,128)(4,1)}, pred[192,768]{1,0:T(8,128)(4,1)S(1)}, u32[]{:S(2)}) copy-start(pred[192,768]{1,0:T(8,128)(4,1)S(1)} %fusion.123) | copy-start | bytes 442372
  296.5 61.8 %copy-start.43 = (bf16[192,16,128]{2,0,1:T(8,128)(2,1)}, bf16[192,16,128]{2,0,1:T(8,128)(2,1)S(1)}, u32[]{:S(2)}) copy-start(bf16[192,16,128]{2,0,1:T(8,128)(2,1)S(1)} %fusion.52) | copy-start | bytes 2359300
  385.4 74.1 %all-gather.11.cloned.1.call-start = ((), (), s32[]{:S(2)}) async-start(), calls=%async_computation.19 | async-start | bytes 1966080 | tf_op jit(solution)/shard_map/all_gather | solution.py:343
  389.5 201.3 %reduce-scatter.17.cloned.1.call-start = ((), (), s32[]{:S(2)}) async-start(), calls=%async_computation.20 | async-start | bytes 3932160 | tf_op jit(solution)/shard_map/reduce_scatter | solution.py:494
  390.0 108.1 %copy-start.144 = (f32[192]{0:T(256)}, f32[192]{0:T(256)S(1)}, u32[]{:S(2)}) copy-start(f32[192]{0:T(256)S(1)} %compare_convert_fusion) | copy-start | bytes 2308
  399.7 61.6 %copy-start.35 = (bf16[192,8,2,128]{3,0,2,1:T(8,128)(2,1)}, bf16[192,8,2,128]{3,0,2,1:T(8,128)(2,1)S(1)}, u32[]{:S(2)}) copy-start(bf16[192,8,2,128]{3,0,2,1:T(8,128)(2,1)S(1)} %fusion.54) | copy-start | bytes 2359300
  424.5 36.9 %copy-start.58 = (pred[192,768]{1,0:T(8,128)(4,1)S(1)}, pred[192,768]{1,0:T(8,128)(4,1)}, u32[]{:S(2)}) copy-start(pred[192,768]{1,0:T(8,128)(4,1)} %copy-done.57) | copy-start | bytes 442372
  479.8 18.3 copy-start.28
  484.6 10.6 slice-start.3
  486.0 9.2 slice-start.4
  499.3 15.2 slice-start
  505.4 9.1 slice-start.1
  531.6 168.2 %reduce-scatter.19.cloned.1.call-start = ((), (), s32[]{:S(2)}) async-start(), calls=%async_computation.21 | async-start | bytes 3932160 | tf_op jit(solution)/shard_map/reduce_scatter | solution.py:494
  543.6 48.6 %copy-start.139 = (f32[128]{0:T(128)S(1)}, f32[128]{0:T(128)}, u32[]{:S(2)}) copy-start(f32[128]{0:T(128)} %copy-done.138) | copy-start | bytes 1540
  596.5 10.4 slice-start.14
  597.8 11.6 copy-start.49
  609.7 14.9 slice-start.5
  639.3 137.2 %reduce-scatter.35.cloned.1.call-start = ((), (), s32[]{:S(2)}) async-start(), calls=%async_computation.29 | async-start | bytes 4456448 | tf_op jit(solution)/shard_map/reduce_scatter | solution.py:624
  643.7 208.6 %reduce-scatter.23.cloned.1.call-start = ((), (), s32[]{:S(2)}) async-start(), calls=%async_computation.23 | async-start | bytes 4456448 | tf_op jit(solution)/shard_map/reduce_scatter | solution.py:619
  648.3 268.4 %reduce-scatter.31.cloned.1.call-start = ((), (), s32[]{:S(2)}) async-start(), calls=%async_computation.27 | async-start | bytes 2228224 | tf_op jit(solution)/shard_map/reduce_scatter | solution.py:621
  651.5 329.8 %reduce-scatter.27.cloned.1.call-start = ((), (), s32[]{:S(2)}) async-start(), calls=%async_computation.25 | async-start | bytes 2228224 | tf_op jit(solution)/shard_map/reduce_scatter | solution.py:620
  653.7 415.8 %reduce-scatter.47.cloned.1.call-start = ((), (), s32[]{:S(2)}) async-start(), calls=%async_computation.35 | async-start | bytes 6684672 | tf_op jit(solution)/shard_map/reduce_scatter | solution.py:628
  658.7 499.6 %reduce-scatter.43.cloned.1.call-start = ((), (), s32[]{:S(2)}) async-start(), calls=%async_computation.33 | async-start | bytes 6684672 | tf_op jit(solution)/shard_map/reduce_scatter | solution.py:627
  664.7 582.2 %reduce-scatter.39.cloned.1.call-start = ((), (), s32[]{:S(2)}) async-start(), calls=%async_computation.31 | async-start | bytes 6684672 | tf_op jit(solution)/shard_map/reduce_scatter | solution.py:626
  670.4 652.7 %reduce-scatter.33.cloned.1.call-start = ((), (), s32[]{:S(2)}) async-start(), calls=%async_computation.28 | async-start | bytes 4456448 | tf_op jit(solution)/shard_map/reduce_scatter | solution.py:624
  674.8 723.6 %reduce-scatter.21.cloned.1.call-start = ((), (), s32[]{:S(2)}) async-start(), calls=%async_computation.22 | async-start | bytes 4456448 | tf_op jit(solution)/shard_map/reduce_scatter | solution.py:619
  687.9 775.1 %reduce-scatter.29.cloned.1.call-start = ((), (), s32[]{:S(2)}) async-start(), calls=%async_computation.26 | async-start | bytes 2228224 | tf_op jit(solution)/shard_map/reduce_scatter | solution.py:621
  703.0 824.2 %reduce-scatter.25.cloned.1.call-start = ((), (), s32[]{:S(2)}) async-start(), calls=%async_computation.24 | async-start | bytes 2228224 | tf_op jit(solution)/shard_map/reduce_scatter | solution.py:620
  708.3 907.4 %reduce-scatter.45.cloned.1.call-start = ((), (), s32[]{:S(2)}) async-start(), calls=%async_computation.34 | async-start | bytes 6684672 | tf_op jit(solution)/shard_map/reduce_scatter | solution.py:628
  712.8 991.4 %reduce-scatter.41.cloned.1.call-start = ((), (), s32[]{:S(2)}) async-start(), calls=%async_computation.32 | async-start | bytes 6684672 | tf_op jit(solution)/shard_map/reduce_scatter | solution.py:627
  718.7 1074.3 %reduce-scatter.37.cloned.1.call-start = ((), (), s32[]{:S(2)}) async-start(), calls=%async_computation.30 | async-start | bytes 6684672 | tf_op jit(solution)/shard_map/reduce_scatter | solution.py:626
  724.5 1071.1 %copy-start.29 = (f32[192,1024]{1,0:T(8,128)S(1)}, f32[192,1024]{1,0:T(8,128)}, u32[]{:S(2)}) copy-start(f32[192,1024]{1,0:T(8,128)} %copy-done.28) | copy-start | bytes 2359300
  724.5 1071.1 %copy-start.75 = (bf16[192,3072]{1,0:T(8,128)(2,1)S(1)}, bf16[192,3072]{1,0:T(8,128)(2,1)}, u32[]{:S(2)}) copy-start(bf16[192,3072]{1,0:T(8,128)(2,1)} %get-tuple-element.111) | copy-start | bytes 3538948
  724.5 1176.3 %all-reduce.22.cloned.1.call-start = ((), (), s32[]{:S(2)}) async-start(), calls=%async_computation.36 | async-start | bytes 7864320 | tf_op jit(solution)/shard_map/psum | solution.py:632
  1804.8 68.4 %copy-start.147 = (f32[192]{0:T(256)S(1)}, f32[192]{0:T(256)}, u32[]{:S(2)}) copy-start(f32[192]{0:T(256)} %copy-done.146) | copy-start | bytes 2308
  (150 other events, 450.9 us)
Sparse Core Ops, SparseCore 0:
  272.6 45.8 all-gather.4
  320.6 35.9 all-gather.6
  385.5 35.9 all-gather.8
  423.5 35.9 all-gather.10
  531.7 59.0 reduce-scatter.16
  639.5 60.2 reduce-scatter.18
  703.6 72.8 reduce-scatter.34
  780.8 71.4 reduce-scatter.22
  856.1 60.5 reduce-scatter.30
  920.7 60.5 reduce-scatter.26
  985.2 84.1 reduce-scatter.46
  1073.8 84.4 reduce-scatter.42
  1162.2 84.5 reduce-scatter.38
  1251.1 71.9 reduce-scatter.32
  1326.8 71.5 reduce-scatter.20
  1402.4 60.4 reduce-scatter.28
  1466.6 60.5 reduce-scatter.24
  1531.5 84.1 reduce-scatter.44
  1619.6 84.4 reduce-scatter.40
  1708.5 84.5 reduce-scatter.36
  1796.2 104.5 all-reduce.21

commit v2 on v1

--- a/solution.py
+++ b/solution.py
@@ -8,6 +8,7 @@
 from jax.experimental.pallas import tpu as pltpu
 from jax.sharding import PartitionSpec as P
 
+D = 1024
 QUERY_HEADS = 16
 KEYVALUE_HEADS = 8
 HEAD_SIZE = 128
@@ -247,6 +248,377 @@
         ],
         compiler_params=pltpu.CompilerParams(collective_id=collective_id, has_side_effects=True),
     )(*shards)
+
+
+SLOTS = 4
+PIECES = 15
+LEFTS, RIGHTS = 7, 12
+
+
+def left_of(j):
+    return jnp.where(j < 4, 0, jnp.where(j < 10, 1, j - 8))
+
+
+def right_of(j):
+    return jnp.where(j < 10, j, jnp.where(j < 12, 10, 11))
+
+
+def reduce_kernel(nx, nz, layers, lefts, rights, out, left_at, right_at, total, y_in, x_in, zup_in, zdown_in, f_in, result, left_sem, right_sem, y_sem, x_sem, zup_sem, zdown_sem, f_sem, result_sem, credit):
+    rows, tokens = lefts.shape[-2:]
+    wide = rights.shape[-1]
+    quarter = wide // 4
+    kept = 3 * quarter
+    pieces = layers * PIECES
+    y = lax.axis_index("rep")
+    shard = lax.axis_index("shard")
+    z = lax.axis_index("ctx")
+    core, x = lax.rem(shard, 2), lax.div(shard, 2)
+    to_core = (y, x * 2 + 1 - core, z)
+    to_y = (1 - y, shard, z)
+
+    def to_x(step):
+        return (y, shard + 2 * step, z)
+
+    def to_z(step):
+        return (y, shard, z + step)
+
+    ring = total.shape[0]
+    kept_at = pl.multiple_of(y * quarter, quarter)
+
+    barrier = pltpu.get_barrier_semaphore()
+    pl.semaphore_signal(barrier, inc=1, device_id=to_core, device_id_type=MESH)
+    pl.semaphore_signal(barrier, inc=1, device_id=to_y, device_id_type=MESH)
+    for here, there in ((z > 0, to_z(-1)), (z < nz - 1, to_z(1)), (x > 0, to_x(-1)), (x < nx - 1, to_x(1))):
+
+        @pl.when(here)
+        def _():
+            pl.semaphore_signal(barrier, inc=1, device_id=there, device_id_type=MESH)
+
+    greeted = 2 + (z > 0).astype(jnp.int32) + (z < nz - 1).astype(jnp.int32)
+    greeted = greeted + (x > 0).astype(jnp.int32) + (x < nx - 1).astype(jnp.int32)
+    pl.semaphore_wait(barrier, greeted)
+
+    def left_copies(b):
+        for xs in range(nx):
+            mine = lefts.at[b, xs, core]
+            yield pltpu.make_async_copy(mine, left_at.at[0, b, xs], left_sem.at[0, b, xs])
+            yield pltpu.make_async_remote_copy(
+                src_ref=lefts.at[b, xs, 1 - core],
+                dst_ref=left_at.at[1, b, xs],
+                send_sem=left_sem.at[2, b, xs],
+                recv_sem=left_sem.at[1, b, xs],
+                device_id=to_core,
+                device_id_type=MESH,
+            )
+
+    def right_copies(b):
+        yield pltpu.make_async_copy(rights.at[b], right_at.at[0, b], right_sem.at[0, b])
+        yield pltpu.make_async_remote_copy(
+            src_ref=rights.at[b],
+            dst_ref=right_at.at[1, b],
+            send_sem=right_sem.at[2, b],
+            recv_sem=right_sem.at[1, b],
+            device_id=to_core,
+            device_id_type=MESH,
+        )
+
+    def first_left(j):
+        return (j == 0) | (j == 4) | (j >= 10)
+
+    def first_right(j):
+        return (j <= 10) | (j == 12)
+
+    def blocks(i):
+        layer, j = lax.div(i, PIECES), lax.rem(i, PIECES)
+        return layer, j, layer * LEFTS + left_of(j), layer * RIGHTS + right_of(j)
+
+    def fetch(i, carry):
+        layer, j, lb, rb = blocks(i)
+
+        @pl.when(first_left(j))
+        def _():
+            for copy in left_copies(lb):
+                copy.start()
+
+        @pl.when(first_right(j))
+        def _():
+            for copy in right_copies(rb):
+                copy.start()
+
+        return carry
+
+    lax.fori_loop(0, pieces, fetch, 0)
+
+    def y_copy(i):
+        return pltpu.make_async_remote_copy(
+            src_ref=total.at[lax.rem(i, ring), :, :, :, pl.ds(pl.multiple_of((1 - y) * kept, quarter), quarter)],
+            dst_ref=y_in.at[lax.rem(i, SLOTS)],
+            send_sem=y_sem.at[0, i],
+            recv_sem=y_sem.at[1, i],
+            device_id=to_y,
+            device_id_type=MESH,
+        )
+
+    def f_copy(i):
+        return pltpu.make_async_remote_copy(
+            src_ref=total.at[lax.rem(i, ring), x, z, :, pl.ds(kept_at, kept)],
+            dst_ref=f_in.at[lax.rem(i, SLOTS)],
+            send_sem=f_sem.at[0, i],
+            recv_sem=f_sem.at[1, i],
+            device_id=to_y,
+            device_id_type=MESH,
+        )
+
+    def use(flow):
+        pl.semaphore_wait(credit.at[flow], 1)
+
+    def give(i, flow, device):
+        @pl.when(i + SLOTS < pieces)
+        def _():
+            pl.semaphore_signal(credit.at[flow], inc=1, device_id=device, device_id_type=MESH)
+
+    def spend(i, flow):
+        @pl.when(i >= SLOTS)
+        def _():
+            use(flow)
+
+    def product(i):
+        layer, j, lb, rb = blocks(i)
+
+        @pl.when(first_left(j))
+        def _():
+            for copy in left_copies(lb):
+                copy.wait()
+
+        @pl.when(first_right(j))
+        def _():
+            for copy in right_copies(rb):
+                copy.wait()
+
+        slot = lax.rem(i, ring)
+
+        def tile(c, carry):
+            at = pl.ds(pl.multiple_of(c * quarter, quarter), quarter)
+            acc = None
+            for who in range(2):
+                left = left_at[who, lb].reshape(nx * nz * rows, tokens)
+                part = jnp.dot(left, right_at[who, rb, :, at], preferred_element_type=jnp.float32)
+                acc = part if acc is None else acc + part
+            total[slot, :, :, :, at] = acc.reshape(nx, nz, rows, quarter).astype(total.dtype)
+            return carry
+
+        lax.fori_loop(0, 4, tile, 0)
+        spend(i, 0)
+        y_copy(i).start()
+
+    def add(slot, xs, zs, at, width, value):
+        where = (slot, xs, zs, slice(None), pl.ds(at, width))
+        total[where] = (total[where].astype(jnp.float32) + value.astype(jnp.float32)).astype(total.dtype)
+
+    def take_y(i):
+        slot, small = lax.rem(i, ring), lax.rem(i, SLOTS)
+        y_copy(i).wait_recv()
+
+        def body(n, carry):
+            xs, zs = lax.div(n, nz), lax.rem(n, nz)
+            add(slot, xs, zs, pl.multiple_of(y * kept, quarter), quarter, y_in[small, xs, zs])
+            return carry
+
+        lax.fori_loop(0, nx * nz, body, 0)
+        give(i, 0, to_y)
+
+    def x_copy(i, up, here):
+        low, high = (here + 1, nx) if up else (0, here)
+        side = 0 if (up or nx == 2) else 1
+        return pltpu.make_async_remote_copy(
+            src_ref=total.at[lax.rem(i, ring), pl.ds(low, high - low), :, :, pl.ds(kept_at, kept)],
+            dst_ref=x_in.at[lax.rem(i, SLOTS), side, pl.ds(low - (1 if up else 0), high - low)],
+            send_sem=x_sem.at[0 if up else 1, i],
+            recv_sem=x_sem.at[2 if up else 3, i],
+            device_id=to_x(1 if up else -1),
+            device_id_type=MESH,
+        )
+
+    def z_copy(i, up, here):
+        low, high = (here + 1, nz) if up else (0, here)
+        into = zup_in if up else zdown_in
+        sems = zup_sem if up else zdown_sem
+        return pltpu.make_async_remote_copy(
+            src_ref=total.at[lax.rem(i, ring), x, pl.ds(low, high - low), :, pl.ds(kept_at, kept)],
+            dst_ref=into.at[lax.rem(i, SLOTS), pl.ds(low - (1 if up else 0), high - low)],
+            send_sem=sems.at[0, i],
+            recv_sem=sems.at[1, i],
+            device_id=to_z(1 if up else -1),
+            device_id_type=MESH,
+        )
+
+    def x_hop(i, h):
+        slot, small = lax.rem(i, ring), lax.rem(i, SLOTS)
+        for up in (True, False):
+            here = h if up else nx - 1 - h
+            side = 0 if (up or nx == 2) else 1
+
+            @pl.when(x == here)
+            def _():
+                if h > 0:
+                    x_copy(i, up, here - 1 if up else here + 1).wait_recv()
+                    for target in range(here, nx) if up else range(here + 1):
+
+                        def body(zs, carry):
+                            add(slot, target, zs, kept_at, kept, x_in[small, side, target - (1 if up else 0), zs])
+                            return carry
+
+                        lax.fori_loop(0, nz, body, 0)
+                    give(i, 1 if up else 2, to_x(-1 if up else 1))
+                if h < nx - 1:
+                    spend(i, 1 if up else 2)
+                    x_copy(i, up, here).start()
+
+    def z_hop(i, h):
+        slot, small = lax.rem(i, ring), lax.rem(i, SLOTS)
+        for up in (True, False):
+            here = h if up else nz - 1 - h
+
+            @pl.when(z == here)
+            def _():
+                if h > 0:
+                    z_copy(i, up, here - 1 if up else here + 1).wait_recv()
+                    into = zup_in if up else zdown_in
+
+                    def body(target, carry):
+                        add(slot, x, target, kept_at, kept, into[small, target - (1 if up else 0)])
+                        return carry
+
+                    lax.fori_loop(here if up else 0, nz if up else here + 1, body, 0)
+                    give(i, 3 if up else 4, to_z(-1 if up else 1))
+                if h < nz - 1:
+                    spend(i, 3 if up else 4)
+                    z_copy(i, up, here).start()
+
+    def send_f(i):
+        spend(i, 5)
+        f_copy(i).start()
+
+    def result_copy(i):
+        return pltpu.make_async_copy(result.at[lax.rem(i, 2)], out.at[i], result_sem.at[lax.rem(i, 2)])
+
+    def finish(i):
+        slot, small, two = lax.rem(i, ring), lax.rem(i, SLOTS), lax.rem(i, 2)
+        f_copy(i).wait_recv()
+
+        @pl.when(i >= 2)
+        def _():
+            result_copy(i - 2).wait()
+
+        mine = total[slot, x, z].astype(jnp.float32)
+        got = f_in[small].astype(jnp.float32)
+
+        @pl.when(y == 0)
+        def _():
+            result[two, :, :quarter] = mine[:, :quarter]
+            result[two, :, quarter:kept] = mine[:, quarter:kept] + got[:, : 2 * quarter]
+            result[two, :, kept:] = got[:, 2 * quarter :]
+
+        @pl.when(y == 1)
+        def _():
+            result[two, :, :quarter] = got[:, :quarter]
+            result[two, :, quarter:kept] = mine[:, quarter:kept] + got[:, quarter:]
+            result[two, :, kept:] = mine[:, kept:]
+
+        give(i, 5, to_y)
+        result_copy(i).start()
+        y_copy(i).wait_send()
+        f_copy(i).wait_send()
+        for here in range(nx):
+
+            @pl.when(x == here)
+            def _():
+                if here < nx - 1:
+                    x_copy(i, True, here).wait_send()
+                if here > 0:
+                    x_copy(i, False, here).wait_send()
+
+        for here in range(nz):
+
+            @pl.when(z == here)
+            def _():
+                if here < nz - 1:
+                    z_copy(i, True, here).wait_send()
+                if here > 0:
+                    z_copy(i, False, here).wait_send()
+
+    plan = [[("product",)]]
+    plan.append([("y",), ("x", 0)])
+    for h in range(1, nx):
+        plan.append([("x", h)])
+    plan[-1].append(("z", 0))
+    for h in range(1, nz):
+        plan.append([("z", h)])
+    plan[-1].append(("f",))
+    plan.append([("end",)])
+    does = {
+        "product": product,
+        "y": take_y,
+        "x": x_hop,
+        "z": z_hop,
+        "f": send_f,
+        "end": finish,
+    }
+
+    def tick(t, carry):
+        for depth in [*range(1, len(plan)), 0]:
+            i = t - depth
+
+            @pl.when((i >= 0) & (i < pieces))
+            def _():
+                for name, *more in plan[depth]:
+                    does[name](i, *more)
+
+        return carry
+
+    lax.fori_loop(0, pieces + len(plan) - 1, tick, 0)
+    result_copy(pieces - 2).wait()
+    result_copy(pieces - 1).wait()
+
+
+def reduce_weights(lefts, rights, nx, nz, layers, collective_id):
+    rows, tokens = lefts.shape[-2:]
+    wide = rights.shape[-1]
+    pieces = layers * PIECES
+    kept = 3 * wide // 4
+    ring = nx + nz + 2
+    sides = 1 if nx == 2 else 2
+    low = jnp.bfloat16
+    dma = pltpu.SemaphoreType.DMA
+    return pl.pallas_call(
+        functools.partial(reduce_kernel, nx, nz, layers),
+        out_shape=jax.ShapeDtypeStruct((pieces, rows, wide), jnp.float32),
+        in_specs=[pl.BlockSpec(memory_space=pl.ANY)] * 2,
+        out_specs=pl.BlockSpec(memory_space=pl.ANY),
+        scratch_shapes=[
+            pltpu.VMEM((2, layers * LEFTS, nx, nz, rows, tokens), low),
+            pltpu.VMEM((2, layers * RIGHTS, tokens, wide), low),
+            pltpu.VMEM((ring, nx, nz, rows, wide), low),
+            pltpu.VMEM((SLOTS, nx, nz, rows, wide // 4), low),
+            pltpu.VMEM((SLOTS, sides, nx - 1, nz, rows, kept), low),
+            pltpu.VMEM((SLOTS, nz - 1, rows, kept), low),
+            pltpu.VMEM((SLOTS, nz - 1, rows, kept), low),
+            pltpu.VMEM((SLOTS, rows, kept), low),
+            pltpu.VMEM((2, rows, wide), jnp.float32),
+            dma((3, layers * LEFTS, nx)),
+            dma((3, layers * RIGHTS)),
+            dma((2, pieces)),
+            dma((4, pieces)),
+            dma((2, pieces)),
+            dma((2, pieces)),
+            dma((2, pieces)),
+            dma((2,)),
+            pltpu.SemaphoreType.REGULAR((6,)),
+        ],
+        compiler_params=pltpu.CompilerParams(
+            collective_id=collective_id, has_side_effects=True, vmem_limit_bytes=56 * 1024 * 1024
+        ),
+    )(lefts, rights)
 
 
 def segment_of(doc_ends, token_index):
@@ -429,14 +801,11 @@
     query_group_size = QUERY_HEADS // KEYVALUE_HEADS
     score_scale = 1.0 / math.sqrt(HEAD_SIZE)
     branch_low = upstream.astype(jnp.bfloat16)
-    grad_down = jnp.einsum("tf,td->fd", activated, branch_low, preferred_element_type=jnp.float32)
     grad_act = jnp.einsum("td,fd->tf", branch_low, down_weight, preferred_element_type=jnp.float32)
     ignored, swiglu_back = jax.vjp(swiglu, gate_pre, upward)
     grad_gate_pre, grad_upward = swiglu_back(grad_act)
     gate_low = grad_gate_pre.astype(jnp.bfloat16)
     up_low = grad_upward.astype(jnp.bfloat16)
-    grad_gate = jnp.einsum("td,tf->df", normed_two, gate_low, preferred_element_type=jnp.float32)
-    grad_up = jnp.einsum("td,tf->df", normed_two, up_low, preferred_element_type=jnp.float32)
     grad_normed_two = jnp.einsum(
         "tf,df->td", gate_low, gate_weight, preferred_element_type=jnp.float32
     ) + jnp.einsum("tf,df->td", up_low, up_weight, preferred_element_type=jnp.float32)
@@ -444,9 +813,6 @@
     grad_mid, grad_gain_second = second_back(grad_normed_two)
     upstream_mid = upstream + grad_mid
     attn_low = upstream_mid.astype(jnp.bfloat16)
-    grad_output = jnp.einsum(
-        "tq,td->qd", attended_low, attn_low, preferred_element_type=jnp.float32
-    )
     grad_attended = (
         jnp.einsum("td,qd->tq", attn_low, output_weight, preferred_element_type=jnp.float32)
         .astype(jnp.bfloat16)
@@ -509,13 +875,6 @@
     query_low = grad_query_proj.reshape(token_rows, QD).astype(jnp.bfloat16)
     key_low = key_projection_gradient.reshape(token_rows, KEY_FEATURES).astype(jnp.bfloat16)
     value_low = local_key_value[:, KEY_FEATURES:].astype(jnp.bfloat16)
-    grad_query = jnp.einsum(
-        "td,tq->dq", normalized_rows, query_low, preferred_element_type=jnp.float32
-    )
-    grad_key = jnp.einsum("td,tk->dk", normalized_rows, key_low, preferred_element_type=jnp.float32)
-    grad_value = jnp.einsum(
-        "td,tk->dk", normalized_rows, value_low, preferred_element_type=jnp.float32
-    )
     grad_normed = jnp.einsum(
         "tq,dq->td", query_low, query_weight, preferred_element_type=jnp.float32
     )
@@ -527,20 +886,10 @@
     )
     ignored, first_back = jax.vjp(rms_scale, hidden, gain_first.astype(jnp.float32))
     grad_hidden, grad_gain_first = first_back(grad_normed)
-    terms = (
-        grad_gain_first,
-        grad_query,
-        grad_key,
-        grad_value,
-        grad_gain_query,
-        key_gain_gradient,
-        grad_output,
-        grad_gain_second,
-        grad_gate,
-        grad_up,
-        grad_down,
-    )
-    return (upstream_mid + grad_hidden, terms)
+    lefts = (normalized_rows, normed_two, attended_low, activated)
+    rights = (query_low, key_low, value_low, gate_low, up_low, attn_low, branch_low)
+    gains = (grad_gain_first, grad_gain_query, key_gain_gradient, grad_gain_second)
+    return (upstream_mid + grad_hidden, (lefts, rights, gains))
 
 
 def near_rows(rows, share):
@@ -600,54 +949,67 @@
     tables = (cosine, sine, token_segment, token_index, doc_ends, token_rows * ctx_count)
     hidden = tokens[0].astype(jnp.float32)
     stored = []
-    held_weights = []
     gathered = gather_all((norm_one, w_query, w_key, w_value, query_gain, key_gain, w_output, norm_two, w_gate, w_up, w_down))
     for which_layer in range(LAYERS):
         weights = gathered[which_layer]
-        held_weights.append(weights)
         hidden, saved = layer_ahead(hidden, weights, tables)
         stored.append(saved)
     output = hidden.astype(jnp.bfloat16)[None]
     live_mask = (token_segment < doc_lengths.shape[0]).astype(jnp.float32)
     upstream = cotangent[0].astype(jnp.float32) * live_mask[:, None]
-    layer_grads = [None] * LAYERS
+    operands = [None] * LAYERS
     for which_layer in reversed(range(LAYERS)):
-        weights = gathered[which_layer]
-        upstream, terms = layer_back(upstream, weights, stored[which_layer], tables)
-        owned = (
-            lax.psum_scatter(terms[0].astype(jnp.bfloat16), ("shard", "ctx"), scatter_dimension=0, tiled=True),
-            lax.psum_scatter(terms[1].astype(jnp.bfloat16), ("shard", "ctx"), scatter_dimension=0, tiled=True),
-            lax.psum_scatter(terms[2].astype(jnp.bfloat16), ("shard", "ctx"), scatter_dimension=0, tiled=True),
-            lax.psum_scatter(terms[3].astype(jnp.bfloat16), ("shard", "ctx"), scatter_dimension=0, tiled=True),
-            lax.psum_scatter(terms[4].astype(jnp.bfloat16), ("shard", "ctx"), scatter_dimension=0, tiled=True),
-            lax.psum_scatter(terms[5].astype(jnp.bfloat16), ("shard", "ctx"), scatter_dimension=0, tiled=True),
-            lax.psum_scatter(terms[6].astype(jnp.bfloat16), ("shard", "ctx"), scatter_dimension=0, tiled=True),
-            lax.psum_scatter(terms[7].astype(jnp.bfloat16), ("shard", "ctx"), scatter_dimension=0, tiled=True),
-            lax.psum_scatter(terms[8].astype(jnp.bfloat16), ("shard", "ctx"), scatter_dimension=0, tiled=True),
-            lax.psum_scatter(terms[9].astype(jnp.bfloat16), ("shard", "ctx"), scatter_dimension=0, tiled=True),
-            lax.psum_scatter(terms[10].astype(jnp.bfloat16), ("shard", "ctx"), scatter_dimension=0, tiled=True),
-        )
-        layer_grads[which_layer] = (
-            lax.psum(owned[0].astype(jnp.bfloat16), "rep").astype(jnp.float32),
-            lax.psum(owned[1].astype(jnp.bfloat16), "rep").astype(jnp.float32),
-            lax.psum(owned[2].astype(jnp.bfloat16), "rep").astype(jnp.float32),
-            lax.psum(owned[3].astype(jnp.bfloat16), "rep").astype(jnp.float32),
-            lax.psum(owned[4].astype(jnp.bfloat16), "rep").astype(jnp.float32),
-            lax.psum(owned[5].astype(jnp.bfloat16), "rep").astype(jnp.float32),
-            lax.psum(owned[6].astype(jnp.bfloat16), "rep").astype(jnp.float32),
-            lax.psum(owned[7].astype(jnp.bfloat16), "rep").astype(jnp.float32),
-            lax.psum(owned[8].astype(jnp.bfloat16), "rep").astype(jnp.float32),
-            lax.psum(owned[9].astype(jnp.bfloat16), "rep").astype(jnp.float32),
-            lax.psum(owned[10].astype(jnp.bfloat16), "rep").astype(jnp.float32),
+        upstream, operands[which_layer] = layer_back(
+            upstream, gathered[which_layer], stored[which_layer], tables
         )
     grad_tokens = upstream.astype(jnp.bfloat16)[None]
-    stacked = tuple(
-        (
-            jnp.stack([layer_grads[which_layer][member] for which_layer in range(LAYERS)])
-            for member in range(11)
-        )
-    )
-    return (output, grad_tokens) + stacked
+    return (output, grad_tokens) + weight_gradients(operands)
+
+
+def weight_gradients(operands):
+    nx, nz = lax.axis_size("shard") // 2, lax.axis_size("ctx")
+    shards = 2 * nx * nz
+    lefts, rights = [], []
+    for layer_lefts, layer_rights, _ in operands:
+        for a in layer_lefts:
+            tokens, features = a.shape
+            rows = D // shards
+            blocks = a.T.reshape(nx, 2, nz, features // D, rows, tokens)
+            lefts.append(jnp.moveaxis(blocks, 3, 0))
+        for a in layer_rights:
+            rights.append(jnp.moveaxis(a.reshape(a.shape[0], -1, D), 1, 0))
+    pieces = reduce_weights(
+        jnp.concatenate(lefts), jnp.concatenate(rights), nx, nz, LAYERS, 1
+    ).reshape(LAYERS, PIECES, -1, D)
+
+    def columns(first, count):
+        part = pieces[:, first : first + count]
+        return jnp.moveaxis(part, 1, 2).reshape(LAYERS, -1, count * D)
+
+    def rows_of(first, count):
+        return pieces[:, first : first + count].reshape(LAYERS, -1, D)
+
+    flat = jnp.stack([jnp.concatenate(gains) for _, _, gains in operands])
+    flat = lax.psum(flat, ("rep", "shard", "ctx"))
+    here = lax.axis_index("shard") * nz + lax.axis_index("ctx")
+    small, used = [], 0
+    for size in (D, HEAD_SIZE, HEAD_SIZE, D):
+        own = size // shards
+        small.append(lax.dynamic_slice_in_dim(flat, used + here * own, own, axis=1))
+        used += size
+    return (
+        small[0],
+        columns(0, 2),
+        columns(2, 1),
+        columns(3, 1),
+        small[1],
+        small[2],
+        rows_of(10, 2),
+        small[3],
+        columns(4, 3),
+        columns(7, 3),
+        rows_of(12, 3),
+    )
 
 
 def solution(mesh):

time: 1930 us -> 1140 us (0.59)
  waiting for transfers between devices: 1270 us -> 179 us
  Pallas kernels: 249 us -> 569 us
  local copies, waits for them, and re-layouts: 85.3 us -> 129 us
  matrix products: 171 us -> 142 us
  blocking collectives: 64.4 us -> 37.3 us
    reduce_scatter x14 -> x0, waiting for transfers between devices: 1070 us -> none  [the longest x2 177 us: local(): lax.psum_scatter(terms[8].astype(jnp.bfloat16), ('shard', 'ctx'), scatter...]
    pallas_call x0 -> x1, Pallas kernels: none -> 320 us  [reduce_weights(): pl.pallas_call(functools.partial(reduce_kernel, nx, nz, layers), out_shap...]
    unnamed x1 -> x0, blocking collectives: 59.4 us -> none
    dot_general x14 -> x0, matrix products: 49.4 us -> none  [the longest x2 8.98 us: layer_back(): jnp.einsum('td,tf->df', normed_two, up_low, preferred_element_type=jnp.fl...]
    psum x1, blocking collectives: 4.98 us -> 37.3 us  [weight_gradients(): flat = lax.psum(flat, ('rep', 'shard', 'ctx'))]
    psum x1 -> x0, waiting for transfers between devices: 26.5 us -> none  [local(): lax.psum(owned[1].astype(jnp.bfloat16), 'rep').astype(jnp.float32)]
    all_gather x2, waiting for transfers between devices: 70.1 us -> 49.6 us  [layer_ahead(): key_portion = lax.all_gather(key_rows, 'ctx', axis=0, tiled=True)]
  transfers between devices with their start and end apart: 21 -> 6, of which waited for: 21 -> 6; matrix products, arithmetic and copies ran while one was open for 7% -> 8% of each run, Pallas kernels for 0% -> 0%
where the time goes in v2:
time: 1140 us; the launch traced here: 1130 us
  Pallas kernels  569 us (50%)
  waiting for transfers between devices  179 us (16%)
  matrix products  142 us (12%)
  local copies, waits for them, and re-layouts  129 us (11%)
  other arithmetic  58.8 us (5%)
  blocking collectives  37.3 us (3%)
  between operations  16.8 us (1%)
    pallas_call x1, Pallas kernels, reduce_weights(): pl.pallas_call(functools.partial(reduce_kernel, nx, nz, layers), out_shap...  320 us
    pallas_call x1, Pallas kernels, gather_weights(): pl.pallas_call(functools.partial(gather_kernel, shapes, nx, nz), out_shap...  249 us
    reduce_scatter x2, waiting for transfers between devices, layer_back(): lax.psum_scatter(grad_keyval.astype(jnp.bfloat16), 'ctx', scatter_dimensi...  67.4 us
    all_gather x2, waiting for transfers between devices, layer_ahead(): value_portion = lax.all_gather(rows_of_values, 'ctx', axis=0, tiled=True)  61.5 us
    all_gather x2, waiting for transfers between devices, layer_ahead(): key_portion = lax.all_gather(key_rows, 'ctx', axis=0, tiled=True)  49.6 us
    unnamed x367, local copies, waits for them, and re-layouts  38.4 us
    psum x1, blocking collectives, weight_gradients(): flat = lax.psum(flat, ('rep', 'shard', 'ctx'))  37.3 us
  transfers between devices with their start and end apart: 6, of which 6 were waited for; matrix products, arithmetic and copies ran while one was open for 8% of the time, Pallas kernels for 0%

profile of v2, /device:TPU:0, one launch (start us, length us, event | category | flops | bytes accessed | tf_op | source)
XLA Modules:
  0.0 1132.2 jit_solution(10484619502072473736)
XLA Ops:
  17.8 249.2 %shard_map.237 = (bf16[256,128]{1,0:T(8,128)(2,1)}, bf16[1024,2048]{1,0:T(8,128)(2,1)}, bf16[1024,1024]{1,0:T(8,128)(2,1)}, bf16[1024,1024]{1,0:T(8,128)(2,1)}, ...) custom-call(bf16[16,128]{1,0:T(8,128)(2,1)} %fusion.172.refs_0_, ...), custom_call_target="tpu_custom_call" | custom-call | tf_op jit(solution)/shard_map/pallas_call | solution.py:234
  268.2 3.9 copy.466
  279.2 3.0 convolution_convert_fusion.3
  282.6 6.4 copy.469
  289.0 3.9 multiply_reduce_fusion.6
  297.8 27.4 %all-gather.7.cloned.1.call-done = bf16[768,1024]{1,0:T(8,128)(2,1)} async-done(((bf16[192,1024]{1,0:T(8,128)(2,1)}), bf16[768,1024]{1,0:T(8,128)(2,1)}) %all-gather.7.cloned.1.call-update) | async-done | bytes 1572880 | tf_op jit(solution)/shard_map/all_gather | solution.py:715
  326.9 5.5 fusion.8
  332.4 30.9 %all-gather.5.cloned.1.call-done = bf16[768,1024]{1,0:T(8,128)(2,1)} async-done(((bf16[192,1024]{1,0:T(8,128)(2,1)}), bf16[768,1024]{1,0:T(8,128)(2,1)}) %all-gather.5.cloned.1.call-update) | async-done | bytes 1572880 | tf_op jit(solution)/shard_map/all_gather | solution.py:716
  365.2 6.5 fusion.12
  372.2 4.3 fusion.199
  378.0 3.6 multiply_reduce_fusion.19
  381.6 4.5 fusion.201
  386.3 2.8 fusion.46
  395.8 2.9 convolution_convert_fusion.2
  399.0 3.4 fusion.203
  409.4 22.2 %all-gather.11.cloned.1.call-done = bf16[768,1024]{1,0:T(8,128)(2,1)} async-done(((bf16[192,1024]{1,0:T(8,128)(2,1)}), bf16[768,1024]{1,0:T(8,128)(2,1)}) %all-gather.11.cloned.1.call-update) | async-done | bytes 1572880 | tf_op jit(solution)/shard_map/all_gather | solution.py:715
  433.6 5.4 fusion.9
  439.0 30.6 %all-gather.9.cloned.1.call-done = bf16[768,1024]{1,0:T(8,128)(2,1)} async-done(((bf16[192,1024]{1,0:T(8,128)(2,1)}), bf16[768,1024]{1,0:T(8,128)(2,1)}) %all-gather.9.cloned.1.call-update) | async-done | bytes 1572880 | tf_op jit(solution)/shard_map/all_gather | solution.py:716
  471.5 6.4 fusion.14
  478.5 4.0 fusion.200
  484.2 3.3 convert_element_type.350
  487.5 3.7 multiply_reduce_fusion.16
  491.2 4.5 fusion.204
  495.8 3.5 fusion.42
  499.9 4.6 multiply_convert_fusion.1
  506.9 3.0 multiply_reduce_fusion.7
  513.5 3.6 reshape.605
  519.6 6.6 bitcast_convert_fusion.1
  526.2 5.2 fusion.3
  534.1 4.5 fusion.35
  541.2 3.9 pad_maximum_fusion
  546.5 4.2 convolution_multiply_fusion.1
  557.2 47.2 %reduce-scatter.3.cloned.1.call-done = bf16[192,2048]{1,0:T(8,128)(2,1)} async-done(((bf16[768,2048]{1,0:T(8,128)(2,1)}), bf16[192,2048]{1,0:T(8,128)(2,1)}) %reduce-scatter.3.cloned.1.call-update) | async-done | bytes 786448 | tf_op jit(solution)/shard_map/reduce_scatter | solution.py:860
  611.8 6.6 multiply_convert_fusion
  626.9 3.6 reshape.611
  633.0 6.6 bitcast_convert_fusion
  639.6 5.2 fusion.1
  647.5 4.5 fusion.34
  654.6 4.0 pad_maximum_fusion.1
  673.9 2.8 convert_element_type.388
  676.7 6.6 fusion.82
  694.2 4.7 fusion.112
  698.9 20.2 %reduce-scatter.5.cloned.1.call-done = bf16[192,2048]{1,0:T(8,128)(2,1)} async-done(((bf16[768,2048]{1,0:T(8,128)(2,1)}), bf16[192,2048]{1,0:T(8,128)(2,1)}) %reduce-scatter.5.cloned.1.call-update) | async-done | bytes 786448 | tf_op jit(solution)/shard_map/reduce_scatter | solution.py:860
  744.3 3.0 copy-done.26
  747.3 320.0 %shard_map.238 = f32[30,64,1024]{2,1,0:T(8,128)} custom-call(bf16[14,2,2,4,64,192]{5,4,3,2,1,0:T(8,128)(2,1)} %copy-done.26, bf16[24,192,1024]{2,1,0:T(8,128)(2,1)} %fusion.136.rights), custom_call_target="tpu_custom_call" | custom-call | tf_op jit(solution)/shard_map/pallas_call | solution.py:593
  1067.3 2.7 fusion.192
  1072.3 4.7 fusion.191
  1077.0 37.3 %psum.7 = f32[2,2304]{1,0:T(2,128)S(1)} all-reduce(f32[2,2304]{1,0:T(2,128)S(1)} %pad_maximum_fusion.4), channel_id=1, replica_groups=mesh['rep'=2,'shard'=4,'ctx'=4] {'rep','shard','ctx'}, use_global_device_ids=true, to_apply=%region_36.37 | all-reduce | flops 4608 | bytes 36864 | tf_op jit(solution)/shard_map/psum | solution.py:993
  (555 shorter events, 158.1 us)
Async XLA Ops:
  7.2 7.9 copy-start.91
  7.2 7.9 copy-start.92
  7.2 318.0 %all-gather.7.cloned.1.call-start = ((), (), s32[]{:S(2)}) async-start(), calls=%async_computation.3 | async-start | bytes 1966080 | tf_op jit(solution)/shard_map/all_gather | solution.py:715
  17.1 251.0 %copy-start.143 = (s32[1,8]{1,0:T(1,128)S(1)}, s32[1,8]{1,0:T(1,128)}, u32[]{:S(2)}) copy-start(s32[1,8]{1,0:T(1,128)} %param.17) | copy-start | bytes 100
  272.3 16.7 %copy-start.105 = (f32[1024]{0:T(1024)}, f32[1024]{0:T(1024)S(1)}, u32[]{:S(2)}) copy-start(f32[1024]{0:T(1024)S(1)} %reshape.632) | copy-start | bytes 12292
  272.5 16.5 %copy-start.123 = (f32[192]{0:T(256)}, f32[192]{0:T(256)S(1)}, u32[]{:S(2)}) copy-start(f32[192]{0:T(256)S(1)} %fusion.173) | copy-start | bytes 2308
  277.1 18.4 %copy-start.118 = (s32[192]{0:T(256)}, s32[192]{0:T(256)S(1)}, u32[]{:S(2)}) copy-start(s32[192]{0:T(256)S(1)} %convert_reduce_fusion.1) | copy-start | bytes 2308
  277.9 19.0 %copy-start.33 = (f32[192,128]{1,0:T(8,128)}, f32[192,128]{1,0:T(8,128)S(1)}, u32[]{:S(2)}) copy-start(f32[192,128]{1,0:T(8,128)S(1)} %get-tuple-element.164) | copy-start | bytes 294916
  279.2 84.1 %all-gather.5.cloned.1.call-start = ((), (), s32[]{:S(2)}) async-start(), calls=%async_computation.2 | async-start | bytes 1966080 | tf_op jit(solution)/shard_map/all_gather | solution.py:716
  282.2 149.4 %all-gather.11.cloned.1.call-start = ((), (), s32[]{:S(2)}) async-start(), calls=%async_computation.5 | async-start | bytes 1966080 | tf_op jit(solution)/shard_map/all_gather | solution.py:715
  294.7 96.2 %copy-start.99 = (f32[1024]{0:T(1024)}, f32[1024]{0:T(1024)S(1)}, u32[]{:S(2)}) copy-start(f32[1024]{0:T(1024)S(1)} %reshape.636) | copy-start | bytes 12292
  295.8 75.9 %copy-start.48 = (pred[192,768]{1,0:T(8,128)(4,1)}, pred[192,768]{1,0:T(8,128)(4,1)S(1)}, u32[]{:S(2)}) copy-start(pred[192,768]{1,0:T(8,128)(4,1)S(1)} %fusion.131) | copy-start | bytes 442372
  297.8 34.6 %copy-start.31 = (bf16[192,16,128]{2,0,1:T(8,128)(2,1)}, bf16[192,16,128]{2,0,1:T(8,128)(2,1)S(1)}, u32[]{:S(2)}) copy-start(bf16[192,16,128]{2,0,1:T(8,128)(2,1)S(1)} %fusion.60) | copy-start | bytes 2359300
  378.0 8.3 slice-start.14
  381.6 7.5 copy-start.5
  381.6 7.5 slice-start.22
  390.9 96.6 %copy-start.11 = (f32[192,1024]{1,0:T(8,128)}, f32[192,1024]{1,0:T(8,128)S(1)}, u32[]{:S(2)}) copy-start(f32[192,1024]{1,0:T(8,128)S(1)} %get-tuple-element.145) | copy-start | bytes 2359300
  395.5 74.1 %all-gather.9.cloned.1.call-start = ((), (), s32[]{:S(2)}) async-start(), calls=%async_computation.4 | async-start | bytes 1966080 | tf_op jit(solution)/shard_map/all_gather | solution.py:716
  395.7 11.1 copy-start.132
  395.8 114.1 %copy-start.134 = (f32[192]{0:T(256)}, f32[192]{0:T(256)S(1)}, u32[]{:S(2)}) copy-start(f32[192]{0:T(256)S(1)} %compare_convert_fusion) | copy-start | bytes 2308
  398.8 205.7 %reduce-scatter.3.cloned.1.call-start = ((), (), s32[]{:S(2)}) async-start(), calls=%async_computation.6 | async-start | bytes 3932160 | tf_op jit(solution)/shard_map/reduce_scatter | solution.py:860
  409.4 24.2 %copy-start.49 = (pred[192,768]{1,0:T(8,128)(4,1)S(1)}, pred[192,768]{1,0:T(8,128)(4,1)}, u32[]{:S(2)}) copy-start(pred[192,768]{1,0:T(8,128)(4,1)} %copy-done.48) | copy-start | bytes 442372
  471.5 7.1 copy-start.78
  487.5 8.3 slice-start.18
  491.2 18.7 %copy-start.7 = (f32[192,1024]{1,0:T(8,128)}, f32[192,1024]{1,0:T(8,128)S(1)}, u32[]{:S(2)}) copy-start(f32[192,1024]{1,0:T(8,128)S(1)} %get-tuple-element.151) | copy-start | bytes 2359300
  491.2 18.7 %copy-start.109 = (f32[192]{0:T(256)}, f32[192]{0:T(256)S(1)}, u32[]{:S(2)}) copy-start(f32[192]{0:T(256)S(1)} %fusion.176) | copy-start | bytes 2308
  491.2 8.1 slice-start.20
  491.2 13.3 %slice-start.10 = ((s8[6291456]{0:T(1024)(128)(4,1)}), s8[4194304]{0:T(1024)(128)(4,1)S(1)}, s32[]{:S(2)}) async-start(s8[6291456]{0:T(1024)(128)(4,1)} %bitcast.565), calls=%async_computation.18 | async-start | bytes 8388608
  495.8 8.8 slice-start.11
  511.1 15.1 %slice-start = ((s8[9437184]{0:T(1024)(128)(4,1)}), s8[1048576]{0:T(1024)(128)(4,1)S(1)}, s32[]{:S(2)}) async-start(s8[9437184]{0:T(1024)(128)(4,1)} %bitcast.548), calls=%async_computation.8 | async-start | bytes 2097152
  517.1 9.1 slice-start.1
  545.2 173.9 %reduce-scatter.5.cloned.1.call-start = ((), (), s32[]{:S(2)}) async-start(), calls=%async_computation.7 | async-start | bytes 3932160 | tf_op jit(solution)/shard_map/reduce_scatter | solution.py:860
  557.2 48.7 %copy-start.129 = (f32[128]{0:T(128)S(1)}, f32[128]{0:T(128)}, u32[]{:S(2)}) copy-start(f32[128]{0:T(128)} %copy-done.127) | copy-start | bytes 1540
  610.1 8.3 slice-start.8
  610.1 10.6 slice-start.16
  611.8 11.5 %copy-start.40 = (f32[192,1024]{1,0:T(8,128)}, f32[192,1024]{1,0:T(8,128)S(1)}, u32[]{:S(2)}) copy-start(f32[192,1024]{1,0:T(8,128)S(1)} %fusion.104) | copy-start | bytes 2359300
  611.8 9.0 slice-start.17
  624.4 15.2 %slice-start.5 = ((s8[9437184]{0:T(1024)(128)(4,1)}), s8[1048576]{0:T(1024)(128)(4,1)S(1)}, s32[]{:S(2)}) async-start(s8[9437184]{0:T(1024)(128)(4,1)} %bitcast.553), calls=%async_computation.13 | async-start | bytes 2097152
  630.5 9.1 slice-start.6
  673.9 10.4 slice-start.3
  676.7 7.6 copy-start.117
  676.7 7.6 copy-start.142
  676.7 7.6 slice-start.4
  676.7 7.6 copy-start.10
  698.9 21.6 %copy-start.17 = (f32[192,8,128]{2,0,1:T(8,128)S(1)}, f32[192,8,128]{2,0,1:T(8,128)}, u32[]{:S(2)}) copy-start(f32[192,8,128]{2,0,1:T(8,128)} %copy-done.16) | copy-start | bytes 2359300
  698.9 21.6 %copy-start.94 = (f32[192,8]{0,1:T(8,128)S(1)}, f32[192,8]{0,1:T(8,128)}, u32[]{:S(2)}) copy-start(f32[192,8]{0,1:T(8,128)} %copy-done.93) | copy-start | bytes 18436
  698.9 21.6 %copy-start.126 = (f32[128]{0:T(128)S(1)}, f32[128]{0:T(128)}, u32[]{:S(2)}) copy-start(f32[128]{0:T(128)} %copy-done.125) | copy-start | bytes 1540
  729.9 12.1 %slice-start.12 = ((s8[7340032]{0:T(1024)(128)(4,1)}), s8[4194304]{0:T(1024)(128)(4,1)S(1)}, s32[]{:S(2)}) async-start(s8[7340032]{0:T(1024)(128)(4,1)} %bitcast.569), calls=%async_computation.20 | async-start | bytes 8388608
  (128 other events, 365.1 us)
Sparse Core Ops, SparseCore 0:
  279.3 45.8 all-gather.6
  327.3 35.9 all-gather.4
  395.6 35.9 all-gather.10
  433.6 35.9 all-gather.8
  545.3 59.1 reduce-scatter.2
  658.7 60.2 reduce-scatter.4

commit v3 on v2

--- a/solution.py
+++ b/solution.py
@@ -20,7 +20,6 @@
 NORM_EPS = 1e-06
 ROPE_BASE = 1000000.0
 VERY_NEGATIVE = -1e30
-
 MESH = pl.DeviceIdType.MESH
 
 
@@ -255,17 +254,34 @@
 LEFTS, RIGHTS = 7, 12
 
 
-def left_of(j):
-    return jnp.where(j < 4, 0, jnp.where(j < 10, 1, j - 8))
+LEFT_BLOCKS = (1, 1, 2, 3)
+RIGHT_BLOCKS = (2, 1, 1, 3, 3, 1, 1)
+RIGHTS = sum(RIGHT_BLOCKS)
+LEFT_FIRST = (0, 4, 10, 12)
+WEIGHTS = ((0, 2, 1), (2, 1, 1), (3, 1, 1), (10, 1, 2), (4, 3, 1), (7, 3, 1), (12, 1, 3))
 
 
 def right_of(j):
     return jnp.where(j < 10, j, jnp.where(j < 12, 10, 11))
 
 
-def reduce_kernel(nx, nz, layers, lefts, rights, out, left_at, right_at, total, y_in, x_in, zup_in, zdown_in, f_in, result, left_sem, right_sem, y_sem, x_sem, zup_sem, zdown_sem, f_sem, result_sem, credit):
-    rows, tokens = lefts.shape[-2:]
-    wide = rights.shape[-1]
+def part_of(j):
+    return jnp.where(j < 10, 0, jnp.where(j < 12, j - 10, j - 12))
+
+
+def reduce_kernel(nx, nz, layers, *refs):
+    per = len(LEFT_BLOCKS) + len(RIGHT_BLOCKS)
+    operands, refs = refs[: layers * per], refs[layers * per :]
+    gains, refs = refs[0], refs[1:]
+    outs, refs = refs[: len(WEIGHTS)], refs[len(WEIGHTS) :]
+    lefts = [operands[n * per : n * per + 4] for n in range(layers)]
+    rights = [operands[n * per + 4 : (n + 1) * per] for n in range(layers)]
+    gains_out, left_at, refs = refs[0], refs[1:5], refs[5:]
+    right_at, turned, total, y_in, x_in, zup_in, zdown_in, f_in, result, refs = *refs[:9], refs[9:]
+    gain_in, gain_up, gain_down, refs = *refs[:3], refs[3:]
+    left_sem, right_sem, y_sem, x_sem, zup_sem, zdown_sem, f_sem, result_sem, gain_sem, credit = refs
+    rows = total.shape[3]
+    tokens, wide = right_at.shape[2:]
     quarter = wide // 4
     kept = 3 * quarter
     pieces = layers * PIECES
@@ -298,23 +314,28 @@
     greeted = greeted + (x > 0).astype(jnp.int32) + (x < nx - 1).astype(jnp.int32)
     pl.semaphore_wait(barrier, greeted)
 
-    def left_copies(b):
+    def left_copies(k, layer, source):
+        width = nz * LEFT_BLOCKS[k] * rows
+        sems = layer * len(LEFT_BLOCKS) + k
+
+        def columns(xs, of_core):
+            return source.at[:, pl.ds(pl.multiple_of((xs * 2 + of_core) * width, 128), width)]
+
         for xs in range(nx):
-            mine = lefts.at[b, xs, core]
-            yield pltpu.make_async_copy(mine, left_at.at[0, b, xs], left_sem.at[0, b, xs])
+            yield pltpu.make_async_copy(columns(xs, core), left_at[k].at[0, layer, xs], left_sem.at[0, sems, xs])
             yield pltpu.make_async_remote_copy(
-                src_ref=lefts.at[b, xs, 1 - core],
-                dst_ref=left_at.at[1, b, xs],
-                send_sem=left_sem.at[2, b, xs],
-                recv_sem=left_sem.at[1, b, xs],
+                src_ref=columns(xs, 1 - core),
+                dst_ref=left_at[k].at[1, layer, xs],
+                send_sem=left_sem.at[2, sems, xs],
+                recv_sem=left_sem.at[1, sems, xs],
                 device_id=to_core,
                 device_id_type=MESH,
             )
 
-    def right_copies(b):
-        yield pltpu.make_async_copy(rights.at[b], right_at.at[0, b], right_sem.at[0, b])
+    def right_copies(b, source):
+        yield pltpu.make_async_copy(source, right_at.at[0, b], right_sem.at[0, b])
         yield pltpu.make_async_remote_copy(
-            src_ref=rights.at[b],
+            src_ref=source,
             dst_ref=right_at.at[1, b],
             send_sem=right_sem.at[2, b],
             recv_sem=right_sem.at[1, b],
@@ -322,32 +343,24 @@
             device_id_type=MESH,
         )
 
-    def first_left(j):
-        return (j == 0) | (j == 4) | (j >= 10)
-
     def first_right(j):
         return (j <= 10) | (j == 12)
 
     def blocks(i):
         layer, j = lax.div(i, PIECES), lax.rem(i, PIECES)
-        return layer, j, layer * LEFTS + left_of(j), layer * RIGHTS + right_of(j)
-
-    def fetch(i, carry):
-        layer, j, lb, rb = blocks(i)
-
-        @pl.when(first_left(j))
-        def _():
-            for copy in left_copies(lb):
-                copy.start()
-
-        @pl.when(first_right(j))
-        def _():
-            for copy in right_copies(rb):
-                copy.start()
-
-        return carry
-
-    lax.fori_loop(0, pieces, fetch, 0)
+        return layer, j, part_of(j), layer * RIGHTS + right_of(j)
+
+    for layer in range(layers):
+        b = layer * RIGHTS
+        for k, source in enumerate(rights[layer]):
+            for k_left, first in enumerate(LEFT_FIRST):
+                if first == b - layer * RIGHTS or (first == 12 and k == 6):
+                    for copy in left_copies(k_left, layer, lefts[layer][k_left]):
+                        copy.start()
+            for n in range(RIGHT_BLOCKS[k]):
+                for copy in right_copies(b, source.at[:, pl.ds(n * wide, wide)]):
+                    copy.start()
+                b += 1
 
     def y_copy(i):
         return pltpu.make_async_remote_copy(
@@ -383,16 +396,23 @@
             use(flow)
 
     def product(i):
-        layer, j, lb, rb = blocks(i)
-
-        @pl.when(first_left(j))
-        def _():
-            for copy in left_copies(lb):
-                copy.wait()
+        layer, j, sub, rb = blocks(i)
+        for k, first in enumerate(LEFT_FIRST):
+
+            @pl.when(j == first)
+            def _():
+                for copy in left_copies(k, layer, lefts[0][k]):
+                    copy.wait()
+
+                for who in range(2):
+                    for xs in range(nx):
+                        flipped = left_at[k][who, layer, xs].T.reshape(nz, LEFT_BLOCKS[k], rows, tokens)
+                        for n in range(LEFT_BLOCKS[k]):
+                            turned[who, n, xs] = flipped[:, n]
 
         @pl.when(first_right(j))
         def _():
-            for copy in right_copies(rb):
+            for copy in right_copies(rb, rights[0][1]):
                 copy.wait()
 
         slot = lax.rem(i, ring)
@@ -401,7 +421,7 @@
             at = pl.ds(pl.multiple_of(c * quarter, quarter), quarter)
             acc = None
             for who in range(2):
-                left = left_at[who, lb].reshape(nx * nz * rows, tokens)
+                left = turned[who, sub].reshape(nx * nz * rows, tokens)
                 part = jnp.dot(left, right_at[who, rb, :, at], preferred_element_type=jnp.float32)
                 acc = part if acc is None else acc + part
             total[slot, :, :, :, at] = acc.reshape(nx, nz, rows, quarter).astype(total.dtype)
@@ -499,8 +519,76 @@
         spend(i, 5)
         f_copy(i).start()
 
-    def result_copy(i):
-        return pltpu.make_async_copy(result.at[lax.rem(i, 2)], out.at[i], result_sem.at[lax.rem(i, 2)])
+    def result_copy(i, into):
+        return pltpu.make_async_copy(result.at[lax.rem(i, 2)], into, result_sem.at[lax.rem(i, 2)])
+
+    def keep_result(i):
+        layer, j = lax.div(i, PIECES), lax.rem(i, PIECES)
+        for into, (first, across, below) in zip(outs, WEIGHTS):
+            for n in range(across * below):
+
+                @pl.when(j == first + n)
+                def _():
+                    place = (pl.ds(0, rows), pl.ds(n * wide, wide)) if below == 1 else (pl.ds(n * rows, rows), pl.ds(0, wide))
+                    result_copy(i, into.at[(layer, *place)]).start()
+
+    def result_kept(i):
+        result_copy(i, outs[1].at[0]).wait()
+
+    def gain_copy(n, source, device):
+        return pltpu.make_async_remote_copy(
+            src_ref=source,
+            dst_ref=gain_in.at[n],
+            send_sem=gain_sem.at[0, n],
+            recv_sem=gain_sem.at[1, n],
+            device_id=device,
+            device_id_type=MESH,
+        )
+
+    def gain_start():
+        copy = pltpu.make_async_copy(gains, gain_in.at[0], gain_sem.at[0, 0])
+        copy.start()
+        copy.wait()
+        gain_copy(1, gain_in.at[0], to_core).start()
+
+    def gain_pair():
+        gain_copy(1, gain_in.at[0], to_core).wait()
+        gain_up[0] = gain_in[0] + gain_in[1]
+        gain_copy(2, gain_up.at[0], to_y).start()
+
+    def gain_y():
+        gain_copy(2, gain_up.at[0], to_y).wait()
+        gain_in[0] = gain_up[0] + gain_in[2]
+
+    def gain_hop(h, n, here, to, first, level):
+        for up in (True, False):
+            buffer = (gain_up if up else gain_down).at[level]
+            slot = first if up else first + 1
+
+            @pl.when(here == (h if up else n - 1 - h))
+            def _():
+                buffer[...] = gain_in[0]
+                if h > 0:
+                    gain_copy(slot, buffer, to(1 if up else -1)).wait_recv()
+                    buffer[...] = gain_in[0] + gain_in[slot]
+                if h < n - 1:
+                    gain_copy(slot, buffer, to(1 if up else -1)).start()
+
+    def gain_line(n, here, to, first, level):
+        @pl.when(here < n - 1)
+        def _():
+            gain_copy(first, gain_up.at[level], to(1)).wait_send()
+
+        @pl.when(here > 0)
+        def _():
+            gain_copy(first + 1, gain_down.at[level], to(-1)).wait_send()
+
+        gain_in[0] = gain_up[level] + gain_down[level] - gain_in[0]
+
+    def gain_end():
+        copy = pltpu.make_async_copy(gain_in.at[0], gains_out, gain_sem.at[0, 0])
+        copy.start()
+        copy.wait()
 
     def finish(i):
         slot, small, two = lax.rem(i, ring), lax.rem(i, SLOTS), lax.rem(i, 2)
@@ -508,7 +596,7 @@
 
         @pl.when(i >= 2)
         def _():
-            result_copy(i - 2).wait()
+            result_kept(i - 2)
 
         mine = total[slot, x, z].astype(jnp.float32)
         got = f_in[small].astype(jnp.float32)
@@ -526,7 +614,7 @@
             result[two, :, kept:] = mine[:, kept:]
 
         give(i, 5, to_y)
-        result_copy(i).start()
+        keep_result(i)
         y_copy(i).wait_send()
         f_copy(i).wait_send()
         for here in range(nx):
@@ -565,7 +653,19 @@
         "end": finish,
     }
 
+    steps = [gain_start, gain_pair, gain_y]
+    for h in range(nx):
+        steps.append(functools.partial(gain_hop, h, nx, x, to_x, 3, 1))
+    steps.append(functools.partial(gain_line, nx, x, to_x, 3, 1))
+    for h in range(nz):
+        steps.append(functools.partial(gain_hop, h, nz, z, to_z, 5, 2))
+    steps.append(functools.partial(gain_line, nz, z, to_z, 5, 2))
+    steps.append(gain_end)
+
     def tick(t, carry):
+        for n, step in enumerate(steps):
+            pl.when(t == n)(step)
+
         for depth in [*range(1, len(plan)), 0]:
             i = t - depth
 
@@ -577,27 +677,34 @@
         return carry
 
     lax.fori_loop(0, pieces + len(plan) - 1, tick, 0)
-    result_copy(pieces - 2).wait()
-    result_copy(pieces - 1).wait()
-
-
-def reduce_weights(lefts, rights, nx, nz, layers, collective_id):
-    rows, tokens = lefts.shape[-2:]
-    wide = rights.shape[-1]
+    result_kept(pieces - 2)
+    result_kept(pieces - 1)
+
+
+def reduce_weights(operands, gains, nx, nz, collective_id):
+    layers = len(operands)
+    flat = [a for layer in operands for a in layer]
+    tokens, wide = flat[0].shape
+    rows = wide // (2 * nx * nz)
     pieces = layers * PIECES
     kept = 3 * wide // 4
     ring = nx + nz + 2
     sides = 1 if nx == 2 else 2
     low = jnp.bfloat16
     dma = pltpu.SemaphoreType.DMA
+    anywhere = pl.BlockSpec(memory_space=pl.ANY)
     return pl.pallas_call(
         functools.partial(reduce_kernel, nx, nz, layers),
-        out_shape=jax.ShapeDtypeStruct((pieces, rows, wide), jnp.float32),
-        in_specs=[pl.BlockSpec(memory_space=pl.ANY)] * 2,
-        out_specs=pl.BlockSpec(memory_space=pl.ANY),
-        scratch_shapes=[
-            pltpu.VMEM((2, layers * LEFTS, nx, nz, rows, tokens), low),
+        out_shape=[
+            jax.ShapeDtypeStruct((layers, rows * below, wide * across), jnp.float32) for _, across, below in WEIGHTS
+        ]
+        + [jax.ShapeDtypeStruct(gains.shape, gains.dtype)],
+        in_specs=[anywhere] * (len(flat) + 1),
+        out_specs=[anywhere] * (len(WEIGHTS) + 1),
+        scratch_shapes=[pltpu.VMEM((2, layers, nx, tokens, nz * n * rows), low) for n in LEFT_BLOCKS]
+        + [
             pltpu.VMEM((2, layers * RIGHTS, tokens, wide), low),
+            pltpu.VMEM((2, max(LEFT_BLOCKS), nx, nz, rows, tokens), low),
             pltpu.VMEM((ring, nx, nz, rows, wide), low),
             pltpu.VMEM((SLOTS, nx, nz, rows, wide // 4), low),
             pltpu.VMEM((SLOTS, sides, nx - 1, nz, rows, kept), low),
@@ -605,7 +712,10 @@
             pltpu.VMEM((SLOTS, nz - 1, rows, kept), low),
             pltpu.VMEM((SLOTS, rows, kept), low),
             pltpu.VMEM((2, rows, wide), jnp.float32),
-            dma((3, layers * LEFTS, nx)),
+            pltpu.VMEM((7, *gains.shape), gains.dtype),
+            pltpu.VMEM((3, *gains.shape), gains.dtype),
+            pltpu.VMEM((3, *gains.shape), gains.dtype),
+            dma((3, layers * len(LEFT_BLOCKS), nx)),
             dma((3, layers * RIGHTS)),
             dma((2, pieces)),
             dma((4, pieces)),
@@ -613,12 +723,339 @@
             dma((2, pieces)),
             dma((2, pieces)),
             dma((2,)),
+            dma((2, 7)),
             pltpu.SemaphoreType.REGULAR((6,)),
         ],
         compiler_params=pltpu.CompilerParams(
             collective_id=collective_id, has_side_effects=True, vmem_limit_bytes=56 * 1024 * 1024
         ),
-    )(lefts, rights)
+    )(*flat, gains)
+
+
+CHUNK_HEADS = 2
+CHUNKS = KEYVALUE_HEADS // CHUNK_HEADS
+CHUNK = CHUNK_HEADS * HEAD_SIZE
+GROUP = QUERY_HEADS // KEYVALUE_HEADS
+SCORE_SCALE = 1.0 / math.sqrt(HEAD_SIZE)
+
+
+def group_place(m):
+    y, shard, z = lax.axis_index("rep"), lax.axis_index("shard"), lax.axis_index("ctx")
+    core, zz = lax.rem(shard, 2), lax.rem(z, m)
+    to_core = (y, shard + 1 - 2 * core, z)
+
+    def to_line(step):
+        return (y, shard, z + step)
+
+    return core, zz, to_core, to_line
+
+
+def greet(m, zz, to_core, to_line):
+    barrier = pltpu.get_barrier_semaphore()
+    pl.semaphore_signal(barrier, inc=1, device_id=to_core, device_id_type=MESH)
+    for here, there in ((zz > 0, to_line(-1)), (zz < m - 1, to_line(1))):
+
+        @pl.when(here)
+        def _():
+            pl.semaphore_signal(barrier, inc=1, device_id=there, device_id_type=MESH)
+
+    pl.semaphore_wait(barrier, 1 + (zz > 0).astype(jnp.int32) + (zz < m - 1).astype(jnp.int32))
+
+
+def remote(src, dst, send_sem, recv_sem, device):
+    return pltpu.make_async_remote_copy(
+        src_ref=src, dst_ref=dst, send_sem=send_sem, recv_sem=recv_sem, device_id=device, device_id_type=MESH
+    )
+
+
+def head_prepare(v, gain, cosine, sine):
+    v = v * lax.rsqrt(jnp.mean(v * v, axis=-1, keepdims=True) + NORM_EPS) * gain
+    return v * cosine + pltpu.roll(v, HEAD_SIZE // 2, 1) * sine
+
+
+def head_prepare_back(grad, v, gain, cosine, sine):
+    grad = grad * cosine + pltpu.roll(grad * sine, HEAD_SIZE // 2, 1)
+    r = lax.rsqrt(jnp.mean(v * v, axis=-1, keepdims=True) + NORM_EPS)
+    unit = v * r
+    by_gain = jnp.sum(grad * unit, axis=0, keepdims=True)
+    grad = grad * gain
+    return r * (grad - unit * jnp.mean(grad * unit, axis=-1, keepdims=True)), by_gain
+
+
+def attend_kernel(m, qp, kp, v, q_gain, k_gain, cosine, sine, place_q, segment_k, q_out, kv, att, att_low, lse, core_sem, line_sem, core_out, line_out):
+    tokens, length = qp.shape[0], kv.shape[0]
+    core, zz, to_core, to_line = group_place(m)
+    greet(m, zz, to_core, to_line)
+    cos, sin = cosine[...], sine[...]
+
+    def part(j, source_zz, of_core=core):
+        rows = pl.multiple_of((source_zz + of_core * m) * tokens, 16)
+        return kv.at[pl.ds(rows, tokens), pl.ds(pl.multiple_of(j * 2 * CHUNK, 128), 2 * CHUNK)]
+
+    def core_copy(j, source_zz, of_core=core):
+        ref = part(j, source_zz, of_core)
+        return remote(ref, ref, core_out.at[j, source_zz], core_sem.at[j, source_zz], to_core)
+
+    def line_copy(j, source_zz, step):
+        ref = part(j, source_zz)
+        return remote(ref, ref, line_out.at[0 if step > 0 else 1, j, source_zz], line_sem.at[j, source_zz], to_line(step))
+
+    def onward(j, source_zz, step, do):
+        @pl.when((zz + step >= 0) & (zz + step < m))
+        def _():
+            do(line_copy(j, source_zz, step))
+
+    begin, ended = lambda copy: copy.start(), lambda copy: copy.wait_send()
+    own_rows = pl.ds(pl.multiple_of((zz + core * m) * tokens, 16), tokens)
+    for j in range(CHUNKS):
+        for n in range(CHUNK_HEADS):
+            h = j * CHUNK_HEADS + n
+            ready = head_prepare(kp[:, h * HEAD_SIZE : (h + 1) * HEAD_SIZE], k_gain[...], cos, sin)
+            kv[own_rows, j * 2 * CHUNK + n * HEAD_SIZE : j * 2 * CHUNK + (n + 1) * HEAD_SIZE] = ready.astype(kv.dtype)
+        kv[own_rows, j * 2 * CHUNK + CHUNK : (j + 1) * 2 * CHUNK] = v[:, j * CHUNK : (j + 1) * CHUNK]
+        for step in (1, -1):
+            onward(j, zz, step, begin)
+        core_copy(j, zz).start()
+    for h in range(QUERY_HEADS):
+        at = slice(h * HEAD_SIZE, (h + 1) * HEAD_SIZE)
+        q_out[:, at] = head_prepare(qp[:, at], q_gain[...], cos, sin).astype(q_out.dtype)
+
+    def arrivals(j):
+        for d in range(1, m):
+            for step in (1, -1):
+                source = zz - step * d
+
+                @pl.when((source >= 0) & (source < m))
+                def _():
+                    line_copy(j, source, step).wait_recv()
+                    onward(j, source, step, begin)
+                    core_copy(j, source).start()
+
+    segment_q = place_q[:, 0:1]
+    index_q = place_q[:, 1:2]
+    index_k = lax.broadcasted_iota(jnp.int32, (tokens, length), 1)
+    allowed = (segment_q == segment_k[...]) & (index_q >= index_k)
+    lane = lax.broadcasted_iota(jnp.int32, (tokens, HEAD_SIZE), 1)
+
+    def attend(j):
+        for source in range(m):
+            core_copy(j, source, 1 - core).wait_recv()
+        for n in range(CHUNK_HEADS):
+            keys = kv[:, pl.ds(pl.multiple_of(j * 2 * CHUNK + n * HEAD_SIZE, 128), HEAD_SIZE)]
+            values = kv[:, pl.ds(pl.multiple_of(j * 2 * CHUNK + CHUNK + n * HEAD_SIZE, 128), HEAD_SIZE)]
+            for g in range(GROUP):
+                h = (j * CHUNK_HEADS + n) * GROUP + g
+                at = pl.ds(pl.multiple_of(h * HEAD_SIZE, 128), HEAD_SIZE)
+                s = lax.dot_general(q_out[:, at], keys, (((1,), (1,)), ((), ())), preferred_element_type=jnp.float32)
+                s = jnp.where(allowed, s * SCORE_SCALE, VERY_NEGATIVE)
+                top = jnp.max(s, axis=-1, keepdims=True)
+                p = jnp.exp(s - top)
+                norm = jnp.sum(p, axis=-1, keepdims=True)
+                o = jnp.dot(p.astype(values.dtype), values, preferred_element_type=jnp.float32) / norm
+                att[:, at] = o
+                att_low[:, at] = o.astype(att_low.dtype)
+                lse[...] = jnp.where(lane == h, top + jnp.log(norm), lse[...])
+
+    lse[...] = jnp.zeros_like(lse)
+
+    def tick(t, carry):
+        @pl.when(t < CHUNKS)
+        def _():
+            arrivals(t)
+
+        @pl.when(t > 0)
+        def _():
+            attend(t - 1)
+
+        return carry
+
+    lax.fori_loop(0, CHUNKS + 1, tick, 0)
+
+    def leave(j, carry):
+        for source in range(m):
+            core_copy(j, source).wait_send()
+        for d in range(m):
+            for step in (1, -1):
+                source = zz - step * d
+
+                @pl.when((source >= 0) & (source < m))
+                def _():
+                    onward(j, source, step, ended)
+
+        return carry
+
+    lax.fori_loop(0, CHUNKS, leave, 0)
+
+
+def attend(m, qp, kp, v, q_gain, k_gain, cosine, sine, place_q, segment_k, collective_id):
+    tokens = qp.shape[0]
+    length = 2 * m * tokens
+    low = jnp.bfloat16
+    dma = pltpu.SemaphoreType.DMA
+    vmem = pl.BlockSpec(memory_space=pltpu.VMEM)
+    return pl.pallas_call(
+        functools.partial(attend_kernel, m),
+        out_shape=[
+            jax.ShapeDtypeStruct((tokens, QD), low),
+            jax.ShapeDtypeStruct((length, 2 * KEY_FEATURES), low),
+            jax.ShapeDtypeStruct((tokens, QD), jnp.float32),
+            jax.ShapeDtypeStruct((tokens, QD), low),
+            jax.ShapeDtypeStruct((tokens, HEAD_SIZE), jnp.float32),
+        ],
+        in_specs=[vmem] * 9,
+        out_specs=[vmem] * 5,
+        scratch_shapes=[dma((CHUNKS, m)), dma((CHUNKS, m)), dma((CHUNKS, m)), dma((2, CHUNKS, m))],
+        compiler_params=pltpu.CompilerParams(
+            collective_id=collective_id, has_side_effects=True, vmem_limit_bytes=48 * 1024 * 1024
+        ),
+    )(qp, kp, v, q_gain, k_gain, cosine, sine, place_q, segment_k)
+
+
+def attend_back_kernel(m, q, kv, d_att, att, lse, qp, kp, q_gain, k_gain, cosine, sine, place_q, segment_k, dq_low, dk_low, dv_low, gains, partial, core_in, up_in, down_in, core_sem, up_sem, down_sem):
+    tokens, length = q.shape[0], kv.shape[0]
+    core, zz, to_core, to_line = group_place(m)
+    greet(m, zz, to_core, to_line)
+    cos, sin = cosine[...], sine[...]
+    segment_q = place_q[:, 0:1]
+    index_q = place_q[:, 1:2]
+    index_k = lax.broadcasted_iota(jnp.int32, (tokens, length), 1)
+    allowed = (segment_q == segment_k[...]) & (index_q >= index_k)
+    lane = lax.broadcasted_iota(jnp.int32, (tokens, HEAD_SIZE), 1)
+    gains[...] = jnp.zeros_like(gains)
+    over_rows = (((0,), (0,)), ((), ()))
+    over_columns = (((1,), (1,)), ((), ()))
+
+    def core_copy(j):
+        return remote(partial.at[j, 1 - core], core_in.at[j], core_sem.at[0, j], core_sem.at[1, j], to_core)
+
+    def line_copy(j, up, here):
+        low, high = (here + 1, m) if up else (0, here)
+        into, sems = (up_in, up_sem) if up else (down_in, down_sem)
+        return remote(
+            partial.at[j, core, pl.ds(low, high - low)],
+            into.at[j, pl.ds(low - (1 if up else 0), high - low)],
+            sems.at[0, j],
+            sems.at[1, j],
+            to_line(1 if up else -1),
+        )
+
+    def add(j, place, value):
+        partial[j, core, place] = (partial[j, core, place].astype(jnp.float32) + value.astype(jnp.float32)).astype(partial.dtype)
+
+    def compute(j):
+        for n in range(CHUNK_HEADS):
+            keys = kv[:, pl.ds(pl.multiple_of(j * 2 * CHUNK + n * HEAD_SIZE, 128), HEAD_SIZE)]
+            values = kv[:, pl.ds(pl.multiple_of(j * 2 * CHUNK + CHUNK + n * HEAD_SIZE, 128), HEAD_SIZE)]
+            dk = dv = None
+            for g in range(GROUP):
+                h = (j * CHUNK_HEADS + n) * GROUP + g
+                at = pl.ds(pl.multiple_of(h * HEAD_SIZE, 128), HEAD_SIZE)
+                queries, grad = q[:, at], d_att[:, at]
+                total = jnp.sum(jnp.where(lane == h, lse[...], 0.0), axis=-1, keepdims=True)
+                delta = jnp.sum(grad.astype(jnp.float32) * att[:, at], axis=-1, keepdims=True)
+                s = lax.dot_general(queries, keys, over_columns, preferred_element_type=jnp.float32)
+                p = jnp.exp(jnp.where(allowed, s * SCORE_SCALE, VERY_NEGATIVE) - total)
+                dp = lax.dot_general(grad, values, over_columns, preferred_element_type=jnp.float32)
+                ds = (p * (dp - delta)).astype(queries.dtype)
+                dq = jnp.dot(ds, keys, preferred_element_type=jnp.float32) * SCORE_SCALE
+                here_k = lax.dot_general(ds, queries, over_rows, preferred_element_type=jnp.float32)
+                here_v = lax.dot_general(p.astype(grad.dtype), grad, over_rows, preferred_element_type=jnp.float32)
+                dk = here_k if dk is None else dk + here_k
+                dv = here_v if dv is None else dv + here_v
+                by_head, by_gain = head_prepare_back(dq, qp[:, at], q_gain[...], cos, sin)
+                dq_low[:, at] = by_head.astype(dq_low.dtype)
+                gains[0:1] += by_gain
+            first = n * HEAD_SIZE
+            partial[j, :, :, :, first : first + HEAD_SIZE] = (dk * SCORE_SCALE).astype(partial.dtype).reshape(2, m, tokens, HEAD_SIZE)
+            first += CHUNK
+            partial[j, :, :, :, first : first + HEAD_SIZE] = dv.astype(partial.dtype).reshape(2, m, tokens, HEAD_SIZE)
+        core_copy(j).start()
+
+    def take_core(j):
+        core_copy(j).wait_recv()
+        for place in range(m):
+            add(j, place, core_in[j, place])
+
+    def hop(j, h):
+        for up in (True, False):
+            here = h if up else m - 1 - h
+
+            @pl.when(zz == here)
+            def _():
+                if h > 0:
+                    line_copy(j, up, here - 1 if up else here + 1).wait_recv()
+                    into = up_in if up else down_in
+                    for place in range(here, m) if up else range(here + 1):
+                        add(j, place, into[j, place - (1 if up else 0)])
+                if h < m - 1:
+                    line_copy(j, up, here).start()
+
+    def finish(j):
+        for n in range(CHUNK_HEADS):
+            at = pl.ds(pl.multiple_of((j * CHUNK_HEADS + n) * HEAD_SIZE, 128), HEAD_SIZE)
+            grad = partial[j, core, zz, :, n * HEAD_SIZE : (n + 1) * HEAD_SIZE].astype(jnp.float32)
+            by_head, by_gain = head_prepare_back(grad, kp[:, at], k_gain[...], cos, sin)
+            dk_low[:, at] = by_head.astype(dk_low.dtype)
+            gains[1:2] += by_gain
+        at = pl.ds(pl.multiple_of(j * CHUNK, 128), CHUNK)
+        dv_low[:, at] = partial[j, core, zz, :, CHUNK:]
+        core_copy(j).wait_send()
+        for here in range(m):
+
+            @pl.when(zz == here)
+            def _():
+                if here < m - 1:
+                    line_copy(j, True, here).wait_send()
+                if here > 0:
+                    line_copy(j, False, here).wait_send()
+
+    plan = [[compute], [take_core, functools.partial(hop, h=0)]]
+    for h in range(1, m):
+        plan.append([functools.partial(hop, h=h)])
+    plan[-1].append(finish)
+
+    def tick(t, carry):
+        for depth in [*range(1, len(plan)), 0]:
+            j = t - depth
+
+            @pl.when((j >= 0) & (j < CHUNKS))
+            def _():
+                for stage in plan[depth]:
+                    stage(j)
+
+        return carry
+
+    lax.fori_loop(0, CHUNKS + len(plan) - 1, tick, 0)
+
+
+def attend_back(m, q, kv, d_att, att, lse, qp, kp, q_gain, k_gain, cosine, sine, place_q, segment_k, collective_id):
+    tokens = q.shape[0]
+    low = jnp.bfloat16
+    dma = pltpu.SemaphoreType.DMA
+    vmem = pl.BlockSpec(memory_space=pltpu.VMEM)
+    return pl.pallas_call(
+        functools.partial(attend_back_kernel, m),
+        out_shape=[
+            jax.ShapeDtypeStruct((tokens, QD), low),
+            jax.ShapeDtypeStruct((tokens, KEY_FEATURES), low),
+            jax.ShapeDtypeStruct((tokens, KEY_FEATURES), low),
+            jax.ShapeDtypeStruct((8, HEAD_SIZE), jnp.float32),
+        ],
+        in_specs=[vmem] * 13,
+        out_specs=[vmem] * 4,
+        scratch_shapes=[
+            pltpu.VMEM((CHUNKS, 2, m, tokens, 2 * CHUNK), low),
+            pltpu.VMEM((CHUNKS, m, tokens, 2 * CHUNK), low),
+            pltpu.VMEM((CHUNKS, max(m - 1, 1), tokens, 2 * CHUNK), low),
+            pltpu.VMEM((CHUNKS, max(m - 1, 1), tokens, 2 * CHUNK), low),
+            dma((2, CHUNKS)),
+            dma((2, CHUNKS)),
+            dma((2, CHUNKS)),
+        ],
+        compiler_params=pltpu.CompilerParams(
+            collective_id=collective_id, has_side_effects=True, vmem_limit_bytes=48 * 1024 * 1024
+        ),
+    )(q, kv, d_att, att, lse, qp, kp, q_gain, k_gain, cosine, sine, place_q, segment_k)
 
 
 def segment_of(doc_ends, token_index):
@@ -643,7 +1080,7 @@
     angles = positions.astype(jnp.float32)[:, None] * inv_rates[None, :]
     cosine = jnp.cos(angles)
     sine = jnp.sin(angles)
-    return (jnp.concatenate([cosine, cosine], axis=1), jnp.concatenate([sine, sine], axis=1))
+    return (jnp.concatenate([cosine, cosine], axis=1), jnp.concatenate([-sine, sine], axis=1))
 
 
 def rms_scale(values, gain_vec):
@@ -652,26 +1089,23 @@
     )
 
 
-def rotate(values, cosine, sine):
-    middle = values.shape[-1] // 2
-    turned = jnp.concatenate([-values[..., middle:], values[..., :middle]], axis=-1)
-    return values * cosine[:, None, :] + turned * sine[:, None, :]
-
-
 def swiglu(gate_pre, upward):
     return jax.nn.silu(gate_pre) * upward
 
 
-def visible(token_segment, token_index, doc_ends, portion_rows):
-    key_index = jnp.arange(portion_rows, dtype=jnp.int32)
-    key_segment = segment_of(doc_ends, key_index)
-    allowed = (token_segment[:, None] == key_segment[None, :]) & (
-        token_index[:, None] >= key_index[None, :]
-    )
-    return allowed[:, None, None, :]
-
-
-def layer_ahead(hidden, weights, tables):
+def product(left, right):
+    return jnp.dot(left, right, preferred_element_type=jnp.float32)
+
+
+def product_back(grad, right):
+    return lax.dot_general(grad, right, (((1,), (1,)), ((), ())), preferred_element_type=jnp.float32)
+
+
+def head_gain(gain):
+    return gain.astype(jnp.float32)[None, :]
+
+
+def layer_ahead(hidden, weights, tables, m):
     (
         gain_first,
         query_weight,
@@ -685,74 +1119,26 @@
         up_weight,
         down_weight,
     ) = weights
-    cosine, sine, token_segment, token_index, doc_ends, sequence_rows = tables
-    token_rows = hidden.shape[0]
-    query_group_size = QUERY_HEADS // KEYVALUE_HEADS
-    score_scale = 1.0 / math.sqrt(HEAD_SIZE)
     normalized_rows = rms_scale(hidden, gain_first.astype(jnp.float32)).astype(jnp.bfloat16)
-    query_proj = jnp.dot(normalized_rows, query_weight, preferred_element_type=jnp.float32).reshape(
-        token_rows, QUERY_HEADS, HEAD_SIZE
+    key_projection = product(normalized_rows, key_matrix)
+    rows_of_values = product(normalized_rows, value_matrix).astype(jnp.bfloat16)
+    query_proj = product(normalized_rows, query_weight)
+    query_rows, keys_values, attended_rows, attended_low, log_sum = attend(
+        m, query_proj, key_projection, rows_of_values, head_gain(gain_query), head_gain(gain_key), *tables, 2
     )
-    key_projection = jnp.dot(
-        normalized_rows, key_matrix, preferred_element_type=jnp.float32
-    ).reshape(token_rows, KEYVALUE_HEADS, HEAD_SIZE)
-    rows_of_values = jnp.dot(
-        normalized_rows, value_matrix, preferred_element_type=jnp.float32
-    ).astype(jnp.bfloat16)
-    query_rows = (
-        rotate(rms_scale(query_proj, gain_query.astype(jnp.float32)), cosine, sine)
-        .astype(jnp.bfloat16)
-        .reshape(token_rows, KEYVALUE_HEADS, query_group_size, HEAD_SIZE)
-    )
-    key_rows = (
-        rotate(rms_scale(key_projection, gain_key.astype(jnp.float32)), cosine, sine)
-        .astype(jnp.bfloat16)
-        .reshape(token_rows, KEY_FEATURES)
-    )
-    running_maximum = jnp.full(
-        (token_rows, KEYVALUE_HEADS, query_group_size), VERY_NEGATIVE, jnp.float32
-    )
-    key_portion = lax.all_gather(key_rows, "ctx", axis=0, tiled=True)
-    value_portion = lax.all_gather(rows_of_values, "ctx", axis=0, tiled=True)
-    portion_rows = key_portion.shape[0]
-    allowed = visible(token_segment, token_index, doc_ends, portion_rows)
-    scores = (
-        jnp.einsum(
-            "thgd,nhd->thgn",
-            query_rows,
-            key_portion.reshape(portion_rows, KEYVALUE_HEADS, HEAD_SIZE),
-            preferred_element_type=jnp.float32,
-        )
-        * score_scale
-    )
-    masked = jnp.where(allowed, scores, VERY_NEGATIVE)
-    new_max = jnp.maximum(running_maximum, jnp.max(masked, axis=-1))
-    unnormed = jnp.where(allowed, jnp.exp(masked - new_max[..., None]), 0.0)
-    running_sum = jnp.sum(unnormed, axis=-1)
-    running_out = jnp.einsum(
-        "thgn,nhd->thgd",
-        unnormed.astype(jnp.bfloat16),
-        value_portion.reshape(portion_rows, KEYVALUE_HEADS, HEAD_SIZE),
-        preferred_element_type=jnp.float32,
-    )
-    running_maximum, running_sum, running_out = (new_max, running_sum, running_out)
-    attended_rows = running_out / running_sum[..., None]
-    log_sum = running_maximum + jnp.log(running_sum)
-    attended_low = attended_rows.reshape(token_rows, QD).astype(jnp.bfloat16)
-    hidden_mid = hidden + jnp.dot(attended_low, output_weight, preferred_element_type=jnp.float32)
+    hidden_mid = hidden + product(attended_low, output_weight)
     normed_two = rms_scale(hidden_mid, gain_second.astype(jnp.float32)).astype(jnp.bfloat16)
-    gate_pre = jnp.dot(normed_two, gate_weight, preferred_element_type=jnp.float32)
-    upward = jnp.dot(normed_two, up_weight, preferred_element_type=jnp.float32)
+    gate_pre = product(normed_two, gate_weight)
+    upward = product(normed_two, up_weight)
     activated = swiglu(gate_pre, upward).astype(jnp.bfloat16)
-    hidden_out = hidden_mid + jnp.dot(activated, down_weight, preferred_element_type=jnp.float32)
+    hidden_out = hidden_mid + product(activated, down_weight)
     saved = (
         hidden,
         normalized_rows,
         query_proj,
         key_projection,
-        rows_of_values,
         query_rows,
-        key_rows,
+        keys_values,
         attended_rows,
         attended_low,
         log_sum,
@@ -765,7 +1151,7 @@
     return (hidden_out, saved)
 
 
-def layer_back(upstream, weights, saved, tables):
+def layer_back(upstream, weights, saved, tables, m):
     (
         gain_first,
         query_weight,
@@ -784,9 +1170,8 @@
         normalized_rows,
         query_proj,
         key_projection,
-        rows_of_values,
         query_rows,
-        key_rows,
+        keys_values,
         attended_rows,
         attended_low,
         log_sum,
@@ -796,100 +1181,41 @@
         upward,
         activated,
     ) = saved
-    cosine, sine, token_segment, token_index, doc_ends, sequence_rows = tables
-    token_rows = upstream.shape[0]
-    query_group_size = QUERY_HEADS // KEYVALUE_HEADS
-    score_scale = 1.0 / math.sqrt(HEAD_SIZE)
     branch_low = upstream.astype(jnp.bfloat16)
-    grad_act = jnp.einsum("td,fd->tf", branch_low, down_weight, preferred_element_type=jnp.float32)
+    grad_act = product_back(branch_low, down_weight)
     ignored, swiglu_back = jax.vjp(swiglu, gate_pre, upward)
     grad_gate_pre, grad_upward = swiglu_back(grad_act)
     gate_low = grad_gate_pre.astype(jnp.bfloat16)
     up_low = grad_upward.astype(jnp.bfloat16)
-    grad_normed_two = jnp.einsum(
-        "tf,df->td", gate_low, gate_weight, preferred_element_type=jnp.float32
-    ) + jnp.einsum("tf,df->td", up_low, up_weight, preferred_element_type=jnp.float32)
+    grad_normed_two = product_back(gate_low, gate_weight) + product_back(up_low, up_weight)
     ignored, second_back = jax.vjp(rms_scale, hidden_mid, gain_second.astype(jnp.float32))
     grad_mid, grad_gain_second = second_back(grad_normed_two)
     upstream_mid = upstream + grad_mid
     attn_low = upstream_mid.astype(jnp.bfloat16)
-    grad_attended = (
-        jnp.einsum("td,qd->tq", attn_low, output_weight, preferred_element_type=jnp.float32)
-        .astype(jnp.bfloat16)
-        .reshape(token_rows, KEYVALUE_HEADS, query_group_size, HEAD_SIZE)
+    grad_attended = product_back(attn_low, output_weight).astype(jnp.bfloat16)
+    query_low, key_low, value_low, head_gains = attend_back(
+        m,
+        query_rows,
+        keys_values,
+        grad_attended,
+        attended_rows,
+        log_sum,
+        query_proj,
+        key_projection,
+        head_gain(gain_query),
+        head_gain(gain_key),
+        *tables,
+        3,
     )
-    row_delta = jnp.sum(grad_attended.astype(jnp.float32) * attended_rows, axis=-1)
-    key_portion = lax.all_gather(key_rows, "ctx", axis=0, tiled=True)
-    value_portion = lax.all_gather(rows_of_values, "ctx", axis=0, tiled=True)
-    portion_rows = key_portion.shape[0]
-    heads_of_keys = key_portion.reshape(portion_rows, KEYVALUE_HEADS, HEAD_SIZE)
-    heads_of_values = value_portion.reshape(portion_rows, KEYVALUE_HEADS, HEAD_SIZE)
-    allowed = visible(token_segment, token_index, doc_ends, portion_rows)
-    scores = (
-        jnp.einsum("thgd,nhd->thgn", query_rows, heads_of_keys, preferred_element_type=jnp.float32)
-        * score_scale
-    )
-    probability = jnp.where(allowed, jnp.exp(scores - log_sum[..., None]), 0.0)
-    grad_prob = jnp.einsum(
-        "thgd,nhd->thgn", grad_attended, heads_of_values, preferred_element_type=jnp.float32
-    )
-    grad_scores = (probability * (grad_prob - row_delta[..., None])).astype(jnp.bfloat16)
-    grad_queries = (
-        jnp.einsum("thgn,nhd->thgd", grad_scores, heads_of_keys, preferred_element_type=jnp.float32)
-        * score_scale
-    )
-    grad_key_piece = (
-        jnp.einsum("thgn,thgd->nhd", grad_scores, query_rows, preferred_element_type=jnp.float32)
-        * score_scale
-    )
-    grad_value_piece = jnp.einsum(
-        "thgn,thgd->nhd",
-        probability.astype(jnp.bfloat16),
-        grad_attended,
-        preferred_element_type=jnp.float32,
-    )
-    update = jnp.concatenate(
-        [
-            grad_key_piece.reshape(portion_rows, KEY_FEATURES),
-            grad_value_piece.reshape(portion_rows, KEY_FEATURES),
-        ],
-        axis=1,
-    )
-    grad_keyval = update
-    grad_queries, grad_keyval = (grad_queries, grad_keyval)
-    local_key_value = lax.psum_scatter(
-        grad_keyval.astype(jnp.bfloat16), "ctx", scatter_dimension=0, tiled=True
-    ).astype(jnp.float32)
-
-    def prepare(projected, gain_vec):
-        return rotate(rms_scale(projected, gain_vec), cosine, sine)
-
-    ignored, query_back = jax.vjp(prepare, query_proj, gain_query.astype(jnp.float32))
-    grad_query_proj, grad_gain_query = query_back(
-        grad_queries.reshape(token_rows, QUERY_HEADS, HEAD_SIZE)
-    )
-    ignored, key_reverse_pass = jax.vjp(prepare, key_projection, gain_key.astype(jnp.float32))
-    key_projection_gradient, key_gain_gradient = key_reverse_pass(
-        local_key_value[:, :KEY_FEATURES].reshape(token_rows, KEYVALUE_HEADS, HEAD_SIZE)
-    )
-    query_low = grad_query_proj.reshape(token_rows, QD).astype(jnp.bfloat16)
-    key_low = key_projection_gradient.reshape(token_rows, KEY_FEATURES).astype(jnp.bfloat16)
-    value_low = local_key_value[:, KEY_FEATURES:].astype(jnp.bfloat16)
-    grad_normed = jnp.einsum(
-        "tq,dq->td", query_low, query_weight, preferred_element_type=jnp.float32
-    )
-    grad_normed = grad_normed + jnp.einsum(
-        "tk,dk->td", key_low, key_matrix, preferred_element_type=jnp.float32
-    )
-    grad_normed = grad_normed + jnp.einsum(
-        "tk,dk->td", value_low, value_matrix, preferred_element_type=jnp.float32
-    )
+    grad_normed = product_back(query_low, query_weight)
+    grad_normed = grad_normed + product_back(key_low, key_matrix)
+    grad_normed = grad_normed + product_back(value_low, value_matrix)
     ignored, first_back = jax.vjp(rms_scale, hidden, gain_first.astype(jnp.float32))
     grad_hidden, grad_gain_first = first_back(grad_normed)
     lefts = (normalized_rows, normed_two, attended_low, activated)
     rights = (query_low, key_low, value_low, gate_low, up_low, attn_low, branch_low)
-    gains = (grad_gain_first, grad_gain_query, key_gain_gradient, grad_gain_second)
-    return (upstream_mid + grad_hidden, (lefts, rights, gains))
+    gains = (grad_gain_first, head_gains[0], head_gains[1], grad_gain_second)
+    return (upstream_mid + grad_hidden, (lefts + rights, gains))
 
 
 def near_rows(rows, share):
@@ -922,6 +1248,24 @@
     return out
 
 
+def weight_gradients(operands):
+    nx, nz = lax.axis_size("shard") // 2, lax.axis_size("ctx")
+    shards = 2 * nx * nz
+    flat = jnp.concatenate([g for _, gains in operands for g in gains])
+    size = -(-flat.shape[0] // 1024) * 1024
+    padded = jnp.zeros((size,), flat.dtype).at[: flat.shape[0]].set(flat).reshape(-1, 128)
+    *grads, summed = reduce_weights([members for members, _ in operands], padded, nx, nz, 1)
+    summed = summed.reshape(-1)[: flat.shape[0]].reshape(LAYERS, -1)
+    here = lax.axis_index("shard") * nz + lax.axis_index("ctx")
+    small, used = [], 0
+    for size in (D, HEAD_SIZE, HEAD_SIZE, D):
+        own = size // shards
+        small.append(lax.dynamic_slice_in_dim(summed, used + here * own, own, axis=1))
+        used += size
+    query, key, value, output, gate, up, down = grads
+    return (small[0], query, key, value, small[1], small[2], output, small[3], gate, up, down)
+
+
 def local(
     tokens,
     lengths,
@@ -939,77 +1283,46 @@
     cotangent,
 ):
     token_rows = tokens.shape[1]
-    ctx_count = lax.axis_size("ctx")
-    token_index = lax.axis_index("ctx") * token_rows + jnp.arange(token_rows, dtype=jnp.int32)
+    nx, nz = lax.axis_size("shard") // 2, lax.axis_size("ctx")
+    m = nz // 2
+    pairs = []
+    for x in range(nx):
+        for z in range(m):
+            low, high = (2 * x + 1) * nz + z, 2 * x * nz + z + m
+            same = (2 * x * nz + z, (2 * x + 1) * nz + z + m)
+            pairs += [(low, high), (high, low)] + [(s, s) for s in same]
+
+    def swap(values):
+        return lax.ppermute(values, ("shard", "ctx"), pairs)
+
+    tokens, lengths, cotangent = swap(tokens), swap(lengths), swap(cotangent)
+    block = lax.axis_index("ctx") % m + (lax.axis_index("shard") % 2) * m
+    token_index = block * token_rows + jnp.arange(token_rows, dtype=jnp.int32)
     doc_lengths = lengths[0]
     upto = jnp.arange(doc_lengths.shape[0])
     doc_ends = jnp.sum(jnp.where(upto[:, None] >= upto[None, :], doc_lengths[None, :], 0), axis=1)
     token_segment, positions = doc_layout(doc_ends, token_index)
     cosine, sine = rotary(positions, HEAD_SIZE)
-    tables = (cosine, sine, token_segment, token_index, doc_ends, token_rows * ctx_count)
+    key_segment = segment_of(doc_ends, jnp.arange(token_rows * nz, dtype=jnp.int32))
+    tables = (cosine, sine, jnp.stack([token_segment, token_index], axis=1), key_segment[None, :])
+    gathered = gather_all(
+        (norm_one, w_query, w_key, w_value, query_gain, key_gain, w_output, norm_two, w_gate, w_up, w_down)
+    )
     hidden = tokens[0].astype(jnp.float32)
     stored = []
-    gathered = gather_all((norm_one, w_query, w_key, w_value, query_gain, key_gain, w_output, norm_two, w_gate, w_up, w_down))
     for which_layer in range(LAYERS):
-        weights = gathered[which_layer]
-        hidden, saved = layer_ahead(hidden, weights, tables)
+        hidden, saved = layer_ahead(hidden, gathered[which_layer], tables, m)
         stored.append(saved)
-    output = hidden.astype(jnp.bfloat16)[None]
+    output = swap(hidden.astype(jnp.bfloat16))[None]
     live_mask = (token_segment < doc_lengths.shape[0]).astype(jnp.float32)
     upstream = cotangent[0].astype(jnp.float32) * live_mask[:, None]
     operands = [None] * LAYERS
     for which_layer in reversed(range(LAYERS)):
         upstream, operands[which_layer] = layer_back(
-            upstream, gathered[which_layer], stored[which_layer], tables
+            upstream, gathered[which_layer], stored[which_layer], tables, m
         )
-    grad_tokens = upstream.astype(jnp.bfloat16)[None]
+    grad_tokens = swap(upstream.astype(jnp.bfloat16))[None]
     return (output, grad_tokens) + weight_gradients(operands)
-
-
-def weight_gradients(operands):
-    nx, nz = lax.axis_size("shard") // 2, lax.axis_size("ctx")
-    shards = 2 * nx * nz
-    lefts, rights = [], []
-    for layer_lefts, layer_rights, _ in operands:
-        for a in layer_lefts:
-            tokens, features = a.shape
-            rows = D // shards
-            blocks = a.T.reshape(nx, 2, nz, features // D, rows, tokens)
-            lefts.append(jnp.moveaxis(blocks, 3, 0))
-        for a in layer_rights:
-            rights.append(jnp.moveaxis(a.reshape(a.shape[0], -1, D), 1, 0))
-    pieces = reduce_weights(
-        jnp.concatenate(lefts), jnp.concatenate(rights), nx, nz, LAYERS, 1
-    ).reshape(LAYERS, PIECES, -1, D)
-
-    def columns(first, count):
-        part = pieces[:, first : first + count]
-        return jnp.moveaxis(part, 1, 2).reshape(LAYERS, -1, count * D)
-
-    def rows_of(first, count):
-        return pieces[:, first : first + count].reshape(LAYERS, -1, D)
-
-    flat = jnp.stack([jnp.concatenate(gains) for _, _, gains in operands])
-    flat = lax.psum(flat, ("rep", "shard", "ctx"))
-    here = lax.axis_index("shard") * nz + lax.axis_index("ctx")
-    small, used = [], 0
-    for size in (D, HEAD_SIZE, HEAD_SIZE, D):
-        own = size // shards
-        small.append(lax.dynamic_slice_in_dim(flat, used + here * own, own, axis=1))
-        used += size
-    return (
-        small[0],
-        columns(0, 2),
-        columns(2, 1),
-        columns(3, 1),
-        small[1],
-        small[2],
-        rows_of(10, 2),
-        small[3],
-        columns(4, 3),
-        columns(7, 3),
-        rows_of(12, 3),
-    )
 
 
 def solution(mesh):

time: 1140 us -> 832 us (0.73)
  waiting for transfers between devices: 179 us -> 0.01 us
  Pallas kernels: 569 us -> 705 us
  local copies, waits for them, and re-layouts: 129 us -> 28.6 us
  matrix products: 142 us -> 72.9 us
  other arithmetic: 58.8 us -> 5.76 us
  blocking collectives: 37.3 us -> 0 us
  between operations: 16.8 us -> 2.3 us
    pallas_call x0 -> x4, Pallas kernels: none -> 114 us  [the longest x2 60 us: attend_back(): pl.pallas_call(functools.partial(attend_back_kernel, m), out_shape=[jax.S...]
    all_gather x4 -> x0, waiting for transfers between devices: 111 us -> none  [the longest x2 61.5 us: layer_ahead(): value_portion = lax.all_gather(rows_of_values, 'ctx', axis=0, tiled=True)]
    dot_general x40 -> x28, matrix products: 142 us -> 72.9 us  [the longest x14 38.8 us: product_back(): lax.dot_general(grad, right, (((1,), (1,)), ((), ())), preferred_element_...]
    reduce_scatter x2 -> x0, waiting for transfers between devices: 67.4 us -> none  [layer_back(): lax.psum_scatter(grad_keyval.astype(jnp.bfloat16), 'ctx', scatter_dimensi...]
    psum x1 -> x0, blocking collectives: 37.3 us -> none  [weight_gradients(): flat = lax.psum(flat, ('rep', 'shard', 'ctx'))]
    reshape x10 -> x2, local copies, waits for them, and re-layouts: 25.4 us -> 1.47 us  [the longest x1 0.86 us: weight_gradients(): summed = summed.reshape(-1)[:flat.shape[0]].reshape(LAYERS, -1)]
    unnamed x367 -> x150, local copies, waits for them, and re-layouts: 38.4 us -> 15 us
    convert_element_type x22 -> x8, local copies, waits for them, and re-layouts: 23.2 us -> 0.66 us  [head_gain(): return gain.astype(jnp.float32)[None, :]]
  transfers between devices with their start and end apart: 6 -> 5, of which waited for: 6 -> 0; matrix products, arithmetic and copies ran while one was open for 8% -> 6% of each run, Pallas kernels for 0% -> 78%
where the time goes in v3:
time: 832 us; the launch traced here: 823 us
  Pallas kernels  705 us (85%)
  matrix products  72.9 us (9%)
  local copies, waits for them, and re-layouts  28.6 us (3%)
  starting transfers between devices  8.94 us (1%)
    pallas_call x1, Pallas kernels, reduce_weights(): pl.pallas_call(functools.partial(reduce_kernel, nx, nz, layers), out_shap...  333 us
    pallas_call x1, Pallas kernels, gather_weights(): pl.pallas_call(functools.partial(gather_kernel, shapes, nx, nz), out_shap...  259 us
    pallas_call x2, Pallas kernels, attend_back(): pl.pallas_call(functools.partial(attend_back_kernel, m), out_shape=[jax.S...  60 us
    pallas_call x2, Pallas kernels, attend(): pl.pallas_call(functools.partial(attend_kernel, m), out_shape=[jax.ShapeD...  53.6 us
    dot_general x14, matrix products, product_back(): lax.dot_general(grad, right, (((1,), (1,)), ((), ())), preferred_element_...  38.8 us
    dot_general x14, matrix products, product(): return jnp.dot(left, right, preferred_element_type=jnp.float32)  34.1 us
  transfers between devices with their start and end apart: 5, of which 0 were waited for; matrix products, arithmetic and copies ran while one was open for 6% of the time, Pallas kernels for 78%

profile of v3, /device:TPU:0, one launch (start us, length us, event | category | flops | bytes accessed | tf_op | source)
XLA Modules:
  0.0 823.3 jit_solution(10220186278473808355)
XLA Ops:
  0.7 1.4 collective-permute-start.1
  2.1 1.6 collective-permute-start
  3.7 4.5 collective-permute-start.3
  8.3 2.1 slice_bitcast_fusion
  10.4 2.1 slice_bitcast_fusion.1
  12.5 0.9 slice_bitcast_fusion.2
  14.3 0.8 slice_bitcast_fusion.7
  17.6 258.6 %shard_map.237 = (bf16[256,128]{1,0:T(8,128)(2,1)}, bf16[1024,2048]{1,0:T(8,128)(2,1)}, bf16[1024,1024]{1,0:T(8,128)(2,1)}, bf16[1024,1024]{1,0:T(8,128)(2,1)}, ...) custom-call(bf16[16,128]{1,0:T(8,128)(2,1)} %fusion.33.refs_0_, ...), custom_call_target="tpu_custom_call" | custom-call | tf_op jit(solution)/shard_map/pallas_call | solution.py:233
  276.3 0.9 reshape.293
  280.3 2.7 fusion.47.kp
  283.0 2.2 fusion.46.qp
  285.8 27.2 %shard_map.238 = (bf16[192,2048]{1,0:T(8,128)(2,1)S(1)}, bf16[768,2048]{1,0:T(8,128)(2,1)}, f32[192,2048]{1,0:T(8,128)S(1)}, bf16[192,2048]{1,0:T(8,128)(2,1)S(1)}, f32[192,128]{1,0:T(8,128)S(1)}) custom-call(f32[192,2048]{1,0:T(8,128)} %fusion.46.qp, f32[192,1024]{1,0:T(8,128)S(1)} %fusion.47.kp, bf16[192,1024]{1,0:T(8,128)(2,1)S(1)} %convolution_convert_fusion.3.v, ...), custom_call_target="tpu_custom_call" | custom-call | tf_op jit(solution)/shard_map/pallas_call | solution.py:896
  313.0 1.1 multiply_reduce_fusion.8
  314.3 4.4 fusion.48
  318.9 3.3 multiply_convert_fusion.3
  322.3 1.5 multiply_reduce_fusion.7
  326.8 2.2 fusion.49.qp
  329.0 26.4 %shard_map.239 = (bf16[192,2048]{1,0:T(8,128)(2,1)S(1)}, bf16[768,2048]{1,0:T(8,128)(2,1)}, f32[192,2048]{1,0:T(8,128)S(1)}, bf16[192,2048]{1,0:T(8,128)(2,1)S(1)}, f32[192,128]{1,0:T(8,128)S(1)}) custom-call(f32[192,2048]{1,0:T(8,128)} %fusion.49.qp, f32[192,1024]{1,0:T(8,128)S(1)} %fusion.50.kp, bf16[192,1024]{1,0:T(8,128)(2,1)S(1)} %convolution_convert_fusion.2.v, ...), custom_call_target="tpu_custom_call" | custom-call | tf_op jit(solution)/shard_map/pallas_call | solution.py:896
  355.4 3.6 multiply_reduce_fusion.6
  359.2 4.4 fusion.52
  363.9 2.8 fusion.51
  366.6 1.1 fusion.20.refs_21_
  367.8 7.9 multiply_convert_fusion.1
  375.7 3.9 fusion.53
  379.7 2.5 multiply_reduce_fusion
  382.2 1.3 fusion.42
  383.5 1.5 convolution_convert_fusion.1.d_att
  385.0 29.9 %shard_map.240 = (bf16[192,2048]{1,0:T(8,128)(2,1)S(1)}, bf16[192,1024]{1,0:T(8,128)(2,1)S(1)}, bf16[192,1024]{1,0:T(8,128)(2,1)S(1)}, f32[8,128]{1,0:T(8,128)S(1)}) custom-call(bf16[192,2048]{1,0:T(8,128)(2,1)S(1)} %get-tuple-element.95.q, bf16[768,2048]{1,0:T(8,128)(2,1)} %get-tuple-element.96.kv, bf16[192,2048]{1,0:T(8,128)(2,1)S(1)} %convolution_convert_fusion.1.d_att, ...), custom_call_target="tpu_custom_call" | custom-call | tf_op jit(solution)/shard_map/pallas_call | solution.py:1036
  415.0 4.3 fusion.54
  419.4 0.8 convolution_add_fusion.3
  420.9 1.1 multiply_reduce_fusion.1
  422.3 1.5 copy-done.32
  423.8 7.1 multiply_convert_fusion
  431.0 2.2 fusion.55
  433.3 2.4 multiply_reduce_fusion.2
  436.0 1.5 convolution_convert_fusion.d_att
  437.5 30.1 %shard_map.241 = (bf16[192,2048]{1,0:T(8,128)(2,1)S(1)}, bf16[192,1024]{1,0:T(8,128)(2,1)S(1)}, bf16[192,1024]{1,0:T(8,128)(2,1)S(1)}, f32[8,128]{1,0:T(8,128)S(1)}) custom-call(bf16[192,2048]{1,0:T(8,128)(2,1)S(1)} %get-tuple-element.102.q, bf16[768,2048]{1,0:T(8,128)(2,1)} %get-tuple-element.103.kv, bf16[192,2048]{1,0:T(8,128)(2,1)S(1)} %convolution_convert_fusion.d_att, ...), custom_call_target="tpu_custom_call" | custom-call | tf_op jit(solution)/shard_map/pallas_call | solution.py:1036
  467.7 1.5 fusion.56
  469.8 0.9 convolution_add_fusion.1
  471.1 1.1 fusion.12
  473.3 4.2 fusion.8
  478.8 332.5 %shard_map.242 = (f32[2,64,2048]{2,1,0:T(8,128)}, f32[2,64,1024]{2,1,0:T(8,128)}, f32[2,64,1024]{2,1,0:T(8,128)}, f32[2,128,1024]{2,1,0:T(8,128)}, f32[2,64,3072...) custom-call(bf16[192,1024]{1,0:T(8,128)(2,1)} %copy-done.15, ...), custom_call_target="tpu_custom_call" | custom-call | tf_op jit(solution)/shard_map/pallas_call | solution.py:696
  811.4 0.9 reshape.299
  815.0 1.0 copy.74
  817.6 1.0 copy.77
  818.6 1.1 copy.78
  819.7 1.1 copy.79
  821.7 1.1 copy.80
  (222 shorter events, 20.5 us)
Async XLA Ops:
  0.6 11.8 %copy-start.43 = (bf16[2,64,3072]{2,1,0:T(8,128)(2,1)S(1)}, bf16[2,64,3072]{2,1,0:T(8,128)(2,1)}, u32[]{:S(2)}) copy-start(bf16[2,64,3072]{2,1,0:T(8,128)(2,1)} %param.28) | copy-start | bytes 2359300
  0.7 278.0 %collective-permute-start.1 = (s32[1,8]{1,0:T(1,128)}, s32[1,8]{1,0:T(1,128)S(1)}, u32[]{:S(2)}, u32[]{:S(2)}) collective-permute-start(s32[1,8]{1,0:T(1,128)} %param.19), channel_id=1, source_target_pairs={{4,2},{2,4},{0,0},{6,6},{5,3},{3,5},{1,1},{7,7},{12,10},{10,12},{8... | collective-permute-start | bytes 104 | tf_op jit(solution)/shard_map/ppermute | solution.py:1296
  2.1 277.8 %collective-permute-start = (bf16[1,192,1024]{2,1,0:T(8,128)(2,1)}, bf16[1,192,1024]{2,1,0:T(8,128)(2,1)S(1)}, u32[]{:S(2)}, u32[]{:S(2)}) collective-permute-start(bf16[1,192,1024]{2,1,0:T(8,128)(2,1)} %param.18), channel_id=1, source_target_pairs={{4,2},{2,4},{0,0},{6,6},{5,3},{3,5},{1,1},{7,7},{12,10},{10,12},{8... | collective-permute-start | bytes 1179656 | tf_op jit(solution)/shard_map/ppermute | solution.py:1296
  3.7 362.9 %collective-permute-start.3 = (bf16[1,192,1024]{2,1,0:T(8,128)(2,1)}, bf16[1,192,1024]{2,1,0:T(8,128)(2,1)}, u32[]{:S(2)}, u32[]{:S(2)}) collective-permute-start(bf16[1,192,1024]{2,1,0:T(8,128)(2,1)} %param.31), channel_id=1, source_target_pairs={{4,2},{2,4},{0,0},{6,6},{5,3},{3,5},{1,1},{7,7},{12,10},{10,12},{8... | collective-permute-start | bytes 1179656 | tf_op jit(solution)/shard_map/ppermute | solution.py:1296
  8.2 5.2 copy-start.44
  10.4 3.9 copy-start.45
  10.4 4.8 copy-start.48
  12.5 3.4 copy-start.49
  12.5 4.1 copy-start.50
  12.5 4.2 copy-start.51
  12.5 4.3 copy-start.52
  12.5 4.4 copy-start.53
  279.7 3.2 copy-start.8
  279.9 33.1 %copy-start.16 = (bf16[1,192,1024]{2,1,0:T(8,128)(2,1)}, bf16[1,192,1024]{2,1,0:T(8,128)(2,1)S(1)}, u32[]{:S(2)}) copy-start(bf16[1,192,1024]{2,1,0:T(8,128)(2,1)S(1)} %collective-permute-done) | copy-start | bytes 1179652
  280.2 4.9 copy-start.15
  285.2 27.8 %copy-start.10 = (bf16[2048,1024]{1,0:T(8,128)(2,1)S(1)}, bf16[2048,1024]{1,0:T(8,128)(2,1)}, u32[]{:S(2)}) copy-start(bf16[2048,1024]{1,0:T(8,128)(2,1)} %get-tuple-element.83) | copy-start | bytes 12582916
  314.1 4.6 slice-start.6
  314.3 4.5 copy-start.26
  314.3 4.7 slice-start.7
  314.3 8.0 slice-start.10
  318.7 3.5 copy-start.31
  318.9 3.3 slice-start.11
  355.4 3.6 copy-start.1
  359.0 4.6 slice-start.4
  359.2 4.4 copy-start.14
  359.2 4.7 slice-start.5
  363.9 15.8 %slice-start = ((s8[6291456]{0:T(1024)(128)(4,1)}), s8[4194304]{0:T(1024)(128)(4,1)S(1)}, s32[]{:S(2)}) async-start(s8[6291456]{0:T(1024)(128)(4,1)} %bitcast.124), calls=%async_computation | async-start | bytes 8388608
  367.8 8.0 copy-start.36
  367.8 11.9 %slice-start.1 = ((s8[6291456]{0:T(1024)(128)(4,1)}), s8[2097152]{0:T(1024)(128)(4,1)S(1)}, s32[]{:S(2)}) async-start(s8[6291456]{0:T(1024)(128)(4,1)} %bitcast.124), calls=%async_computation.1 | async-start | bytes 4194304
  375.7 3.9 copy-start.27
  379.7 3.8 copy-start.13
  415.0 4.4 copy-start.2
  415.0 4.4 copy-start.5
  415.0 5.2 copy-start.4
  415.0 4.4 copy-start.25
  422.1 8.9 %slice-start.2 = ((s8[6291456]{0:T(1024)(128)(4,1)}), s8[4194304]{0:T(1024)(128)(4,1)S(1)}, s32[]{:S(2)}) async-start(s8[6291456]{0:T(1024)(128)(4,1)} %bitcast.126), calls=%async_computation.2 | async-start | bytes 8388608
  422.1 11.2 %slice-start.8 = ((s8[6291456]{0:T(1024)(128)(4,1)}), s8[4194304]{0:T(1024)(128)(4,1)S(1)}, s32[]{:S(2)}) async-start(s8[6291456]{0:T(1024)(128)(4,1)} %bitcast.132), calls=%async_computation.8 | async-start | bytes 8388608
  422.3 8.6 %copy-start.37 = (bf16[192,1024]{1,0:T(8,128)(2,1)}, bf16[192,1024]{1,0:T(8,128)(2,1)S(1)}, u32[]{:S(2)}) copy-start(bf16[192,1024]{1,0:T(8,128)(2,1)S(1)} %get-tuple-element.133.refs_10_) | copy-start | bytes 1179652
  423.8 7.1 slice-start.3
  423.8 9.4 %slice-start.9 = ((s8[6291456]{0:T(1024)(128)(4,1)}), s8[2097152]{0:T(1024)(128)(4,1)S(1)}, s32[]{:S(2)}) async-start(s8[6291456]{0:T(1024)(128)(4,1)} %bitcast.132), calls=%async_computation.9 | async-start | bytes 4194304
  437.5 30.2 %copy-start.9 = (bf16[1024,2048]{1,0:T(8,128)(2,1)S(1)}, bf16[1024,2048]{1,0:T(8,128)(2,1)}, u32[]{:S(2)}) copy-start(bf16[1024,2048]{1,0:T(8,128)(2,1)} %get-tuple-element.79) | copy-start | bytes 12582916
  467.7 3.0 copy-start.7
  472.6 340.9 %collective-permute-start.4 = (bf16[192,1024]{1,0:T(8,128)(2,1)S(1)}, bf16[192,1024]{1,0:T(8,128)(2,1)S(1)}, u32[]{:S(2)}, u32[]{:S(2)}) collective-permute-start(bf16[192,1024]{1,0:T(8,128)(2,1)S(1)} %fusion.17), channel_id=1, source_target_pairs={{4,2},{2,4},{0,0},{6,6},{5,3},{3,5},{1,1},{7,7},{12,10},{10,12},{8... | collective-permute-start | bytes 1179656 | tf_op jit(solution)/shard_map/ppermute | solution.py:1296
  477.5 336.0 %collective-permute-start.2 = (bf16[192,1024]{1,0:T(8,128)(2,1)S(1)}, bf16[192,1024]{1,0:T(8,128)(2,1)S(1)}, u32[]{:S(2)}, u32[]{:S(2)}) collective-permute-start(bf16[192,1024]{1,0:T(8,128)(2,1)S(1)} %fusion.8), channel_id=1, source_target_pairs={{4,2},{2,4},{0,0},{6,6},{5,3},{3,5},{1,1},{7,7},{12,10},{10,12},{8... | collective-permute-start | bytes 1179656 | tf_op jit(solution)/shard_map/ppermute | solution.py:1296
  811.3 3.7 copy-start.42
  811.4 4.6 copy-start.47
  813.5 3.3 copy-start.46
  814.3 3.3 copy-start.41
  (23 other events, 44.9 us)

commit v4 on v3

--- a/solution.py
+++ b/solution.py
@@ -251,40 +251,40 @@
 
 SLOTS = 4
 PIECES = 15
-LEFTS, RIGHTS = 7, 12
-
-
-LEFT_BLOCKS = (1, 1, 2, 3)
-RIGHT_BLOCKS = (2, 1, 1, 3, 3, 1, 1)
-RIGHTS = sum(RIGHT_BLOCKS)
-LEFT_FIRST = (0, 4, 10, 12)
-WEIGHTS = ((0, 2, 1), (2, 1, 1), (3, 1, 1), (10, 1, 2), (4, 3, 1), (7, 3, 1), (12, 1, 3))
-
-
-def right_of(j):
-    return jnp.where(j < 10, j, jnp.where(j < 12, 10, 11))
-
-
-def part_of(j):
-    return jnp.where(j < 10, 0, jnp.where(j < 12, j - 10, j - 12))
+LEFT_BLOCKS = (3, 2, 1, 1)
+LEFT_FIRST = (0, 3, 5, 11)
+RIGHTS = 7
+RIGHT_FIRST = (0, 3, 5, 7, 9, 11, 13)
+WEIGHT_BLOCKS = ((1, 3), (1, 2), (3, 1), (3, 1), (2, 1), (1, 1), (1, 1))
+
+
+def piece_place(j, replica):
+    if j < 2:
+        return 0, replica, j
+    if j == 2:
+        return 0, 2, replica
+    if j < 5:
+        return 1, replica, j - 3
+    if j < 11:
+        return 2 + replica, 0, j - 5
+    if replica == 0:
+        return 4, 0, j - 11
+    return (5, 0, j - 11) if j < 13 else (6, 0, j - 13)
 
 
 def reduce_kernel(nx, nz, layers, *refs):
-    per = len(LEFT_BLOCKS) + len(RIGHT_BLOCKS)
+    per = 4 + 4 + 7 + 1
     operands, refs = refs[: layers * per], refs[layers * per :]
     gains, refs = refs[0], refs[1:]
-    outs, refs = refs[: len(WEIGHTS)], refs[len(WEIGHTS) :]
-    lefts = [operands[n * per : n * per + 4] for n in range(layers)]
-    rights = [operands[n * per + 4 : (n + 1) * per] for n in range(layers)]
+    outs, refs = refs[: len(WEIGHT_BLOCKS)], refs[len(WEIGHT_BLOCKS) :]
     gains_out, left_at, refs = refs[0], refs[1:5], refs[5:]
-    right_at, turned, total, y_in, x_in, zup_in, zdown_in, f_in, result, refs = *refs[:9], refs[9:]
+    right_at, turned, total, x_in, zup_in, zdown_in, f_in, result, refs = *refs[:8], refs[8:]
     gain_in, gain_up, gain_down, refs = *refs[:3], refs[3:]
-    left_sem, right_sem, y_sem, x_sem, zup_sem, zdown_sem, f_sem, result_sem, gain_sem, credit = refs
-    rows = total.shape[3]
+    left_sem, right_sem, x_sem, zup_sem, zdown_sem, f_sem, result_sem, gain_sem, credit = refs
+    rows, width = total.shape[3:]
     tokens, wide = right_at.shape[2:]
-    quarter = wide // 4
-    kept = 3 * quarter
     pieces = layers * PIECES
+    ring = total.shape[0]
     y = lax.axis_index("rep")
     shard = lax.axis_index("shard")
     z = lax.axis_index("ctx")
@@ -298,9 +298,6 @@
     def to_z(step):
         return (y, shard, z + step)
 
-    ring = total.shape[0]
-    kept_at = pl.multiple_of(y * quarter, quarter)
-
     barrier = pltpu.get_barrier_semaphore()
     pl.semaphore_signal(barrier, inc=1, device_id=to_core, device_id_type=MESH)
     pl.semaphore_signal(barrier, inc=1, device_id=to_y, device_id_type=MESH)
@@ -314,162 +311,183 @@
     greeted = greeted + (x > 0).astype(jnp.int32) + (x < nx - 1).astype(jnp.int32)
     pl.semaphore_wait(barrier, greeted)
 
-    def left_copies(k, layer, source):
-        width = nz * LEFT_BLOCKS[k] * rows
-        sems = layer * len(LEFT_BLOCKS) + k
-
-        def columns(xs, of_core):
-            return source.at[:, pl.ds(pl.multiple_of((xs * 2 + of_core) * width, 128), width)]
-
-        for xs in range(nx):
-            yield pltpu.make_async_copy(columns(xs, core), left_at[k].at[0, layer, xs], left_sem.at[0, sems, xs])
-            yield pltpu.make_async_remote_copy(
-                src_ref=columns(xs, 1 - core),
-                dst_ref=left_at[k].at[1, layer, xs],
-                send_sem=left_sem.at[2, sems, xs],
-                recv_sem=left_sem.at[1, sems, xs],
-                device_id=to_core,
-                device_id_type=MESH,
-            )
-
-    def right_copies(b, source):
-        yield pltpu.make_async_copy(source, right_at.at[0, b], right_sem.at[0, b])
-        yield pltpu.make_async_remote_copy(
-            src_ref=source,
-            dst_ref=right_at.at[1, b],
-            send_sem=right_sem.at[2, b],
-            recv_sem=right_sem.at[1, b],
-            device_id=to_core,
-            device_id_type=MESH,
-        )
-
-    def first_right(j):
-        return (j <= 10) | (j == 12)
-
-    def blocks(i):
-        layer, j = lax.div(i, PIECES), lax.rem(i, PIECES)
-        return layer, j, part_of(j), layer * RIGHTS + right_of(j)
-
-    for layer in range(layers):
-        b = layer * RIGHTS
-        for k, source in enumerate(rights[layer]):
-            for k_left, first in enumerate(LEFT_FIRST):
-                if first == b - layer * RIGHTS or (first == 12 and k == 6):
-                    for copy in left_copies(k_left, layer, lefts[layer][k_left]):
-                        copy.start()
-            for n in range(RIGHT_BLOCKS[k]):
-                for copy in right_copies(b, source.at[:, pl.ds(n * wide, wide)]):
+    def left_copies(k, layer, sources):
+        span = nz * LEFT_BLOCKS[k] * rows
+        sems = layer * 4 + k
+        for whose, source in zip((0, 2), sources):
+
+            def columns(xs, of_core):
+                return source.at[:, pl.ds(pl.multiple_of((xs * 2 + of_core) * span, 128), span)]
+
+            for xs in range(nx):
+                yield pltpu.make_async_copy(
+                    columns(xs, core), left_at[k].at[whose, layer, xs], left_sem.at[whose, sems, xs]
+                )
+                yield remote(
+                    columns(xs, 1 - core),
+                    left_at[k].at[whose + 1, layer, xs],
+                    left_sem.at[4 + whose, sems, xs],
+                    left_sem.at[whose + 1, sems, xs],
+                    to_core,
+                )
+
+    def own_right(b, source):
+        return pltpu.make_async_copy(source, right_at.at[0, b], right_sem.at[0, b])
+
+    def pair_right(b, source):
+        return remote(source, right_at.at[1, b], right_sem.at[4, b], right_sem.at[1, b], to_core)
+
+    def held_right(b, source):
+        return pltpu.make_async_copy(source, right_at.at[2, b], right_sem.at[2, b])
+
+    def replica_right(b, source):
+        return remote(source, right_at.at[2, b], right_sem.at[5, b], right_sem.at[2, b], to_y)
+
+    def passed_right(b, source):
+        return remote(source, right_at.at[3, b], right_sem.at[6, b], right_sem.at[3, b], to_core)
+
+    def fetch(i):
+        for layer in range(layers):
+            mine = operands[layer * per : (layer + 1) * per]
+            lefts, their_lefts = mine[:4], mine[4:8]
+            down, output, gate, up, query, key, value, their_down = mine[8:]
+            blocks = [((down, 0), (down, 0)), ((output, 0), (output, 0))]
+            blocks += [((gate, n), (up, n)) for n in range(3)]
+            blocks += [((query, 0), (key, 0)), ((query, 1), (value, 0))]
+            for n in range(RIGHTS):
+
+                @pl.when(i == layer * PIECES + RIGHT_FIRST[n])
+                def _():
+                    fetch_block(layer, n, lefts, their_lefts, blocks[n], their_down)
+
+    def fetch_block(layer, n, lefts, their_lefts, block, their_down):
+        b = layer * RIGHTS + n
+        for replica in range(2):
+
+            @pl.when(y == replica)
+            def _():
+                here, there = (
+                    source.at[:, pl.ds(at * wide, wide)] for source, at in (block[replica], block[1 - replica])
+                )
+                if n > 0:
+                    replica_right(b, there).start()
+                own_right(b, here).start()
+                pair_right(b, here).start()
+
+        if n == 0:
+            held_right(b, their_down).start()
+            passed_right(b, their_down).start()
+        for k, first in enumerate(LEFT_FIRST):
+            if first == RIGHT_FIRST[n]:
+                for copy in left_copies(k, layer, (lefts[k], their_lefts[k])):
                     copy.start()
-                b += 1
-
-    def y_copy(i):
-        return pltpu.make_async_remote_copy(
-            src_ref=total.at[lax.rem(i, ring), :, :, :, pl.ds(pl.multiple_of((1 - y) * kept, quarter), quarter)],
-            dst_ref=y_in.at[lax.rem(i, SLOTS)],
-            send_sem=y_sem.at[0, i],
-            recv_sem=y_sem.at[1, i],
-            device_id=to_y,
-            device_id_type=MESH,
-        )
-
-    def f_copy(i):
-        return pltpu.make_async_remote_copy(
-            src_ref=total.at[lax.rem(i, ring), x, z, :, pl.ds(kept_at, kept)],
-            dst_ref=f_in.at[lax.rem(i, SLOTS)],
-            send_sem=f_sem.at[0, i],
-            recv_sem=f_sem.at[1, i],
-            device_id=to_y,
-            device_id_type=MESH,
-        )
-
-    def use(flow):
-        pl.semaphore_wait(credit.at[flow], 1)
-
-    def give(i, flow, device):
-        @pl.when(i + SLOTS < pieces)
-        def _():
-            pl.semaphore_signal(credit.at[flow], inc=1, device_id=device, device_id_type=MESH)
-
-    def spend(i, flow):
-        @pl.when(i >= SLOTS)
-        def _():
-            use(flow)
+
+    def place(i):
+        return lax.div(i, PIECES), lax.rem(i, PIECES)
+
+    def right_block(j):
+        return jnp.where(j < 3, 0, jnp.where(j < 5, 1, lax.div(j - 1, 2)))
+
+    def any_of(j, values):
+        hit = j == values[0]
+        for value in values[1:]:
+            hit = hit | (j == value)
+        return hit
+
+    some_right = operands[8]
+
+    def forward(i):
+        layer, j = place(i)
+
+        @pl.when(any_of(j, RIGHT_FIRST[1:]))
+        def _():
+            b = layer * RIGHTS + right_block(j)
+            replica_right(b, some_right).wait_recv()
+            passed_right(b, right_at.at[2, b]).start()
 
     def product(i):
-        layer, j, sub, rb = blocks(i)
+        layer, j = place(i)
+        b = layer * RIGHTS + right_block(j)
         for k, first in enumerate(LEFT_FIRST):
 
             @pl.when(j == first)
             def _():
-                for copy in left_copies(k, layer, lefts[0][k]):
+                for copy in left_copies(k, layer, (operands[k], operands[k])):
                     copy.wait()
 
-                for who in range(2):
+                for who in range(4):
                     for xs in range(nx):
                         flipped = left_at[k][who, layer, xs].T.reshape(nz, LEFT_BLOCKS[k], rows, tokens)
                         for n in range(LEFT_BLOCKS[k]):
                             turned[who, n, xs] = flipped[:, n]
 
-        @pl.when(first_right(j))
-        def _():
-            for copy in right_copies(rb, rights[0][1]):
-                copy.wait()
+        @pl.when(any_of(j, RIGHT_FIRST))
+        def _():
+            own_right(b, some_right).wait()
+            pair_right(b, some_right).wait()
+            passed_right(b, some_right).wait()
+
+        @pl.when(j == 0)
+        def _():
+            held_right(b, some_right).wait()
+
+        @pl.when(any_of(j, RIGHT_FIRST[1:]))
+        def _():
+            replica_right(b, some_right).wait_send()
 
         slot = lax.rem(i, ring)
-
-        def tile(c, carry):
-            at = pl.ds(pl.multiple_of(c * quarter, quarter), quarter)
+        part = jnp.where(j == 2, 2, jnp.where(j < 5, y, 0))
+        half = jnp.where(j < 2, j, jnp.where(j == 2, y, lax.rem(j + 1, 2)))
+        tile = width // 2
+
+        def columns(c, carry):
+            source = pl.ds(pl.multiple_of(half * width + c * tile, tile), tile)
             acc = None
-            for who in range(2):
-                left = turned[who, sub].reshape(nx * nz * rows, tokens)
-                part = jnp.dot(left, right_at[who, rb, :, at], preferred_element_type=jnp.float32)
-                acc = part if acc is None else acc + part
-            total[slot, :, :, :, at] = acc.reshape(nx, nz, rows, quarter).astype(total.dtype)
+            for who in range(4):
+                left = turned[who, part].reshape(nx * nz * rows, tokens)
+                term = jnp.dot(left, right_at[who, b, :, source], preferred_element_type=jnp.float32)
+                acc = term if acc is None else acc + term
+            into = pl.ds(pl.multiple_of(c * tile, tile), tile)
+            total[slot, :, :, :, into] = acc.reshape(nx, nz, rows, tile).astype(total.dtype)
             return carry
 
-        lax.fori_loop(0, 4, tile, 0)
-        spend(i, 0)
-        y_copy(i).start()
-
-    def add(slot, xs, zs, at, width, value):
-        where = (slot, xs, zs, slice(None), pl.ds(at, width))
+        lax.fori_loop(0, 2, columns, 0)
+
+    def give(i, flow, device):
+        @pl.when(i + SLOTS < pieces)
+        def _():
+            pl.semaphore_signal(credit.at[flow], inc=1, device_id=device, device_id_type=MESH)
+
+    def spend(i, flow):
+        @pl.when(i >= SLOTS)
+        def _():
+            pl.semaphore_wait(credit.at[flow], 1)
+
+    def add(slot, xs, zs, value):
+        where = (slot, xs, zs)
         total[where] = (total[where].astype(jnp.float32) + value.astype(jnp.float32)).astype(total.dtype)
-
-    def take_y(i):
-        slot, small = lax.rem(i, ring), lax.rem(i, SLOTS)
-        y_copy(i).wait_recv()
-
-        def body(n, carry):
-            xs, zs = lax.div(n, nz), lax.rem(n, nz)
-            add(slot, xs, zs, pl.multiple_of(y * kept, quarter), quarter, y_in[small, xs, zs])
-            return carry
-
-        lax.fori_loop(0, nx * nz, body, 0)
-        give(i, 0, to_y)
 
     def x_copy(i, up, here):
         low, high = (here + 1, nx) if up else (0, here)
         side = 0 if (up or nx == 2) else 1
-        return pltpu.make_async_remote_copy(
-            src_ref=total.at[lax.rem(i, ring), pl.ds(low, high - low), :, :, pl.ds(kept_at, kept)],
-            dst_ref=x_in.at[lax.rem(i, SLOTS), side, pl.ds(low - (1 if up else 0), high - low)],
-            send_sem=x_sem.at[0 if up else 1, i],
-            recv_sem=x_sem.at[2 if up else 3, i],
-            device_id=to_x(1 if up else -1),
-            device_id_type=MESH,
+        return remote(
+            total.at[lax.rem(i, ring), pl.ds(low, high - low)],
+            x_in.at[lax.rem(i, SLOTS), side, pl.ds(low - (1 if up else 0), high - low)],
+            x_sem.at[0 if up else 1, i],
+            x_sem.at[2 if up else 3, i],
+            to_x(1 if up else -1),
         )
 
     def z_copy(i, up, here):
         low, high = (here + 1, nz) if up else (0, here)
         into = zup_in if up else zdown_in
         sems = zup_sem if up else zdown_sem
-        return pltpu.make_async_remote_copy(
-            src_ref=total.at[lax.rem(i, ring), x, pl.ds(low, high - low), :, pl.ds(kept_at, kept)],
-            dst_ref=into.at[lax.rem(i, SLOTS), pl.ds(low - (1 if up else 0), high - low)],
-            send_sem=sems.at[0, i],
-            recv_sem=sems.at[1, i],
-            device_id=to_z(1 if up else -1),
-            device_id_type=MESH,
+        return remote(
+            total.at[lax.rem(i, ring), x, pl.ds(low, high - low)],
+            into.at[lax.rem(i, SLOTS), pl.ds(low - (1 if up else 0), high - low)],
+            sems.at[0, i],
+            sems.at[1, i],
+            to_z(1 if up else -1),
         )
 
     def x_hop(i, h):
@@ -485,13 +503,13 @@
                     for target in range(here, nx) if up else range(here + 1):
 
                         def body(zs, carry):
-                            add(slot, target, zs, kept_at, kept, x_in[small, side, target - (1 if up else 0), zs])
+                            add(slot, target, zs, x_in[small, side, target - (1 if up else 0), zs])
                             return carry
 
                         lax.fori_loop(0, nz, body, 0)
-                    give(i, 1 if up else 2, to_x(-1 if up else 1))
+                    give(i, 0 if up else 1, to_x(-1 if up else 1))
                 if h < nx - 1:
-                    spend(i, 1 if up else 2)
+                    spend(i, 0 if up else 1)
                     x_copy(i, up, here).start()
 
     def z_hop(i, h):
@@ -506,44 +524,77 @@
                     into = zup_in if up else zdown_in
 
                     def body(target, carry):
-                        add(slot, x, target, kept_at, kept, into[small, target - (1 if up else 0)])
+                        add(slot, x, target, into[small, target - (1 if up else 0)])
                         return carry
 
                     lax.fori_loop(here if up else 0, nz if up else here + 1, body, 0)
-                    give(i, 3 if up else 4, to_z(-1 if up else 1))
+                    give(i, 2 if up else 3, to_z(-1 if up else 1))
                 if h < nz - 1:
-                    spend(i, 3 if up else 4)
+                    spend(i, 2 if up else 3)
                     z_copy(i, up, here).start()
 
+    def f_copy(i):
+        return remote(
+            total.at[lax.rem(i, ring), x, z], f_in.at[lax.rem(i, SLOTS)], f_sem.at[0, i], f_sem.at[1, i], to_y
+        )
+
     def send_f(i):
-        spend(i, 5)
+        spend(i, 4)
         f_copy(i).start()
 
-    def result_copy(i, into):
-        return pltpu.make_async_copy(result.at[lax.rem(i, 2)], into, result_sem.at[lax.rem(i, 2)])
-
-    def keep_result(i):
-        layer, j = lax.div(i, PIECES), lax.rem(i, PIECES)
-        for into, (first, across, below) in zip(outs, WEIGHTS):
-            for n in range(across * below):
-
-                @pl.when(j == first + n)
+    def result_copy(i, replica, into):
+        two = lax.rem(i, 2)
+        return pltpu.make_async_copy(result.at[two, replica], into, result_sem.at[two, replica])
+
+    def keep_result(i, replica):
+        layer, j = place(i)
+        for n in range(PIECES):
+            for r in range(2):
+
+                @pl.when((j == n) & (replica == r))
                 def _():
-                    place = (pl.ds(0, rows), pl.ds(n * wide, wide)) if below == 1 else (pl.ds(n * rows, rows), pl.ds(0, wide))
-                    result_copy(i, into.at[(layer, *place)]).start()
+                    which, part, column = piece_place(n, r)
+                    into = outs[which].at[layer, pl.ds(part * rows, rows), pl.ds(column * width, width)]
+                    result_copy(i, r, into).start()
 
     def result_kept(i):
-        result_copy(i, outs[1].at[0]).wait()
+        for r in range(2):
+            result_copy(i, r, outs[5].at[0, :, pl.ds(0, width)]).wait()
+
+    def finish(i):
+        slot, small, two = lax.rem(i, ring), lax.rem(i, SLOTS), lax.rem(i, 2)
+        f_copy(i).wait_recv()
+
+        @pl.when(i >= 2)
+        def _():
+            result_kept(i - 2)
+
+        result[two, y] = total[slot, x, z].astype(jnp.float32)
+        result[two, 1 - y] = f_in[small].astype(jnp.float32)
+        give(i, 4, to_y)
+        keep_result(i, 0)
+        keep_result(i, 1)
+        f_copy(i).wait_send()
+        for here in range(nx):
+
+            @pl.when(x == here)
+            def _():
+                if here < nx - 1:
+                    x_copy(i, True, here).wait_send()
+                if here > 0:
+                    x_copy(i, False, here).wait_send()
+
+        for here in range(nz):
+
+            @pl.when(z == here)
+            def _():
+                if here < nz - 1:
+                    z_copy(i, True, here).wait_send()
+                if here > 0:
+                    z_copy(i, False, here).wait_send()
 
     def gain_copy(n, source, device):
-        return pltpu.make_async_remote_copy(
-            src_ref=source,
-            dst_ref=gain_in.at[n],
-            send_sem=gain_sem.at[0, n],
-            recv_sem=gain_sem.at[1, n],
-            device_id=device,
-            device_id_type=MESH,
-        )
+        return remote(source, gain_in.at[n], gain_sem.at[0, n], gain_sem.at[1, n], device)
 
     def gain_start():
         copy = pltpu.make_async_copy(gains, gain_in.at[0], gain_sem.at[0, 0])
@@ -589,69 +640,6 @@
         copy = pltpu.make_async_copy(gain_in.at[0], gains_out, gain_sem.at[0, 0])
         copy.start()
         copy.wait()
-
-    def finish(i):
-        slot, small, two = lax.rem(i, ring), lax.rem(i, SLOTS), lax.rem(i, 2)
-        f_copy(i).wait_recv()
-
-        @pl.when(i >= 2)
-        def _():
-            result_kept(i - 2)
-
-        mine = total[slot, x, z].astype(jnp.float32)
-        got = f_in[small].astype(jnp.float32)
-
-        @pl.when(y == 0)
-        def _():
-            result[two, :, :quarter] = mine[:, :quarter]
-            result[two, :, quarter:kept] = mine[:, quarter:kept] + got[:, : 2 * quarter]
-            result[two, :, kept:] = got[:, 2 * quarter :]
-
-        @pl.when(y == 1)
-        def _():
-            result[two, :, :quarter] = got[:, :quarter]
-            result[two, :, quarter:kept] = mine[:, quarter:kept] + got[:, quarter:]
-            result[two, :, kept:] = mine[:, kept:]
-
-        give(i, 5, to_y)
-        keep_result(i)
-        y_copy(i).wait_send()
-        f_copy(i).wait_send()
-        for here in range(nx):
-
-            @pl.when(x == here)
-            def _():
-                if here < nx - 1:
-                    x_copy(i, True, here).wait_send()
-                if here > 0:
-                    x_copy(i, False, here).wait_send()
-
-        for here in range(nz):
-
-            @pl.when(z == here)
-            def _():
-                if here < nz - 1:
-                    z_copy(i, True, here).wait_send()
-                if here > 0:
-                    z_copy(i, False, here).wait_send()
-
-    plan = [[("product",)]]
-    plan.append([("y",), ("x", 0)])
-    for h in range(1, nx):
-        plan.append([("x", h)])
-    plan[-1].append(("z", 0))
-    for h in range(1, nz):
-        plan.append([("z", h)])
-    plan[-1].append(("f",))
-    plan.append([("end",)])
-    does = {
-        "product": product,
-        "y": take_y,
-        "x": x_hop,
-        "z": z_hop,
-        "f": send_f,
-        "end": finish,
-    }
 
     steps = [gain_start, gain_pair, gain_y]
     for h in range(nx):
@@ -662,18 +650,28 @@
     steps.append(functools.partial(gain_line, nz, z, to_z, 5, 2))
     steps.append(gain_end)
 
+    plan = [[fetch], [], [], [forward], [], [product], [functools.partial(x_hop, h=0)]]
+    for h in range(1, nx):
+        plan += [[], [functools.partial(x_hop, h=h)]]
+    plan[-1].append(functools.partial(z_hop, h=0))
+    for h in range(1, nz):
+        plan.append([functools.partial(z_hop, h=h)])
+    plan[-1].append(send_f)
+    plan.append([finish])
+
     def tick(t, carry):
+        for depth in [*range(6, len(plan)), 0, 3, 5]:
+            if not plan[depth]:
+                continue
+            i = t - depth
+
+            @pl.when((i >= 0) & (i < pieces))
+            def _():
+                for stage in plan[depth]:
+                    stage(i)
+
         for n, step in enumerate(steps):
             pl.when(t == n)(step)
-
-        for depth in [*range(1, len(plan)), 0]:
-            i = t - depth
-
-            @pl.when((i >= 0) & (i < pieces))
-            def _():
-                for name, *more in plan[depth]:
-                    does[name](i, *more)
-
         return carry
 
     lax.fori_loop(0, pieces + len(plan) - 1, tick, 0)
@@ -684,11 +682,10 @@
 def reduce_weights(operands, gains, nx, nz, collective_id):
     layers = len(operands)
     flat = [a for layer in operands for a in layer]
-    tokens, wide = flat[0].shape
-    rows = wide // (2 * nx * nz)
+    tokens, wide = operands[0][8].shape
+    rows, width = wide // (2 * nx * nz), wide // 2
     pieces = layers * PIECES
-    kept = 3 * wide // 4
-    ring = nx + nz + 2
+    ring = 2 * nx + nz + 1
     sides = 1 if nx == 2 else 2
     low = jnp.bfloat16
     dma = pltpu.SemaphoreType.DMA
@@ -696,35 +693,33 @@
     return pl.pallas_call(
         functools.partial(reduce_kernel, nx, nz, layers),
         out_shape=[
-            jax.ShapeDtypeStruct((layers, rows * below, wide * across), jnp.float32) for _, across, below in WEIGHTS
+            jax.ShapeDtypeStruct((layers, rows * below, wide * across), jnp.float32) for across, below in WEIGHT_BLOCKS
         ]
         + [jax.ShapeDtypeStruct(gains.shape, gains.dtype)],
         in_specs=[anywhere] * (len(flat) + 1),
-        out_specs=[anywhere] * (len(WEIGHTS) + 1),
-        scratch_shapes=[pltpu.VMEM((2, layers, nx, tokens, nz * n * rows), low) for n in LEFT_BLOCKS]
+        out_specs=[anywhere] * (len(WEIGHT_BLOCKS) + 1),
+        scratch_shapes=[pltpu.VMEM((4, layers, nx, tokens, nz * n * rows), low) for n in LEFT_BLOCKS]
         + [
-            pltpu.VMEM((2, layers * RIGHTS, tokens, wide), low),
-            pltpu.VMEM((2, max(LEFT_BLOCKS), nx, nz, rows, tokens), low),
-            pltpu.VMEM((ring, nx, nz, rows, wide), low),
-            pltpu.VMEM((SLOTS, nx, nz, rows, wide // 4), low),
-            pltpu.VMEM((SLOTS, sides, nx - 1, nz, rows, kept), low),
-            pltpu.VMEM((SLOTS, nz - 1, rows, kept), low),
-            pltpu.VMEM((SLOTS, nz - 1, rows, kept), low),
-            pltpu.VMEM((SLOTS, rows, kept), low),
-            pltpu.VMEM((2, rows, wide), jnp.float32),
+            pltpu.VMEM((4, layers * RIGHTS, tokens, wide), low),
+            pltpu.VMEM((4, max(LEFT_BLOCKS), nx, nz, rows, tokens), low),
+            pltpu.VMEM((ring, nx, nz, rows, width), low),
+            pltpu.VMEM((SLOTS, sides, nx - 1, nz, rows, width), low),
+            pltpu.VMEM((SLOTS, nz - 1, rows, width), low),
+            pltpu.VMEM((SLOTS, nz - 1, rows, width), low),
+            pltpu.VMEM((SLOTS, rows, width), low),
+            pltpu.VMEM((2, 2, rows, width), jnp.float32),
             pltpu.VMEM((7, *gains.shape), gains.dtype),
             pltpu.VMEM((3, *gains.shape), gains.dtype),
             pltpu.VMEM((3, *gains.shape), gains.dtype),
-            dma((3, layers * len(LEFT_BLOCKS), nx)),
-            dma((3, layers * RIGHTS)),
-            dma((2, pieces)),
+            dma((7, layers * 4, nx)),
+            dma((7, layers * RIGHTS)),
             dma((4, pieces)),
             dma((2, pieces)),
             dma((2, pieces)),
             dma((2, pieces)),
-            dma((2,)),
+            dma((2, 2)),
             dma((2, 7)),
-            pltpu.SemaphoreType.REGULAR((6,)),
+            pltpu.SemaphoreType.REGULAR((5,)),
         ],
         compiler_params=pltpu.CompilerParams(
             collective_id=collective_id, has_side_effects=True, vmem_limit_bytes=56 * 1024 * 1024
@@ -1101,11 +1096,20 @@
     return lax.dot_general(grad, right, (((1,), (1,)), ((), ())), preferred_element_type=jnp.float32)
 
 
+def over_replica(values):
+    return lax.ppermute(values, "rep", [(0, 1), (1, 0)])
+
+
+def after(value, others):
+    value, *others = lax.optimization_barrier((value, *others))
+    return value, others
+
+
 def head_gain(gain):
     return gain.astype(jnp.float32)[None, :]
 
 
-def layer_ahead(hidden, weights, tables, m):
+def layer_ahead(hidden, weights, tables, m, which_layer, waiting):
     (
         gain_first,
         query_weight,
@@ -1123,14 +1127,20 @@
     key_projection = product(normalized_rows, key_matrix)
     rows_of_values = product(normalized_rows, value_matrix).astype(jnp.bfloat16)
     query_proj = product(normalized_rows, query_weight)
+    waiting.append(over_replica(normalized_rows))
     query_rows, keys_values, attended_rows, attended_low, log_sum = attend(
         m, query_proj, key_projection, rows_of_values, head_gain(gain_query), head_gain(gain_key), *tables, 2
     )
+    attended_low, before = after(attended_low, waiting if which_layer == 0 else waiting[:3])
+    waiting[: len(before)] = before
+    waiting.append(over_replica(attended_low))
     hidden_mid = hidden + product(attended_low, output_weight)
     normed_two = rms_scale(hidden_mid, gain_second.astype(jnp.float32)).astype(jnp.bfloat16)
+    waiting.append(over_replica(normed_two))
     gate_pre = product(normed_two, gate_weight)
     upward = product(normed_two, up_weight)
     activated = swiglu(gate_pre, upward).astype(jnp.bfloat16)
+    waiting.append(over_replica(activated))
     hidden_out = hidden_mid + product(activated, down_weight)
     saved = (
         hidden,
@@ -1151,7 +1161,7 @@
     return (hidden_out, saved)
 
 
-def layer_back(upstream, weights, saved, tables, m):
+def layer_back(upstream, weights, saved, tables, m, which_layer, waiting):
     (
         gain_first,
         query_weight,
@@ -1182,6 +1192,7 @@
         activated,
     ) = saved
     branch_low = upstream.astype(jnp.bfloat16)
+    waiting.append(over_replica(branch_low))
     grad_act = product_back(branch_low, down_weight)
     ignored, swiglu_back = jax.vjp(swiglu, gate_pre, upward)
     grad_gate_pre, grad_upward = swiglu_back(grad_act)
@@ -1193,6 +1204,8 @@
     upstream_mid = upstream + grad_mid
     attn_low = upstream_mid.astype(jnp.bfloat16)
     grad_attended = product_back(attn_low, output_weight).astype(jnp.bfloat16)
+    ready = 5 if which_layer == 1 else 8
+    grad_attended, waiting[:ready] = after(grad_attended, waiting[:ready])
     query_low, key_low, value_low, head_gains = attend_back(
         m,
         query_rows,
@@ -1207,15 +1220,17 @@
         *tables,
         3,
     )
+    ready = 7 if which_layer == 1 else 10
+    query_low, waiting[:ready] = after(query_low, waiting[:ready])
     grad_normed = product_back(query_low, query_weight)
     grad_normed = grad_normed + product_back(key_low, key_matrix)
     grad_normed = grad_normed + product_back(value_low, value_matrix)
     ignored, first_back = jax.vjp(rms_scale, hidden, gain_first.astype(jnp.float32))
     grad_hidden, grad_gain_first = first_back(grad_normed)
-    lefts = (normalized_rows, normed_two, attended_low, activated)
-    rights = (query_low, key_low, value_low, gate_low, up_low, attn_low, branch_low)
+    lefts = (activated, attended_low, normed_two, normalized_rows)
+    rights = (branch_low, attn_low, gate_low, up_low, query_low, key_low, value_low)
     gains = (grad_gain_first, head_gains[0], head_gains[1], grad_gain_second)
-    return (upstream_mid + grad_hidden, (lefts + rights, gains))
+    return (upstream_mid + grad_hidden, (lefts, rights, gains))
 
 
 def near_rows(rows, share):
@@ -1262,7 +1277,7 @@
         own = size // shards
         small.append(lax.dynamic_slice_in_dim(summed, used + here * own, own, axis=1))
         used += size
-    query, key, value, output, gate, up, down = grads
+    down, output, gate, up, query, key, value = grads
     return (small[0], query, key, value, small[1], small[2], output, small[3], gate, up, down)
 
 
@@ -1309,9 +1324,9 @@
         (norm_one, w_query, w_key, w_value, query_gain, key_gain, w_output, norm_two, w_gate, w_up, w_down)
     )
     hidden = tokens[0].astype(jnp.float32)
-    stored = []
+    stored, waiting = [], []
     for which_layer in range(LAYERS):
-        hidden, saved = layer_ahead(hidden, gathered[which_layer], tables, m)
+        hidden, saved = layer_ahead(hidden, gathered[which_layer], tables, m, which_layer, waiting)
         stored.append(saved)
     output = swap(hidden.astype(jnp.bfloat16))[None]
     live_mask = (token_segment < doc_lengths.shape[0]).astype(jnp.float32)
@@ -1319,9 +1334,13 @@
     operands = [None] * LAYERS
     for which_layer in reversed(range(LAYERS)):
         upstream, operands[which_layer] = layer_back(
-            upstream, gathered[which_layer], stored[which_layer], tables, m
+            upstream, gathered[which_layer], stored[which_layer], tables, m, which_layer, waiting
         )
     grad_tokens = swap(upstream.astype(jnp.bfloat16))[None]
+    for which_layer, (lefts, rights, gains) in enumerate(operands):
+        normed, attended, normed_two, activated = waiting[which_layer * 4 : which_layer * 4 + 4]
+        theirs = (activated, attended, normed_two, normed)
+        operands[which_layer] = (lefts + theirs + rights + (waiting[9 - which_layer],), gains)
     return (output, grad_tokens) + weight_gradients(operands)
 
 

time: 832 us -> 724 us (0.87)
  Pallas kernels: 705 us -> 587 us
  starting transfers between devices: 8.94 us -> 17.9 us
    pallas_call x1, Pallas kernels: 333 us -> 205 us  [reduce_weights(): pl.pallas_call(functools.partial(reduce_kernel, nx, nz, layers), out_shap...]
    ppermute x0 -> x10, starting transfers between devices: none -> 10.7 us  [over_replica(): return lax.ppermute(values, 'rep', [(0, 1), (1, 0)])]
  transfers between devices with their start and end apart: 5 -> 15, of which waited for: 0 -> 0; matrix products, arithmetic and copies ran while one was open for 6% -> 13% of each run, Pallas kernels for 78% -> 82%
where the time goes in v4:
time: 724 us; the launch traced here: 716 us
  Pallas kernels  587 us (81%)
  matrix products  77.9 us (11%)
  local copies, waits for them, and re-layouts  26.7 us (4%)
  starting transfers between devices  17.9 us (2%)
    pallas_call x1, Pallas kernels, gather_weights(): pl.pallas_call(functools.partial(gather_kernel, shapes, nx, nz), out_shap...  262 us
    pallas_call x1, Pallas kernels, reduce_weights(): pl.pallas_call(functools.partial(reduce_kernel, nx, nz, layers), out_shap...  205 us
    pallas_call x2, Pallas kernels, attend_back(): pl.pallas_call(functools.partial(attend_back_kernel, m), out_shape=[jax.S...  67.8 us
    pallas_call x2, Pallas kernels, attend(): pl.pallas_call(functools.partial(attend_kernel, m), out_shape=[jax.ShapeD...  52.4 us
    dot_general x14, matrix products, product_back(): lax.dot_general(grad, right, (((1,), (1,)), ((), ())), preferred_element_...  39.2 us
    dot_general x14, matrix products, product(): return jnp.dot(left, right, preferred_element_type=jnp.float32)  38.7 us
  transfers between devices with their start and end apart: 15, of which 0 were waited for; matrix products, arithmetic and copies ran while one was open for 13% of the time, Pallas kernels for 82%

profile of v4, /device:TPU:0, one launch (start us, length us, event | category | flops | bytes accessed | tf_op | source)
XLA Modules:
  0.0 715.8 jit_solution(16004415802289235092)
XLA Ops:
  0.7 1.4 collective-permute-start.1
  2.1 1.6 collective-permute-start
  3.7 1.6 collective-permute-start.6
  5.4 2.1 slice_bitcast_fusion
  7.5 2.1 slice_bitcast_fusion.1
  14.7 261.5 %shard_map.237 = (bf16[256,128]{1,0:T(8,128)(2,1)}, bf16[1024,2048]{1,0:T(8,128)(2,1)}, bf16[1024,1024]{1,0:T(8,128)(2,1)}, bf16[1024,1024]{1,0:T(8,128)(2,1)}, ...) custom-call(bf16[16,128]{1,0:T(8,128)(2,1)} %fusion.35.refs_0_, ...), custom_call_target="tpu_custom_call" | custom-call | tf_op jit(solution)/shard_map/pallas_call | solution.py:233
  280.9 2.3 convolution_convert_fusion.3.v
  283.2 2.2 fusion.49.kp
  285.6 1.5 collective-permute-start.12
  287.1 2.2 fusion.48.qp
  289.3 26.2 %shard_map.238 = (bf16[192,2048]{1,0:T(8,128)(2,1)S(1)}, bf16[768,2048]{1,0:T(8,128)(2,1)}, f32[192,2048]{1,0:T(8,128)S(1)}, bf16[192,2048]{1,0:T(8,128)(2,1)S(1)}, f32[192,128]{1,0:T(8,128)S(1)}) custom-call(f32[192,2048]{1,0:T(8,128)} %fusion.48.qp, f32[192,1024]{1,0:T(8,128)S(1)} %fusion.49.kp, bf16[192,1024]{1,0:T(8,128)(2,1)S(1)} %convolution_convert_fusion.3.v, ...), custom_call_target="tpu_custom_call" | custom-call | tf_op jit(solution)/shard_map/pallas_call | solution.py:891
  316.2 3.3 multiply_reduce_fusion.8
  319.6 1.5 collective-permute-start.4
  321.2 4.3 fusion.50
  325.6 3.6 multiply_convert_fusion.3
  330.1 3.0 multiply_reduce_fusion.7
  333.3 1.2 collective-permute-start.8
  335.6 1.1 copy-done.11
  336.7 2.2 fusion.51.qp
  338.9 26.2 %shard_map.239 = (bf16[192,2048]{1,0:T(8,128)(2,1)S(1)}, bf16[768,2048]{1,0:T(8,128)(2,1)}, f32[192,2048]{1,0:T(8,128)S(1)}, bf16[192,2048]{1,0:T(8,128)(2,1)S(1)}, f32[192,128]{1,0:T(8,128)S(1)}) custom-call(f32[192,2048]{1,0:T(8,128)} %fusion.51.qp, f32[192,1024]{1,0:T(8,128)S(1)} %fusion.52.kp, bf16[192,1024]{1,0:T(8,128)(2,1)S(1)} %convolution_convert_fusion.2.v, ...), custom_call_target="tpu_custom_call" | custom-call | tf_op jit(solution)/shard_map/pallas_call | solution.py:891
  365.2 1.1 collective-permute-start.9
  366.2 3.3 multiply_reduce_fusion.6
  369.7 4.4 fusion.54
  374.4 1.4 fusion.53
  375.8 7.0 multiply_convert_fusion.1
  382.8 4.0 fusion.55
  386.8 5.4 fusion.10
  392.2 1.8 collective-permute-start.5
  394.1 2.4 multiply_reduce_fusion
  396.9 1.5 convolution_convert_fusion.1.d_att
  398.4 1.1 collective-permute-start.10
  399.5 1.0 collective-permute-start.11
  400.5 37.6 %shard_map.240 = (bf16[192,2048]{1,0:T(8,128)(2,1)S(1)}, bf16[192,1024]{1,0:T(8,128)(2,1)S(1)}, bf16[192,1024]{1,0:T(8,128)(2,1)S(1)}, f32[8,128]{1,0:T(8,128)S(1)}) custom-call(bf16[192,2048]{1,0:T(8,128)(2,1)S(1)} %get-tuple-element.138.q, bf16[768,2048]{1,0:T(8,128)(2,1)} %get-tuple-element.139.kv, bf16[192,2048]{1,0:T(8,128)(2,1)S(1)} %convolution_convert_fusion.1.d_att, ...), custom_call_target="tpu_custom_call" | custom-call | tf_op jit(solution)/shard_map/pallas_call | solution.py:1031
  438.2 3.0 fusion.56
  442.2 1.8 multiply_reduce_fusion.1
  444.4 1.1 collective-permute-start.13
  445.9 5.9 multiply_convert_fusion
  451.8 2.3 fusion.58
  454.1 5.4 multiply_reduce_fusion.2
  459.8 1.5 convolution_convert_fusion.d_att
  461.4 30.2 %shard_map.241 = (bf16[192,2048]{1,0:T(8,128)(2,1)S(1)}, bf16[192,1024]{1,0:T(8,128)(2,1)S(1)}, bf16[192,1024]{1,0:T(8,128)(2,1)S(1)}, f32[8,128]{1,0:T(8,128)S(1)}) custom-call(bf16[192,2048]{1,0:T(8,128)(2,1)S(1)} %get-tuple-element.155.q, bf16[768,2048]{1,0:T(8,128)(2,1)} %get-tuple-element.156.kv, bf16[192,2048]{1,0:T(8,128)(2,1)S(1)} %convolution_convert_fusion.d_att, ...), custom_call_target="tpu_custom_call" | custom-call | tf_op jit(solution)/shard_map/pallas_call | solution.py:1031
  492.5 1.4 copy-done.17
  495.1 1.8 fusion.14
  498.6 205.3 %shard_map.242 = (f32[2,192,1024]{2,1,0:T(8,128)}, f32[2,128,1024]{2,1,0:T(8,128)}, f32[2,64,3072]{2,1,0:T(8,128)}, f32[2,64,3072]{2,1,0:T(8,128)}, f32[2,64,204...) custom-call(bf16[192,3072]{1,0:T(8,128)(2,1)} %get-tuple-element.253.refs_0_, ...), custom_call_target="tpu_custom_call" | custom-call | tf_op jit(solution)/shard_map/pallas_call | solution.py:693
  707.6 1.0 copy.74
  711.1 1.1 copy.78
  712.2 1.1 copy.79
  714.2 1.1 copy.80
  (247 shorter events, 26.1 us)
Async XLA Ops:
  0.6 9.0 %copy-start.40 = (bf16[2,64,3072]{2,1,0:T(8,128)(2,1)S(1)}, bf16[2,64,3072]{2,1,0:T(8,128)(2,1)}, u32[]{:S(2)}) copy-start(bf16[2,64,3072]{2,1,0:T(8,128)(2,1)} %param.28) | copy-start | bytes 2359300
  0.7 278.0 %collective-permute-start.1 = (s32[1,8]{1,0:T(1,128)}, s32[1,8]{1,0:T(1,128)S(1)}, u32[]{:S(2)}, u32[]{:S(2)}) collective-permute-start(s32[1,8]{1,0:T(1,128)} %param.19), channel_id=1, source_target_pairs={{4,2},{2,4},{0,0},{6,6},{5,3},{3,5},{1,1},{7,7},{12,10},{10,12},{8... | collective-permute-start | bytes 104 | tf_op jit(solution)/shard_map/ppermute | solution.py:1311
  2.1 277.8 %collective-permute-start = (bf16[1,192,1024]{2,1,0:T(8,128)(2,1)}, bf16[1,192,1024]{2,1,0:T(8,128)(2,1)S(1)}, u32[]{:S(2)}, u32[]{:S(2)}) collective-permute-start(bf16[1,192,1024]{2,1,0:T(8,128)(2,1)} %param.18), channel_id=1, source_target_pairs={{4,2},{2,4},{0,0},{6,6},{5,3},{3,5},{1,1},{7,7},{12,10},{10,12},{8... | collective-permute-start | bytes 1179656 | tf_op jit(solution)/shard_map/ppermute | solution.py:1311
  3.7 281.6 %collective-permute-start.6 = (bf16[1,192,1024]{2,1,0:T(8,128)(2,1)}, bf16[1,192,1024]{2,1,0:T(8,128)(2,1)S(1)}, u32[]{:S(2)}, u32[]{:S(2)}) collective-permute-start(bf16[1,192,1024]{2,1,0:T(8,128)(2,1)} %param.31), channel_id=1, source_target_pairs={{4,2},{2,4},{0,0},{6,6},{5,3},{3,5},{1,1},{7,7},{12,10},{10,12},{8... | collective-permute-start | bytes 1179656 | tf_op jit(solution)/shard_map/ppermute | solution.py:1311
  5.4 5.2 copy-start.41
  7.5 4.8 copy-start.52
  9.6 4.1 copy-start.54
  9.6 4.1 copy-start.55
  9.7 4.2 copy-start.56
  9.7 4.3 copy-start.57
  280.2 6.9 copy-start.15
  280.2 35.3 %collective-permute-start.2 = (bf16[192,1024]{1,0:T(8,128)(2,1)S(1)}, bf16[192,1024]{1,0:T(8,128)(2,1)S(1)}, u32[]{:S(2)}, u32[]{:S(2)}) collective-permute-start(bf16[192,1024]{1,0:T(8,128)(2,1)S(1)} %fusion.13.refs_3_), channel_id=1, source_target_pairs={{0,16},{16,0},{1,17},{17,1},{2,18},{18,2},{3,19},{19,3},{4,20},{20... | collective-permute-start | bytes 1179656 | tf_op jit(solution)/shard_map/ppermute | solution.py:1100
  280.9 6.2 copy-start.8
  285.5 90.2 %copy-start.34 = (bf16[192,1024]{1,0:T(8,128)(2,1)}, bf16[192,1024]{1,0:T(8,128)(2,1)S(1)}, u32[]{:S(2)}) copy-start(bf16[192,1024]{1,0:T(8,128)(2,1)S(1)} %fusion.22.refs_24_) | copy-start | bytes 1179652
  285.6 206.0 %collective-permute-start.12 = (bf16[192,1024]{1,0:T(8,128)(2,1)S(1)}, bf16[192,1024]{1,0:T(8,128)(2,1)}, u32[]{:S(2)}, u32[]{:S(2)}) collective-permute-start(bf16[192,1024]{1,0:T(8,128)(2,1)S(1)} %fusion.22.refs_24_), channel_id=1, source_target_pairs={{0,16},{16,0},{1,17},{17,1},{2,18},{18,2},{3,19},{19,3},{4,20},{20... | collective-permute-start | bytes 1179656 | tf_op jit(solution)/shard_map/ppermute | solution.py:1100
  315.5 49.6 %collective-permute-start.3 = (bf16[192,2048]{1,0:T(8,128)(2,1)S(1)}, bf16[192,2048]{1,0:T(8,128)(2,1)S(1)}, u32[]{:S(2)}, u32[]{:S(2)}) collective-permute-start(bf16[192,2048]{1,0:T(8,128)(2,1)S(1)} %get-tuple-element.123.refs_1_), channel_id=1, source_target_pairs={{0,16},{16,0},{1,17},{17,1},{2,18},{18,2},{3,19},{19,3},{4,20},{20... | collective-permute-start | bytes 2359304 | tf_op jit(solution)/shard_map/ppermute | solution.py:1100
  319.5 6.0 slice-start.6
  319.6 5.9 copy-start.22
  319.6 45.5 %collective-permute-start.4 = (bf16[192,1024]{1,0:T(8,128)(2,1)S(1)}, bf16[192,1024]{1,0:T(8,128)(2,1)S(1)}, u32[]{:S(2)}, u32[]{:S(2)}) collective-permute-start(bf16[192,1024]{1,0:T(8,128)(2,1)S(1)} %multiply_convert_fusion.6.refs_2_), channel_id=1, source_target_pairs={{0,16},{16,0},{1,17},{17,1},{2,18},{18,2},{3,19},{19,3},{4,20},{20... | collective-permute-start | bytes 1179656 | tf_op jit(solution)/shard_map/ppermute | solution.py:1100
  321.2 4.4 slice-start.7
  321.2 9.0 %slice-start.8 = ((s8[6291456]{0:T(1024)(128)(4,1)}), s8[4194304]{0:T(1024)(128)(4,1)S(1)}, s32[]{:S(2)}) async-start(s8[6291456]{0:T(1024)(128)(4,1)} %bitcast.138), calls=%async_computation.8 | async-start | bytes 8388608
  325.5 4.6 slice-start.9
  329.2 70.4 %collective-permute-start.7 = (bf16[192,3072]{1,0:T(8,128)(2,1)}, bf16[192,3072]{1,0:T(8,128)(2,1)}, u32[]{:S(2)}, u32[]{:S(2)}) collective-permute-start(bf16[192,3072]{1,0:T(8,128)(2,1)} %get-tuple-element.253.refs_0_), channel_id=1, source_target_pairs={{0,16},{16,0},{1,17},{17,1},{2,18},{18,2},{3,19},{19,3},{4,20},{20... | collective-permute-start | bytes 3538952 | tf_op jit(solution)/shard_map/ppermute | solution.py:1100
  330.1 4.3 copy-start.21
  333.3 65.1 %collective-permute-start.8 = (bf16[192,1024]{1,0:T(8,128)(2,1)S(1)}, bf16[192,1024]{1,0:T(8,128)(2,1)S(1)}, u32[]{:S(2)}, u32[]{:S(2)}) collective-permute-start(bf16[192,1024]{1,0:T(8,128)(2,1)S(1)} %multiply_convert_fusion.5.refs_19_), channel_id=1, source_target_pairs={{0,16},{16,0},{1,17},{17,1},{2,18},{18,2},{3,19},{19,3},{4,20},{20... | collective-permute-start | bytes 1179656 | tf_op jit(solution)/shard_map/ppermute | solution.py:1100
  365.1 4.4 copy-start.2
  365.1 4.4 copy-start.48
  365.2 77.0 %collective-permute-start.9 = (bf16[192,2048]{1,0:T(8,128)(2,1)S(1)}, bf16[192,2048]{1,0:T(8,128)(2,1)}, u32[]{:S(2)}, u32[]{:S(2)}) collective-permute-start(bf16[192,2048]{1,0:T(8,128)(2,1)S(1)} %get-tuple-element.133.refs_17_), channel_id=1, source_target_pairs={{0,16},{16,0},{1,17},{17,1},{2,18},{18,2},{3,19},{19,3},{4,20},{20... | collective-permute-start | bytes 2359304 | tf_op jit(solution)/shard_map/ppermute | solution.py:1100
  369.5 4.6 slice-start.4
  369.7 28.7 %copy-start.14 = (bf16[192,1024]{1,0:T(8,128)(2,1)}, bf16[192,1024]{1,0:T(8,128)(2,1)S(1)}, u32[]{:S(2)}) copy-start(bf16[192,1024]{1,0:T(8,128)(2,1)S(1)} %multiply_convert_fusion.4.refs_18_) | copy-start | bytes 1179652
  369.7 4.7 slice-start.5
  382.8 11.2 %copy-start.23 = (bf16[192,3072]{1,0:T(8,128)(2,1)}, bf16[192,3072]{1,0:T(8,128)(2,1)S(1)}, u32[]{:S(2)}) copy-start(bf16[192,3072]{1,0:T(8,128)(2,1)S(1)} %get-tuple-element.219.refs_27_) | copy-start | bytes 3538948
  382.8 11.2 %slice-start = ((s8[6291456]{0:T(1024)(128)(4,1)}), s8[4194304]{0:T(1024)(128)(4,1)S(1)}, s32[]{:S(2)}) async-start(s8[6291456]{0:T(1024)(128)(4,1)} %bitcast.124), calls=%async_computation | async-start | bytes 8388608
  386.8 7.3 %slice-start.1 = ((s8[6291456]{0:T(1024)(128)(4,1)}), s8[2097152]{0:T(1024)(128)(4,1)S(1)}, s32[]{:S(2)}) async-start(s8[6291456]{0:T(1024)(128)(4,1)} %bitcast.124), calls=%async_computation.1 | async-start | bytes 4194304
  392.2 49.0 %collective-permute-start.5 = (bf16[192,1024]{1,0:T(8,128)(2,1)}, bf16[192,1024]{1,0:T(8,128)(2,1)S(1)}, u32[]{:S(2)}, u32[]{:S(2)}) collective-permute-start(bf16[192,1024]{1,0:T(8,128)(2,1)} %fusion.10), channel_id=1, source_target_pairs={{4,2},{2,4},{0,0},{6,6},{5,3},{3,5},{1,1},{7,7},{12,10},{10,12},{8... | collective-permute-start | bytes 1179656 | tf_op jit(solution)/shard_map/ppermute | solution.py:1311
  398.4 43.7 %collective-permute-start.10 = (bf16[192,1024]{1,0:T(8,128)(2,1)S(1)}, bf16[192,1024]{1,0:T(8,128)(2,1)S(1)}, u32[]{:S(2)}, u32[]{:S(2)}) collective-permute-start(bf16[192,1024]{1,0:T(8,128)(2,1)S(1)} %multiply_convert_fusion.4.refs_18_), channel_id=1, source_target_pairs={{0,16},{16,0},{1,17},{17,1},{2,18},{18,2},{3,19},{19,3},{4,20},{20... | collective-permute-start | bytes 1179656 | tf_op jit(solution)/shard_map/ppermute | solution.py:1100
  399.5 61.8 %collective-permute-start.11 = (bf16[192,3072]{1,0:T(8,128)(2,1)}, bf16[192,3072]{1,0:T(8,128)(2,1)}, u32[]{:S(2)}, u32[]{:S(2)}) collective-permute-start(bf16[192,3072]{1,0:T(8,128)(2,1)} %get-tuple-element.221.refs_16_), channel_id=1, source_target_pairs={{0,16},{16,0},{1,17},{17,1},{2,18},{18,2},{3,19},{19,3},{4,20},{20... | collective-permute-start | bytes 3538952 | tf_op jit(solution)/shard_map/ppermute | solution.py:1100
  438.2 4.0 copy-start.3
  438.2 4.0 copy-start.12
  444.1 7.7 %slice-start.2 = ((s8[6291456]{0:T(1024)(128)(4,1)}), s8[4194304]{0:T(1024)(128)(4,1)S(1)}, s32[]{:S(2)}) async-start(s8[6291456]{0:T(1024)(128)(4,1)} %bitcast.126), calls=%async_computation.2 | async-start | bytes 8388608
  444.4 7.4 %copy-start.35 = (bf16[192,1024]{1,0:T(8,128)(2,1)}, bf16[192,1024]{1,0:T(8,128)(2,1)S(1)}, u32[]{:S(2)}) copy-start(bf16[192,1024]{1,0:T(8,128)(2,1)S(1)} %get-tuple-element.213.refs_8_) | copy-start | bytes 1179652
  444.4 47.2 %collective-permute-start.13 = (bf16[192,1024]{1,0:T(8,128)(2,1)S(1)}, bf16[192,1024]{1,0:T(8,128)(2,1)S(1)}, u32[]{:S(2)}, u32[]{:S(2)}) collective-permute-start(bf16[192,1024]{1,0:T(8,128)(2,1)S(1)} %get-tuple-element.213.refs_8_), channel_id=1, source_target_pairs={{0,16},{16,0},{1,17},{17,1},{2,18},{18,2},{3,19},{19,3},{4,20},{20... | collective-permute-start | bytes 1179656 | tf_op jit(solution)/shard_map/ppermute | solution.py:1100
  445.9 5.9 slice-start.3
  454.1 5.7 copy-start.10
  461.4 30.3 %copy-start.18 = (bf16[1024,1024]{1,0:T(8,128)(2,1)S(1)}, bf16[1024,1024]{1,0:T(8,128)(2,1)}, u32[]{:S(2)}) copy-start(bf16[1024,1024]{1,0:T(8,128)(2,1)} %get-tuple-element.120) | copy-start | bytes 6291460
  497.3 208.8 %collective-permute-start.14 = (bf16[192,1024]{1,0:T(8,128)(2,1)S(1)}, bf16[192,1024]{1,0:T(8,128)(2,1)S(1)}, u32[]{:S(2)}, u32[]{:S(2)}) collective-permute-start(bf16[192,1024]{1,0:T(8,128)(2,1)S(1)} %fusion.19), channel_id=1, source_target_pairs={{4,2},{2,4},{0,0},{6,6},{5,3},{3,5},{1,1},{7,7},{12,10},{10,12},{8... | collective-permute-start | bytes 1179656 | tf_op jit(solution)/shard_map/ppermute | solution.py:1311
  498.6 207.5 %copy-start.46 = (bf16[192,1024]{1,0:T(8,128)(2,1)S(1)}, bf16[192,1024]{1,0:T(8,128)(2,1)}, u32[]{:S(2)}) copy-start(bf16[192,1024]{1,0:T(8,128)(2,1)} %copy-done.45) | copy-start | bytes 1179652
  703.9 4.6 copy-start.44
  (36 other events, 101.6 us)

commit v5 on v4

--- a/solution.py
+++ b/solution.py
@@ -23,16 +23,236 @@
 MESH = pl.DeviceIdType.MESH
 
 
-def gather_kernel(shapes, nx, nz, *refs):
-    count = len(shapes)
-    shards, wholes = refs[:count], refs[count : 2 * count]
-    own_sem, z_sem, x_sem, y_sem, core_sem, out_sem = refs[2 * count :]
+CHUNK_HEADS = 2
+CHUNKS = KEYVALUE_HEADS // CHUNK_HEADS
+CHUNK = CHUNK_HEADS * HEAD_SIZE
+GROUP = QUERY_HEADS // KEYVALUE_HEADS
+SCORE_SCALE = 1.0 / math.sqrt(HEAD_SIZE)
+
+
+def group_place(m):
+    y, shard, z = lax.axis_index("rep"), lax.axis_index("shard"), lax.axis_index("ctx")
+    core, zz = lax.rem(shard, 2), lax.rem(z, m)
+    to_core = (y, shard + 1 - 2 * core, z)
+
+    def to_line(step):
+        return (y, shard, z + step)
+
+    return core, zz, to_core, to_line
+
+
+def greet(m, zz, to_core, to_line):
+    barrier = pltpu.get_barrier_semaphore()
+    pl.semaphore_signal(barrier, inc=1, device_id=to_core, device_id_type=MESH)
+    for here, there in ((zz > 0, to_line(-1)), (zz < m - 1, to_line(1))):
+
+        @pl.when(here)
+        def _():
+            pl.semaphore_signal(barrier, inc=1, device_id=there, device_id_type=MESH)
+
+    pl.semaphore_wait(barrier, 1 + (zz > 0).astype(jnp.int32) + (zz < m - 1).astype(jnp.int32))
+
+
+def remote(src, dst, send_sem, recv_sem, device):
+    return pltpu.make_async_remote_copy(
+        src_ref=src, dst_ref=dst, send_sem=send_sem, recv_sem=recv_sem, device_id=device, device_id_type=MESH
+    )
+
+
+def head_prepare(v, gain, cosine, sine):
+    v = v * lax.rsqrt(jnp.mean(v * v, axis=-1, keepdims=True) + NORM_EPS) * gain
+    return v * cosine + pltpu.roll(v, HEAD_SIZE // 2, 1) * sine
+
+
+def head_prepare_back(grad, v, gain, cosine, sine):
+    grad = grad * cosine + pltpu.roll(grad * sine, HEAD_SIZE // 2, 1)
+    r = lax.rsqrt(jnp.mean(v * v, axis=-1, keepdims=True) + NORM_EPS)
+    unit = v * r
+    by_gain = jnp.sum(grad * unit, axis=0, keepdims=True)
+    grad = grad * gain
+    return r * (grad - unit * jnp.mean(grad * unit, axis=-1, keepdims=True)), by_gain
+
+
+def attend_back_kernel(m, q, kv, d_att, att, lse, qp, kp, q_gain, k_gain, cosine, sine, place_q, segment_k, dq_low, dk_low, dv_low, gains, partial, core_in, up_in, down_in, core_sem, up_sem, down_sem):
+    tokens, length = q.shape[0], kv.shape[0]
+    core, zz, to_core, to_line = group_place(m)
+    greet(m, zz, to_core, to_line)
+    cos, sin = cosine[...], sine[...]
+    segment_q = place_q[:, 0:1]
+    index_q = place_q[:, 1:2]
+    index_k = lax.broadcasted_iota(jnp.int32, (tokens, length), 1)
+    allowed = (segment_q == segment_k[...]) & (index_q >= index_k)
+    lane = lax.broadcasted_iota(jnp.int32, (tokens, HEAD_SIZE), 1)
+    gains[...] = jnp.zeros_like(gains)
+    over_rows = (((0,), (0,)), ((), ()))
+    over_columns = (((1,), (1,)), ((), ()))
+
+    def core_copy(j):
+        return remote(partial.at[j, 1 - core], core_in.at[j], core_sem.at[0, j], core_sem.at[1, j], to_core)
+
+    def line_copy(j, up, here):
+        low, high = (here + 1, m) if up else (0, here)
+        into, sems = (up_in, up_sem) if up else (down_in, down_sem)
+        return remote(
+            partial.at[j, core, pl.ds(low, high - low)],
+            into.at[j, pl.ds(low - (1 if up else 0), high - low)],
+            sems.at[0, j],
+            sems.at[1, j],
+            to_line(1 if up else -1),
+        )
+
+    def add(j, place, value):
+        partial[j, core, place] = (partial[j, core, place].astype(jnp.float32) + value.astype(jnp.float32)).astype(partial.dtype)
+
+    def compute(j):
+        for n in range(CHUNK_HEADS):
+            keys = kv[:, pl.ds(pl.multiple_of(j * 2 * CHUNK + n * HEAD_SIZE, 128), HEAD_SIZE)]
+            values = kv[:, pl.ds(pl.multiple_of(j * 2 * CHUNK + CHUNK + n * HEAD_SIZE, 128), HEAD_SIZE)]
+            dk = dv = None
+            for g in range(GROUP):
+                h = (j * CHUNK_HEADS + n) * GROUP + g
+                at = pl.ds(pl.multiple_of(h * HEAD_SIZE, 128), HEAD_SIZE)
+                queries, grad = q[:, at], d_att[:, at]
+                total = jnp.sum(jnp.where(lane == h, lse[...], 0.0), axis=-1, keepdims=True)
+                delta = jnp.sum(grad.astype(jnp.float32) * att[:, at], axis=-1, keepdims=True)
+                s = lax.dot_general(queries, keys, over_columns, preferred_element_type=jnp.float32)
+                p = jnp.exp(jnp.where(allowed, s * SCORE_SCALE, VERY_NEGATIVE) - total)
+                dp = lax.dot_general(grad, values, over_columns, preferred_element_type=jnp.float32)
+                ds = (p * (dp - delta)).astype(queries.dtype)
+                dq = jnp.dot(ds, keys, preferred_element_type=jnp.float32) * SCORE_SCALE
+                here_k = lax.dot_general(ds, queries, over_rows, preferred_element_type=jnp.float32)
+                here_v = lax.dot_general(p.astype(grad.dtype), grad, over_rows, preferred_element_type=jnp.float32)
+                dk = here_k if dk is None else dk + here_k
+                dv = here_v if dv is None else dv + here_v
+                by_head, by_gain = head_prepare_back(dq, qp[:, at], q_gain[...], cos, sin)
+                dq_low[:, at] = by_head.astype(dq_low.dtype)
+                gains[0:1] += by_gain
+            first = n * HEAD_SIZE
+            partial[j, :, :, :, first : first + HEAD_SIZE] = (dk * SCORE_SCALE).astype(partial.dtype).reshape(2, m, tokens, HEAD_SIZE)
+            first += CHUNK
+            partial[j, :, :, :, first : first + HEAD_SIZE] = dv.astype(partial.dtype).reshape(2, m, tokens, HEAD_SIZE)
+        core_copy(j).start()
+
+    def take_core(j):
+        core_copy(j).wait_recv()
+        for place in range(m):
+            add(j, place, core_in[j, place])
+
+    def hop(j, h):
+        for up in (True, False):
+            here = h if up else m - 1 - h
+
+            @pl.when(zz == here)
+            def _():
+                if h > 0:
+                    line_copy(j, up, here - 1 if up else here + 1).wait_recv()
+                    into = up_in if up else down_in
+                    for place in range(here, m) if up else range(here + 1):
+                        add(j, place, into[j, place - (1 if up else 0)])
+                if h < m - 1:
+                    line_copy(j, up, here).start()
+
+    def finish(j):
+        for n in range(CHUNK_HEADS):
+            at = pl.ds(pl.multiple_of((j * CHUNK_HEADS + n) * HEAD_SIZE, 128), HEAD_SIZE)
+            grad = partial[j, core, zz, :, n * HEAD_SIZE : (n + 1) * HEAD_SIZE].astype(jnp.float32)
+            by_head, by_gain = head_prepare_back(grad, kp[:, at], k_gain[...], cos, sin)
+            dk_low[:, at] = by_head.astype(dk_low.dtype)
+            gains[1:2] += by_gain
+        at = pl.ds(pl.multiple_of(j * CHUNK, 128), CHUNK)
+        dv_low[:, at] = partial[j, core, zz, :, CHUNK:]
+        core_copy(j).wait_send()
+        for here in range(m):
+
+            @pl.when(zz == here)
+            def _():
+                if here < m - 1:
+                    line_copy(j, True, here).wait_send()
+                if here > 0:
+                    line_copy(j, False, here).wait_send()
+
+    plan = [[compute], [take_core, functools.partial(hop, h=0)]]
+    for h in range(1, m):
+        plan.append([functools.partial(hop, h=h)])
+    plan[-1].append(finish)
+
+    def tick(t, carry):
+        for depth in [*range(1, len(plan)), 0]:
+            j = t - depth
+
+            @pl.when((j >= 0) & (j < CHUNKS))
+            def _():
+                for stage in plan[depth]:
+                    stage(j)
+
+        return carry
+
+    lax.fori_loop(0, CHUNKS + len(plan) - 1, tick, 0)
+
+
+def attend_back(m, q, kv, d_att, att, lse, qp, kp, q_gain, k_gain, cosine, sine, place_q, segment_k, collective_id):
+    tokens = q.shape[0]
+    low = jnp.bfloat16
+    dma = pltpu.SemaphoreType.DMA
+    vmem = pl.BlockSpec(memory_space=pltpu.VMEM)
+    return pl.pallas_call(
+        functools.partial(attend_back_kernel, m),
+        out_shape=[
+            jax.ShapeDtypeStruct((tokens, QD), low),
+            jax.ShapeDtypeStruct((tokens, KEY_FEATURES), low),
+            jax.ShapeDtypeStruct((tokens, KEY_FEATURES), low),
+            jax.ShapeDtypeStruct((8, HEAD_SIZE), jnp.float32),
+        ],
+        in_specs=[vmem] * 13,
+        out_specs=[vmem] * 4,
+        scratch_shapes=[
+            pltpu.VMEM((CHUNKS, 2, m, tokens, 2 * CHUNK), low),
+            pltpu.VMEM((CHUNKS, m, tokens, 2 * CHUNK), low),
+            pltpu.VMEM((CHUNKS, max(m - 1, 1), tokens, 2 * CHUNK), low),
+            pltpu.VMEM((CHUNKS, max(m - 1, 1), tokens, 2 * CHUNK), low),
+            dma((2, CHUNKS)),
+            dma((2, CHUNKS)),
+            dma((2, CHUNKS)),
+        ],
+        compiler_params=pltpu.CompilerParams(
+            collective_id=collective_id, has_side_effects=True, vmem_limit_bytes=48 * 1024 * 1024
+        ),
+    )(q, kv, d_att, att, lse, qp, kp, q_gain, k_gain, cosine, sine, place_q, segment_k)
+
+
+WIDE_TILE, NARROW_TILE = 512, 256
+
+
+def unit_rms(values):
+    return values * lax.rsqrt(jnp.mean(values * values, axis=-1, keepdims=True) + NORM_EPS)
+
+
+def forward_kernel(chunks, nx, nz, *refs):
+    count = len(chunks)
+    weights = 7
+    gain_shard, shards, refs = refs[0], refs[1 : 1 + weights], refs[1 + weights :]
+    tokens_here, cosine, sine, place_q, segment_k, refs = *refs[:5], refs[5:]
+    wholes, refs = refs[:count], refs[count:]
+    gains_out, tokens_out, hidden_out, last_out, refs = *refs[:4], refs[4:]
+    saved_out, refs = [refs[n * SAVED : (n + 1) * SAVED] for n in range(LAYERS)], refs[LAYERS * SAVED :]
+    own_sem, z_sem, x_sem, y_sem, core_sem, out_sem, refs = *refs[:6], refs[6:]
+    gain_all, gains, low_tokens, h, normed, qp, kp, v, q, kv, att, att_low, lse, h_mid, n2, gate, up, act, last, refs = (
+        *refs[:19],
+        refs[19:],
+    )
+    wide_buf, output_buf, down_buf, refs = *refs[:3], refs[3:]
+    tile_sem, save_sem, misc_sem, kv_core_sem, kv_line_sem, kv_core_out, kv_line_out = refs
+    tokens, length = q.shape[0], kv.shape[1]
+    m = nz // 2
     y = lax.axis_index("rep")
     shard = lax.axis_index("shard")
     z = lax.axis_index("ctx")
     core, x = lax.rem(shard, 2), lax.div(shard, 2)
     to_core = (y, x * 2 + 1 - core, z)
     to_y = (1 - y, shard, z)
+    upper = z >= m
+    moves = ((core == 0) & upper) | ((core == 1) & (z < m))
+    to_swap = (y, x * 2 + 1 - core, jnp.where(upper, z - m, z + m))
 
     def to_x(step):
         return (y, shard + 2 * step, z)
@@ -40,50 +260,45 @@
     def to_z(step):
         return (y, shard, z + step)
 
+    def own_shard(k):
+        weight, layer = chunks[k][:2]
+        return gain_shard if weight < 0 else shards[weight].at[layer]
+
     def rows_of(k, xs, zs, start, size, of_core=core):
-        rows = shapes[k][0]
+        rows = chunks[k][2]
         first = ((xs * 2 + of_core) * nz + zs) * rows + start
         return wholes[k].at[pl.ds(pl.multiple_of(first, 16), size)]
 
     def inplane(k):
-        rows, _, near = shapes[k]
+        rows, near = chunks[k][2:]
         return y * (rows - near), near
-
-    def send(src, dst, send_sem, recv_sem, device):
-        pltpu.make_async_remote_copy(
-            src_ref=src,
-            dst_ref=dst,
-            send_sem=send_sem,
-            recv_sem=recv_sem,
-            device_id=device,
-            device_id_type=MESH,
-        ).start()
 
     def arrived(ref, sem):
         pltpu.make_async_copy(ref, ref, sem).wait()
 
     def pass_z(k, src, zs, step, kind):
         start, size = inplane(k)
-        send(src, rows_of(k, x, zs, start, size), out_sem.at[k, kind], z_sem.at[k, zs], to_z(step))
+        remote(src, rows_of(k, x, zs, start, size), out_sem.at[k, kind], z_sem.at[k, zs], to_z(step)).start()
 
     def pass_x(k, src, xs, zs, step, kind):
         start, size = inplane(k)
-        send(src, rows_of(k, xs, zs, start, size), out_sem.at[k, kind], x_sem.at[k, xs * nz + zs], to_x(step))
+        into = rows_of(k, xs, zs, start, size)
+        remote(src, into, out_sem.at[k, kind], x_sem.at[k, xs * nz + zs], to_x(step)).start()
 
     def pass_y(k, xs, zs):
-        rows, _, near = shapes[k]
+        rows, near = chunks[k][2:]
         if rows > near:
             part = rows_of(k, xs, zs, y * near, rows - near)
-            send(part, part, out_sem.at[k, 4], y_sem.at[k, xs * nz + zs], to_y)
+            remote(part, part, out_sem.at[k, 4], y_sem.at[k, xs * nz + zs], to_y).start()
 
     def pass_core(k, xs, zs, start, size):
         part = rows_of(k, xs, zs, start, size)
-        send(part, part, out_sem.at[k, 5], core_sem.at[k], to_core)
+        remote(part, part, out_sem.at[k, 5], core_sem.at[k], to_core).start()
 
     def stage_own(k):
-        rows, _, near = shapes[k]
+        rows = chunks[k][2]
         start, size = inplane(k)
-        part = shards[k].at[pl.ds(pl.multiple_of(start, 16), size)]
+        part = own_shard(k).at[pl.ds(pl.multiple_of(start, 16), size)]
 
         @pl.when(z < nz - 1)
         def _():
@@ -101,8 +316,8 @@
         def _():
             pass_x(k, part, x, z, -1, 3)
 
-        send(shards[k], rows_of(k, x, z, 0, rows), out_sem.at[k, 5], core_sem.at[k], to_core)
-        pltpu.make_async_copy(shards[k], rows_of(k, x, z, 0, rows), own_sem.at[k]).start()
+        remote(own_shard(k), rows_of(k, x, z, 0, rows), out_sem.at[k, 5], core_sem.at[k], to_core).start()
+        pltpu.make_async_copy(own_shard(k), rows_of(k, x, z, 0, rows), own_sem.at[k]).start()
 
     def stage_z(k, d):
         start, size = inplane(k)
@@ -152,7 +367,7 @@
                 lax.fori_loop(0, nz, body, 0)
 
     def stage_y(k):
-        rows, _, near = shapes[k]
+        rows, near = chunks[k][2:]
         if rows > near:
 
             def body(i, carry):
@@ -171,10 +386,13 @@
     def first_rows(k, size):
         return wholes[k].at[pl.ds(0, size)]
 
-    def stage_end(k):
-        rows, _, near = shapes[k]
+    def complete(k):
+        rows = chunks[k][2]
         arrived(first_rows(k, nx * nz * rows), core_sem.at[k])
         arrived(first_rows(k, rows), own_sem.at[k])
+
+    def sent(k):
+        rows, near = chunks[k][2:]
         for zz in range(nz):
 
             @pl.when(z == zz)
@@ -195,58 +413,393 @@
 
         if rows > near:
             arrived(first_rows(k, (nx * nz - 1) * (rows - near)), out_sem.at[k, 4])
-            arrived(
-                first_rows(k, nx * nz * rows), out_sem.at[k, 5]
-            )
-        else:
-            arrived(first_rows(k, nx * nz * rows), out_sem.at[k, 5])
+        arrived(first_rows(k, nx * nz * rows), out_sem.at[k, 5])
 
     barrier = pltpu.get_barrier_semaphore()
     pl.semaphore_signal(barrier, inc=1, device_id=to_core, device_id_type=MESH)
     pl.semaphore_signal(barrier, inc=1, device_id=to_y, device_id_type=MESH)
-    for here, there in ((z > 0, to_z(-1)), (z < nz - 1, to_z(1)), (x > 0, to_x(-1)), (x < nx - 1, to_x(1))):
+    meets = ((z > 0, to_z(-1)), (z < nz - 1, to_z(1)), (x > 0, to_x(-1)), (x < nx - 1, to_x(1)), (moves, to_swap))
+    greeted = 2
+    for here, there in meets:
 
         @pl.when(here)
         def _():
             pl.semaphore_signal(barrier, inc=1, device_id=there, device_id_type=MESH)
 
-    greeted = 2 + (z > 0).astype(jnp.int32) + (z < nz - 1).astype(jnp.int32)
-    greeted = greeted + (x > 0).astype(jnp.int32) + (x < nx - 1).astype(jnp.int32)
+        greeted = greeted + here.astype(jnp.int32)
     pl.semaphore_wait(barrier, greeted)
+
+    def swap_copy():
+        return remote(tokens_here, low_tokens, misc_sem.at[0], misc_sem.at[1], to_swap)
+
+    def stay_copy():
+        return pltpu.make_async_copy(tokens_here, low_tokens, misc_sem.at[1])
+
+    @pl.when(moves)
+    def _():
+        swap_copy().start()
+
+    @pl.when(~moves)
+    def _():
+        stay_copy().start()
+
+    def begin():
+        @pl.when(moves)
+        def _():
+            swap_copy().wait()
+
+        @pl.when(~moves)
+        def _():
+            stay_copy().wait()
+
+        h[...] = low_tokens[...].astype(jnp.float32)
+        pltpu.make_async_copy(low_tokens, tokens_out, misc_sem.at[2]).start()
+
+    def read_gains():
+        complete(0)
+        copy = pltpu.make_async_copy(wholes[0], gain_all, misc_sem.at[3])
+        copy.start()
+        copy.wait()
+        gains[...] = jnp.zeros_like(gains)
+
+        def body(n, carry):
+            gains[...] += gain_all[pl.ds(pl.multiple_of(n * 16, 16), 16)].astype(jnp.float32)
+            return carry
+
+        lax.fori_loop(0, 2 * nx * nz, body, 0)
+        pltpu.make_async_copy(gains, gains_out, misc_sem.at[4]).start()
+
+    zz = lax.rem(z, m)
+
+    def kv_part(layer, j, source, of_core=core):
+        rows = pl.multiple_of((source + of_core * m) * tokens, 16)
+        at = j * 2 * CHUNK if isinstance(j, int) else pl.multiple_of(j * 2 * CHUNK, 128)
+        return kv.at[layer, pl.ds(rows, tokens), pl.ds(at, 2 * CHUNK)]
+
+    def kv_core(layer, j, source, of_core=core):
+        ref = kv_part(layer, j, source, of_core)
+        return remote(ref, ref, kv_core_out.at[layer, j, source], kv_core_sem.at[layer, j, source], to_core)
+
+    def kv_line(layer, j, source, step):
+        ref = kv_part(layer, j, source)
+        send_sem = kv_line_out.at[0 if step > 0 else 1, layer, j, source]
+        return remote(ref, ref, send_sem, kv_line_sem.at[layer, j, source], to_z(step))
+
+    def onward(layer, j, source, step, do):
+        @pl.when((zz + step >= 0) & (zz + step < m))
+        def _():
+            do(kv_line(layer, j, source, step))
+
+    start, ended = lambda copy: copy.start(), lambda copy: copy.wait_send()
+
+    def kv_left(layer):
+        for j in range(CHUNKS):
+            for source in range(m):
+                kv_core(layer, j, source).wait_send()
+            for d in range(m):
+                for step in (1, -1):
+                    source = zz - step * d
+
+                    @pl.when((source >= 0) & (source < m))
+                    def _():
+                        onward(layer, j, source, step, ended)
+
+    saves = (normed, qp, kp, q, None, att, att_low, lse, h_mid, n2, gate, up, act)
+
+    def save_copy(layer, n):
+        source = kv.at[layer] if saves[n] is None else saves[n]
+        return pltpu.make_async_copy(source, saved_out[layer][n], save_sem.at[layer, n])
+
+    def save(layer, *which):
+        for n in which:
+            save_copy(layer, n).start()
+
+    def reusable(layer, *which):
+        if layer > 0:
+            for n in which:
+                save_copy(layer - 1, n).wait()
+
+    def layer_tasks(layer):
+        chunk = {c[0]: k for k, c in enumerate(chunks) if c[1] == layer and c[0] >= 0}
+        row = lambda n, width=D: gains[n + layer : n + layer + 1, :width]
+        tasks = []
+
+        def streamed(weight, buf, base, sems, tile, use, tiles, lead=None):
+            k = chunk[weight]
+
+            def copy(i):
+                slot = base + i % 2
+                source = wholes[k].at[:, pl.ds(i * tile, tile)]
+                return pltpu.make_async_copy(source, buf.at[slot], tile_sem.at[sems + i % 2])
+
+            def first():
+                complete(k)
+                copy(0).start()
+
+            def one(i):
+                copy(i).wait()
+                if i + 1 < tiles:
+                    copy(i + 1).start()
+                use(i, buf.at[base + i % 2])
+
+            return first, [functools.partial(one, i) for i in range(tiles)], k
+
+        def put(k, *steps):
+            tasks.append((k, lambda: [step() for step in steps]))
+
+        def norm_first():
+            if layer == 0:
+                begin()
+                read_gains()
+            reusable(layer, 0)
+            normed[...] = (unit_rms(h[...]) * row(0)).astype(normed.dtype)
+            save(layer, 0)
+            if layer > 0:
+                pltpu.make_async_copy(h, hidden_out, misc_sem.at[5]).start()
+
+        def keys(i, w):
+            if i == 0:
+                reusable(layer, 2)
+            kp[:, i * WIDE_TILE : (i + 1) * WIDE_TILE] = jnp.dot(normed[...], w[...], preferred_element_type=jnp.float32)
+            if i == 1:
+                save(layer, 2)
+
+        def values(i, w):
+            term = jnp.dot(normed[...], w[...], preferred_element_type=jnp.float32)
+            v[:, i * WIDE_TILE : (i + 1) * WIDE_TILE] = term.astype(v.dtype)
+
+        def queries(i, w):
+            if i == 0:
+                reusable(layer, 1)
+            qp[:, i * WIDE_TILE : (i + 1) * WIDE_TILE] = jnp.dot(normed[...], w[...], preferred_element_type=jnp.float32)
+            if i == 3:
+                save(layer, 1)
+
+        cos = lambda: cosine[...]
+        sin = lambda: sine[...]
+        own_rows = pl.ds(pl.multiple_of((zz + core * m) * tokens, 16), tokens)
+
+        def send_keys(j):
+            for n in range(CHUNK_HEADS):
+                hd = j * CHUNK_HEADS + n
+                ready = head_prepare(kp[:, hd * HEAD_SIZE : (hd + 1) * HEAD_SIZE], row(6, HEAD_SIZE), cos(), sin())
+                first = j * 2 * CHUNK + n * HEAD_SIZE
+                kv[layer, own_rows, first : first + HEAD_SIZE] = ready.astype(kv.dtype)
+            kv[layer, own_rows, j * 2 * CHUNK + CHUNK : (j + 1) * 2 * CHUNK] = v[:, j * CHUNK : (j + 1) * CHUNK]
+            for step in (1, -1):
+                onward(layer, j, zz, step, start)
+            kv_core(layer, j, zz).start()
+
+        def prepare_queries(part):
+            if part == 0:
+                reusable(layer, 3)
+            for hd in range(part * 4, part * 4 + 4):
+                at = slice(hd * HEAD_SIZE, (hd + 1) * HEAD_SIZE)
+                q[:, at] = head_prepare(qp[:, at], row(4, HEAD_SIZE), cos(), sin()).astype(q.dtype)
+            if part == 3:
+                save(layer, 3)
+
+        def arrivals(j):
+            for d in range(1, m):
+                for step in (1, -1):
+                    source = zz - step * d
+
+                    @pl.when((source >= 0) & (source < m))
+                    def _():
+                        kv_line(layer, j, source, step).wait_recv()
+                        onward(layer, j, source, step, start)
+                        kv_core(layer, j, source).start()
+
+        def attend(j):
+            if j == 0:
+                reusable(layer, 5, 6, 7)
+                lse[...] = jnp.zeros_like(lse)
+            for source in range(m):
+                kv_core(layer, j, source, 1 - core).wait_recv()
+            index_k = lax.broadcasted_iota(jnp.int32, (tokens, length), 1)
+            allowed = (place_q[:, 0:1] == segment_k[...]) & (place_q[:, 1:2] >= index_k)
+            lane = lax.broadcasted_iota(jnp.int32, (tokens, HEAD_SIZE), 1)
+
+            def head(n, carry):
+                first = j * 2 * CHUNK + lax.div(n, GROUP) * HEAD_SIZE
+                their_keys = kv[layer, :, pl.ds(pl.multiple_of(first, 128), HEAD_SIZE)]
+                their_values = kv[layer, :, pl.ds(pl.multiple_of(first + CHUNK, 128), HEAD_SIZE)]
+                hd = j * CHUNK_HEADS * GROUP + n
+                at = pl.ds(pl.multiple_of(hd * HEAD_SIZE, 128), HEAD_SIZE)
+                s = lax.dot_general(q[:, at], their_keys, (((1,), (1,)), ((), ())), preferred_element_type=jnp.float32)
+                s = jnp.where(allowed, s * SCORE_SCALE, VERY_NEGATIVE)
+                top = jnp.max(s, axis=-1, keepdims=True)
+                p = jnp.exp(s - top)
+                total = jnp.sum(p, axis=-1, keepdims=True)
+                o = jnp.dot(p.astype(jnp.bfloat16), their_values, preferred_element_type=jnp.float32) / total
+                att[:, at] = o
+                att_low[:, at] = o.astype(att_low.dtype)
+                lse[...] = jnp.where(lane == hd, top + jnp.log(total), lse[...])
+                return carry
+
+            lax.fori_loop(0, CHUNK_HEADS * GROUP, head, 0)
+            if j == CHUNKS - 1:
+                save(layer, 4, 5, 6, 7)
+
+        def outputs(i, w):
+            if i == 0:
+                reusable(layer, 8)
+            at = slice(i * NARROW_TILE, (i + 1) * NARROW_TILE)
+            h_mid[:, at] = h[:, at] + jnp.dot(att_low[...], w[...], preferred_element_type=jnp.float32)
+            if i == 3:
+                save(layer, 8)
+
+        def norm_second():
+            reusable(layer, 9)
+            n2[...] = (unit_rms(h_mid[...]) * row(2)).astype(n2.dtype)
+            save(layer, 9)
+
+        def gates(i, w):
+            if i == 0:
+                reusable(layer, 10, 12)
+            gate[:, i * WIDE_TILE : (i + 1) * WIDE_TILE] = jnp.dot(n2[...], w[...], preferred_element_type=jnp.float32)
+
+        def ups(i, w):
+            if i == 0:
+                reusable(layer, 11)
+            at = slice(i * WIDE_TILE, (i + 1) * WIDE_TILE)
+            term = jnp.dot(n2[...], w[...], preferred_element_type=jnp.float32)
+            up[:, at] = term
+            opened = gate[:, at]
+            act[:, at] = (opened / (1.0 + jnp.exp(-opened)) * term).astype(act.dtype)
+            if i == 5:
+                save(layer, 10, 11, 12)
+
+        def downs(i, w):
+            if layer > 0 and i == 0:
+                pltpu.make_async_copy(h, hidden_out, misc_sem.at[5]).wait()
+            at = slice(i * NARROW_TILE, (i + 1) * NARROW_TILE)
+            h[:, at] = h_mid[:, at] + jnp.dot(act[...], w[...], preferred_element_type=jnp.float32)
+
+        first_k, key_tiles, kk = streamed(1, wide_buf, 0, 0, WIDE_TILE, keys, 2)
+        first_v, value_tiles, kv_chunk = streamed(2, wide_buf, 2, 2, WIDE_TILE, values, 2)
+        first_q, query_tiles, kq = streamed(0, wide_buf, 0, 0, WIDE_TILE, queries, 4)
+        first_o, output_tiles, ko = streamed(3, output_buf, 0, 4, NARROW_TILE, outputs, 4)
+        first_g, gate_tiles, kg = streamed(4, wide_buf, 0, 0, WIDE_TILE, gates, 6)
+        first_u, up_tiles, ku = streamed(5, wide_buf, 2, 2, WIDE_TILE, ups, 6)
+        first_d, down_tiles, kd = streamed(6, down_buf, 0, 6, NARROW_TILE, downs, 4)
+        kqkv = max(kk, kv_chunk, kq)
+        put(kqkv, norm_first, first_k, first_v)
+        put(kqkv, *key_tiles)
+        put(kqkv, first_q, *value_tiles)
+        put(kqkv, functools.partial(send_keys, 0), functools.partial(send_keys, 1))
+        put(kqkv, functools.partial(send_keys, 2), functools.partial(send_keys, 3))
+        put(kqkv, *query_tiles[:2])
+        put(kqkv, *query_tiles[2:])
+        for part in range(4):
+            put(kqkv, functools.partial(prepare_queries, part))
+        put(kqkv, functools.partial(arrivals, 0))
+        for j in range(CHUNKS):
+            if j + 1 < CHUNKS:
+                put(kqkv, functools.partial(arrivals, j + 1))
+            if j + 1 == CHUNKS:
+                put(kqkv)
+            put(kqkv, functools.partial(attend, j))
+        put(ko, first_o)
+        put(ko, *output_tiles[:2])
+        put(ko, *output_tiles[2:])
+        put(kg, norm_second, first_g)
+        for n in range(3):
+            put(kg, *gate_tiles[2 * n : 2 * n + 2])
+        put(ku, first_u)
+        for n in range(3):
+            put(ku, *up_tiles[2 * n : 2 * n + 2])
+        put(kd, first_d)
+        put(kd, *down_tiles[:2])
+        put(kd, *down_tiles[2:])
+        return tasks
 
     stages = [stage_own]
     stages += [functools.partial(stage_z, d=d) for d in range(1, nz)]
     stages += [functools.partial(stage_x, d=d) for d in range(1, nx)]
     stages += [stage_y]
+    tasks = [task for layer in range(LAYERS) for task in layer_tasks(layer)]
     for tick in range(count + len(stages) - 1):
         for depth, stage in enumerate(stages):
             k = tick - depth
             if 0 <= k < count:
                 stage(k)
+            if tasks and tasks[0][0] + len(stages) <= tick:
+                tasks.pop(0)[1]()
+    for _, task in tasks:
+        task()
+    last[...] = h[...].astype(last.dtype)
+    pltpu.make_async_copy(last, last_out, misc_sem.at[6]).start()
     for k in range(count):
-        stage_end(k)
-
-
-def gather_weights(shards, nears, nx, nz, collective_id):
-    count = len(shards)
-    shapes = tuple((a.shape[0], a.shape[1], near) for a, near in zip(shards, nears))
-    return pl.pallas_call(
-        functools.partial(gather_kernel, shapes, nx, nz),
-        out_shape=[
-            jax.ShapeDtypeStruct((a.shape[0] * 2 * nx * nz, a.shape[1]), a.dtype) for a in shards
+        sent(k)
+    for layer in range(LAYERS):
+        kv_left(layer)
+    for n in range(SAVED):
+        save_copy(LAYERS - 1, n).wait()
+    save_copy(0, 4).wait()
+    pltpu.make_async_copy(low_tokens, tokens_out, misc_sem.at[2]).wait()
+    pltpu.make_async_copy(gains, gains_out, misc_sem.at[4]).wait()
+    pltpu.make_async_copy(last, last_out, misc_sem.at[6]).wait()
+
+
+SAVED = 13
+
+
+def forward(gain_shard, shards, tokens, tables, chunks, nx, nz, collective_id):
+    count, m = len(chunks), nz // 2
+    rows = tokens.shape[0]
+    low, wide = jnp.bfloat16, jnp.float32
+    dma, vmem = pltpu.SemaphoreType.DMA, pltpu.VMEM
+    anywhere = pl.BlockSpec(memory_space=pl.ANY)
+    arrays = [gain_shard if c[0] < 0 else shards[c[0]] for c in chunks]
+    ff = shards[4].shape[-1]
+    kept = [((rows, D), low), ((rows, QD), wide), ((rows, KEY_FEATURES), wide), ((rows, QD), low)]
+    kept += [((2 * m * rows, 2 * KEY_FEATURES), low), ((rows, QD), wide), ((rows, QD), low), ((rows, HEAD_SIZE), wide)]
+    kept += [((rows, D), wide), ((rows, D), low), ((rows, ff), wide), ((rows, ff), wide), ((rows, ff), low)]
+    shape = jax.ShapeDtypeStruct
+    outs = pl.pallas_call(
+        functools.partial(forward_kernel, chunks, nx, nz),
+        out_shape=[shape((a.shape[-2] * 2 * nx * nz, a.shape[-1]), low) for a in arrays]
+        + [shape((16, D), wide), shape((rows, D), low), shape((rows, D), wide), shape((rows, D), low)]
+        + [shape(*k) for k in kept] * LAYERS,
+        in_specs=[anywhere] * (2 + len(shards)) + [pl.BlockSpec(memory_space=pltpu.VMEM)] * 4,
+        out_specs=[anywhere] * (count + 4 + SAVED * LAYERS),
+        scratch_shapes=[
+            dma((count,)),
+            dma((count, nz)),
+            dma((count, nx * nz)),
+            dma((count, nx * nz)),
+            dma((count,)),
+            dma((count, 6)),
+            vmem((16 * 2 * nx * nz, D), low),
+            vmem((16, D), wide),
+            vmem((rows, D), low),
+            vmem((rows, D), wide),
+            vmem(*kept[0]),
+            vmem(*kept[1]),
+            vmem(*kept[2]),
+            vmem((rows, KEY_FEATURES), low),
+            vmem(*kept[3]),
+            vmem((LAYERS, *kept[4][0]), low),
+            *[vmem(*k) for k in kept[5:]],
+            vmem((rows, D), low),
+            vmem((4, D, WIDE_TILE), low),
+            vmem((2, QD, NARROW_TILE), low),
+            vmem((2, ff, NARROW_TILE), low),
+            dma((8,)),
+            dma((LAYERS, SAVED)),
+            dma((7,)),
+            dma((LAYERS, CHUNKS, m)),
+            dma((LAYERS, CHUNKS, m)),
+            dma((LAYERS, CHUNKS, m)),
+            dma((2, LAYERS, CHUNKS, m)),
         ],
-        in_specs=[pl.BlockSpec(memory_space=pl.ANY)] * count,
-        out_specs=[pl.BlockSpec(memory_space=pl.ANY)] * count,
-        scratch_shapes=[
-            pltpu.SemaphoreType.DMA((count,)),
-            pltpu.SemaphoreType.DMA((count, nz)),
-            pltpu.SemaphoreType.DMA((count, nx * nz)),
-            pltpu.SemaphoreType.DMA((count, nx * nz)),
-            pltpu.SemaphoreType.DMA((count,)),
-            pltpu.SemaphoreType.DMA((count, 6)),
-        ],
-        compiler_params=pltpu.CompilerParams(collective_id=collective_id, has_side_effects=True),
-    )(*shards)
+        compiler_params=pltpu.CompilerParams(
+            collective_id=collective_id, has_side_effects=True, vmem_limit_bytes=56 * 1024 * 1024
+        ),
+    )(gain_shard, *shards, tokens, *tables)
+    wholes, outs = outs[:count], outs[count:]
+    return wholes, outs[:4], [outs[4 + n * SAVED : 4 + (n + 1) * SAVED] for n in range(LAYERS)]
 
 
 SLOTS = 4
@@ -727,332 +1280,6 @@
     )(*flat, gains)
 
 
-CHUNK_HEADS = 2
-CHUNKS = KEYVALUE_HEADS // CHUNK_HEADS
-CHUNK = CHUNK_HEADS * HEAD_SIZE
-GROUP = QUERY_HEADS // KEYVALUE_HEADS
-SCORE_SCALE = 1.0 / math.sqrt(HEAD_SIZE)
-
-
-def group_place(m):
-    y, shard, z = lax.axis_index("rep"), lax.axis_index("shard"), lax.axis_index("ctx")
-    core, zz = lax.rem(shard, 2), lax.rem(z, m)
-    to_core = (y, shard + 1 - 2 * core, z)
-
-    def to_line(step):
-        return (y, shard, z + step)
-
-    return core, zz, to_core, to_line
-
-
-def greet(m, zz, to_core, to_line):
-    barrier = pltpu.get_barrier_semaphore()
-    pl.semaphore_signal(barrier, inc=1, device_id=to_core, device_id_type=MESH)
-    for here, there in ((zz > 0, to_line(-1)), (zz < m - 1, to_line(1))):
-
-        @pl.when(here)
-        def _():
-            pl.semaphore_signal(barrier, inc=1, device_id=there, device_id_type=MESH)
-
-    pl.semaphore_wait(barrier, 1 + (zz > 0).astype(jnp.int32) + (zz < m - 1).astype(jnp.int32))
-
-
-def remote(src, dst, send_sem, recv_sem, device):
-    return pltpu.make_async_remote_copy(
-        src_ref=src, dst_ref=dst, send_sem=send_sem, recv_sem=recv_sem, device_id=device, device_id_type=MESH
-    )
-
-
-def head_prepare(v, gain, cosine, sine):
-    v = v * lax.rsqrt(jnp.mean(v * v, axis=-1, keepdims=True) + NORM_EPS) * gain
-    return v * cosine + pltpu.roll(v, HEAD_SIZE // 2, 1) * sine
-
-
-def head_prepare_back(grad, v, gain, cosine, sine):
-    grad = grad * cosine + pltpu.roll(grad * sine, HEAD_SIZE // 2, 1)
-    r = lax.rsqrt(jnp.mean(v * v, axis=-1, keepdims=True) + NORM_EPS)
-    unit = v * r
-    by_gain = jnp.sum(grad * unit, axis=0, keepdims=True)
-    grad = grad * gain
-    return r * (grad - unit * jnp.mean(grad * unit, axis=-1, keepdims=True)), by_gain
-
-
-def attend_kernel(m, qp, kp, v, q_gain, k_gain, cosine, sine, place_q, segment_k, q_out, kv, att, att_low, lse, core_sem, line_sem, core_out, line_out):
-    tokens, length = qp.shape[0], kv.shape[0]
-    core, zz, to_core, to_line = group_place(m)
-    greet(m, zz, to_core, to_line)
-    cos, sin = cosine[...], sine[...]
-
-    def part(j, source_zz, of_core=core):
-        rows = pl.multiple_of((source_zz + of_core * m) * tokens, 16)
-        return kv.at[pl.ds(rows, tokens), pl.ds(pl.multiple_of(j * 2 * CHUNK, 128), 2 * CHUNK)]
-
-    def core_copy(j, source_zz, of_core=core):
-        ref = part(j, source_zz, of_core)
-        return remote(ref, ref, core_out.at[j, source_zz], core_sem.at[j, source_zz], to_core)
-
-    def line_copy(j, source_zz, step):
-        ref = part(j, source_zz)
-        return remote(ref, ref, line_out.at[0 if step > 0 else 1, j, source_zz], line_sem.at[j, source_zz], to_line(step))
-
-    def onward(j, source_zz, step, do):
-        @pl.when((zz + step >= 0) & (zz + step < m))
-        def _():
-            do(line_copy(j, source_zz, step))
-
-    begin, ended = lambda copy: copy.start(), lambda copy: copy.wait_send()
-    own_rows = pl.ds(pl.multiple_of((zz + core * m) * tokens, 16), tokens)
-    for j in range(CHUNKS):
-        for n in range(CHUNK_HEADS):
-            h = j * CHUNK_HEADS + n
-            ready = head_prepare(kp[:, h * HEAD_SIZE : (h + 1) * HEAD_SIZE], k_gain[...], cos, sin)
-            kv[own_rows, j * 2 * CHUNK + n * HEAD_SIZE : j * 2 * CHUNK + (n + 1) * HEAD_SIZE] = ready.astype(kv.dtype)
-        kv[own_rows, j * 2 * CHUNK + CHUNK : (j + 1) * 2 * CHUNK] = v[:, j * CHUNK : (j + 1) * CHUNK]
-        for step in (1, -1):
-            onward(j, zz, step, begin)
-        core_copy(j, zz).start()
-    for h in range(QUERY_HEADS):
-        at = slice(h * HEAD_SIZE, (h + 1) * HEAD_SIZE)
-        q_out[:, at] = head_prepare(qp[:, at], q_gain[...], cos, sin).astype(q_out.dtype)
-
-    def arrivals(j):
-        for d in range(1, m):
-            for step in (1, -1):
-                source = zz - step * d
-
-                @pl.when((source >= 0) & (source < m))
-                def _():
-                    line_copy(j, source, step).wait_recv()
-                    onward(j, source, step, begin)
-                    core_copy(j, source).start()
-
-    segment_q = place_q[:, 0:1]
-    index_q = place_q[:, 1:2]
-    index_k = lax.broadcasted_iota(jnp.int32, (tokens, length), 1)
-    allowed = (segment_q == segment_k[...]) & (index_q >= index_k)
-    lane = lax.broadcasted_iota(jnp.int32, (tokens, HEAD_SIZE), 1)
-
-    def attend(j):
-        for source in range(m):
-            core_copy(j, source, 1 - core).wait_recv()
-        for n in range(CHUNK_HEADS):
-            keys = kv[:, pl.ds(pl.multiple_of(j * 2 * CHUNK + n * HEAD_SIZE, 128), HEAD_SIZE)]
-            values = kv[:, pl.ds(pl.multiple_of(j * 2 * CHUNK + CHUNK + n * HEAD_SIZE, 128), HEAD_SIZE)]
-            for g in range(GROUP):
-                h = (j * CHUNK_HEADS + n) * GROUP + g
-                at = pl.ds(pl.multiple_of(h * HEAD_SIZE, 128), HEAD_SIZE)
-                s = lax.dot_general(q_out[:, at], keys, (((1,), (1,)), ((), ())), preferred_element_type=jnp.float32)
-                s = jnp.where(allowed, s * SCORE_SCALE, VERY_NEGATIVE)
-                top = jnp.max(s, axis=-1, keepdims=True)
-                p = jnp.exp(s - top)
-                norm = jnp.sum(p, axis=-1, keepdims=True)
-                o = jnp.dot(p.astype(values.dtype), values, preferred_element_type=jnp.float32) / norm
-                att[:, at] = o
-                att_low[:, at] = o.astype(att_low.dtype)
-                lse[...] = jnp.where(lane == h, top + jnp.log(norm), lse[...])
-
-    lse[...] = jnp.zeros_like(lse)
-
-    def tick(t, carry):
-        @pl.when(t < CHUNKS)
-        def _():
-            arrivals(t)
-
-        @pl.when(t > 0)
-        def _():
-            attend(t - 1)
-
-        return carry
-
-    lax.fori_loop(0, CHUNKS + 1, tick, 0)
-
-    def leave(j, carry):
-        for source in range(m):
-            core_copy(j, source).wait_send()
-        for d in range(m):
-            for step in (1, -1):
-                source = zz - step * d
-
-                @pl.when((source >= 0) & (source < m))
-                def _():
-                    onward(j, source, step, ended)
-
-        return carry
-
-    lax.fori_loop(0, CHUNKS, leave, 0)
-
-
-def attend(m, qp, kp, v, q_gain, k_gain, cosine, sine, place_q, segment_k, collective_id):
-    tokens = qp.shape[0]
-    length = 2 * m * tokens
-    low = jnp.bfloat16
-    dma = pltpu.SemaphoreType.DMA
-    vmem = pl.BlockSpec(memory_space=pltpu.VMEM)
-    return pl.pallas_call(
-        functools.partial(attend_kernel, m),
-        out_shape=[
-            jax.ShapeDtypeStruct((tokens, QD), low),
-            jax.ShapeDtypeStruct((length, 2 * KEY_FEATURES), low),
-            jax.ShapeDtypeStruct((tokens, QD), jnp.float32),
-            jax.ShapeDtypeStruct((tokens, QD), low),
-            jax.ShapeDtypeStruct((tokens, HEAD_SIZE), jnp.float32),
-        ],
-        in_specs=[vmem] * 9,
-        out_specs=[vmem] * 5,
-        scratch_shapes=[dma((CHUNKS, m)), dma((CHUNKS, m)), dma((CHUNKS, m)), dma((2, CHUNKS, m))],
-        compiler_params=pltpu.CompilerParams(
-            collective_id=collective_id, has_side_effects=True, vmem_limit_bytes=48 * 1024 * 1024
-        ),
-    )(qp, kp, v, q_gain, k_gain, cosine, sine, place_q, segment_k)
-
-
-def attend_back_kernel(m, q, kv, d_att, att, lse, qp, kp, q_gain, k_gain, cosine, sine, place_q, segment_k, dq_low, dk_low, dv_low, gains, partial, core_in, up_in, down_in, core_sem, up_sem, down_sem):
-    tokens, length = q.shape[0], kv.shape[0]
-    core, zz, to_core, to_line = group_place(m)
-    greet(m, zz, to_core, to_line)
-    cos, sin = cosine[...], sine[...]
-    segment_q = place_q[:, 0:1]
-    index_q = place_q[:, 1:2]
-    index_k = lax.broadcasted_iota(jnp.int32, (tokens, length), 1)
-    allowed = (segment_q == segment_k[...]) & (index_q >= index_k)
-    lane = lax.broadcasted_iota(jnp.int32, (tokens, HEAD_SIZE), 1)
-    gains[...] = jnp.zeros_like(gains)
-    over_rows = (((0,), (0,)), ((), ()))
-    over_columns = (((1,), (1,)), ((), ()))
-
-    def core_copy(j):
-        return remote(partial.at[j, 1 - core], core_in.at[j], core_sem.at[0, j], core_sem.at[1, j], to_core)
-
-    def line_copy(j, up, here):
-        low, high = (here + 1, m) if up else (0, here)
-        into, sems = (up_in, up_sem) if up else (down_in, down_sem)
-        return remote(
-            partial.at[j, core, pl.ds(low, high - low)],
-            into.at[j, pl.ds(low - (1 if up else 0), high - low)],
-            sems.at[0, j],
-            sems.at[1, j],
-            to_line(1 if up else -1),
-        )
-
-    def add(j, place, value):
-        partial[j, core, place] = (partial[j, core, place].astype(jnp.float32) + value.astype(jnp.float32)).astype(partial.dtype)
-
-    def compute(j):
-        for n in range(CHUNK_HEADS):
-            keys = kv[:, pl.ds(pl.multiple_of(j * 2 * CHUNK + n * HEAD_SIZE, 128), HEAD_SIZE)]
-            values = kv[:, pl.ds(pl.multiple_of(j * 2 * CHUNK + CHUNK + n * HEAD_SIZE, 128), HEAD_SIZE)]
-            dk = dv = None
-            for g in range(GROUP):
-                h = (j * CHUNK_HEADS + n) * GROUP + g
-                at = pl.ds(pl.multiple_of(h * HEAD_SIZE, 128), HEAD_SIZE)
-                queries, grad = q[:, at], d_att[:, at]
-                total = jnp.sum(jnp.where(lane == h, lse[...], 0.0), axis=-1, keepdims=True)
-                delta = jnp.sum(grad.astype(jnp.float32) * att[:, at], axis=-1, keepdims=True)
-                s = lax.dot_general(queries, keys, over_columns, preferred_element_type=jnp.float32)
-                p = jnp.exp(jnp.where(allowed, s * SCORE_SCALE, VERY_NEGATIVE) - total)
-                dp = lax.dot_general(grad, values, over_columns, preferred_element_type=jnp.float32)
-                ds = (p * (dp - delta)).astype(queries.dtype)
-                dq = jnp.dot(ds, keys, preferred_element_type=jnp.float32) * SCORE_SCALE
-                here_k = lax.dot_general(ds, queries, over_rows, preferred_element_type=jnp.float32)
-                here_v = lax.dot_general(p.astype(grad.dtype), grad, over_rows, preferred_element_type=jnp.float32)
-                dk = here_k if dk is None else dk + here_k
-                dv = here_v if dv is None else dv + here_v
-                by_head, by_gain = head_prepare_back(dq, qp[:, at], q_gain[...], cos, sin)
-                dq_low[:, at] = by_head.astype(dq_low.dtype)
-                gains[0:1] += by_gain
-            first = n * HEAD_SIZE
-            partial[j, :, :, :, first : first + HEAD_SIZE] = (dk * SCORE_SCALE).astype(partial.dtype).reshape(2, m, tokens, HEAD_SIZE)
-            first += CHUNK
-            partial[j, :, :, :, first : first + HEAD_SIZE] = dv.astype(partial.dtype).reshape(2, m, tokens, HEAD_SIZE)
-        core_copy(j).start()
-
-    def take_core(j):
-        core_copy(j).wait_recv()
-        for place in range(m):
-            add(j, place, core_in[j, place])
-
-    def hop(j, h):
-        for up in (True, False):
-            here = h if up else m - 1 - h
-
-            @pl.when(zz == here)
-            def _():
-                if h > 0:
-                    line_copy(j, up, here - 1 if up else here + 1).wait_recv()
-                    into = up_in if up else down_in
-                    for place in range(here, m) if up else range(here + 1):
-                        add(j, place, into[j, place - (1 if up else 0)])
-                if h < m - 1:
-                    line_copy(j, up, here).start()
-
-    def finish(j):
-        for n in range(CHUNK_HEADS):
-            at = pl.ds(pl.multiple_of((j * CHUNK_HEADS + n) * HEAD_SIZE, 128), HEAD_SIZE)
-            grad = partial[j, core, zz, :, n * HEAD_SIZE : (n + 1) * HEAD_SIZE].astype(jnp.float32)
-            by_head, by_gain = head_prepare_back(grad, kp[:, at], k_gain[...], cos, sin)
-            dk_low[:, at] = by_head.astype(dk_low.dtype)
-            gains[1:2] += by_gain
-        at = pl.ds(pl.multiple_of(j * CHUNK, 128), CHUNK)
-        dv_low[:, at] = partial[j, core, zz, :, CHUNK:]
-        core_copy(j).wait_send()
-        for here in range(m):
-
-            @pl.when(zz == here)
-            def _():
-                if here < m - 1:
-                    line_copy(j, True, here).wait_send()
-                if here > 0:
-                    line_copy(j, False, here).wait_send()
-
-    plan = [[compute], [take_core, functools.partial(hop, h=0)]]
-    for h in range(1, m):
-        plan.append([functools.partial(hop, h=h)])
-    plan[-1].append(finish)
-
-    def tick(t, carry):
-        for depth in [*range(1, len(plan)), 0]:
-            j = t - depth
-
-            @pl.when((j >= 0) & (j < CHUNKS))
-            def _():
-                for stage in plan[depth]:
-                    stage(j)
-
-        return carry
-
-    lax.fori_loop(0, CHUNKS + len(plan) - 1, tick, 0)
-
-
-def attend_back(m, q, kv, d_att, att, lse, qp, kp, q_gain, k_gain, cosine, sine, place_q, segment_k, collective_id):
-    tokens = q.shape[0]
-    low = jnp.bfloat16
-    dma = pltpu.SemaphoreType.DMA
-    vmem = pl.BlockSpec(memory_space=pltpu.VMEM)
-    return pl.pallas_call(
-        functools.partial(attend_back_kernel, m),
-        out_shape=[
-            jax.ShapeDtypeStruct((tokens, QD), low),
-            jax.ShapeDtypeStruct((tokens, KEY_FEATURES), low),
-            jax.ShapeDtypeStruct((tokens, KEY_FEATURES), low),
-            jax.ShapeDtypeStruct((8, HEAD_SIZE), jnp.float32),
-        ],
-        in_specs=[vmem] * 13,
-        out_specs=[vmem] * 4,
-        scratch_shapes=[
-            pltpu.VMEM((CHUNKS, 2, m, tokens, 2 * CHUNK), low),
-            pltpu.VMEM((CHUNKS, m, tokens, 2 * CHUNK), low),
-            pltpu.VMEM((CHUNKS, max(m - 1, 1), tokens, 2 * CHUNK), low),
-            pltpu.VMEM((CHUNKS, max(m - 1, 1), tokens, 2 * CHUNK), low),
-            dma((2, CHUNKS)),
-            dma((2, CHUNKS)),
-            dma((2, CHUNKS)),
-        ],
-        compiler_params=pltpu.CompilerParams(
-            collective_id=collective_id, has_side_effects=True, vmem_limit_bytes=48 * 1024 * 1024
-        ),
-    )(q, kv, d_att, att, lse, qp, kp, q_gain, k_gain, cosine, sine, place_q, segment_k)
-
-
 def segment_of(doc_ends, token_index):
     return jnp.sum((token_index[:, None] >= doc_ends[None, :]).astype(jnp.int32), axis=1)
 
@@ -1105,78 +1332,19 @@
     return value, others
 
 
-def head_gain(gain):
-    return gain.astype(jnp.float32)[None, :]
-
-
-def layer_ahead(hidden, weights, tables, m, which_layer, waiting):
+def layer_back(upstream, hidden, weights, gains, saved, tables, m, which_layer, waiting):
     (
-        gain_first,
         query_weight,
         key_matrix,
         value_matrix,
-        gain_query,
-        gain_key,
         output_weight,
-        gain_second,
         gate_weight,
         up_weight,
         down_weight,
     ) = weights
-    normalized_rows = rms_scale(hidden, gain_first.astype(jnp.float32)).astype(jnp.bfloat16)
-    key_projection = product(normalized_rows, key_matrix)
-    rows_of_values = product(normalized_rows, value_matrix).astype(jnp.bfloat16)
-    query_proj = product(normalized_rows, query_weight)
-    waiting.append(over_replica(normalized_rows))
-    query_rows, keys_values, attended_rows, attended_low, log_sum = attend(
-        m, query_proj, key_projection, rows_of_values, head_gain(gain_query), head_gain(gain_key), *tables, 2
-    )
-    attended_low, before = after(attended_low, waiting if which_layer == 0 else waiting[:3])
-    waiting[: len(before)] = before
-    waiting.append(over_replica(attended_low))
-    hidden_mid = hidden + product(attended_low, output_weight)
-    normed_two = rms_scale(hidden_mid, gain_second.astype(jnp.float32)).astype(jnp.bfloat16)
-    waiting.append(over_replica(normed_two))
-    gate_pre = product(normed_two, gate_weight)
-    upward = product(normed_two, up_weight)
-    activated = swiglu(gate_pre, upward).astype(jnp.bfloat16)
-    waiting.append(over_replica(activated))
-    hidden_out = hidden_mid + product(activated, down_weight)
-    saved = (
-        hidden,
-        normalized_rows,
-        query_proj,
-        key_projection,
-        query_rows,
-        keys_values,
-        attended_rows,
-        attended_low,
-        log_sum,
-        hidden_mid,
-        normed_two,
-        gate_pre,
-        upward,
-        activated,
-    )
-    return (hidden_out, saved)
-
-
-def layer_back(upstream, weights, saved, tables, m, which_layer, waiting):
+    gain_first, gain_second = gains[which_layer], gains[2 + which_layer]
+    gain_query, gain_key = gains[4 + which_layer, :HEAD_SIZE], gains[6 + which_layer, :HEAD_SIZE]
     (
-        gain_first,
-        query_weight,
-        key_matrix,
-        value_matrix,
-        gain_query,
-        gain_key,
-        output_weight,
-        gain_second,
-        gate_weight,
-        up_weight,
-        down_weight,
-    ) = weights
-    (
-        hidden,
         normalized_rows,
         query_proj,
         key_projection,
@@ -1199,12 +1367,12 @@
     gate_low = grad_gate_pre.astype(jnp.bfloat16)
     up_low = grad_upward.astype(jnp.bfloat16)
     grad_normed_two = product_back(gate_low, gate_weight) + product_back(up_low, up_weight)
-    ignored, second_back = jax.vjp(rms_scale, hidden_mid, gain_second.astype(jnp.float32))
+    ignored, second_back = jax.vjp(rms_scale, hidden_mid, gain_second)
     grad_mid, grad_gain_second = second_back(grad_normed_two)
     upstream_mid = upstream + grad_mid
     attn_low = upstream_mid.astype(jnp.bfloat16)
     grad_attended = product_back(attn_low, output_weight).astype(jnp.bfloat16)
-    ready = 5 if which_layer == 1 else 8
+    ready = 0 if which_layer == 1 else 4
     grad_attended, waiting[:ready] = after(grad_attended, waiting[:ready])
     query_low, key_low, value_low, head_gains = attend_back(
         m,
@@ -1215,17 +1383,17 @@
         log_sum,
         query_proj,
         key_projection,
-        head_gain(gain_query),
-        head_gain(gain_key),
+        gain_query[None],
+        gain_key[None],
         *tables,
         3,
     )
-    ready = 7 if which_layer == 1 else 10
+    ready = 3 if which_layer == 1 else 8
     query_low, waiting[:ready] = after(query_low, waiting[:ready])
     grad_normed = product_back(query_low, query_weight)
     grad_normed = grad_normed + product_back(key_low, key_matrix)
     grad_normed = grad_normed + product_back(value_low, value_matrix)
-    ignored, first_back = jax.vjp(rms_scale, hidden, gain_first.astype(jnp.float32))
+    ignored, first_back = jax.vjp(rms_scale, hidden, gain_first)
     grad_hidden, grad_gain_first = first_back(grad_normed)
     lefts = (activated, attended_low, normed_two, normalized_rows)
     rights = (branch_low, attn_low, gate_low, up_low, query_low, key_low, value_low)
@@ -1237,30 +1405,25 @@
     return min(rows, -(-int(rows * share) // 16) * 16)
 
 
-def gather_all(parts):
+NEAR_SHARES = (0.75, 0.75, 0.75, 0.6, 0.5, 0.75, 0.55)
+ARRIVAL = [(weight, layer) for layer in range(LAYERS) for weight in range(7)]
+
+
+def run_forward(tokens, tables, weights, gains):
     nx, nz = lax.axis_size("shard") // 2, lax.axis_size("ctx")
-    gains = (parts[0], parts[4], parts[5], parts[7])
-    flat = jnp.concatenate([g.reshape(-1) for g in gains])
-    small = jnp.zeros((16 * 128,), flat.dtype).at[: flat.shape[0]].set(flat).reshape(16, 128)
-    big = (1, 2, 3, 6, 8, 9, 10)
-    shares = (0.75, 0.75, 0.75, 0.6, 0.5, 0.75, 0.55)
-    shards, nears = [small], [16]
-    for which_layer in range(LAYERS):
-        for member, share in zip(big, shares):
-            shards.append(parts[member][which_layer])
-            nears.append(near_rows(parts[member].shape[1], share))
-    wholes = gather_weights(shards, nears, nx, nz, 0)
-    every = wholes[0].reshape(2 * nx * nz, 16 * 128)[:, : flat.shape[0]]
-    out, used = [[None] * 11 for _ in range(LAYERS)], 0
-    for member, g in zip((0, 4, 5, 7), gains):
-        here = every[:, used : used + g.size].reshape(-1, LAYERS, g.shape[1])
-        used += g.size
-        for which_layer in range(LAYERS):
-            out[which_layer][member] = here[:, which_layer].reshape(-1)
-    for which_layer in range(LAYERS):
-        for i, member in enumerate(big):
-            out[which_layer][member] = wholes[1 + which_layer * 7 + i]
-    return out
+    here = lax.axis_index("shard") * nz + lax.axis_index("ctx")
+    block = jnp.zeros((16, D), jnp.bfloat16)
+    for row, parts in ((0, gains[:2]), (4, gains[2:])):
+        part = jnp.concatenate(parts)
+        block = lax.dynamic_update_slice(block, part, (row, here * part.shape[1]))
+    chunks = [(-1, 0, 16, 16)]
+    for weight, layer in ARRIVAL:
+        rows = weights[weight].shape[1]
+        chunks.append((weight, layer, rows, near_rows(rows, NEAR_SHARES[weight])))
+    wholes, outs, saved = forward(block, weights, tokens, tables, tuple(chunks), nx, nz, 0)
+    by_place = dict(zip(ARRIVAL, wholes[1:]))
+    gathered = [[by_place[weight, layer] for weight in range(7)] for layer in range(LAYERS)]
+    return gathered, outs, saved
 
 
 def weight_gradients(operands):
@@ -1310,7 +1473,7 @@
     def swap(values):
         return lax.ppermute(values, ("shard", "ctx"), pairs)
 
-    tokens, lengths, cotangent = swap(tokens), swap(lengths), swap(cotangent)
+    lengths = swap(lengths)
     block = lax.axis_index("ctx") % m + (lax.axis_index("shard") % 2) * m
     token_index = block * token_rows + jnp.arange(token_rows, dtype=jnp.int32)
     doc_lengths = lengths[0]
@@ -1320,21 +1483,32 @@
     cosine, sine = rotary(positions, HEAD_SIZE)
     key_segment = segment_of(doc_ends, jnp.arange(token_rows * nz, dtype=jnp.int32))
     tables = (cosine, sine, jnp.stack([token_segment, token_index], axis=1), key_segment[None, :])
-    gathered = gather_all(
-        (norm_one, w_query, w_key, w_value, query_gain, key_gain, w_output, norm_two, w_gate, w_up, w_down)
+    gathered, (gains, tokens, hidden, last), saved = run_forward(
+        tokens[0],
+        tables,
+        (w_query, w_key, w_value, w_output, w_gate, w_up, w_down),
+        (norm_one, norm_two, query_gain, key_gain),
     )
-    hidden = tokens[0].astype(jnp.float32)
-    stored, waiting = [], []
-    for which_layer in range(LAYERS):
-        hidden, saved = layer_ahead(hidden, gathered[which_layer], tables, m, which_layer, waiting)
-        stored.append(saved)
-    output = swap(hidden.astype(jnp.bfloat16))[None]
+    cotangent = swap(cotangent)
+    output = swap(last)[None]
+    hiddens = (tokens.astype(jnp.float32), hidden)
+    waiting = []
+    for normed, _, _, _, _, _, attended, _, _, normed_two, _, _, activated in saved:
+        waiting += [over_replica(a) for a in (normed, attended, normed_two, activated)]
     live_mask = (token_segment < doc_lengths.shape[0]).astype(jnp.float32)
     upstream = cotangent[0].astype(jnp.float32) * live_mask[:, None]
     operands = [None] * LAYERS
     for which_layer in reversed(range(LAYERS)):
         upstream, operands[which_layer] = layer_back(
-            upstream, gathered[which_layer], stored[which_layer], tables, m, which_layer, waiting
+            upstream,
+            hiddens[which_layer],
+            gathered[which_layer],
+            gains,
+            saved[which_layer],
+            tables,
+            m,
+            which_layer,
+            waiting,
         )
     grad_tokens = swap(upstream.astype(jnp.bfloat16))[None]
     for which_layer, (lefts, rights, gains) in enumerate(operands):

time: 724 us -> 674 us (0.931)
  matrix products: 77.9 us -> 37.6 us
  Pallas kernels: 587 us -> 554 us
  waiting for transfers between devices: 0.04 us -> 21.1 us
    dot_general x14 -> x0, matrix products: 38.7 us -> none  [product(): return jnp.dot(left, right, preferred_element_type=jnp.float32)]
    ppermute x10, waiting for transfers between devices: 0.03 us -> 21.1 us  [over_replica(): return lax.ppermute(values, 'rep', [(0, 1), (1, 0)])]
    pallas_call x3 -> x1, Pallas kernels: 314 us -> 294 us  [forward(): pl.pallas_call(functools.partial(forward_kernel, chunks, nx, nz), out_sha...]
    pallas_call x2, Pallas kernels: 67.8 us -> 59.3 us  [attend_back(): pl.pallas_call(functools.partial(attend_back_kernel, m), out_shape=[jax.S...]
    squeeze x7 -> x0, local copies, waits for them, and re-layouts: 8.22 us -> none  [gather_all(): shards.append(parts[member][which_layer])]
  transfers between devices with their start and end apart: 15 -> 14, of which waited for: 0 -> 4; matrix products, arithmetic and copies ran while one was open for 13% -> 8% of each run, Pallas kernels for 82% -> 84%
where the time goes in v5:
time: 674 us; the launch traced here: 663 us
  Pallas kernels  554 us (82%)
  matrix products  37.6 us (6%)
  waiting for transfers between devices  21.1 us (3%)
  local copies, waits for them, and re-layouts  21 us (3%)
  starting transfers between devices  17.1 us (3%)
  other arithmetic  10.1 us (1%)
    pallas_call x1, Pallas kernels, forward(): pl.pallas_call(functools.partial(forward_kernel, chunks, nx, nz), out_sha...  294 us
    pallas_call x1, Pallas kernels, reduce_weights(): pl.pallas_call(functools.partial(reduce_kernel, nx, nz, layers), out_shap...  201 us
    pallas_call x2, Pallas kernels, attend_back(): pl.pallas_call(functools.partial(attend_back_kernel, m), out_shape=[jax.S...  59.3 us
    dot_general x14, matrix products, product_back(): lax.dot_general(grad, right, (((1,), (1,)), ((), ())), preferred_element_...  37.6 us
    ppermute x10, waiting for transfers between devices, over_replica(): return lax.ppermute(values, 'rep', [(0, 1), (1, 0)])  21.1 us
    unnamed x156, local copies, waits for them, and re-layouts  14.5 us
  transfers between devices with their start and end apart: 14, of which 4 were waited for; matrix products, arithmetic and copies ran while one was open for 8% of the time, Pallas kernels for 84%

profile of v5, /device:TPU:0, one launch (start us, length us, event | category | flops | bytes accessed | tf_op | source)
XLA Modules:
  0.0 663.4 jit_solution(8509316752020646624)
XLA Ops:
  0.6 1.3 collective-permute-start
  2.0 1.6 collective-permute-start.2
  6.2 0.8 copy.31.refs_11_.place_q
  8.0 0.8 pad_maximum_fusion
  8.8 293.7 %shard_map.237 = (bf16[256,1024]{1,0:T(8,128)(2,1)}, bf16[1024,2048]{1,0:T(8,128)(2,1)}, bf16[1024,1024]{1,0:T(8,128)(2,1)}, bf16[1024,1024]{1,0:T(8,128)(2,1)},...) custom-call(bf16[16,1024]{1,0:T(8,128)(2,1)} %copy-done.54, ...), custom_call_target="tpu_custom_call" | custom-call | tf_op jit(solution)/shard_map/pallas_call | solution.py:760
  302.5 1.4 multiply_reduce_fusion.8
  303.9 0.8 fusion.30
  305.0 1.7 collective-permute-start.3
  307.1 1.3 multiply_reduce_fusion.6
  308.9 1.3 multiply_reduce_fusion.4
  310.7 1.7 collective-permute-start.6
  313.8 0.9 fusion.29
  314.7 4.7 collective-permute-start.1
  319.6 7.2 %multiply_convert_fusion.1 = (bf16[192,3072]{1,0:T(8,128)(2,1)S(1)}, bf16[192,3072]{1,0:T(8,128)(2,1)S(1)}) fusion(f32[192,3072]{1,0:T(8,128)} %get-tuple-element.106, f32[192,3072]{1,0:T(8,128)} %get-tuple-element.105, bf16[192,1024]{1,0:T(8,128)(2,1)S(1)} %fusion.17.refs_24_, bf16[3072,1024]{1,0:T(8,128)(2,1)} %get-tuple-element.104), kind=kOutput, calls=%fused_computation.12 | convolution fusion | flops 1216217088 | bytes 13762560 | tf_op jit(solution)/shard_map/dot_general | solution.py:1323
  326.8 5.9 fusion.31
  332.8 2.5 multiply_reduce_fusion
  335.7 1.5 convolution_convert_fusion.1.d_att
  337.8 29.6 %shard_map.238 = (bf16[192,2048]{1,0:T(8,128)(2,1)S(1)}, bf16[192,1024]{1,0:T(8,128)(2,1)S(1)}, bf16[192,1024]{1,0:T(8,128)(2,1)S(1)}, f32[8,128]{1,0:T(8,128)S(1)}) custom-call(bf16[192,2048]{1,0:T(8,128)(2,1)S(1)} %copy-done.14, bf16[768,2048]{1,0:T(8,128)(2,1)} %get-tuple-element.112.kv, bf16[192,2048]{1,0:T(8,128)(2,1)S(1)} %convolution_convert_fusion.1.d_att, ...), custom_call_target="tpu_custom_call" | custom-call | tf_op jit(solution)/shard_map/pallas_call | solution.py:198
  367.5 0.8 fusion.32
  368.4 0.8 fusion.33
  369.3 1.1 copy-done.40
  370.7 1.7 collective-permute-start.8
  372.8 1.7 collective-permute-start.9
  374.5 1.8 multiply_reduce_fusion.1
  376.6 7.3 %multiply_convert_fusion = (bf16[192,3072]{1,0:T(8,128)(2,1)S(1)}, bf16[192,3072]{1,0:T(8,128)(2,1)S(1)}) fusion(f32[192,3072]{1,0:T(8,128)} %get-tuple-element.131, f32[192,3072]{1,0:T(8,128)} %get-tuple-element.130, bf16[192,1024]{1,0:T(8,128)(2,1)S(1)} %get-tuple-element.191.refs_8_, bf16[3072,1024]{1,0:T(8,128)(2,1)} %get-tuple-element.129), kind=kOutput, calls=%fused_computation.10 | convolution fusion | flops 1216217088 | bytes 13762560 | tf_op jit(solution)/shard_map/dot_general | solution.py:1323
  384.0 2.2 fusion.34
  386.3 2.5 multiply_reduce_fusion.2
  389.1 1.5 convolution_convert_fusion.d_att
  391.1 29.7 %shard_map.239 = (bf16[192,2048]{1,0:T(8,128)(2,1)S(1)}, bf16[192,1024]{1,0:T(8,128)(2,1)S(1)}, bf16[192,1024]{1,0:T(8,128)(2,1)S(1)}, f32[8,128]{1,0:T(8,128)S(1)}) custom-call(bf16[192,2048]{1,0:T(8,128)(2,1)S(1)} %copy-done.12, bf16[768,2048]{1,0:T(8,128)(2,1)} %get-tuple-element.136.kv, bf16[192,2048]{1,0:T(8,128)(2,1)S(1)} %convolution_convert_fusion.d_att, ...), custom_call_target="tpu_custom_call" | custom-call | tf_op jit(solution)/shard_map/pallas_call | solution.py:198
  420.9 3.8 collective-permute-done.7.refs_23_
  425.0 8.1 %collective-permute-done.9.refs_22_ = bf16[192,1024]{1,0:T(8,128)(2,1)} collective-permute-done((bf16[192,1024]{1,0:T(8,128)(2,1)S(1)}, bf16[192,1024]{1,0:T(8,128)(2,1)}, u32[]{:S(2)}, u32[]{:S(2)}) %collective-permute-start.9) | collective-permute-done | bytes 393248 | tf_op jit(solution)/shard_map/ppermute | solution.py:1327
  433.1 0.8 fusion.35
  434.0 0.8 fusion.36
  434.9 0.9 copy-done.23
  435.8 1.8 fusion.16
  439.2 2.2 collective-permute-done.13.refs_31_
  441.4 7.0 %collective-permute-done.12.refs_15_ = bf16[192,1024]{1,0:T(8,128)(2,1)S(1)} collective-permute-done((bf16[192,1024]{1,0:T(8,128)(2,1)S(1)}, bf16[192,1024]{1,0:T(8,128)(2,1)S(1)}, u32[]{:S(2)}, u32[]{:S(2)}) %collective-permute-start.12) | collective-permute-done | bytes 393248 | tf_op jit(solution)/shard_map/ppermute | solution.py:1327
  449.2 201.2 %shard_map.240 = (f32[2,192,1024]{2,1,0:T(8,128)}, f32[2,128,1024]{2,1,0:T(8,128)}, f32[2,64,3072]{2,1,0:T(8,128)}, f32[2,64,3072]{2,1,0:T(8,128)}, f32[2,64,204...) custom-call(bf16[192,3072]{1,0:T(8,128)(2,1)} %get-tuple-element.141.refs_0_, ...), custom_call_target="tpu_custom_call" | custom-call | tf_op jit(solution)/shard_map/pallas_call | solution.py:1246
  650.4 0.9 reshape.162
  652.6 1.8 copy.52
  655.1 1.0 copy.54
  656.1 0.8 copy.55
  656.9 0.8 copy.56
  657.7 1.0 copy.57
  658.7 1.1 copy.58
  659.8 1.1 copy.59
  661.0 0.8 copy-done.34
  661.8 1.1 copy.60
  (201 shorter events, 14.1 us)
Async XLA Ops:
  0.6 5.0 collective-permute-start
  2.0 312.8 %collective-permute-start.2 = (bf16[1,192,1024]{2,1,0:T(8,128)(2,1)}, bf16[1,192,1024]{2,1,0:T(8,128)(2,1)S(1)}, u32[]{:S(2)}, u32[]{:S(2)}) collective-permute-start(bf16[1,192,1024]{2,1,0:T(8,128)(2,1)} %param.29), channel_id=1, source_target_pairs={{4,2},{2,4},{0,0},{6,6},{5,3},{3,5},{1,1},{7,7},{12,10},{10,12},{8... | collective-permute-start | bytes 1179656 | tf_op jit(solution)/shard_map/ppermute | solution.py:1474
  5.7 3.1 copy-start.54
  302.5 8.3 %copy-start.39 = (bf16[192,3072]{1,0:T(8,128)(2,1)S(1)}, bf16[192,3072]{1,0:T(8,128)(2,1)}, u32[]{:S(2)}) copy-start(bf16[192,3072]{1,0:T(8,128)(2,1)} %get-tuple-element.141.refs_0_) | copy-start | bytes 3538948
  302.5 10.0 %copy-start.27 = (bf16[192,1024]{1,0:T(8,128)(2,1)S(1)}, bf16[192,1024]{1,0:T(8,128)(2,1)}, u32[]{:S(2)}) copy-start(bf16[192,1024]{1,0:T(8,128)(2,1)} %get-tuple-element.162) | copy-start | bytes 1179652
  304.7 68.1 %collective-permute-start.4 = (bf16[192,2048]{1,0:T(8,128)(2,1)}, bf16[192,2048]{1,0:T(8,128)(2,1)}, u32[]{:S(2)}, u32[]{:S(2)}) collective-permute-start(bf16[192,2048]{1,0:T(8,128)(2,1)} %get-tuple-element.120.refs_1_), channel_id=1, source_target_pairs={{0,16},{16,0},{1,17},{17,1},{2,18},{18,2},{3,19},{19,3},{4,20},{20... | collective-permute-start | bytes 2359304 | tf_op jit(solution)/shard_map/ppermute | solution.py:1327
  305.0 65.7 %collective-permute-start.3 = (bf16[192,1024]{1,0:T(8,128)(2,1)}, bf16[192,1024]{1,0:T(8,128)(2,1)}, u32[]{:S(2)}, u32[]{:S(2)}) collective-permute-start(bf16[192,1024]{1,0:T(8,128)(2,1)} %get-tuple-element.119.refs_3_), channel_id=1, source_target_pairs={{0,16},{16,0},{1,17},{17,1},{2,18},{18,2},{3,19},{19,3},{4,20},{20... | collective-permute-start | bytes 1179656 | tf_op jit(solution)/shard_map/ppermute | solution.py:1327
  306.7 65.7 %collective-permute-start.5 = (bf16[192,1024]{1,0:T(8,128)(2,1)}, bf16[192,1024]{1,0:T(8,128)(2,1)}, u32[]{:S(2)}, u32[]{:S(2)}) collective-permute-start(bf16[192,1024]{1,0:T(8,128)(2,1)} %get-tuple-element.121.refs_2_), channel_id=1, source_target_pairs={{0,16},{16,0},{1,17},{17,1},{2,18},{18,2},{3,19},{19,3},{4,20},{20... | collective-permute-start | bytes 1179656 | tf_op jit(solution)/shard_map/ppermute | solution.py:1327
  310.7 79.9 %collective-permute-start.6 = (bf16[192,3072]{1,0:T(8,128)(2,1)S(1)}, bf16[192,3072]{1,0:T(8,128)(2,1)S(1)}, u32[]{:S(2)}, u32[]{:S(2)}) collective-permute-start(bf16[192,3072]{1,0:T(8,128)(2,1)S(1)} %copy-done.39), channel_id=1, source_target_pairs={{0,16},{16,0},{1,17},{17,1},{2,18},{18,2},{3,19},{19,3},{4,20},{20... | collective-permute-start | bytes 3538952 | tf_op jit(solution)/shard_map/ppermute | solution.py:1327
  314.7 54.5 %collective-permute-start.1 = (bf16[192,1024]{1,0:T(8,128)(2,1)}, bf16[192,1024]{1,0:T(8,128)(2,1)}, u32[]{:S(2)}, u32[]{:S(2)}) collective-permute-start(bf16[192,1024]{1,0:T(8,128)(2,1)} %get-tuple-element.103), channel_id=1, source_target_pairs={{4,2},{2,4},{0,0},{6,6},{5,3},{3,5},{1,1},{7,7},{12,10},{10,12},{8... | collective-permute-start | bytes 1179656 | tf_op jit(solution)/shard_map/ppermute | solution.py:1474
  319.4 13.3 %slice-start.2 = ((s8[6291456]{0:T(1024)(128)(4,1)}), s8[4194304]{0:T(1024)(128)(4,1)S(1)}, s32[]{:S(2)}) async-start(s8[6291456]{0:T(1024)(128)(4,1)} %bitcast.55), calls=%async_computation.2 | async-start | bytes 8388608
  319.5 71.1 %copy-start.37 = (bf16[192,1024]{1,0:T(8,128)(2,1)}, bf16[192,1024]{1,0:T(8,128)(2,1)S(1)}, u32[]{:S(2)}) copy-start(bf16[192,1024]{1,0:T(8,128)(2,1)S(1)} %fusion.17.refs_24_) | copy-start | bytes 1179652
  319.6 13.2 %slice-start.3 = ((s8[6291456]{0:T(1024)(128)(4,1)}), s8[2097152]{0:T(1024)(128)(4,1)S(1)}, s32[]{:S(2)}) async-start(s8[6291456]{0:T(1024)(128)(4,1)} %bitcast.55), calls=%async_computation.3 | async-start | bytes 4194304
  326.8 5.9 copy-start.42
  326.8 5.9 copy-start.21
  326.8 5.9 copy-start.18
  337.8 29.7 %copy-start.33 = (bf16[1024,1024]{1,0:T(8,128)(2,1)S(1)}, bf16[1024,1024]{1,0:T(8,128)(2,1)}, u32[]{:S(2)}) copy-start(bf16[1024,1024]{1,0:T(8,128)(2,1)} %get-tuple-element.125) | copy-start | bytes 6291460
  337.8 30.6 %copy-start.32 = (bf16[1024,1024]{1,0:T(8,128)(2,1)S(1)}, bf16[1024,1024]{1,0:T(8,128)(2,1)}, u32[]{:S(2)}) copy-start(bf16[1024,1024]{1,0:T(8,128)(2,1)} %get-tuple-element.127) | copy-start | bytes 6291460
  337.8 32.9 %copy-start.47 = (bf16[192,2048]{1,0:T(8,128)(2,1)S(1)}, bf16[192,2048]{1,0:T(8,128)(2,1)}, u32[]{:S(2)}) copy-start(bf16[192,2048]{1,0:T(8,128)(2,1)} %get-tuple-element.153.refs_17_) | copy-start | bytes 2359300
  337.8 35.0 %copy-start.51 = (bf16[192,1024]{1,0:T(8,128)(2,1)S(1)}, bf16[192,1024]{1,0:T(8,128)(2,1)}, u32[]{:S(2)}) copy-start(bf16[192,1024]{1,0:T(8,128)(2,1)} %get-tuple-element.154.refs_18_) | copy-start | bytes 1179652
  367.5 7.0 %copy-start.1 = (bf16[192,2048]{1,0:T(8,128)(2,1)}, bf16[192,2048]{1,0:T(8,128)(2,1)S(1)}, u32[]{:S(2)}) copy-start(bf16[192,2048]{1,0:T(8,128)(2,1)S(1)} %get-tuple-element.122.refs_28_) | copy-start | bytes 2359300
  367.5 7.0 %copy-start.26 = (bf16[1024,2048]{1,0:T(8,128)(2,1)S(1)}, bf16[1024,2048]{1,0:T(8,128)(2,1)}, u32[]{:S(2)}) copy-start(bf16[1024,2048]{1,0:T(8,128)(2,1)} %get-tuple-element.123) | copy-start | bytes 12582916
  368.3 4.1 copy-start.50
  368.4 6.1 copy-start.20
  368.4 6.1 copy-start.63
  370.4 62.7 %collective-permute-start.10 = (bf16[192,3072]{1,0:T(8,128)(2,1)S(1)}, bf16[192,3072]{1,0:T(8,128)(2,1)S(1)}, u32[]{:S(2)}, u32[]{:S(2)}) collective-permute-start(bf16[192,3072]{1,0:T(8,128)(2,1)S(1)} %copy-done.40), channel_id=1, source_target_pairs={{0,16},{16,0},{1,17},{17,1},{2,18},{18,2},{3,19},{19,3},{4,20},{20... | collective-permute-start | bytes 3538952 | tf_op jit(solution)/shard_map/ppermute | solution.py:1327
  370.7 62.4 %collective-permute-start.8 = (bf16[192,2048]{1,0:T(8,128)(2,1)S(1)}, bf16[192,2048]{1,0:T(8,128)(2,1)}, u32[]{:S(2)}, u32[]{:S(2)}) collective-permute-start(bf16[192,2048]{1,0:T(8,128)(2,1)S(1)} %copy-done.47), channel_id=1, source_target_pairs={{0,16},{16,0},{1,17},{17,1},{2,18},{18,2},{3,19},{19,3},{4,20},{20... | collective-permute-start | bytes 2359304 | tf_op jit(solution)/shard_map/ppermute | solution.py:1327
  372.4 52.2 %collective-permute-start.7 = (bf16[192,1024]{1,0:T(8,128)(2,1)S(1)}, bf16[192,1024]{1,0:T(8,128)(2,1)}, u32[]{:S(2)}, u32[]{:S(2)}) collective-permute-start(bf16[192,1024]{1,0:T(8,128)(2,1)S(1)} %copy-done.50), channel_id=1, source_target_pairs={{0,16},{16,0},{1,17},{17,1},{2,18},{18,2},{3,19},{19,3},{4,20},{20... | collective-permute-start | bytes 1179656 | tf_op jit(solution)/shard_map/ppermute | solution.py:1327
  372.8 60.3 %collective-permute-start.9 = (bf16[192,1024]{1,0:T(8,128)(2,1)S(1)}, bf16[192,1024]{1,0:T(8,128)(2,1)}, u32[]{:S(2)}, u32[]{:S(2)}) collective-permute-start(bf16[192,1024]{1,0:T(8,128)(2,1)S(1)} %copy-done.51), channel_id=1, source_target_pairs={{0,16},{16,0},{1,17},{17,1},{2,18},{18,2},{3,19},{19,3},{4,20},{20... | collective-permute-start | bytes 1179656 | tf_op jit(solution)/shard_map/ppermute | solution.py:1327
  376.3 7.6 %slice-start.4 = ((s8[6291456]{0:T(1024)(128)(4,1)}), s8[2097152]{0:T(1024)(128)(4,1)S(1)}, s32[]{:S(2)}) async-start(s8[6291456]{0:T(1024)(128)(4,1)} %bitcast.69), calls=%async_computation.4 | async-start | bytes 4194304
  376.3 9.9 %slice-start = ((s8[6291456]{0:T(1024)(128)(4,1)}), s8[4194304]{0:T(1024)(128)(4,1)S(1)}, s32[]{:S(2)}) async-start(s8[6291456]{0:T(1024)(128)(4,1)} %bitcast.53), calls=%async_computation | async-start | bytes 8388608
  376.6 48.1 %copy-start.38 = (bf16[192,1024]{1,0:T(8,128)(2,1)}, bf16[192,1024]{1,0:T(8,128)(2,1)S(1)}, u32[]{:S(2)}) copy-start(bf16[192,1024]{1,0:T(8,128)(2,1)S(1)} %get-tuple-element.191.refs_8_) | copy-start | bytes 1179652
  376.6 7.3 %slice-start.5 = ((s8[6291456]{0:T(1024)(128)(4,1)}), s8[4194304]{0:T(1024)(128)(4,1)S(1)}, s32[]{:S(2)}) async-start(s8[6291456]{0:T(1024)(128)(4,1)} %bitcast.69), calls=%async_computation.5 | async-start | bytes 8388608
  376.6 9.6 %slice-start.1 = ((s8[6291456]{0:T(1024)(128)(4,1)}), s8[2097152]{0:T(1024)(128)(4,1)S(1)}, s32[]{:S(2)}) async-start(s8[6291456]{0:T(1024)(128)(4,1)} %bitcast.53), calls=%async_computation.1 | async-start | bytes 4194304
  390.7 30.1 %copy-start.41 = (bf16[192,3072]{1,0:T(8,128)(2,1)}, bf16[192,3072]{1,0:T(8,128)(2,1)S(1)}, u32[]{:S(2)}) copy-start(bf16[192,3072]{1,0:T(8,128)(2,1)S(1)} %collective-permute-done.6.refs_4_) | copy-start | bytes 3538948
  390.7 50.7 %collective-permute-start.13 = (bf16[192,1024]{1,0:T(8,128)(2,1)S(1)}, bf16[192,1024]{1,0:T(8,128)(2,1)S(1)}, u32[]{:S(2)}, u32[]{:S(2)}) collective-permute-start(bf16[192,1024]{1,0:T(8,128)(2,1)S(1)} %fusion.17.refs_24_), channel_id=1, source_target_pairs={{0,16},{16,0},{1,17},{17,1},{2,18},{18,2},{3,19},{19,3},{4,20},{20... | collective-permute-start | bytes 1179656 | tf_op jit(solution)/shard_map/ppermute | solution.py:1327
  391.1 42.0 %copy-start.31 = (bf16[1024,1024]{1,0:T(8,128)(2,1)S(1)}, bf16[1024,1024]{1,0:T(8,128)(2,1)}, u32[]{:S(2)}) copy-start(bf16[1024,1024]{1,0:T(8,128)(2,1)} %get-tuple-element.159) | copy-start | bytes 6291460
  420.8 14.0 %copy-start.9 = (bf16[192,1024]{1,0:T(8,128)(2,1)}, bf16[192,1024]{1,0:T(8,128)(2,1)S(1)}, u32[]{:S(2)}) copy-start(bf16[192,1024]{1,0:T(8,128)(2,1)S(1)} %get-tuple-element.158.refs_13_) | copy-start | bytes 1179652
  420.8 14.0 %copy-start.10 = (bf16[192,1024]{1,0:T(8,128)(2,1)}, bf16[192,1024]{1,0:T(8,128)(2,1)S(1)}, u32[]{:S(2)}) copy-start(bf16[192,1024]{1,0:T(8,128)(2,1)S(1)} %get-tuple-element.160.refs_14_) | copy-start | bytes 1179652
  420.8 14.0 %copy-start = (bf16[192,2048]{1,0:T(8,128)(2,1)}, bf16[192,2048]{1,0:T(8,128)(2,1)S(1)}, u32[]{:S(2)}) copy-start(bf16[192,2048]{1,0:T(8,128)(2,1)S(1)} %get-tuple-element.156.refs_12_) | copy-start | bytes 2359300
  420.9 13.2 %copy-start.30 = (bf16[1024,1024]{1,0:T(8,128)(2,1)S(1)}, bf16[1024,1024]{1,0:T(8,128)(2,1)}, u32[]{:S(2)}) copy-start(bf16[1024,1024]{1,0:T(8,128)(2,1)} %get-tuple-element.161) | copy-start | bytes 6291460
  424.7 23.7 %collective-permute-start.12 = (bf16[192,1024]{1,0:T(8,128)(2,1)S(1)}, bf16[192,1024]{1,0:T(8,128)(2,1)S(1)}, u32[]{:S(2)}, u32[]{:S(2)}) collective-permute-start(bf16[192,1024]{1,0:T(8,128)(2,1)S(1)} %get-tuple-element.191.refs_8_), channel_id=1, source_target_pairs={{0,16},{16,0},{1,17},{17,1},{2,18},{18,2},{3,19},{19,3},{4,20},{20... | collective-permute-start | bytes 1179656 | tf_op jit(solution)/shard_map/ppermute | solution.py:1327
  437.9 214.7 %collective-permute-start.11 = (bf16[192,1024]{1,0:T(8,128)(2,1)S(1)}, bf16[192,1024]{1,0:T(8,128)(2,1)S(1)}, u32[]{:S(2)}, u32[]{:S(2)}) collective-permute-start(bf16[192,1024]{1,0:T(8,128)(2,1)S(1)} %fusion.12), channel_id=1, source_target_pairs={{4,2},{2,4},{0,0},{6,6},{5,3},{3,5},{1,1},{7,7},{12,10},{10,12},{8... | collective-permute-start | bytes 1179656 | tf_op jit(solution)/shard_map/ppermute | solution.py:1474
  441.4 7.0 %copy-start.52 = (bf16[192,1024]{1,0:T(8,128)(2,1)}, bf16[192,1024]{1,0:T(8,128)(2,1)S(1)}, u32[]{:S(2)}) copy-start(bf16[192,1024]{1,0:T(8,128)(2,1)S(1)} %collective-permute-done.13.refs_31_) | copy-start | bytes 1179652
  650.4 4.7 copy-start.46
  650.4 5.7 copy-start.49
  652.6 4.3 copy-start.48
  654.4 3.3 copy-start.45
  (36 other events, 69.5 us)

commit v6 on v5

--- a/solution.py
+++ b/solution.py
@@ -221,6 +221,11 @@
 
 
 WIDE_TILE, NARROW_TILE = 512, 256
+IDLE = 2
+
+
+def wholes_of(chunks):
+    return list(dict.fromkeys(c[:2] for c in chunks))
 
 
 def unit_rms(values):
@@ -229,10 +234,11 @@
 
 def forward_kernel(chunks, nx, nz, *refs):
     count = len(chunks)
+    arrays = wholes_of(chunks)
     weights = 7
     gain_shard, shards, refs = refs[0], refs[1 : 1 + weights], refs[1 + weights :]
     tokens_here, cosine, sine, place_q, segment_k, refs = *refs[:5], refs[5:]
-    wholes, refs = refs[:count], refs[count:]
+    wholes, refs = refs[: len(arrays)], refs[len(arrays) :]
     gains_out, tokens_out, hidden_out, last_out, refs = *refs[:4], refs[4:]
     saved_out, refs = [refs[n * SAVED : (n + 1) * SAVED] for n in range(LAYERS)], refs[LAYERS * SAVED :]
     own_sem, z_sem, x_sem, y_sem, core_sem, out_sem, refs = *refs[:6], refs[6:]
@@ -260,17 +266,21 @@
     def to_z(step):
         return (y, shard, z + step)
 
-    def own_shard(k):
-        weight, layer = chunks[k][:2]
-        return gain_shard if weight < 0 else shards[weight].at[layer]
+    def own_part(k, start, size):
+        weight, layer, column, width = chunks[k][:4]
+        ref = gain_shard if weight < 0 else shards[weight].at[layer]
+        return ref.at[pl.ds(start, size), pl.ds(column, width)]
+
+    def whole_rows(k, first, size):
+        weight, layer, column, width = chunks[k][:4]
+        return wholes[arrays.index((weight, layer))].at[pl.ds(first, size), pl.ds(column, width)]
 
     def rows_of(k, xs, zs, start, size, of_core=core):
-        rows = chunks[k][2]
-        first = ((xs * 2 + of_core) * nz + zs) * rows + start
-        return wholes[k].at[pl.ds(pl.multiple_of(first, 16), size)]
+        first = ((xs * 2 + of_core) * nz + zs) * chunks[k][4] + start
+        return whole_rows(k, pl.multiple_of(first, 16), size)
 
     def inplane(k):
-        rows, near = chunks[k][2:]
+        rows, near = chunks[k][4:]
         return y * (rows - near), near
 
     def arrived(ref, sem):
@@ -286,7 +296,7 @@
         remote(src, into, out_sem.at[k, kind], x_sem.at[k, xs * nz + zs], to_x(step)).start()
 
     def pass_y(k, xs, zs):
-        rows, near = chunks[k][2:]
+        rows, near = chunks[k][4:]
         if rows > near:
             part = rows_of(k, xs, zs, y * near, rows - near)
             remote(part, part, out_sem.at[k, 4], y_sem.at[k, xs * nz + zs], to_y).start()
@@ -296,9 +306,9 @@
         remote(part, part, out_sem.at[k, 5], core_sem.at[k], to_core).start()
 
     def stage_own(k):
-        rows = chunks[k][2]
+        rows = chunks[k][4]
         start, size = inplane(k)
-        part = own_shard(k).at[pl.ds(pl.multiple_of(start, 16), size)]
+        part = own_part(k, pl.multiple_of(start, 16), size)
 
         @pl.when(z < nz - 1)
         def _():
@@ -316,8 +326,9 @@
         def _():
             pass_x(k, part, x, z, -1, 3)
 
-        remote(own_shard(k), rows_of(k, x, z, 0, rows), out_sem.at[k, 5], core_sem.at[k], to_core).start()
-        pltpu.make_async_copy(own_shard(k), rows_of(k, x, z, 0, rows), own_sem.at[k]).start()
+        every = own_part(k, 0, rows)
+        remote(every, rows_of(k, x, z, 0, rows), out_sem.at[k, 5], core_sem.at[k], to_core).start()
+        pltpu.make_async_copy(every, rows_of(k, x, z, 0, rows), own_sem.at[k]).start()
 
     def stage_z(k, d):
         start, size = inplane(k)
@@ -367,7 +378,7 @@
                 lax.fori_loop(0, nz, body, 0)
 
     def stage_y(k):
-        rows, near = chunks[k][2:]
+        rows, near = chunks[k][4:]
         if rows > near:
 
             def body(i, carry):
@@ -384,15 +395,15 @@
             lax.fori_loop(0, nx * nz, body, 0)
 
     def first_rows(k, size):
-        return wholes[k].at[pl.ds(0, size)]
+        return whole_rows(k, 0, size)
 
     def complete(k):
-        rows = chunks[k][2]
+        rows = chunks[k][4]
         arrived(first_rows(k, nx * nz * rows), core_sem.at[k])
         arrived(first_rows(k, rows), own_sem.at[k])
 
     def sent(k):
-        rows, near = chunks[k][2:]
+        rows, near = chunks[k][4:]
         for zz in range(nz):
 
             @pl.when(z == zz)
@@ -508,7 +519,10 @@
 
     def save_copy(layer, n):
         source = kv.at[layer] if saves[n] is None else saves[n]
-        return pltpu.make_async_copy(source, saved_out[layer][n], save_sem.at[layer, n])
+        into = saved_out[layer][SAVE_TO[n]]
+        if n in LEFT_AT:
+            into = into.at[:, pl.ds(LEFT_AT[n] * D, source.shape[1])]
+        return pltpu.make_async_copy(source, into, save_sem.at[layer, n])
 
     def save(layer, *which):
         for n in which:
@@ -520,29 +534,31 @@
                 save_copy(layer - 1, n).wait()
 
     def layer_tasks(layer):
-        chunk = {c[0]: k for k, c in enumerate(chunks) if c[1] == layer and c[0] >= 0}
+        parts = {w: [k for k, c in enumerate(chunks) if c[:2] == (w, layer)] for w in range(weights)}
         row = lambda n, width=D: gains[n + layer : n + layer + 1, :width]
         tasks = []
 
-        def streamed(weight, buf, base, sems, tile, use, tiles, lead=None):
-            k = chunk[weight]
+        def streamed(weight, buf, base, sems, tile, use, tiles):
+            whole = wholes[arrays.index((weight, layer))]
 
             def copy(i):
                 slot = base + i % 2
-                source = wholes[k].at[:, pl.ds(i * tile, tile)]
+                source = whole.at[:, pl.ds(i * tile, tile)]
                 return pltpu.make_async_copy(source, buf.at[slot], tile_sem.at[sems + i % 2])
 
             def first():
-                complete(k)
+                for k in parts[weight]:
+                    complete(k)
                 copy(0).start()
+                copy(1).start()
 
             def one(i):
                 copy(i).wait()
-                if i + 1 < tiles:
-                    copy(i + 1).start()
                 use(i, buf.at[base + i % 2])
-
-            return first, [functools.partial(one, i) for i in range(tiles)], k
+                if i + 2 < tiles:
+                    copy(i + 2).start()
+
+            return first, [functools.partial(one, i) for i in range(tiles)], max(parts[weight])
 
         def put(k, *steps):
             tasks.append((k, lambda: [step() for step in steps]))
@@ -678,29 +694,32 @@
 
         first_k, key_tiles, kk = streamed(1, wide_buf, 0, 0, WIDE_TILE, keys, 2)
         first_v, value_tiles, kv_chunk = streamed(2, wide_buf, 2, 2, WIDE_TILE, values, 2)
-        first_q, query_tiles, kq = streamed(0, wide_buf, 0, 0, WIDE_TILE, queries, 4)
+        first_q, query_tiles, kq = streamed(0, wide_buf, 4, 8, WIDE_TILE, queries, 4)
         first_o, output_tiles, ko = streamed(3, output_buf, 0, 4, NARROW_TILE, outputs, 4)
         first_g, gate_tiles, kg = streamed(4, wide_buf, 0, 0, WIDE_TILE, gates, 6)
         first_u, up_tiles, ku = streamed(5, wide_buf, 2, 2, WIDE_TILE, ups, 6)
         first_d, down_tiles, kd = streamed(6, down_buf, 0, 6, NARROW_TILE, downs, 4)
         kqkv = max(kk, kv_chunk, kq)
-        put(kqkv, norm_first, first_k, first_v)
+        put(kqkv, first_k, first_v, first_q)
+        put(kqkv, norm_first)
         put(kqkv, *key_tiles)
-        put(kqkv, first_q, *value_tiles)
+        put(kqkv, *value_tiles)
         put(kqkv, functools.partial(send_keys, 0), functools.partial(send_keys, 1))
         put(kqkv, functools.partial(send_keys, 2), functools.partial(send_keys, 3))
         put(kqkv, *query_tiles[:2])
         put(kqkv, *query_tiles[2:])
         for part in range(4):
             put(kqkv, functools.partial(prepare_queries, part))
-        put(kqkv, functools.partial(arrivals, 0))
         for j in range(CHUNKS):
-            if j + 1 < CHUNKS:
-                put(kqkv, functools.partial(arrivals, j + 1))
-            if j + 1 == CHUNKS:
+            for _ in range(IDLE):
                 put(kqkv)
-            put(kqkv, functools.partial(attend, j))
+            put(kqkv, functools.partial(arrivals, j))
+            if j > 0:
+                put(kqkv, functools.partial(attend, j - 1))
+        for _ in range(IDLE // 2):
+            put(kqkv)
         put(ko, first_o)
+        put(kqkv, functools.partial(attend, CHUNKS - 1))
         put(ko, *output_tiles[:2])
         put(ko, *output_tiles[2:])
         put(kg, norm_second, first_g)
@@ -734,7 +753,7 @@
         sent(k)
     for layer in range(LAYERS):
         kv_left(layer)
-    for n in range(SAVED):
+    for n in range(len(saves)):
         save_copy(LAYERS - 1, n).wait()
     save_copy(0, 4).wait()
     pltpu.make_async_copy(low_tokens, tokens_out, misc_sem.at[2]).wait()
@@ -742,7 +761,9 @@
     pltpu.make_async_copy(last, last_out, misc_sem.at[6]).wait()
 
 
-SAVED = 13
+LEFT_AT = {0: 6, 6: 3, 9: 5, 12: 0}
+SAVE_TO = (0, 1, 2, 3, 4, 5, 0, 6, 7, 0, 8, 9, 0)
+SAVED = 10
 
 
 def forward(gain_shard, shards, tokens, tables, chunks, nx, nz, collective_id):
@@ -751,8 +772,9 @@
     low, wide = jnp.bfloat16, jnp.float32
     dma, vmem = pltpu.SemaphoreType.DMA, pltpu.VMEM
     anywhere = pl.BlockSpec(memory_space=pl.ANY)
-    arrays = [gain_shard if c[0] < 0 else shards[c[0]] for c in chunks]
+    arrays = [gain_shard if weight < 0 else shards[weight] for weight, _ in wholes_of(chunks)]
     ff = shards[4].shape[-1]
+    left = ((rows, 7 * D), low)
     kept = [((rows, D), low), ((rows, QD), wide), ((rows, KEY_FEATURES), wide), ((rows, QD), low)]
     kept += [((2 * m * rows, 2 * KEY_FEATURES), low), ((rows, QD), wide), ((rows, QD), low), ((rows, HEAD_SIZE), wide)]
     kept += [((rows, D), wide), ((rows, D), low), ((rows, ff), wide), ((rows, ff), wide), ((rows, ff), low)]
@@ -761,9 +783,9 @@
         functools.partial(forward_kernel, chunks, nx, nz),
         out_shape=[shape((a.shape[-2] * 2 * nx * nz, a.shape[-1]), low) for a in arrays]
         + [shape((16, D), wide), shape((rows, D), low), shape((rows, D), wide), shape((rows, D), low)]
-        + [shape(*k) for k in kept] * LAYERS,
+        + [shape(*k) for k in [left, *kept[1:6], *kept[7:9], *kept[10:12]]] * LAYERS,
         in_specs=[anywhere] * (2 + len(shards)) + [pl.BlockSpec(memory_space=pltpu.VMEM)] * 4,
-        out_specs=[anywhere] * (count + 4 + SAVED * LAYERS),
+        out_specs=[anywhere] * (len(arrays) + 4 + SAVED * LAYERS),
         scratch_shapes=[
             dma((count,)),
             dma((count, nz)),
@@ -783,11 +805,11 @@
             vmem((LAYERS, *kept[4][0]), low),
             *[vmem(*k) for k in kept[5:]],
             vmem((rows, D), low),
-            vmem((4, D, WIDE_TILE), low),
+            vmem((6, D, WIDE_TILE), low),
             vmem((2, QD, NARROW_TILE), low),
             vmem((2, ff, NARROW_TILE), low),
-            dma((8,)),
-            dma((LAYERS, SAVED)),
+            dma((10,)),
+            dma((LAYERS, len(SAVE_TO))),
             dma((7,)),
             dma((LAYERS, CHUNKS, m)),
             dma((LAYERS, CHUNKS, m)),
@@ -798,8 +820,8 @@
             collective_id=collective_id, has_side_effects=True, vmem_limit_bytes=56 * 1024 * 1024
         ),
     )(gain_shard, *shards, tokens, *tables)
-    wholes, outs = outs[:count], outs[count:]
-    return wholes, outs[:4], [outs[4 + n * SAVED : 4 + (n + 1) * SAVED] for n in range(LAYERS)]
+    wholes, outs = outs[: len(arrays)], outs[len(arrays) :]
+    return dict(zip(wholes_of(chunks), wholes)), outs[:4], [outs[4 + n * SAVED : 4 + (n + 1) * SAVED] for n in range(LAYERS)]
 
 
 SLOTS = 4
@@ -826,7 +848,8 @@
 
 
 def reduce_kernel(nx, nz, layers, *refs):
-    per = 4 + 4 + 7 + 1
+    per = 1 + 1 + 7
+    held, refs = refs[0], refs[1:]
     operands, refs = refs[: layers * per], refs[layers * per :]
     gains, refs = refs[0], refs[1:]
     outs, refs = refs[: len(WEIGHT_BLOCKS)], refs[len(WEIGHT_BLOCKS) :]
@@ -866,11 +889,12 @@
 
     def left_copies(k, layer, sources):
         span = nz * LEFT_BLOCKS[k] * rows
+        base = sum(LEFT_BLOCKS[:k]) * wide
         sems = layer * 4 + k
         for whose, source in zip((0, 2), sources):
 
             def columns(xs, of_core):
-                return source.at[:, pl.ds(pl.multiple_of((xs * 2 + of_core) * span, 128), span)]
+                return source.at[:, pl.ds(pl.multiple_of(base + (xs * 2 + of_core) * span, 128), span)]
 
             for xs in range(nx):
                 yield pltpu.make_async_copy(
@@ -902,8 +926,7 @@
     def fetch(i):
         for layer in range(layers):
             mine = operands[layer * per : (layer + 1) * per]
-            lefts, their_lefts = mine[:4], mine[4:8]
-            down, output, gate, up, query, key, value, their_down = mine[8:]
+            lefts, their_lefts, down, output, gate, up, query, key, value = mine
             blocks = [((down, 0), (down, 0)), ((output, 0), (output, 0))]
             blocks += [((gate, n), (up, n)) for n in range(3)]
             blocks += [((query, 0), (key, 0)), ((query, 1), (value, 0))]
@@ -911,7 +934,7 @@
 
                 @pl.when(i == layer * PIECES + RIGHT_FIRST[n])
                 def _():
-                    fetch_block(layer, n, lefts, their_lefts, blocks[n], their_down)
+                    fetch_block(layer, n, lefts, their_lefts, blocks[n], held)
 
     def fetch_block(layer, n, lefts, their_lefts, block, their_down):
         b = layer * RIGHTS + n
@@ -922,17 +945,17 @@
                 here, there = (
                     source.at[:, pl.ds(at * wide, wide)] for source, at in (block[replica], block[1 - replica])
                 )
-                if n > 0:
+                if n > 0 or layer > 0:
                     replica_right(b, there).start()
                 own_right(b, here).start()
                 pair_right(b, here).start()
 
-        if n == 0:
+        if n == 0 and layer == 0:
             held_right(b, their_down).start()
             passed_right(b, their_down).start()
         for k, first in enumerate(LEFT_FIRST):
             if first == RIGHT_FIRST[n]:
-                for copy in left_copies(k, layer, (lefts[k], their_lefts[k])):
+                for copy in left_copies(k, layer, (lefts, their_lefts)):
                     copy.start()
 
     def place(i):
@@ -947,12 +970,12 @@
             hit = hit | (j == value)
         return hit
 
-    some_right = operands[8]
+    some_right = operands[2]
 
     def forward(i):
         layer, j = place(i)
 
-        @pl.when(any_of(j, RIGHT_FIRST[1:]))
+        @pl.when(any_of(j, RIGHT_FIRST) & (i > 0))
         def _():
             b = layer * RIGHTS + right_block(j)
             replica_right(b, some_right).wait_recv()
@@ -965,7 +988,7 @@
 
             @pl.when(j == first)
             def _():
-                for copy in left_copies(k, layer, (operands[k], operands[k])):
+                for copy in left_copies(k, layer, operands[:2]):
                     copy.wait()
 
                 for who in range(4):
@@ -980,11 +1003,11 @@
             pair_right(b, some_right).wait()
             passed_right(b, some_right).wait()
 
-        @pl.when(j == 0)
+        @pl.when(i == 0)
         def _():
             held_right(b, some_right).wait()
 
-        @pl.when(any_of(j, RIGHT_FIRST[1:]))
+        @pl.when(any_of(j, RIGHT_FIRST) & (i > 0))
         def _():
             replica_right(b, some_right).wait_send()
 
@@ -1107,7 +1130,7 @@
                 @pl.when((j == n) & (replica == r))
                 def _():
                     which, part, column = piece_place(n, r)
-                    into = outs[which].at[layer, pl.ds(part * rows, rows), pl.ds(column * width, width)]
+                    into = outs[which].at[layers - 1 - layer, pl.ds(part * rows, rows), pl.ds(column * width, width)]
                     result_copy(i, r, into).start()
 
     def result_kept(i):
@@ -1232,10 +1255,10 @@
     result_kept(pieces - 1)
 
 
-def reduce_weights(operands, gains, nx, nz, collective_id):
+def reduce_weights(operands, held, gains, nx, nz, collective_id):
     layers = len(operands)
     flat = [a for layer in operands for a in layer]
-    tokens, wide = operands[0][8].shape
+    tokens, wide = held.shape
     rows, width = wide // (2 * nx * nz), wide // 2
     pieces = layers * PIECES
     ring = 2 * nx + nz + 1
@@ -1249,7 +1272,7 @@
             jax.ShapeDtypeStruct((layers, rows * below, wide * across), jnp.float32) for across, below in WEIGHT_BLOCKS
         ]
         + [jax.ShapeDtypeStruct(gains.shape, gains.dtype)],
-        in_specs=[anywhere] * (len(flat) + 1),
+        in_specs=[anywhere] * (len(flat) + 2),
         out_specs=[anywhere] * (len(WEIGHT_BLOCKS) + 1),
         scratch_shapes=[pltpu.VMEM((4, layers, nx, tokens, nz * n * rows), low) for n in LEFT_BLOCKS]
         + [
@@ -1277,7 +1300,7 @@
         compiler_params=pltpu.CompilerParams(
             collective_id=collective_id, has_side_effects=True, vmem_limit_bytes=56 * 1024 * 1024
         ),
-    )(*flat, gains)
+    )(held, *flat, gains)
 
 
 def segment_of(doc_ends, token_index):
@@ -1345,22 +1368,20 @@
     gain_first, gain_second = gains[which_layer], gains[2 + which_layer]
     gain_query, gain_key = gains[4 + which_layer, :HEAD_SIZE], gains[6 + which_layer, :HEAD_SIZE]
     (
-        normalized_rows,
+        lefts,
         query_proj,
         key_projection,
         query_rows,
         keys_values,
         attended_rows,
-        attended_low,
         log_sum,
         hidden_mid,
-        normed_two,
         gate_pre,
         upward,
-        activated,
     ) = saved
     branch_low = upstream.astype(jnp.bfloat16)
-    waiting.append(over_replica(branch_low))
+    if which_layer == LAYERS - 1:
+        waiting.append(over_replica(branch_low))
     grad_act = product_back(branch_low, down_weight)
     ignored, swiglu_back = jax.vjp(swiglu, gate_pre, upward)
     grad_gate_pre, grad_upward = swiglu_back(grad_act)
@@ -1372,8 +1393,8 @@
     upstream_mid = upstream + grad_mid
     attn_low = upstream_mid.astype(jnp.bfloat16)
     grad_attended = product_back(attn_low, output_weight).astype(jnp.bfloat16)
-    ready = 0 if which_layer == 1 else 4
-    grad_attended, waiting[:ready] = after(grad_attended, waiting[:ready])
+    if which_layer == 0:
+        grad_attended, waiting[:1] = after(grad_attended, waiting[:1])
     query_low, key_low, value_low, head_gains = attend_back(
         m,
         query_rows,
@@ -1388,17 +1409,14 @@
         *tables,
         3,
     )
-    ready = 3 if which_layer == 1 else 8
-    query_low, waiting[:ready] = after(query_low, waiting[:ready])
     grad_normed = product_back(query_low, query_weight)
     grad_normed = grad_normed + product_back(key_low, key_matrix)
     grad_normed = grad_normed + product_back(value_low, value_matrix)
     ignored, first_back = jax.vjp(rms_scale, hidden, gain_first)
     grad_hidden, grad_gain_first = first_back(grad_normed)
-    lefts = (activated, attended_low, normed_two, normalized_rows)
     rights = (branch_low, attn_low, gate_low, up_low, query_low, key_low, value_low)
-    gains = (grad_gain_first, head_gains[0], head_gains[1], grad_gain_second)
-    return (upstream_mid + grad_hidden, (lefts, rights, gains))
+    gain_grads = (grad_gain_first, head_gains[0], head_gains[1], grad_gain_second)
+    return (upstream_mid + grad_hidden, (lefts, rights, gain_grads))
 
 
 def near_rows(rows, share):
@@ -1406,7 +1424,8 @@
 
 
 NEAR_SHARES = (0.75, 0.75, 0.75, 0.6, 0.5, 0.75, 0.55)
-ARRIVAL = [(weight, layer) for layer in range(LAYERS) for weight in range(7)]
+CUTS = (2, 1, 1, 2, 3, 3, 2)
+ARRIVAL = [(weight, layer) for layer in range(LAYERS) for weight in (1, 2, 0, 3, 4, 5, 6)]
 
 
 def run_forward(tokens, tables, weights, gains):
@@ -1416,23 +1435,25 @@
     for row, parts in ((0, gains[:2]), (4, gains[2:])):
         part = jnp.concatenate(parts)
         block = lax.dynamic_update_slice(block, part, (row, here * part.shape[1]))
-    chunks = [(-1, 0, 16, 16)]
+    chunks = [(-1, 0, 0, D, 16, 16)]
     for weight, layer in ARRIVAL:
-        rows = weights[weight].shape[1]
-        chunks.append((weight, layer, rows, near_rows(rows, NEAR_SHARES[weight])))
+        rows, columns = weights[weight].shape[1:]
+        near = near_rows(rows, NEAR_SHARES[weight])
+        width = columns // CUTS[weight]
+        for n in range(CUTS[weight]):
+            chunks.append((weight, layer, n * width, width, rows, near))
     wholes, outs, saved = forward(block, weights, tokens, tables, tuple(chunks), nx, nz, 0)
-    by_place = dict(zip(ARRIVAL, wholes[1:]))
-    gathered = [[by_place[weight, layer] for weight in range(7)] for layer in range(LAYERS)]
+    gathered = [[wholes[weight, layer] for weight in range(7)] for layer in range(LAYERS)]
     return gathered, outs, saved
 
 
-def weight_gradients(operands):
+def weight_gradients(operands, held):
     nx, nz = lax.axis_size("shard") // 2, lax.axis_size("ctx")
     shards = 2 * nx * nz
     flat = jnp.concatenate([g for _, gains in operands for g in gains])
     size = -(-flat.shape[0] // 1024) * 1024
     padded = jnp.zeros((size,), flat.dtype).at[: flat.shape[0]].set(flat).reshape(-1, 128)
-    *grads, summed = reduce_weights([members for members, _ in operands], padded, nx, nz, 1)
+    *grads, summed = reduce_weights([members for members, _ in operands[::-1]], held, padded, nx, nz, 1)
     summed = summed.reshape(-1)[: flat.shape[0]].reshape(LAYERS, -1)
     here = lax.axis_index("shard") * nz + lax.axis_index("ctx")
     small, used = [], 0
@@ -1492,9 +1513,7 @@
     cotangent = swap(cotangent)
     output = swap(last)[None]
     hiddens = (tokens.astype(jnp.float32), hidden)
-    waiting = []
-    for normed, _, _, _, _, _, attended, _, _, normed_two, _, _, activated in saved:
-        waiting += [over_replica(a) for a in (normed, attended, normed_two, activated)]
+    waiting = [over_replica(lefts) for lefts, *_ in saved]
     live_mask = (token_segment < doc_lengths.shape[0]).astype(jnp.float32)
     upstream = cotangent[0].astype(jnp.float32) * live_mask[:, None]
     operands = [None] * LAYERS
@@ -1511,11 +1530,9 @@
             waiting,
         )
     grad_tokens = swap(upstream.astype(jnp.bfloat16))[None]
-    for which_layer, (lefts, rights, gains) in enumerate(operands):
-        normed, attended, normed_two, activated = waiting[which_layer * 4 : which_layer * 4 + 4]
-        theirs = (activated, attended, normed_two, normed)
-        operands[which_layer] = (lefts + theirs + rights + (waiting[9 - which_layer],), gains)
-    return (output, grad_tokens) + weight_gradients(operands)
+    for which_layer, (lefts, rights, layer_gains) in enumerate(operands):
+        operands[which_layer] = ((lefts, waiting[which_layer]) + rights, layer_gains)
+    return (output, grad_tokens) + weight_gradients(operands, waiting[-1])
 
 
 def solution(mesh):

time: 674 us -> 650 us (0.964)
  Pallas kernels: 554 us -> 545 us
    pallas_call x1, Pallas kernels: 294 us -> 282 us  [forward(): pl.pallas_call(functools.partial(forward_kernel, chunks, nx, nz), out_sha...]
    unnamed x156 -> x132, local copies, waits for them, and re-layouts: 14.5 us -> 15 us
    ppermute x10 -> x3, waiting for transfers between devices: 21.1 us -> 20.7 us  [over_replica(): return lax.ppermute(values, 'rep', [(0, 1), (1, 0)])]
  transfers between devices with their start and end apart: 14 -> 7, of which waited for: 4 -> 1; matrix products, arithmetic and copies ran while one was open for 8% -> 7% of each run, Pallas kernels for 84% -> 85%
where the time goes in v6:
time: 650 us; the launch traced here: 641 us
  Pallas kernels  545 us (84%)
  matrix products  32.3 us (5%)
  local copies, waits for them, and re-layouts  21.6 us (3%)
  waiting for transfers between devices  20.8 us (3%)
  starting transfers between devices  10.5 us (2%)
  other arithmetic  8.41 us (1%)
    pallas_call x1, Pallas kernels, forward(): pl.pallas_call(functools.partial(forward_kernel, chunks, nx, nz), out_sha...  282 us
    pallas_call x1, Pallas kernels, reduce_weights(): pl.pallas_call(functools.partial(reduce_kernel, nx, nz, layers), out_shap...  203 us
    pallas_call x2, Pallas kernels, attend_back(): pl.pallas_call(functools.partial(attend_back_kernel, m), out_shape=[jax.S...  60.2 us
    dot_general x14, matrix products, product_back(): lax.dot_general(grad, right, (((1,), (1,)), ((), ())), preferred_element_...  32.3 us
    ppermute x3, waiting for transfers between devices, over_replica(): return lax.ppermute(values, 'rep', [(0, 1), (1, 0)])  20.7 us
    unnamed x132, local copies, waits for them, and re-layouts  15 us
  transfers between devices with their start and end apart: 7, of which 1 were waited for; matrix products, arithmetic and copies ran while one was open for 7% of the time, Pallas kernels for 85%

profile of v6, /device:TPU:0, one launch (start us, length us, event | category | flops | bytes accessed | tf_op | source)
XLA Modules:
  0.0 640.8 jit_solution(3048136247175005038)
XLA Ops:
  0.6 1.3 collective-permute-start
  2.0 1.6 collective-permute-start.2
  3.6 0.7 pad_maximum_fusion.2
  4.3 0.7 pad_maximum_fusion.3
  6.2 0.8 copy.31.refs_11_.place_q
  8.0 0.8 pad_maximum_fusion
  8.8 282.2 %shard_map.237 = (bf16[256,1024]{1,0:T(8,128)(2,1)}, bf16[1024,1024]{1,0:T(8,128)(2,1)}, bf16[1024,1024]{1,0:T(8,128)(2,1)}, bf16[1024,2048]{1,0:T(8,128)(2,1)},...) custom-call(bf16[16,1024]{1,0:T(8,128)(2,1)} %copy-done.46, ...), custom_call_target="tpu_custom_call" | custom-call | tf_op jit(solution)/shard_map/pallas_call | solution.py:782
  291.0 1.4 multiply_reduce_fusion.8
  292.5 0.8 fusion.28
  293.3 1.3 multiply_reduce_fusion.6
  294.6 1.3 multiply_reduce_fusion.4
  296.2 2.0 collective-permute-start.6
  298.2 4.6 collective-permute-start.1
  302.8 0.9 fusion.27
  304.1 6.6 %multiply_convert_fusion.1 = (bf16[192,3072]{1,0:T(8,128)(2,1)S(1)}, bf16[192,3072]{1,0:T(8,128)(2,1)S(1)}) fusion(f32[192,3072]{1,0:T(8,128)S(1)} %copy-done.49, f32[192,3072]{1,0:T(8,128)} %get-tuple-element.83, bf16[192,1024]{1,0:T(8,128)(2,1)S(1)} %fusion.15.refs_3_, bf16[3072,1024]{1,0:T(8,128)(2,1)} %get-tuple-element.82), kind=kOutput, calls=%fused_computation.12 | convolution fusion | flops 1216217088 | bytes 13762560 | tf_op jit(solution)/shard_map/dot_general | solution.py:1346
  310.8 2.2 fusion.29
  313.0 2.4 multiply_reduce_fusion
  315.9 1.5 convolution_convert_fusion.1.d_att
  317.9 29.9 %shard_map.238 = (bf16[192,2048]{1,0:T(8,128)(2,1)S(1)}, bf16[192,1024]{1,0:T(8,128)(2,1)S(1)}, bf16[192,1024]{1,0:T(8,128)(2,1)S(1)}, f32[8,128]{1,0:T(8,128)S(1)}) custom-call(bf16[192,2048]{1,0:T(8,128)(2,1)S(1)} %copy-done.14, bf16[768,2048]{1,0:T(8,128)(2,1)} %get-tuple-element.90.kv, bf16[192,2048]{1,0:T(8,128)(2,1)S(1)} %convolution_convert_fusion.1.d_att, ...), custom_call_target="tpu_custom_call" | custom-call | tf_op jit(solution)/shard_map/pallas_call | solution.py:198
  347.9 1.5 fusion.30
  350.0 0.8 convolution_add_fusion.3
  351.4 1.1 multiply_reduce_fusion.1
  353.1 1.4 copy-done.47
  354.5 6.4 multiply_convert_fusion
  360.9 2.2 fusion.31
  363.2 2.4 multiply_reduce_fusion.2
  366.0 1.5 convolution_convert_fusion.d_att
  367.9 30.3 %shard_map.239 = (bf16[192,2048]{1,0:T(8,128)(2,1)S(1)}, bf16[192,1024]{1,0:T(8,128)(2,1)S(1)}, bf16[192,1024]{1,0:T(8,128)(2,1)S(1)}, f32[8,128]{1,0:T(8,128)S(1)}) custom-call(bf16[192,2048]{1,0:T(8,128)(2,1)S(1)} %copy-done.12, bf16[768,2048]{1,0:T(8,128)(2,1)} %get-tuple-element.110.kv, bf16[192,2048]{1,0:T(8,128)(2,1)S(1)} %convolution_convert_fusion.d_att, ...), custom_call_target="tpu_custom_call" | custom-call | tf_op jit(solution)/shard_map/pallas_call | solution.py:198
  398.3 1.5 fusion.32
  400.4 0.8 convolution_add_fusion.1
  401.6 1.1 fusion.14
  403.0 0.7 collective-permute-start.4
  403.8 0.6 pad_bitcast_fusion.refs_19_
  404.4 20.7 %collective-permute-done.5.refs_0_ = bf16[192,1024]{1,0:T(8,128)(2,1)} collective-permute-done((bf16[192,1024]{1,0:T(8,128)(2,1)S(1)}, bf16[192,1024]{1,0:T(8,128)(2,1)}, u32[]{:S(2)}, u32[]{:S(2)}) %collective-permute-start.5) | collective-permute-done | bytes 393248 | tf_op jit(solution)/shard_map/ppermute | solution.py:1350
  425.1 202.7 %shard_map.240 = (f32[2,192,1024]{2,1,0:T(8,128)}, f32[2,128,1024]{2,1,0:T(8,128)}, f32[2,64,3072]{2,1,0:T(8,128)}, f32[2,64,3072]{2,1,0:T(8,128)}, f32[2,64,204...) custom-call(bf16[192,1024]{1,0:T(8,128)(2,1)} %collective-permute-done.5.refs_0_, ...), custom_call_target="tpu_custom_call" | custom-call | tf_op jit(solution)/shard_map/pallas_call | solution.py:1269
  627.9 0.9 reshape.162
  628.7 0.6 constant_dynamic-slice_fusion.1
  629.4 0.6 constant_dynamic-slice_fusion
  630.0 1.8 copy.52
  631.8 0.7 copy.53
  632.6 1.0 copy.54
  633.6 0.8 copy.55
  634.4 0.8 copy.56
  635.2 1.0 copy.57
  636.1 1.1 copy.58
  637.3 1.1 copy.59
  638.4 0.8 copy-done.35
  639.2 1.1 copy.60
  (164 shorter events, 7.2 us)
Async XLA Ops:
  0.6 5.0 collective-permute-start
  2.0 301.8 %collective-permute-start.2 = (bf16[1,192,1024]{2,1,0:T(8,128)(2,1)}, bf16[1,192,1024]{2,1,0:T(8,128)(2,1)S(1)}, u32[]{:S(2)}, u32[]{:S(2)}) collective-permute-start(bf16[1,192,1024]{2,1,0:T(8,128)(2,1)} %param.29), channel_id=1, source_target_pairs={{4,2},{2,4},{0,0},{6,6},{5,3},{3,5},{1,1},{7,7},{12,10},{10,12},{8... | collective-permute-start | bytes 1179656 | tf_op jit(solution)/shard_map/ppermute | solution.py:1495
  5.7 3.1 copy-start.46
  291.0 5.0 copy-start.27
  291.0 13.0 %copy-start.49 = (f32[192,3072]{1,0:T(8,128)S(1)}, f32[192,3072]{1,0:T(8,128)}, u32[]{:S(2)}) copy-start(f32[192,3072]{1,0:T(8,128)} %get-tuple-element.84) | copy-start | bytes 7077892
  295.9 71.7 %collective-permute-start.3 = (bf16[192,7168]{1,0:T(8,128)(2,1)}, bf16[192,7168]{1,0:T(8,128)(2,1)S(1)}, u32[]{:S(2)}, u32[]{:S(2)}) collective-permute-start(bf16[192,7168]{1,0:T(8,128)(2,1)} %get-tuple-element.112.refs_10_), channel_id=1, source_target_pairs={{0,16},{16,0},{1,17},{17,1},{2,18},{18,2},{3,19},{19,3},{4,20},{20... | collective-permute-start | bytes 8257544 | tf_op jit(solution)/shard_map/ppermute | solution.py:1350
  296.2 128.9 %collective-permute-start.6 = (bf16[192,7168]{1,0:T(8,128)(2,1)}, bf16[192,7168]{1,0:T(8,128)(2,1)}, u32[]{:S(2)}, u32[]{:S(2)}) collective-permute-start(bf16[192,7168]{1,0:T(8,128)(2,1)} %get-tuple-element.125.refs_1_), channel_id=1, source_target_pairs={{0,16},{16,0},{1,17},{17,1},{2,18},{18,2},{3,19},{19,3},{4,20},{20... | collective-permute-start | bytes 8257544 | tf_op jit(solution)/shard_map/ppermute | solution.py:1350
  298.2 69.4 %collective-permute-start.1 = (bf16[192,1024]{1,0:T(8,128)(2,1)}, bf16[192,1024]{1,0:T(8,128)(2,1)}, u32[]{:S(2)}, u32[]{:S(2)}) collective-permute-start(bf16[192,1024]{1,0:T(8,128)(2,1)} %get-tuple-element.81), channel_id=1, source_target_pairs={{4,2},{2,4},{0,0},{6,6},{5,3},{3,5},{1,1},{7,7},{12,10},{10,12},{8... | collective-permute-start | bytes 1179656 | tf_op jit(solution)/shard_map/ppermute | solution.py:1495
  303.8 7.0 %slice-start.6 = ((s8[6291456]{0:T(1024)(128)(4,1)}), s8[4194304]{0:T(1024)(128)(4,1)S(1)}, s32[]{:S(2)}) async-start(s8[6291456]{0:T(1024)(128)(4,1)} %bitcast.71), calls=%async_computation.6 | async-start | bytes 8388608
  303.8 9.2 %slice-start.2 = ((s8[6291456]{0:T(1024)(128)(4,1)}), s8[4194304]{0:T(1024)(128)(4,1)S(1)}, s32[]{:S(2)}) async-start(s8[6291456]{0:T(1024)(128)(4,1)} %bitcast.55), calls=%async_computation.2 | async-start | bytes 8388608
  303.9 6.8 %copy-start.38 = (bf16[192,1024]{1,0:T(8,128)(2,1)}, bf16[192,1024]{1,0:T(8,128)(2,1)S(1)}, u32[]{:S(2)}) copy-start(bf16[192,1024]{1,0:T(8,128)(2,1)S(1)} %fusion.15.refs_3_) | copy-start | bytes 1179652
  303.9 121.2 %collective-permute-start.5 = (bf16[192,1024]{1,0:T(8,128)(2,1)S(1)}, bf16[192,1024]{1,0:T(8,128)(2,1)}, u32[]{:S(2)}, u32[]{:S(2)}) collective-permute-start(bf16[192,1024]{1,0:T(8,128)(2,1)S(1)} %fusion.15.refs_3_), channel_id=1, source_target_pairs={{0,16},{16,0},{1,17},{17,1},{2,18},{18,2},{3,19},{19,3},{4,20},{20... | collective-permute-start | bytes 1179656 | tf_op jit(solution)/shard_map/ppermute | solution.py:1350
  304.1 6.7 %slice-start.7 = ((s8[6291456]{0:T(1024)(128)(4,1)}), s8[2097152]{0:T(1024)(128)(4,1)S(1)}, s32[]{:S(2)}) async-start(s8[6291456]{0:T(1024)(128)(4,1)} %bitcast.71), calls=%async_computation.7 | async-start | bytes 4194304
  304.1 8.9 %slice-start.3 = ((s8[6291456]{0:T(1024)(128)(4,1)}), s8[2097152]{0:T(1024)(128)(4,1)S(1)}, s32[]{:S(2)}) async-start(s8[6291456]{0:T(1024)(128)(4,1)} %bitcast.55), calls=%async_computation.3 | async-start | bytes 4194304
  310.7 2.3 copy-start.40
  310.7 2.3 copy-start.21
  310.7 2.3 copy-start.18
  313.0 2.8 copy-start.26
  315.9 2.1 copy-start.14
  315.9 2.1 copy-start.16
  315.9 2.1 copy-start.17
  317.9 30.0 %copy-start.25 = (bf16[1024,2048]{1,0:T(8,128)(2,1)S(1)}, bf16[1024,2048]{1,0:T(8,128)(2,1)}, u32[]{:S(2)}) copy-start(bf16[1024,2048]{1,0:T(8,128)(2,1)} %get-tuple-element.97) | copy-start | bytes 12582916
  347.9 3.0 copy-start.7
  347.9 2.1 copy-start.34
  349.5 2.0 copy-start.33
  352.5 8.4 %slice-start.4 = ((s8[6291456]{0:T(1024)(128)(4,1)}), s8[4194304]{0:T(1024)(128)(4,1)S(1)}, s32[]{:S(2)}) async-start(s8[6291456]{0:T(1024)(128)(4,1)} %bitcast.69), calls=%async_computation.4 | async-start | bytes 8388608
  352.5 10.6 %slice-start = ((s8[6291456]{0:T(1024)(128)(4,1)}), s8[4194304]{0:T(1024)(128)(4,1)S(1)}, s32[]{:S(2)}) async-start(s8[6291456]{0:T(1024)(128)(4,1)} %bitcast.53), calls=%async_computation | async-start | bytes 8388608
  352.8 8.1 %copy-start.39 = (bf16[192,1024]{1,0:T(8,128)(2,1)}, bf16[192,1024]{1,0:T(8,128)(2,1)S(1)}, u32[]{:S(2)}) copy-start(bf16[192,1024]{1,0:T(8,128)(2,1)S(1)} %get-tuple-element.147.refs_12_) | copy-start | bytes 1179652
  354.5 6.4 %slice-start.5 = ((s8[6291456]{0:T(1024)(128)(4,1)}), s8[2097152]{0:T(1024)(128)(4,1)S(1)}, s32[]{:S(2)}) async-start(s8[6291456]{0:T(1024)(128)(4,1)} %bitcast.69), calls=%async_computation.5 | async-start | bytes 4194304
  354.5 8.7 %slice-start.1 = ((s8[6291456]{0:T(1024)(128)(4,1)}), s8[2097152]{0:T(1024)(128)(4,1)S(1)}, s32[]{:S(2)}) async-start(s8[6291456]{0:T(1024)(128)(4,1)} %bitcast.53), calls=%async_computation.1 | async-start | bytes 4194304
  360.9 2.3 copy-start.41
  360.9 2.3 copy-start.22
  360.9 2.3 copy-start.19
  363.2 2.7 copy-start.24
  366.0 2.0 copy-start.12
  366.0 2.0 copy-start.15
  367.5 30.7 %copy-start.30 = (bf16[192,7168]{1,0:T(8,128)(2,1)}, bf16[192,7168]{1,0:T(8,128)(2,1)S(1)}, u32[]{:S(2)}) copy-start(bf16[192,7168]{1,0:T(8,128)(2,1)S(1)} %collective-permute-done.3.refs_11_) | copy-start | bytes 8257540
  367.9 30.3 %copy-start.23 = (bf16[1024,2048]{1,0:T(8,128)(2,1)S(1)}, bf16[1024,2048]{1,0:T(8,128)(2,1)}, u32[]{:S(2)}) copy-start(bf16[1024,2048]{1,0:T(8,128)(2,1)} %get-tuple-element.119) | copy-start | bytes 12582916
  398.2 3.0 copy-start.10
  398.3 2.1 copy-start.32
  403.0 227.0 %collective-permute-start.4 = (bf16[192,1024]{1,0:T(8,128)(2,1)S(1)}, bf16[192,1024]{1,0:T(8,128)(2,1)S(1)}, u32[]{:S(2)}, u32[]{:S(2)}) collective-permute-start(bf16[192,1024]{1,0:T(8,128)(2,1)S(1)} %fusion.10), channel_id=1, source_target_pairs={{4,2},{2,4},{0,0},{6,6},{5,3},{3,5},{1,1},{7,7},{12,10},{10,12},{8... | collective-permute-start | bytes 1179656 | tf_op jit(solution)/shard_map/ppermute | solution.py:1495
  627.8 4.7 copy-start.43
  627.8 5.7 copy-start.45
  630.0 4.3 copy-start.44
  631.8 3.3 copy-start.42
  633.6 2.6 copy-start.37
  635.2 2.1 copy-start.36
  637.3 2.0 copy-start.35
  (17 other events, 28.2 us)

commit v7 on v6

--- a/solution.py
+++ b/solution.py
@@ -26,6 +26,9 @@
 CHUNK_HEADS = 2
 CHUNKS = KEYVALUE_HEADS // CHUNK_HEADS
 CHUNK = CHUNK_HEADS * HEAD_SIZE
+BACK_HEADS = 2
+BACK_CHUNKS = KEYVALUE_HEADS // BACK_HEADS
+BACK_WIDTH = BACK_HEADS * HEAD_SIZE
 GROUP = QUERY_HEADS // KEYVALUE_HEADS
 SCORE_SCALE = 1.0 / math.sqrt(HEAD_SIZE)
 
@@ -105,12 +108,14 @@
         partial[j, core, place] = (partial[j, core, place].astype(jnp.float32) + value.astype(jnp.float32)).astype(partial.dtype)
 
     def compute(j):
-        for n in range(CHUNK_HEADS):
-            keys = kv[:, pl.ds(pl.multiple_of(j * 2 * CHUNK + n * HEAD_SIZE, 128), HEAD_SIZE)]
-            values = kv[:, pl.ds(pl.multiple_of(j * 2 * CHUNK + CHUNK + n * HEAD_SIZE, 128), HEAD_SIZE)]
+        for n in range(BACK_HEADS):
+            one = j * BACK_HEADS + n
+            first = lax.div(one, CHUNK_HEADS) * 2 * CHUNK + lax.rem(one, CHUNK_HEADS) * HEAD_SIZE
+            keys = kv[:, pl.ds(pl.multiple_of(first, 128), HEAD_SIZE)]
+            values = kv[:, pl.ds(pl.multiple_of(first + CHUNK, 128), HEAD_SIZE)]
             dk = dv = None
             for g in range(GROUP):
-                h = (j * CHUNK_HEADS + n) * GROUP + g
+                h = one * GROUP + g
                 at = pl.ds(pl.multiple_of(h * HEAD_SIZE, 128), HEAD_SIZE)
                 queries, grad = q[:, at], d_att[:, at]
                 total = jnp.sum(jnp.where(lane == h, lse[...], 0.0), axis=-1, keepdims=True)
@@ -129,7 +134,7 @@
                 gains[0:1] += by_gain
             first = n * HEAD_SIZE
             partial[j, :, :, :, first : first + HEAD_SIZE] = (dk * SCORE_SCALE).astype(partial.dtype).reshape(2, m, tokens, HEAD_SIZE)
-            first += CHUNK
+            first += BACK_WIDTH
             partial[j, :, :, :, first : first + HEAD_SIZE] = dv.astype(partial.dtype).reshape(2, m, tokens, HEAD_SIZE)
         core_copy(j).start()
 
@@ -153,14 +158,14 @@
                     line_copy(j, up, here).start()
 
     def finish(j):
-        for n in range(CHUNK_HEADS):
-            at = pl.ds(pl.multiple_of((j * CHUNK_HEADS + n) * HEAD_SIZE, 128), HEAD_SIZE)
+        for n in range(BACK_HEADS):
+            at = pl.ds(pl.multiple_of((j * BACK_HEADS + n) * HEAD_SIZE, 128), HEAD_SIZE)
             grad = partial[j, core, zz, :, n * HEAD_SIZE : (n + 1) * HEAD_SIZE].astype(jnp.float32)
             by_head, by_gain = head_prepare_back(grad, kp[:, at], k_gain[...], cos, sin)
             dk_low[:, at] = by_head.astype(dk_low.dtype)
             gains[1:2] += by_gain
-        at = pl.ds(pl.multiple_of(j * CHUNK, 128), CHUNK)
-        dv_low[:, at] = partial[j, core, zz, :, CHUNK:]
+        at = pl.ds(pl.multiple_of(j * BACK_WIDTH, 128), BACK_WIDTH)
+        dv_low[:, at] = partial[j, core, zz, :, BACK_WIDTH:]
         core_copy(j).wait_send()
         for here in range(m):
 
@@ -177,17 +182,17 @@
     plan[-1].append(finish)
 
     def tick(t, carry):
-        for depth in [*range(1, len(plan)), 0]:
+        for depth in range(len(plan)):
             j = t - depth
 
-            @pl.when((j >= 0) & (j < CHUNKS))
+            @pl.when((j >= 0) & (j < BACK_CHUNKS))
             def _():
                 for stage in plan[depth]:
                     stage(j)
 
         return carry
 
-    lax.fori_loop(0, CHUNKS + len(plan) - 1, tick, 0)
+    lax.fori_loop(0, BACK_CHUNKS + len(plan) - 1, tick, 0)
 
 
 def attend_back(m, q, kv, d_att, att, lse, qp, kp, q_gain, k_gain, cosine, sine, place_q, segment_k, collective_id):
@@ -206,13 +211,13 @@
         in_specs=[vmem] * 13,
         out_specs=[vmem] * 4,
         scratch_shapes=[
-            pltpu.VMEM((CHUNKS, 2, m, tokens, 2 * CHUNK), low),
-            pltpu.VMEM((CHUNKS, m, tokens, 2 * CHUNK), low),
-            pltpu.VMEM((CHUNKS, max(m - 1, 1), tokens, 2 * CHUNK), low),
-            pltpu.VMEM((CHUNKS, max(m - 1, 1), tokens, 2 * CHUNK), low),
-            dma((2, CHUNKS)),
-            dma((2, CHUNKS)),
-            dma((2, CHUNKS)),
+            pltpu.VMEM((BACK_CHUNKS, 2, m, tokens, 2 * BACK_WIDTH), low),
+            pltpu.VMEM((BACK_CHUNKS, m, tokens, 2 * BACK_WIDTH), low),
+            pltpu.VMEM((BACK_CHUNKS, max(m - 1, 1), tokens, 2 * BACK_WIDTH), low),
+            pltpu.VMEM((BACK_CHUNKS, max(m - 1, 1), tokens, 2 * BACK_WIDTH), low),
+            dma((2, BACK_CHUNKS)),
+            dma((2, BACK_CHUNKS)),
+            dma((2, BACK_CHUNKS)),
         ],
         compiler_params=pltpu.CompilerParams(
             collective_id=collective_id, has_side_effects=True, vmem_limit_bytes=48 * 1024 * 1024
@@ -761,9 +766,9 @@
     pltpu.make_async_copy(last, last_out, misc_sem.at[6]).wait()
 
 
-LEFT_AT = {0: 6, 6: 3, 9: 5, 12: 0}
-SAVE_TO = (0, 1, 2, 3, 4, 5, 0, 6, 7, 0, 8, 9, 0)
-SAVED = 10
+LEFT_AT = {0: 4, 9: 3, 12: 0}
+SAVE_TO = (0, 2, 3, 4, 5, 6, 1, 7, 8, 0, 9, 10, 0)
+SAVED = 11
 
 
 def forward(gain_shard, shards, tokens, tables, chunks, nx, nz, collective_id):
@@ -774,7 +779,7 @@
     anywhere = pl.BlockSpec(memory_space=pl.ANY)
     arrays = [gain_shard if weight < 0 else shards[weight] for weight, _ in wholes_of(chunks)]
     ff = shards[4].shape[-1]
-    left = ((rows, 7 * D), low)
+    lefts = [((rows, ff + 2 * D), low), ((rows, QD), low)]
     kept = [((rows, D), low), ((rows, QD), wide), ((rows, KEY_FEATURES), wide), ((rows, QD), low)]
     kept += [((2 * m * rows, 2 * KEY_FEATURES), low), ((rows, QD), wide), ((rows, QD), low), ((rows, HEAD_SIZE), wide)]
     kept += [((rows, D), wide), ((rows, D), low), ((rows, ff), wide), ((rows, ff), wide), ((rows, ff), low)]
@@ -783,7 +788,7 @@
         functools.partial(forward_kernel, chunks, nx, nz),
         out_shape=[shape((a.shape[-2] * 2 * nx * nz, a.shape[-1]), low) for a in arrays]
         + [shape((16, D), wide), shape((rows, D), low), shape((rows, D), wide), shape((rows, D), low)]
-        + [shape(*k) for k in [left, *kept[1:6], *kept[7:9], *kept[10:12]]] * LAYERS,
+        + [shape(*k) for k in [*lefts, *kept[1:6], *kept[7:9], *kept[10:12]]] * LAYERS,
         in_specs=[anywhere] * (2 + len(shards)) + [pl.BlockSpec(memory_space=pltpu.VMEM)] * 4,
         out_specs=[anywhere] * (len(arrays) + 4 + SAVED * LAYERS),
         scratch_shapes=[
@@ -825,9 +830,11 @@
 
 
 SLOTS = 4
+AHEAD = 6
 PIECES = 15
 LEFT_BLOCKS = (3, 2, 1, 1)
 LEFT_FIRST = (0, 3, 5, 11)
+LEFT_BASE = (0, 0, 3, 4)
 RIGHTS = 7
 RIGHT_FIRST = (0, 3, 5, 7, 9, 11, 13)
 WEIGHT_BLOCKS = ((1, 3), (1, 2), (3, 1), (3, 1), (2, 1), (1, 1), (1, 1))
@@ -848,15 +855,15 @@
 
 
 def reduce_kernel(nx, nz, layers, *refs):
-    per = 1 + 1 + 7
+    per = 2 + 2 + 7
     held, refs = refs[0], refs[1:]
     operands, refs = refs[: layers * per], refs[layers * per :]
     gains, refs = refs[0], refs[1:]
     outs, refs = refs[: len(WEIGHT_BLOCKS)], refs[len(WEIGHT_BLOCKS) :]
     gains_out, left_at, refs = refs[0], refs[1:5], refs[5:]
-    right_at, turned, total, x_in, zup_in, zdown_in, f_in, result, refs = *refs[:8], refs[8:]
+    right_at, turned, total, x_in, zup_in, zdown_in, f_in, result, landed, refs = *refs[:9], refs[9:]
     gain_in, gain_up, gain_down, refs = *refs[:3], refs[3:]
-    left_sem, right_sem, x_sem, zup_sem, zdown_sem, f_sem, result_sem, gain_sem, credit = refs
+    left_sem, right_sem, x_sem, zup_sem, zdown_sem, f_sem, result_sem, gain_sem, landed_sem, credit = refs
     rows, width = total.shape[3:]
     tokens, wide = right_at.shape[2:]
     pieces = layers * PIECES
@@ -889,7 +896,7 @@
 
     def left_copies(k, layer, sources):
         span = nz * LEFT_BLOCKS[k] * rows
-        base = sum(LEFT_BLOCKS[:k]) * wide
+        base = LEFT_BASE[k] * wide
         sems = layer * 4 + k
         for whose, source in zip((0, 2), sources):
 
@@ -923,10 +930,20 @@
     def passed_right(b, source):
         return remote(source, right_at.at[3, b], right_sem.at[6, b], right_sem.at[3, b], to_core)
 
+    def attended_copy(layer, source):
+        return remote(source, landed.at[layer - 1], landed_sem.at[0, layer], landed_sem.at[1, layer], to_y)
+
     def fetch(i):
+        for layer in range(1, layers):
+
+            @pl.when(i == layer * PIECES - AHEAD)
+            def _():
+                attended_copy(layer, operands[layer * per + 1]).start()
+
         for layer in range(layers):
             mine = operands[layer * per : (layer + 1) * per]
-            lefts, their_lefts, down, output, gate, up, query, key, value = mine
+            lefts, their_lefts = mine[:2], mine[2:4]
+            down, output, gate, up, query, key, value = mine[4:]
             blocks = [((down, 0), (down, 0)), ((output, 0), (output, 0))]
             blocks += [((gate, n), (up, n)) for n in range(3)]
             blocks += [((query, 0), (key, 0)), ((query, 1), (value, 0))]
@@ -955,7 +972,12 @@
             passed_right(b, their_down).start()
         for k, first in enumerate(LEFT_FIRST):
             if first == RIGHT_FIRST[n]:
-                for copy in left_copies(k, layer, (lefts, their_lefts)):
+                n_left = 1 if k == 1 else 0
+                theirs = their_lefts[n_left]
+                if k == 1 and layer > 0:
+                    theirs = landed.at[layer - 1]
+                    attended_copy(layer, lefts[1]).wait_recv()
+                for copy in left_copies(k, layer, (lefts[n_left], theirs)):
                     copy.start()
 
     def place(i):
@@ -970,7 +992,7 @@
             hit = hit | (j == value)
         return hit
 
-    some_right = operands[2]
+    some_right = operands[4]
 
     def forward(i):
         layer, j = place(i)
@@ -988,7 +1010,7 @@
 
             @pl.when(j == first)
             def _():
-                for copy in left_copies(k, layer, operands[:2]):
+                for copy in left_copies(k, layer, (operands[int(k == 1)],) * 2):
                     copy.wait()
 
                 for who in range(4):
@@ -1233,7 +1255,7 @@
     for h in range(1, nz):
         plan.append([functools.partial(z_hop, h=h)])
     plan[-1].append(send_f)
-    plan.append([finish])
+    plan += [[], [finish]]
 
     def tick(t, carry):
         for depth in [*range(6, len(plan)), 0, 3, 5]:
@@ -1253,6 +1275,8 @@
     lax.fori_loop(0, pieces + len(plan) - 1, tick, 0)
     result_kept(pieces - 2)
     result_kept(pieces - 1)
+    for layer in range(1, layers):
+        attended_copy(layer, operands[layer * per + 1]).wait_send()
 
 
 def reduce_weights(operands, held, gains, nx, nz, collective_id):
@@ -1261,7 +1285,7 @@
     tokens, wide = held.shape
     rows, width = wide // (2 * nx * nz), wide // 2
     pieces = layers * PIECES
-    ring = 2 * nx + nz + 1
+    ring = 2 * nx + nz + 2
     sides = 1 if nx == 2 else 2
     low = jnp.bfloat16
     dma = pltpu.SemaphoreType.DMA
@@ -1284,6 +1308,7 @@
             pltpu.VMEM((SLOTS, nz - 1, rows, width), low),
             pltpu.VMEM((SLOTS, rows, width), low),
             pltpu.VMEM((2, 2, rows, width), jnp.float32),
+            pltpu.VMEM((layers - 1, tokens, 2 * wide), low),
             pltpu.VMEM((7, *gains.shape), gains.dtype),
             pltpu.VMEM((3, *gains.shape), gains.dtype),
             pltpu.VMEM((3, *gains.shape), gains.dtype),
@@ -1295,6 +1320,7 @@
             dma((2, pieces)),
             dma((2, 2)),
             dma((2, 7)),
+            dma((2, layers)),
             pltpu.SemaphoreType.REGULAR((5,)),
         ],
         compiler_params=pltpu.CompilerParams(
@@ -1369,6 +1395,7 @@
     gain_query, gain_key = gains[4 + which_layer, :HEAD_SIZE], gains[6 + which_layer, :HEAD_SIZE]
     (
         lefts,
+        attended_low,
         query_proj,
         key_projection,
         query_rows,
@@ -1416,7 +1443,7 @@
     grad_hidden, grad_gain_first = first_back(grad_normed)
     rights = (branch_low, attn_low, gate_low, up_low, query_low, key_low, value_low)
     gain_grads = (grad_gain_first, head_gains[0], head_gains[1], grad_gain_second)
-    return (upstream_mid + grad_hidden, (lefts, rights, gain_grads))
+    return (upstream_mid + grad_hidden, ((lefts, attended_low), rights, gain_grads))
 
 
 def near_rows(rows, share):
@@ -1514,6 +1541,7 @@
     output = swap(last)[None]
     hiddens = (tokens.astype(jnp.float32), hidden)
     waiting = [over_replica(lefts) for lefts, *_ in saved]
+    their_attended = over_replica(saved[LAYERS - 1][1])
     live_mask = (token_segment < doc_lengths.shape[0]).astype(jnp.float32)
     upstream = cotangent[0].astype(jnp.float32) * live_mask[:, None]
     operands = [None] * LAYERS
@@ -1531,7 +1559,7 @@
         )
     grad_tokens = swap(upstream.astype(jnp.bfloat16))[None]
     for which_layer, (lefts, rights, layer_gains) in enumerate(operands):
-        operands[which_layer] = ((lefts, waiting[which_layer]) + rights, layer_gains)
+        operands[which_layer] = (lefts + (waiting[which_layer], their_attended) + rights, layer_gains)
     return (output, grad_tokens) + weight_gradients(operands, waiting[-1])
 
 

time: 650 us -> 646 us (level)
  waiting for transfers between devices: 20.8 us -> 0.02 us
  Pallas kernels: 545 us -> 554 us
  matrix products: 32.3 us -> 39.6 us
    ppermute x3 -> x4, waiting for transfers between devices: 20.7 us -> 0.01 us  [over_replica(): return lax.ppermute(values, 'rep', [(0, 1), (1, 0)])]
    pallas_call x1, Pallas kernels: 203 us -> 214 us  [reduce_weights(): pl.pallas_call(functools.partial(reduce_kernel, nx, nz, layers), out_shap...]
    dot_general x14, matrix products: 32.3 us -> 39.6 us  [product_back(): lax.dot_general(grad, right, (((1,), (1,)), ((), ())), preferred_element_...]
    unnamed x132 -> x124, local copies, waits for them, and re-layouts: 15 us -> 14.8 us
  transfers between devices with their start and end apart: 7 -> 8, of which waited for: 1 -> 0; matrix products, arithmetic and copies ran while one was open for 7% -> 9% of each run, Pallas kernels for 85% -> 87%
where the time goes in v7:
time: 646 us; the launch traced here: 637 us
  Pallas kernels  554 us (86%)
  matrix products  39.6 us (6%)
  local copies, waits for them, and re-layouts  21.3 us (3%)
  starting transfers between devices  10.6 us (2%)
  other arithmetic  9.17 us (1%)
    pallas_call x1, Pallas kernels, forward(): pl.pallas_call(functools.partial(forward_kernel, chunks, nx, nz), out_sha...  282 us
    pallas_call x1, Pallas kernels, reduce_weights(): pl.pallas_call(functools.partial(reduce_kernel, nx, nz, layers), out_shap...  214 us
    pallas_call x2, Pallas kernels, attend_back(): pl.pallas_call(functools.partial(attend_back_kernel, m), out_shape=[jax.S...  57.7 us
    dot_general x14, matrix products, product_back(): lax.dot_general(grad, right, (((1,), (1,)), ((), ())), preferred_element_...  39.6 us
    unnamed x124, local copies, waits for them, and re-layouts  14.8 us
  transfers between devices with their start and end apart: 8, of which 0 were waited for; matrix products, arithmetic and copies ran while one was open for 9% of the time, Pallas kernels for 87%

profile of v7, /device:TPU:0, one launch (start us, length us, event | category | flops | bytes accessed | tf_op | source)
XLA Modules:
  0.0 637.1 jit_solution(16497879941486354934)
XLA Ops:
  0.6 1.3 collective-permute-start
  2.0 1.6 collective-permute-start.2
  3.6 0.7 pad_maximum_fusion.2
  4.3 0.7 pad_maximum_fusion.3
  6.2 0.8 copy.31.refs_11_.place_q
  8.0 0.8 pad_maximum_fusion
  8.8 282.2 %shard_map.237 = (bf16[256,1024]{1,0:T(8,128)(2,1)}, bf16[1024,1024]{1,0:T(8,128)(2,1)}, bf16[1024,1024]{1,0:T(8,128)(2,1)}, bf16[1024,2048]{1,0:T(8,128)(2,1)},...) custom-call(bf16[16,1024]{1,0:T(8,128)(2,1)} %copy-done.47, ...), custom_call_target="tpu_custom_call" | custom-call | tf_op jit(solution)/shard_map/pallas_call | solution.py:787
  291.0 1.4 multiply_reduce_fusion.8
  292.5 0.8 fusion.28
  293.3 1.3 multiply_reduce_fusion.6
  294.6 1.3 multiply_reduce_fusion.4
  296.2 2.0 collective-permute-start.6
  298.3 1.8 collective-permute-start.1
  300.1 0.9 fusion.27
  301.2 2.0 collective-permute-start.5
  303.2 7.1 %multiply_convert_fusion.1 = (bf16[192,3072]{1,0:T(8,128)(2,1)S(1)}, bf16[192,3072]{1,0:T(8,128)(2,1)S(1)}) fusion(f32[192,3072]{1,0:T(8,128)} %get-tuple-element.86, f32[192,3072]{1,0:T(8,128)} %get-tuple-element.85, bf16[192,1024]{1,0:T(8,128)(2,1)S(1)} %fusion.15.refs_5_, bf16[3072,1024]{1,0:T(8,128)(2,1)} %get-tuple-element.84), kind=kOutput, calls=%fused_computation.12 | convolution fusion | flops 1216217088 | bytes 13762560 | tf_op jit(solution)/shard_map/dot_general | solution.py:1372
  310.4 5.9 fusion.29
  316.3 2.5 multiply_reduce_fusion
  319.2 1.5 convolution_convert_fusion.1.d_att
  321.2 28.7 %shard_map.238 = (bf16[192,2048]{1,0:T(8,128)(2,1)S(1)}, bf16[192,1024]{1,0:T(8,128)(2,1)S(1)}, bf16[192,1024]{1,0:T(8,128)(2,1)S(1)}, f32[8,128]{1,0:T(8,128)S(1)}) custom-call(bf16[192,2048]{1,0:T(8,128)(2,1)S(1)} %copy-done.14, bf16[768,2048]{1,0:T(8,128)(2,1)} %get-tuple-element.92.kv, bf16[192,2048]{1,0:T(8,128)(2,1)S(1)} %convolution_convert_fusion.1.d_att, ...), custom_call_target="tpu_custom_call" | custom-call | tf_op jit(solution)/shard_map/pallas_call | solution.py:203
  349.9 1.5 fusion.30
  352.1 0.9 convolution_add_fusion.3
  353.5 1.1 multiply_reduce_fusion.1
  355.1 1.4 copy-done.48
  356.5 5.9 multiply_convert_fusion
  362.4 5.9 fusion.31
  368.4 2.4 multiply_reduce_fusion.2
  371.1 1.5 convolution_convert_fusion.d_att
  373.1 29.1 %shard_map.239 = (bf16[192,2048]{1,0:T(8,128)(2,1)S(1)}, bf16[192,1024]{1,0:T(8,128)(2,1)S(1)}, bf16[192,1024]{1,0:T(8,128)(2,1)S(1)}, f32[8,128]{1,0:T(8,128)S(1)}) custom-call(bf16[192,2048]{1,0:T(8,128)(2,1)S(1)} %copy-done.12, bf16[768,2048]{1,0:T(8,128)(2,1)} %get-tuple-element.112.kv, bf16[192,2048]{1,0:T(8,128)(2,1)S(1)} %convolution_convert_fusion.d_att, ...), custom_call_target="tpu_custom_call" | custom-call | tf_op jit(solution)/shard_map/pallas_call | solution.py:203
  402.2 1.5 fusion.32
  404.3 0.9 convolution_add_fusion.1
  405.5 1.1 fusion.14
  406.6 1.0 fusion.10
  407.6 1.6 collective-permute-start.4
  410.0 0.9 copy-done.30
  410.8 214.3 %shard_map.240 = (f32[2,192,1024]{2,1,0:T(8,128)}, f32[2,128,1024]{2,1,0:T(8,128)}, f32[2,64,3072]{2,1,0:T(8,128)}, f32[2,64,3072]{2,1,0:T(8,128)}, f32[2,64,204...) custom-call(bf16[192,1024]{1,0:T(8,128)(2,1)} %collective-permute-done.5.refs_0_, ...), custom_call_target="tpu_custom_call" | custom-call | tf_op jit(solution)/shard_map/pallas_call | solution.py:1293
  625.2 0.9 reshape.162
  626.0 0.6 constant_dynamic-slice_fusion.1
  627.3 0.7 copy.52
  628.1 0.7 copy.53
  628.8 1.0 copy.54
  629.8 0.8 copy.55
  630.6 0.8 copy.56
  631.4 1.0 copy.57
  632.3 1.1 copy.58
  633.5 1.1 copy.59
  634.6 0.8 copy-done.36
  635.5 1.1 copy.60
  (156 shorter events, 8.1 us)
Async XLA Ops:
  0.6 5.0 collective-permute-start
  2.0 299.0 %collective-permute-start.2 = (bf16[1,192,1024]{2,1,0:T(8,128)(2,1)}, bf16[1,192,1024]{2,1,0:T(8,128)(2,1)S(1)}, u32[]{:S(2)}, u32[]{:S(2)}) collective-permute-start(bf16[1,192,1024]{2,1,0:T(8,128)(2,1)} %param.29), channel_id=1, source_target_pairs={{4,2},{2,4},{0,0},{6,6},{5,3},{3,5},{1,1},{7,7},{12,10},{10,12},{8... | collective-permute-start | bytes 1179656 | tf_op jit(solution)/shard_map/ppermute | solution.py:1522
  5.7 3.1 copy-start.47
  291.0 4.8 copy-start.35
  291.0 5.0 copy-start.27
  295.9 76.8 %collective-permute-start.3 = (bf16[192,5120]{1,0:T(8,128)(2,1)S(1)}, bf16[192,5120]{1,0:T(8,128)(2,1)}, u32[]{:S(2)}, u32[]{:S(2)}) collective-permute-start(bf16[192,5120]{1,0:T(8,128)(2,1)S(1)} %copy-done.35), channel_id=1, source_target_pairs={{0,16},{16,0},{1,17},{17,1},{2,18},{18,2},{3,19},{19,3},{4,20},{20... | collective-permute-start | bytes 5898248 | tf_op jit(solution)/shard_map/ppermute | solution.py:1376
  296.2 113.8 %collective-permute-start.6 = (bf16[192,5120]{1,0:T(8,128)(2,1)}, bf16[192,5120]{1,0:T(8,128)(2,1)}, u32[]{:S(2)}, u32[]{:S(2)}) collective-permute-start(bf16[192,5120]{1,0:T(8,128)(2,1)} %get-tuple-element.127.refs_1_), channel_id=1, source_target_pairs={{0,16},{16,0},{1,17},{17,1},{2,18},{18,2},{3,19},{19,3},{4,20},{20... | collective-permute-start | bytes 5898248 | tf_op jit(solution)/shard_map/ppermute | solution.py:1376
  298.2 111.8 %collective-permute-start.7 = (bf16[192,2048]{1,0:T(8,128)(2,1)}, bf16[192,2048]{1,0:T(8,128)(2,1)S(1)}, u32[]{:S(2)}, u32[]{:S(2)}) collective-permute-start(bf16[192,2048]{1,0:T(8,128)(2,1)} %get-tuple-element.128.refs_2_), channel_id=1, source_target_pairs={{0,16},{16,0},{1,17},{17,1},{2,18},{18,2},{3,19},{19,3},{4,20},{20... | collective-permute-start | bytes 2359304 | tf_op jit(solution)/shard_map/ppermute | solution.py:1376
  298.3 74.4 %collective-permute-start.1 = (bf16[192,1024]{1,0:T(8,128)(2,1)}, bf16[192,1024]{1,0:T(8,128)(2,1)S(1)}, u32[]{:S(2)}, u32[]{:S(2)}) collective-permute-start(bf16[192,1024]{1,0:T(8,128)(2,1)} %get-tuple-element.83), channel_id=1, source_target_pairs={{4,2},{2,4},{0,0},{6,6},{5,3},{3,5},{1,1},{7,7},{12,10},{10,12},{8... | collective-permute-start | bytes 1179656 | tf_op jit(solution)/shard_map/ppermute | solution.py:1522
  301.0 15.2 %slice-start.2 = ((s8[6291456]{0:T(1024)(128)(4,1)}), s8[4194304]{0:T(1024)(128)(4,1)S(1)}, s32[]{:S(2)}) async-start(s8[6291456]{0:T(1024)(128)(4,1)} %bitcast.55), calls=%async_computation.2 | async-start | bytes 8388608
  301.1 9.2 %copy-start.39 = (bf16[192,1024]{1,0:T(8,128)(2,1)}, bf16[192,1024]{1,0:T(8,128)(2,1)S(1)}, u32[]{:S(2)}) copy-start(bf16[192,1024]{1,0:T(8,128)(2,1)S(1)} %fusion.15.refs_5_) | copy-start | bytes 1179652
  301.2 108.8 %collective-permute-start.5 = (bf16[192,1024]{1,0:T(8,128)(2,1)S(1)}, bf16[192,1024]{1,0:T(8,128)(2,1)}, u32[]{:S(2)}, u32[]{:S(2)}) collective-permute-start(bf16[192,1024]{1,0:T(8,128)(2,1)S(1)} %fusion.15.refs_5_), channel_id=1, source_target_pairs={{0,16},{16,0},{1,17},{17,1},{2,18},{18,2},{3,19},{19,3},{4,20},{20... | collective-permute-start | bytes 1179656 | tf_op jit(solution)/shard_map/ppermute | solution.py:1376
  303.2 13.1 %slice-start.3 = ((s8[6291456]{0:T(1024)(128)(4,1)}), s8[2097152]{0:T(1024)(128)(4,1)S(1)}, s32[]{:S(2)}) async-start(s8[6291456]{0:T(1024)(128)(4,1)} %bitcast.55), calls=%async_computation.3 | async-start | bytes 4194304
  310.3 5.9 copy-start.41
  310.3 5.9 copy-start.21
  310.3 5.9 copy-start.18
  316.3 2.8 copy-start.26
  319.1 1.8 copy-start.13
  319.1 2.1 copy-start.14
  319.1 2.1 copy-start.16
  319.2 2.1 copy-start.17
  321.2 28.7 %copy-start.25 = (bf16[1024,2048]{1,0:T(8,128)(2,1)S(1)}, bf16[1024,2048]{1,0:T(8,128)(2,1)}, u32[]{:S(2)}) copy-start(bf16[1024,2048]{1,0:T(8,128)(2,1)} %get-tuple-element.99) | copy-start | bytes 12582916
  349.9 3.0 copy-start.7
  349.9 2.1 copy-start.34
  351.5 2.0 copy-start.33
  354.5 2.0 copy-start.48
  354.5 13.8 %slice-start = ((s8[6291456]{0:T(1024)(128)(4,1)}), s8[4194304]{0:T(1024)(128)(4,1)S(1)}, s32[]{:S(2)}) async-start(s8[6291456]{0:T(1024)(128)(4,1)} %bitcast.53), calls=%async_computation | async-start | bytes 8388608
  354.8 7.6 %copy-start.40 = (bf16[192,1024]{1,0:T(8,128)(2,1)}, bf16[192,1024]{1,0:T(8,128)(2,1)S(1)}, u32[]{:S(2)}) copy-start(bf16[192,1024]{1,0:T(8,128)(2,1)S(1)} %get-tuple-element.151.refs_16_) | copy-start | bytes 1179652
  356.5 11.8 %slice-start.1 = ((s8[6291456]{0:T(1024)(128)(4,1)}), s8[2097152]{0:T(1024)(128)(4,1)S(1)}, s32[]{:S(2)}) async-start(s8[6291456]{0:T(1024)(128)(4,1)} %bitcast.53), calls=%async_computation.1 | async-start | bytes 4194304
  362.4 5.9 copy-start.42
  362.4 5.9 copy-start.22
  362.4 5.9 copy-start.19
  368.4 2.7 copy-start.24
  371.1 1.7 copy-start.11
  371.1 2.0 copy-start.12
  371.1 2.0 copy-start.15
  373.1 29.1 %copy-start.23 = (bf16[1024,2048]{1,0:T(8,128)(2,1)S(1)}, bf16[1024,2048]{1,0:T(8,128)(2,1)}, u32[]{:S(2)}) copy-start(bf16[1024,2048]{1,0:T(8,128)(2,1)} %get-tuple-element.121) | copy-start | bytes 12582916
  402.2 3.0 copy-start.10
  402.2 2.1 copy-start.32
  403.8 1.7 copy-start.31
  407.6 219.7 %collective-permute-start.4 = (bf16[192,1024]{1,0:T(8,128)(2,1)}, bf16[192,1024]{1,0:T(8,128)(2,1)S(1)}, u32[]{:S(2)}, u32[]{:S(2)}) collective-permute-start(bf16[192,1024]{1,0:T(8,128)(2,1)} %fusion.10), channel_id=1, source_target_pairs={{4,2},{2,4},{0,0},{6,6},{5,3},{3,5},{1,1},{7,7},{12,10},{10,12},{8... | collective-permute-start | bytes 1179656 | tf_op jit(solution)/shard_map/ppermute | solution.py:1522
  625.1 3.7 copy-start.44
  625.1 4.6 copy-start.46
  627.3 3.3 copy-start.45
  628.1 3.3 copy-start.43
  629.8 2.6 copy-start.38
  631.4 2.1 copy-start.37
  633.5 2.0 copy-start.36
  (14 other events, 21.8 us)

commit v8 on v7

--- a/solution.py
+++ b/solution.py
@@ -830,7 +830,7 @@
 
 
 SLOTS = 4
-AHEAD = 6
+AHEAD = 4
 PIECES = 15
 LEFT_BLOCKS = (3, 2, 1, 1)
 LEFT_FIRST = (0, 3, 5, 11)

time: 646 us -> 646 us (level)
  no operation moved by 1% of the time
where the time goes in v8:
time: 646 us; the launch traced here: 637 us
  Pallas kernels  554 us (86%)
  matrix products  39.6 us (6%)
  local copies, waits for them, and re-layouts  21.3 us (3%)
  starting transfers between devices  10.6 us (2%)
  other arithmetic  9.17 us (1%)
    pallas_call x1, Pallas kernels, forward(): pl.pallas_call(functools.partial(forward_kernel, chunks, nx, nz), out_sha...  282 us
    pallas_call x1, Pallas kernels, reduce_weights(): pl.pallas_call(functools.partial(reduce_kernel, nx, nz, layers), out_shap...  214 us
    pallas_call x2, Pallas kernels, attend_back(): pl.pallas_call(functools.partial(attend_back_kernel, m), out_shape=[jax.S...  57.7 us
    dot_general x14, matrix products, product_back(): lax.dot_general(grad, right, (((1,), (1,)), ((), ())), preferred_element_...  39.6 us
    unnamed x124, local copies, waits for them, and re-layouts  14.8 us
  transfers between devices with their start and end apart: 8, of which 0 were waited for; matrix products, arithmetic and copies ran while one was open for 9% of the time, Pallas kernels for 87%

profile of v8, /device:TPU:0, one launch (start us, length us, event | category | flops | bytes accessed | tf_op | source)
XLA Modules:
  0.0 637.1 jit_solution(17751931333195704469)
XLA Ops:
  0.6 1.3 collective-permute-start
  2.0 1.6 collective-permute-start.2
  3.6 0.7 pad_maximum_fusion.2
  4.3 0.7 pad_maximum_fusion.3
  6.2 0.8 copy.31.refs_11_.place_q
  8.0 0.8 pad_maximum_fusion
  8.8 282.2 %shard_map.237 = (bf16[256,1024]{1,0:T(8,128)(2,1)}, bf16[1024,1024]{1,0:T(8,128)(2,1)}, bf16[1024,1024]{1,0:T(8,128)(2,1)}, bf16[1024,2048]{1,0:T(8,128)(2,1)},...) custom-call(bf16[16,1024]{1,0:T(8,128)(2,1)} %copy-done.47, ...), custom_call_target="tpu_custom_call" | custom-call | tf_op jit(solution)/shard_map/pallas_call | solution.py:787
  291.0 1.4 multiply_reduce_fusion.8
  292.5 0.8 fusion.28
  293.3 1.3 multiply_reduce_fusion.6
  294.6 1.3 multiply_reduce_fusion.4
  296.2 2.0 collective-permute-start.6
  298.3 1.8 collective-permute-start.1
  300.1 0.9 fusion.27
  301.2 2.0 collective-permute-start.5
  303.2 7.1 %multiply_convert_fusion.1 = (bf16[192,3072]{1,0:T(8,128)(2,1)S(1)}, bf16[192,3072]{1,0:T(8,128)(2,1)S(1)}) fusion(f32[192,3072]{1,0:T(8,128)} %get-tuple-element.86, f32[192,3072]{1,0:T(8,128)} %get-tuple-element.85, bf16[192,1024]{1,0:T(8,128)(2,1)S(1)} %fusion.15.refs_5_, bf16[3072,1024]{1,0:T(8,128)(2,1)} %get-tuple-element.84), kind=kOutput, calls=%fused_computation.12 | convolution fusion | flops 1216217088 | bytes 13762560 | tf_op jit(solution)/shard_map/dot_general | solution.py:1372
  310.4 5.9 fusion.29
  316.3 2.5 multiply_reduce_fusion
  319.2 1.5 convolution_convert_fusion.1.d_att
  321.2 28.7 %shard_map.238 = (bf16[192,2048]{1,0:T(8,128)(2,1)S(1)}, bf16[192,1024]{1,0:T(8,128)(2,1)S(1)}, bf16[192,1024]{1,0:T(8,128)(2,1)S(1)}, f32[8,128]{1,0:T(8,128)S(1)}) custom-call(bf16[192,2048]{1,0:T(8,128)(2,1)S(1)} %copy-done.14, bf16[768,2048]{1,0:T(8,128)(2,1)} %get-tuple-element.92.kv, bf16[192,2048]{1,0:T(8,128)(2,1)S(1)} %convolution_convert_fusion.1.d_att, ...), custom_call_target="tpu_custom_call" | custom-call | tf_op jit(solution)/shard_map/pallas_call | solution.py:203
  349.9 1.5 fusion.30
  352.1 0.9 convolution_add_fusion.3
  353.5 1.1 multiply_reduce_fusion.1
  355.1 1.4 copy-done.48
  356.5 5.9 multiply_convert_fusion
  362.4 5.9 fusion.31
  368.4 2.4 multiply_reduce_fusion.2
  371.1 1.5 convolution_convert_fusion.d_att
  373.1 29.1 %shard_map.239 = (bf16[192,2048]{1,0:T(8,128)(2,1)S(1)}, bf16[192,1024]{1,0:T(8,128)(2,1)S(1)}, bf16[192,1024]{1,0:T(8,128)(2,1)S(1)}, f32[8,128]{1,0:T(8,128)S(1)}) custom-call(bf16[192,2048]{1,0:T(8,128)(2,1)S(1)} %copy-done.12, bf16[768,2048]{1,0:T(8,128)(2,1)} %get-tuple-element.112.kv, bf16[192,2048]{1,0:T(8,128)(2,1)S(1)} %convolution_convert_fusion.d_att, ...), custom_call_target="tpu_custom_call" | custom-call | tf_op jit(solution)/shard_map/pallas_call | solution.py:203
  402.2 1.5 fusion.32
  404.3 0.9 convolution_add_fusion.1
  405.5 1.1 fusion.14
  406.6 1.0 fusion.10
  407.6 1.6 collective-permute-start.4
  410.0 0.9 copy-done.30
  410.8 214.3 %shard_map.240 = (f32[2,192,1024]{2,1,0:T(8,128)}, f32[2,128,1024]{2,1,0:T(8,128)}, f32[2,64,3072]{2,1,0:T(8,128)}, f32[2,64,3072]{2,1,0:T(8,128)}, f32[2,64,204...) custom-call(bf16[192,1024]{1,0:T(8,128)(2,1)} %collective-permute-done.5.refs_0_, ...), custom_call_target="tpu_custom_call" | custom-call | tf_op jit(solution)/shard_map/pallas_call | solution.py:1293
  625.2 0.9 reshape.162
  626.0 0.6 constant_dynamic-slice_fusion.1
  627.3 0.7 copy.52
  628.1 0.7 copy.53
  628.8 1.0 copy.54
  629.8 0.8 copy.55
  630.6 0.8 copy.56
  631.4 1.0 copy.57
  632.3 1.1 copy.58
  633.5 1.1 copy.59
  634.6 0.8 copy-done.36
  635.5 1.1 copy.60
  (156 shorter events, 8.1 us)
Async XLA Ops:
  0.6 5.0 collective-permute-start
  2.0 299.0 %collective-permute-start.2 = (bf16[1,192,1024]{2,1,0:T(8,128)(2,1)}, bf16[1,192,1024]{2,1,0:T(8,128)(2,1)S(1)}, u32[]{:S(2)}, u32[]{:S(2)}) collective-permute-start(bf16[1,192,1024]{2,1,0:T(8,128)(2,1)} %param.29), channel_id=1, source_target_pairs={{4,2},{2,4},{0,0},{6,6},{5,3},{3,5},{1,1},{7,7},{12,10},{10,12},{8... | collective-permute-start | bytes 1179656 | tf_op jit(solution)/shard_map/ppermute | solution.py:1522
  5.7 3.1 copy-start.47
  291.0 4.8 copy-start.35
  291.0 5.0 copy-start.27
  295.9 76.8 %collective-permute-start.3 = (bf16[192,5120]{1,0:T(8,128)(2,1)S(1)}, bf16[192,5120]{1,0:T(8,128)(2,1)}, u32[]{:S(2)}, u32[]{:S(2)}) collective-permute-start(bf16[192,5120]{1,0:T(8,128)(2,1)S(1)} %copy-done.35), channel_id=1, source_target_pairs={{0,16},{16,0},{1,17},{17,1},{2,18},{18,2},{3,19},{19,3},{4,20},{20... | collective-permute-start | bytes 5898248 | tf_op jit(solution)/shard_map/ppermute | solution.py:1376
  296.2 113.8 %collective-permute-start.6 = (bf16[192,5120]{1,0:T(8,128)(2,1)}, bf16[192,5120]{1,0:T(8,128)(2,1)}, u32[]{:S(2)}, u32[]{:S(2)}) collective-permute-start(bf16[192,5120]{1,0:T(8,128)(2,1)} %get-tuple-element.127.refs_1_), channel_id=1, source_target_pairs={{0,16},{16,0},{1,17},{17,1},{2,18},{18,2},{3,19},{19,3},{4,20},{20... | collective-permute-start | bytes 5898248 | tf_op jit(solution)/shard_map/ppermute | solution.py:1376
  298.2 111.8 %collective-permute-start.7 = (bf16[192,2048]{1,0:T(8,128)(2,1)}, bf16[192,2048]{1,0:T(8,128)(2,1)S(1)}, u32[]{:S(2)}, u32[]{:S(2)}) collective-permute-start(bf16[192,2048]{1,0:T(8,128)(2,1)} %get-tuple-element.128.refs_2_), channel_id=1, source_target_pairs={{0,16},{16,0},{1,17},{17,1},{2,18},{18,2},{3,19},{19,3},{4,20},{20... | collective-permute-start | bytes 2359304 | tf_op jit(solution)/shard_map/ppermute | solution.py:1376
  298.3 74.4 %collective-permute-start.1 = (bf16[192,1024]{1,0:T(8,128)(2,1)}, bf16[192,1024]{1,0:T(8,128)(2,1)S(1)}, u32[]{:S(2)}, u32[]{:S(2)}) collective-permute-start(bf16[192,1024]{1,0:T(8,128)(2,1)} %get-tuple-element.83), channel_id=1, source_target_pairs={{4,2},{2,4},{0,0},{6,6},{5,3},{3,5},{1,1},{7,7},{12,10},{10,12},{8... | collective-permute-start | bytes 1179656 | tf_op jit(solution)/shard_map/ppermute | solution.py:1522
  301.0 15.2 %slice-start.2 = ((s8[6291456]{0:T(1024)(128)(4,1)}), s8[4194304]{0:T(1024)(128)(4,1)S(1)}, s32[]{:S(2)}) async-start(s8[6291456]{0:T(1024)(128)(4,1)} %bitcast.55), calls=%async_computation.2 | async-start | bytes 8388608
  301.1 9.2 %copy-start.39 = (bf16[192,1024]{1,0:T(8,128)(2,1)}, bf16[192,1024]{1,0:T(8,128)(2,1)S(1)}, u32[]{:S(2)}) copy-start(bf16[192,1024]{1,0:T(8,128)(2,1)S(1)} %fusion.15.refs_5_) | copy-start | bytes 1179652
  301.2 108.8 %collective-permute-start.5 = (bf16[192,1024]{1,0:T(8,128)(2,1)S(1)}, bf16[192,1024]{1,0:T(8,128)(2,1)}, u32[]{:S(2)}, u32[]{:S(2)}) collective-permute-start(bf16[192,1024]{1,0:T(8,128)(2,1)S(1)} %fusion.15.refs_5_), channel_id=1, source_target_pairs={{0,16},{16,0},{1,17},{17,1},{2,18},{18,2},{3,19},{19,3},{4,20},{20... | collective-permute-start | bytes 1179656 | tf_op jit(solution)/shard_map/ppermute | solution.py:1376
  303.2 13.1 %slice-start.3 = ((s8[6291456]{0:T(1024)(128)(4,1)}), s8[2097152]{0:T(1024)(128)(4,1)S(1)}, s32[]{:S(2)}) async-start(s8[6291456]{0:T(1024)(128)(4,1)} %bitcast.55), calls=%async_computation.3 | async-start | bytes 4194304
  310.3 5.9 copy-start.41
  310.3 5.9 copy-start.21
  310.3 5.9 copy-start.18
  316.3 2.8 copy-start.26
  319.1 1.8 copy-start.13
  319.1 2.1 copy-start.14
  319.1 2.1 copy-start.16
  319.2 2.1 copy-start.17
  321.2 28.7 %copy-start.25 = (bf16[1024,2048]{1,0:T(8,128)(2,1)S(1)}, bf16[1024,2048]{1,0:T(8,128)(2,1)}, u32[]{:S(2)}) copy-start(bf16[1024,2048]{1,0:T(8,128)(2,1)} %get-tuple-element.99) | copy-start | bytes 12582916
  349.9 3.0 copy-start.7
  349.9 2.1 copy-start.34
  351.5 2.0 copy-start.33
  354.5 2.0 copy-start.48
  354.5 13.8 %slice-start = ((s8[6291456]{0:T(1024)(128)(4,1)}), s8[4194304]{0:T(1024)(128)(4,1)S(1)}, s32[]{:S(2)}) async-start(s8[6291456]{0:T(1024)(128)(4,1)} %bitcast.53), calls=%async_computation | async-start | bytes 8388608
  354.8 7.6 %copy-start.40 = (bf16[192,1024]{1,0:T(8,128)(2,1)}, bf16[192,1024]{1,0:T(8,128)(2,1)S(1)}, u32[]{:S(2)}) copy-start(bf16[192,1024]{1,0:T(8,128)(2,1)S(1)} %get-tuple-element.151.refs_16_) | copy-start | bytes 1179652
  356.5 11.8 %slice-start.1 = ((s8[6291456]{0:T(1024)(128)(4,1)}), s8[2097152]{0:T(1024)(128)(4,1)S(1)}, s32[]{:S(2)}) async-start(s8[6291456]{0:T(1024)(128)(4,1)} %bitcast.53), calls=%async_computation.1 | async-start | bytes 4194304
  362.4 5.9 copy-start.42
  362.4 5.9 copy-start.22
  362.4 5.9 copy-start.19
  368.4 2.7 copy-start.24
  371.1 1.7 copy-start.11
  371.1 2.0 copy-start.12
  371.1 2.0 copy-start.15
  373.1 29.1 %copy-start.23 = (bf16[1024,2048]{1,0:T(8,128)(2,1)S(1)}, bf16[1024,2048]{1,0:T(8,128)(2,1)}, u32[]{:S(2)}) copy-start(bf16[1024,2048]{1,0:T(8,128)(2,1)} %get-tuple-element.121) | copy-start | bytes 12582916
  402.2 3.0 copy-start.10
  402.2 2.1 copy-start.32
  403.8 1.7 copy-start.31
  407.6 219.7 %collective-permute-start.4 = (bf16[192,1024]{1,0:T(8,128)(2,1)}, bf16[192,1024]{1,0:T(8,128)(2,1)S(1)}, u32[]{:S(2)}, u32[]{:S(2)}) collective-permute-start(bf16[192,1024]{1,0:T(8,128)(2,1)} %fusion.10), channel_id=1, source_target_pairs={{4,2},{2,4},{0,0},{6,6},{5,3},{3,5},{1,1},{7,7},{12,10},{10,12},{8... | collective-permute-start | bytes 1179656 | tf_op jit(solution)/shard_map/ppermute | solution.py:1522
  625.1 3.7 copy-start.44
  625.1 4.6 copy-start.46
  627.3 3.3 copy-start.45
  628.1 3.3 copy-start.43
  629.8 2.6 copy-start.38
  631.4 2.1 copy-start.37
  633.5 2.0 copy-start.36
  (14 other events, 21.8 us)
